TPU v7x, 128 devices: a whole 4x4x4 slice. The times are simulated.
128 devices in a mesh: row: 16 (over y, z_hi, core), col: 8 (over x, z_lo).
Axes of the slice: x: 4, y: 4, z: 4 (z_hi: 2, z_lo: 2; z = z_hi * 2 + z_lo), core: 2. Of those that a mesh axis runs over, the one named last changes fastest.
Arguments:
- embeddings: bfloat16 [65536, 1024], P('row'), may hold values from -1 to 1
- labels: int32 [65536], P(('row', 'col')), may hold values from 0 to 127
- pair_rows: int32 [16, 8, 24], P('row', 'col'), may hold values from 0 to 7, as said below
- pair_cols: int32 [16, 8, 24], P('row', 'col'), may hold values from 0 to 15, as said below
- pair_count: int32 [16, 8], P('row', 'col'), may hold values from 1 to 24, as said below
Outputs:
- vectors: float32 [64, 65536], P(None, ('row', 'col'))
Inputs may be any that keep to these rules, and one draw needn't show every extreme that they name: `pair_rows`: within one list the pairs (t, q) are distinct; slot 0 of slab r and block c is t = c, q = r. `pair_cols`: see pair_rows. `pair_count`: some device has exactly 24 live slots in every draw.
All inputs are finite; a program needn't handle non-finite values.
Results may differ from a plain program's by a relative error of at most 0.0036.
Values may be sent and summed in bfloat16 or wider, within the bound.
No kernel may reach another device: no remote copies, remote signals or barrier semaphores. Data moves between devices by JAX's collectives and lax.ppermute only.
A program may use at most 128 MiB of HBM per device.

v0:
```python
import jax
import jax.numpy as jnp
from jax import lax
from jax.sharding import PartitionSpec as P

TILE = 512
K = 64
ITERS = 2
PAIRS = 24


KERNEL_SCALE = 0.5


def affinity(left_rows, left_sq, right_rows, right_sq, on_diagonal):
    inner_dot = jnp.dot(left_rows, right_rows.T, preferred_element_type=jnp.float32)
    distance = left_sq[:, None] + right_sq[None, :] - 2.0 * inner_dot
    kernel = jnp.exp(-distance / KERNEL_SCALE)
    extent = kernel.shape[0]
    diagonal_mask = lax.broadcasted_iota(jnp.int32, (extent, extent), 0) == lax.broadcasted_iota(
        jnp.int32, (extent, extent), 1
    )
    kernel = jnp.where(jnp.logical_and(on_diagonal, diagonal_mask), 0.0, kernel)
    return kernel.astype(jnp.bfloat16)


def shards(embeddings, labels, pair_rows, pair_cols, pair_count):
    slab_tiles = lax.axis_size("col")
    block_tiles = lax.axis_size("row")
    block_index = lax.axis_index("col")
    slab_index = lax.axis_index("row")
    row_tiles = pair_rows[0, 0]
    col_tiles = pair_cols[0, 0]
    live_count = pair_count[0, 0]
    slab_squares = jnp.sum(jnp.square(embeddings.astype(jnp.float32)), axis=1)
    own_rows = lax.dynamic_slice_in_dim(embeddings, block_index * TILE, TILE, 0)
    column_rows = lax.all_gather(own_rows, "row", axis=0, tiled=True)
    column_squares = jnp.sum(jnp.square(column_rows.astype(jnp.float32)), axis=1)

    def build(position, carried):
        tile_store, partial_value = carried
        row_tile = row_tiles[position]
        col_tile = col_tiles[position]
        left_rows = lax.dynamic_slice_in_dim(embeddings, row_tile * TILE, TILE, 0)
        left_sq = lax.dynamic_slice_in_dim(slab_squares, row_tile * TILE, TILE, 0)
        right_rows = lax.dynamic_slice_in_dim(column_rows, col_tile * TILE, TILE, 0)
        right_sq = lax.dynamic_slice_in_dim(column_squares, col_tile * TILE, TILE, 0)
        kernel = affinity(
            left_rows,
            left_sq,
            right_rows,
            right_sq,
            jnp.logical_and(col_tile == slab_index, row_tile == block_index),
        )
        tile_store = lax.dynamic_update_index_in_dim(tile_store, kernel, position, 0)
        current = lax.dynamic_slice_in_dim(partial_value, row_tile * TILE, TILE, 0)
        partial_value = lax.dynamic_update_slice_in_dim(
            partial_value, current + jnp.sum(kernel.astype(jnp.float32), axis=1), row_tile * TILE, 0
        )
        return (tile_store, partial_value)

    tile_store = jnp.zeros((PAIRS, TILE, TILE), jnp.bfloat16)
    partial_value = jnp.zeros((slab_tiles * TILE,), jnp.float32)
    tile_store, partial_value = lax.fori_loop(0, live_count, build, (tile_store, partial_value))
    summed = lax.psum(partial_value, "col")
    degree = lax.dynamic_slice_in_dim(summed, block_index * TILE, TILE, 0)
    row_total = block_tiles * slab_tiles * TILE
    inv_root = lax.rsqrt(degree)
    root_degree = jnp.sqrt(degree)
    local_total = jnp.sum(degree)
    label_sign = jnp.where(labels < K, 1.0, -1.0).astype(jnp.float32)
    vectors = ((labels % K)[None, :] == lax.broadcasted_iota(jnp.int32, (K, TILE), 0)).astype(
        jnp.float32
    ) * label_sign[None, :]
    for iteration in range(ITERS):
        scaled = (vectors * inv_root[None, :]).astype(jnp.bfloat16)
        column_block = lax.all_gather(scaled, "row", axis=1, tiled=True)

        def add_slot(position, running):
            row_tile = row_tiles[position]
            vec_piece = lax.dynamic_slice_in_dim(column_block, col_tiles[position] * TILE, TILE, 1)
            contribution = lax.dot_general(
                vec_piece,
                tile_store[position],
                (((1,), (1,)), ((), ())),
                preferred_element_type=jnp.float32,
            )
            current = lax.dynamic_slice_in_dim(running, row_tile * TILE, TILE, 1)
            return lax.dynamic_update_slice_in_dim(
                running, current + contribution, row_tile * TILE, 1
            )

        running = jnp.zeros((K, slab_tiles * TILE), jnp.float32)
        running = lax.fori_loop(0, live_count, add_slot, running)
        image_block = (
            lax.psum_scatter(running, "col", scatter_dimension=1, tiled=True) * inv_root[None, :]
        )
        local_top = jnp.dot(image_block, root_degree, precision=lax.Precision.HIGHEST)
        top_weight, degree_total = lax.psum((local_top, local_total), ("row", "col"))
        projected = image_block - top_weight[:, None] * root_degree[None, :] / degree_total
        gram_matrix = lax.psum(
            jnp.dot(projected, projected.T, precision=lax.Precision.HIGHEST), ("row", "col")
        )
        gram_matrix = gram_matrix / row_total
        cholesky_factor = jnp.linalg.cholesky(gram_matrix)
        vectors = jax.scipy.linalg.solve_triangular(cholesky_factor, projected, lower=True)
    return vectors


def solution(mesh):
    in_specs = (
        P("row", None),
        P(("row", "col")),
        P("row", "col", None),
        P("row", "col", None),
        P("row", "col"),
    )
    out_specs = P(None, ("row", "col"))
    return jax.shard_map(shards, mesh=mesh, in_specs=in_specs, out_specs=out_specs, check_vma=False)
```

profile of v0, /device:TPU:1, one launch (start us, length us, event | category | flops | bytes accessed | tf_op | source)
XLA Modules:
  0.0 1050.5 jit_solution(15516947482034630522)
XLA Ops:
  6.5 2.3 constant_dynamic-slice_fusion
  10.3 5.1 multiply_reduce_fusion.1
  15.4 108.4 %all-gather.4.cloned.1.call-done = bf16[8192,1024]{1,0:T(8,128)(2,1)} async-done(((bf16[512,1024]{1,0:T(8,128)(2,1)}), bf16[8192,1024]{1,0:T(8,128)(2,1)}) %all-gather.4.cloned.1.call-update) | async-done | bytes 16777232 | tf_op jit(solution)/shard_map/all_gather | solution.py:37
  123.8 7.2 multiply_reduce_fusion
  131.0 5.9 broadcast_in_dim.25.clone
  136.9 34.6 %while.32 = (s32[]{:T(128)}, bf16[24,512,512]{2,1,0:T(8,128)(2,1)}, f32[4096]{0:T(1024)S(1)}, s32[]{:T(128)}, s32[24]{0:T(128)S(1)}, /*index=5*/s32[]{:T(128)}, ...) while((s32[]{:T(128)}, bf16[24,512,512]{2,1,0:T(8,128)(2,1)}, ...), condition=%wide.region_4.5_spmd, body=%wide.region_2.4_spmd.sunk | while | flops 539754496 | bytes 4739433 | solution.py:64
  141.7 2.5 convert_reduce_fusion.2
  150.1 2.5 convert_reduce_fusion.2
  158.6 2.5 convert_reduce_fusion.2
  167.1 2.5 convert_reduce_fusion.2
  171.5 77.2 %psum.45 = f32[4096]{0:T(1024)S(1)} all-reduce(f32[4096]{0:T(1024)S(1)} %get-tuple-element.147), channel_id=1, replica_groups=mesh['row'=16,'col'=8] {'col'}, use_global_device_ids=true, to_apply=%region_5.6 | all-reduce | flops 4096 | bytes 32768 | tf_op jit(solution)/shard_map/psum | solution.py:65
  250.1 164.6 %all-gather.6.cloned.1.call-done = bf16[64,8192]{1,0:T(8,128)(2,1)} async-done(((bf16[64,512]{1,0:T(8,128)(2,1)}), bf16[64,8192]{1,0:T(8,128)(2,1)}) %all-gather.6.cloned.1.call-update) | async-done | bytes 1048592 | tf_op jit(solution)/shard_map/all_gather | solution.py:77
  414.8 18.8 %while.33 = (s32[]{:T(128)}, f32[64,4096]{1,0:T(8,128)S(1)}, s32[]{:T(128)}, s32[24]{0:T(128)S(1)}, s32[24]{0:T(128)S(1)}, /*index=5*/bf16[64,8192]{1,0:T(8,128)...) while((s32[]{:T(128)}, f32[64,4096]{1,0:T(8,128)S(1)}, ...), condition=%wide.region_7.8_spmd, body=%wide.region_6.7_spmd.sunk | while | flops 33587212 | bytes 852255 | solution.py:94
  422.4 1.4 fusion.47
  431.5 1.4 fusion.47
  434.6 123.4 %reduce-scatter.3.cloned.1.call-done = f32[64,512]{1,0:T(8,128)} async-done(((f32[64,4096]{1,0:T(8,128)}), f32[64,512]{1,0:T(8,128)}) %reduce-scatter.3.cloned.1.call-update) | async-done | bytes 131088 | tf_op jit(solution)/shard_map/reduce_scatter | solution.py:96
  559.1 68.0 %all-reduce = (f32[]{:T(128)}, f32[64]{0:T(128)S(1)}) all-reduce(f32[]{:T(128)} %get-tuple-element.222, f32[64]{0:T(128)S(1)} %convolution_bitcast_fusion.1), channel_id=1, replica_groups=mesh['row'=16,'col'=8] {'row','col'}, use_global_device_ids=true, to_apply=%region_11.12 | all-reduce | flops 65 | bytes 520 | tf_op jit(solution)/shard_map/psum | solution.py:99
  627.1 1.9 fusion.35
  629.0 64.0 %psum.48 = f32[64,64]{0,1:T(8,128)S(1)} all-reduce(f32[64,64]{0,1:T(8,128)S(1)} %fusion.35), channel_id=1, replica_groups=mesh['row'=16,'col'=8] {'row','col'}, use_global_device_ids=true, to_apply=%region_12.13 | all-reduce | flops 4096 | bytes 32768 | tf_op jit(solution)/shard_map/psum | solution.py:101
  693.2 5.8 cholesky.44
  700.4 4.9 custom-call.6
  705.3 2.5 fusion.20
  707.8 42.8 %all-gather.8.cloned.1.call-done = bf16[64,8192]{1,0:T(8,128)(2,1)} async-done(((bf16[64,512]{1,0:T(8,128)(2,1)}), bf16[64,8192]{1,0:T(8,128)(2,1)}) %all-gather.8.cloned.1.call-update) | async-done | bytes 1048592 | tf_op jit(solution)/shard_map/all_gather | solution.py:77
  750.7 18.8 %while.34 = (s32[]{:T(128)}, f32[64,4096]{1,0:T(8,128)S(1)}, s32[]{:T(128)}, s32[24]{0:T(128)S(1)}, s32[24]{0:T(128)S(1)}, /*index=5*/bf16[64,8192]{1,0:T(8,128)...) while((s32[]{:T(128)}, f32[64,4096]{1,0:T(8,128)S(1)}, ...), condition=%wide.region_16.19_spmd, body=%wide.region_15.18_spmd.sunk | while | flops 33587212 | bytes 852255 | solution.py:94
  758.4 1.4 fusion.50
  770.5 123.9 %reduce-scatter.5.cloned.1.call-done = f32[64,512]{1,0:T(8,128)} async-done(((f32[64,4096]{1,0:T(8,128)}), f32[64,512]{1,0:T(8,128)}) %reduce-scatter.5.cloned.1.call-update) | async-done | bytes 131088 | tf_op jit(solution)/shard_map/reduce_scatter | solution.py:96
  895.5 67.7 %psum.49 = f32[64]{0:T(128)S(1)} all-reduce(f32[64]{0:T(128)S(1)} %convolution_bitcast_fusion), channel_id=1, replica_groups=mesh['row'=16,'col'=8] {'row','col'}, use_global_device_ids=true, to_apply=%region_18.21 | all-reduce | flops 64 | bytes 512 | tf_op jit(solution)/shard_map/psum | solution.py:99
  963.2 1.9 fusion.36
  965.2 64.1 %psum.50 = f32[64,64]{0,1:T(8,128)S(1)} all-reduce(f32[64,64]{0,1:T(8,128)S(1)} %fusion.36), channel_id=1, replica_groups=mesh['row'=16,'col'=8] {'row','col'}, use_global_device_ids=true, to_apply=%region_19.22 | all-reduce | flops 4096 | bytes 32768 | tf_op jit(solution)/shard_map/psum | solution.py:101
  1029.3 5.8 cholesky.55
  1036.5 4.9 custom-call.7
  1041.4 2.5 fusion.27
  (88 shorter events, 37.1 us)
Async XLA Ops:
  6.5 117.2 %all-gather.4.cloned.1.call-start = ((), (), s32[]{:S(2)}) async-start(), calls=%async_computation.2 | async-start | bytes 17825792 | tf_op jit(solution)/shard_map/all_gather | solution.py:37
  8.8 405.8 %all-gather.6.cloned.1.call-start = ((), (), s32[]{:S(2)}) async-start(), calls=%async_computation.3 | async-start | bytes 1114112 | tf_op jit(solution)/shard_map/all_gather | solution.py:77
  15.4 121.5 %copy-start.2 = (s32[1,1,24]{2,1,0:T(1,128)S(1)}, s32[1,1,24]{2,1,0:T(1,128)}, u32[]{:S(2)}) copy-start(s32[1,1,24]{2,1,0:T(1,128)} %param.17) | copy-start | bytes 292
  15.4 121.5 %copy-start.3 = (s32[1,1,24]{2,1,0:T(1,128)S(1)}, s32[1,1,24]{2,1,0:T(1,128)}, u32[]{:S(2)}) copy-start(s32[1,1,24]{2,1,0:T(1,128)} %param.16) | copy-start | bytes 292
  250.0 308.0 %reduce-scatter.3.cloned.1.call-start = ((), (), s32[]{:S(2)}) async-start(), calls=%async_computation.4 | async-start | bytes 1179648 | tf_op jit(solution)/shard_map/reduce_scatter | solution.py:96
  433.5 1.0 copy-start.1
  434.5 316.1 %all-gather.8.cloned.1.call-start = ((), (), s32[]{:S(2)}) async-start(), calls=%async_computation.5 | async-start | bytes 1114112 | tf_op jit(solution)/shard_map/all_gather | solution.py:77
  707.8 186.6 %reduce-scatter.5.cloned.1.call-start = ((), (), s32[]{:S(2)}) async-start(), calls=%async_computation.6 | async-start | bytes 1179648 | tf_op jit(solution)/shard_map/reduce_scatter | solution.py:96
  769.5 1.0 copy-start
Sparse Core Ops, SparseCore 0:
  9.8 113.9 all-gather.3
  250.2 164.4 all-gather.5
  434.7 123.3 reduce-scatter.2
  707.9 42.6 all-gather.7
  770.6 123.7 reduce-scatter.4
where the time goes:
time: 1050 us
  waiting for transfers between devices  563 us (54%)
  blocking collectives  341 us (32%)
  other arithmetic  39.8 us (4%)
  matrix products  31.9 us (3%)
  loops' own time  31.1 us (3%)
  local copies, waits for them, and re-layouts  30 us (3%)
  between operations  13.3 us (1%)
    reduce_scatter x2, waiting for transfers between devices, shards(): lax.psum_scatter(running, 'col', scatter_dimension=1, tiled=True)  247 us
    all_gather x2, waiting for transfers between devices, shards(): column_block = lax.all_gather(scaled, 'row', axis=1, tiled=True)  207 us
    psum x2, blocking collectives, shards(): lax.psum((local_top, local_total), ('row', 'col'))  136 us
    psum x2, blocking collectives, shards(): lax.psum(jnp.dot(projected, projected.T, precision=lax.Precision.HIGHEST)...  128 us
    all_gather x1, waiting for transfers between devices, shards(): column_rows = lax.all_gather(own_rows, 'row', axis=0, tiled=True)  108 us
    psum x1, blocking collectives, shards(): summed = lax.psum(partial_value, 'col')  77.2 us
  transfers between devices with their start and end apart: 5, of which 5 were waited for; matrix products, arithmetic and copies ran while one was open for 1% of the time, Pallas kernels for 0%

commit v1 on v0

v1 whole, which is shorter than its diff:
```python
import functools

import jax
import jax.numpy as jnp
import numpy as np
from jax import lax
from jax.experimental import pallas as pl
from jax.experimental.pallas import tpu as pltpu
from jax.sharding import Mesh
from jax.sharding import PartitionSpec as P

TILE = 512
K = 64
ITERS = 2
PAIRS = 24
WIDTH = 1024
KERNEL_SCALE = 0.5
RATE = 2.0 / KERNEL_SCALE * float(np.log2(np.e))
F32 = jnp.float32
BF16 = jnp.bfloat16

ROW = ("y", "zh", "core")
COL = ("x", "zl")
CHIPS = ("y", "zh", "x", "zl")
SLAB_TILES = 8
BLOCK_TILES = 16
VMEM_LIMIT = 48 * 1024 * 1024


def build_kernel(info, slab, column, half_rows, tiles, degree, left, right, made, sem_in, sem_out):
    count = info[0]
    slab_index = info[1]
    block_index = info[2]
    degree[...] = jnp.zeros_like(degree)

    def fetches(position, slot):
        t = info[8 + position]
        q = info[8 + PAIRS + position]
        return (
            pltpu.make_async_copy(slab.at[t], left.at[slot], sem_in.at[0, slot]),
            pltpu.make_async_copy(column.at[q], right.at[slot], sem_in.at[1, slot]),
        )

    def store(position, slot):
        return pltpu.make_async_copy(made.at[slot], tiles.at[position], sem_out.at[slot])

    for copy in fetches(0, 0):
        copy.start()

    def step(position, carry):
        slot = lax.rem(position, 2)

        @pl.when(position + 1 < count)
        def _():
            for copy in fetches(position + 1, 1 - slot):
                copy.start()

        @pl.when(position >= 2)
        def _():
            store(position - 2, slot).wait()

        for copy in fetches(position, slot):
            copy.wait()
        t = info[8 + position]
        q = info[8 + PAIRS + position]
        b = right[slot]
        bf = b.astype(F32)
        half_b = 0.5 * jnp.sum(bf * bf, axis=1, keepdims=True)
        sums = []
        for n in range(2):
            lanes = pl.ds(n * 256, 256)
            inner = lax.dot_general(
                b, left[slot, lanes, :], (((1,), (1,)), ((), ())), preferred_element_type=F32
            )
            half_a = half_rows[pl.ds(t, 1), lanes]
            w = jnp.exp2(RATE * ((inner - half_a) - half_b)).astype(BF16)
            made[slot, :, lanes] = w
            sums.append(jnp.sum(w.astype(F32), axis=0, keepdims=True))
        on_diagonal = jnp.logical_and(t == block_index, q == slab_index)
        old = degree[pl.ds(t, 1), :]
        degree[pl.ds(t, 1), :] = old + jnp.concatenate(sums, axis=1)

        @pl.when(on_diagonal)
        def _():
            w = made[slot]
            same = lax.broadcasted_iota(jnp.int32, (TILE, TILE), 0) == lax.broadcasted_iota(
                jnp.int32, (TILE, TILE), 1
            )
            w = jnp.where(same, jnp.zeros_like(w), w)
            made[slot] = w
            degree[pl.ds(t, 1), :] = old + jnp.sum(w.astype(F32), axis=0, keepdims=True)

        store(position, slot).start()
        return carry

    lax.fori_loop(0, count, step, 0)

    @pl.when(count >= 2)
    def _():
        store(count - 2, lax.rem(count, 2)).wait()

    store(count - 1, lax.rem(count - 1, 2)).wait()


def build(info, slab, column, half_rows):
    any_space = pl.BlockSpec(memory_space=pl.ANY)
    return pl.pallas_call(
        build_kernel,
        out_shape=(
            jax.ShapeDtypeStruct((PAIRS, TILE, TILE), BF16),
            jax.ShapeDtypeStruct((SLAB_TILES, TILE), F32),
        ),
        in_specs=[
            pl.BlockSpec(memory_space=pltpu.SMEM),
            any_space,
            any_space,
            pl.BlockSpec(memory_space=pltpu.VMEM),
        ],
        out_specs=(any_space, pl.BlockSpec(memory_space=pltpu.VMEM)),
        scratch_shapes=[
            pltpu.VMEM((2, TILE, WIDTH), BF16),
            pltpu.VMEM((2, TILE, WIDTH), BF16),
            pltpu.VMEM((2, TILE, TILE), BF16),
            pltpu.SemaphoreType.DMA((2, 2)),
            pltpu.SemaphoreType.DMA((2,)),
        ],
        compiler_params=pltpu.CompilerParams(vmem_limit_bytes=VMEM_LIMIT),
        name="build_tiles",
    )(info, slab, column, half_rows)


def product_kernel(first, info, tiles, *refs):
    if first:
        labels, inv_root, running, held, sem = refs
    else:
        scaled, running, held, sem = refs
    count = info[0]
    running[...] = jnp.zeros_like(running)
    depth = held.shape[0]

    def fetch(position):
        slot = lax.rem(position, depth)
        return pltpu.make_async_copy(tiles.at[position], held.at[slot], sem.at[slot])

    for ahead in range(depth - 1):

        @pl.when(ahead < count)
        def _():
            fetch(ahead).start()

    def step(position, carry):
        @pl.when(position + depth - 1 < count)
        def _():
            fetch(position + depth - 1).start()

        t = info[8 + position]
        q = info[8 + PAIRS + position]
        if first:
            label = labels[pl.ds(q, 1), :]
            value = inv_root[pl.ds(q, 1), :]
            value = jnp.where(label < K, value, -value)
            mine = (label & (K - 1)) == lax.broadcasted_iota(jnp.int32, (K, TILE), 0)
            piece = jnp.where(mine, jnp.broadcast_to(value, (K, TILE)), 0.0).astype(BF16)
        else:
            piece = scaled[q]
        fetch(position).wait()
        running[t] += jnp.dot(
            piece, held[lax.rem(position, depth)], preferred_element_type=F32
        )
        return carry

    lax.fori_loop(0, count, step, 0)


def product(info, tiles, *operands):
    vmem = pl.BlockSpec(memory_space=pltpu.VMEM)
    return pl.pallas_call(
        functools.partial(product_kernel, len(operands) == 2),
        out_shape=jax.ShapeDtypeStruct((SLAB_TILES, K, TILE), F32),
        in_specs=[
            pl.BlockSpec(memory_space=pltpu.SMEM),
            pl.BlockSpec(memory_space=pl.ANY),
        ]
        + [vmem] * len(operands),
        out_specs=vmem,
        scratch_shapes=[
            pltpu.VMEM((4, TILE, TILE), BF16),
            pltpu.SemaphoreType.DMA((4,)),
        ],
        compiler_params=pltpu.CompilerParams(vmem_limit_bytes=VMEM_LIMIT),
        name="product",
    )(info, tiles, *operands)


def weigh_kernel(parts, inv_root, root, image, message):
    block = jnp.sum(parts[...], axis=0) * inv_root[...]
    image[...] = block
    heavy = jnp.concatenate([block, jnp.broadcast_to(root[...], (8, TILE))], axis=0)
    weights = lax.dot_general(
        heavy,
        heavy,
        (((1,), (1,)), ((), ())),
        precision=lax.Precision.HIGHEST,
        preferred_element_type=F32,
    )
    half = K // 2
    message[...] = jnp.concatenate(
        [
            weights[:half, :half],
            weights[half:K, :half],
            weights[half:K, half:K],
            weights[:half, K : K + 8],
            weights[half:K, K : K + 8],
            jnp.broadcast_to(weights[K : K + 1, K : K + 1], (half, 16)),
        ],
        axis=1,
    )


def weigh(parts, inv_root, root):
    vmem = pl.BlockSpec(memory_space=pltpu.VMEM)
    return pl.pallas_call(
        weigh_kernel,
        out_shape=(
            jax.ShapeDtypeStruct((K, TILE), F32),
            jax.ShapeDtypeStruct((K // 2, 128), F32),
        ),
        in_specs=[vmem] * 3,
        out_specs=(vmem, vmem),
        compiler_params=pltpu.CompilerParams(vmem_limit_bytes=VMEM_LIMIT),
        name="weigh",
    )(parts, inv_root, root)


def orthonormalize_kernel(scale, message, image, inv_root, root, out):
    half = K // 2
    sums = message[...]
    lower = sums[:, half : 2 * half]
    gram = jnp.concatenate(
        [
            jnp.concatenate([sums[:, :half], lower.T], axis=1),
            jnp.concatenate([lower, sums[:, 2 * half : 3 * half]], axis=1),
        ],
        axis=0,
    )
    top = jnp.concatenate([sums[:, 96:97], sums[:, 104:105]], axis=0)
    total = sums[:1, 112:113]
    rows = lax.broadcasted_iota(jnp.int32, (K, K), 0)
    columns = lax.broadcasted_iota(jnp.int32, (K, K), 1)
    across = jnp.sum(jnp.where(rows == columns, top, 0.0), axis=0, keepdims=True)
    gram = (gram - top * across / total) * scale
    work = jnp.concatenate([gram, (rows == columns).astype(F32)], axis=1)
    index = lax.broadcasted_iota(jnp.int32, (K, 1), 0)
    pivots = jnp.ones((K, 1), F32)
    for j in range(K):
        row = work[j : j + 1, :]
        pivot = work[j : j + 1, j : j + 1]
        column = work[:, j : j + 1]
        pivots = jnp.where(index == j, pivot, pivots)
        if j < K - 1:
            first = j // 8 * 8
            below = jnp.where(index[first:] > j, column[first:], 0.0)
            rest = work[first:] - below * (row / pivot)
            work = jnp.concatenate([work[:first], rest], axis=0) if first else rest
    inverse = work[:, K:] * lax.rsqrt(pivots)
    projected = image[...] - top * root[...] / total
    vectors = jnp.dot(
        inverse, projected, precision=lax.Precision.HIGHEST, preferred_element_type=F32
    )
    if out.dtype == BF16:
        out[...] = (vectors * inv_root[...]).astype(BF16)
    else:
        out[...] = vectors


def orthonormalize(message, image, inv_root, root, scale, dtype):
    vmem = pl.BlockSpec(memory_space=pltpu.VMEM)
    return pl.pallas_call(
        functools.partial(orthonormalize_kernel, scale),
        out_shape=jax.ShapeDtypeStruct((K, TILE), dtype),
        in_specs=[vmem] * 4,
        out_specs=vmem,
        compiler_params=pltpu.CompilerParams(vmem_limit_bytes=VMEM_LIMIT),
        name="orthonormalize",
    )(message, image, inv_root, root)


def swap_cores(value):
    return lax.ppermute(value, "core", [(0, 1), (1, 0)])


def share(value, axes):
    size = lax.axis_size(axes)
    return lax.all_to_all(
        jnp.broadcast_to(value[None], (size,) + value.shape), axes, 0, 0, tiled=True
    )


def share_row(value):
    mine = share(value, ("y", "zh"))
    other = swap_cores(mine)
    first = lax.axis_index("core") == 0
    pair = jnp.where(first, jnp.stack([mine, other], 1), jnp.stack([other, mine], 1))
    return pair.reshape((BLOCK_TILES,) + value.shape)


def sum_all(message):
    rows = message.shape[0] // 2
    core = lax.axis_index("core")
    keep = lax.dynamic_slice_in_dim(message, core * rows, rows, 0)
    give = lax.dynamic_slice_in_dim(message, (1 - core) * rows, rows, 0)
    summed = jnp.sum(share(keep + swap_cores(give), CHIPS), axis=0)
    other = swap_cores(summed)
    first = core == 0
    return jnp.concatenate([jnp.where(first, summed, other), jnp.where(first, other, summed)], 0)


def shards(embeddings, labels, pair_rows, pair_cols, pair_count):
    slab_index = lax.axis_index(ROW)
    block_index = lax.axis_index(COL)
    head = jnp.stack([pair_count[0, 0], slab_index, block_index] + [jnp.int32(0)] * 5)
    info = jnp.concatenate([head, pair_rows[0, 0], pair_cols[0, 0]]).astype(jnp.int32)
    slab = embeddings.reshape(SLAB_TILES, TILE, WIDTH)
    own = lax.dynamic_index_in_dim(slab, block_index, 0, keepdims=False)
    column = lax.all_gather(own, ROW, axis=0)
    half_rows = 0.5 * jnp.sum(jnp.square(slab.astype(F32)), axis=2)
    tiles, partial_degree = build(info, slab, column, half_rows)

    degree = jnp.sum(
        lax.all_to_all(partial_degree.reshape(SLAB_TILES, 1, TILE), COL, 0, 0, tiled=True), axis=0
    )
    inv_root = lax.rsqrt(degree)
    root = jnp.sqrt(degree)
    known = share_row(jnp.concatenate([inv_root, labels.astype(F32)[None]], axis=0))
    column_inv_root = known[:, 0]
    column_labels = known[:, 1].astype(jnp.int32)

    out = None
    for iteration in range(ITERS):
        if iteration == 0:
            running = product(info, tiles, column_labels, column_inv_root)
        else:
            running = product(info, tiles, share_row(out))
        parts = lax.all_to_all(running, COL, 0, 0, tiled=True)
        image, message = weigh(parts, inv_root, root)
        dtype = F32 if iteration == ITERS - 1 else BF16
        out = orthonormalize(
            sum_all(message), image, inv_root, root, 1.0 / (BLOCK_TILES * SLAB_TILES * TILE), dtype
        )
    return out


def solution(mesh):
    fine = Mesh(np.asarray(mesh.devices).reshape(4, 2, 2, 4, 2), ROW + COL)
    in_specs = (
        P(ROW, None),
        P(ROW + COL),
        P(ROW, COL, None),
        P(ROW, COL, None),
        P(ROW, COL),
    )
    return jax.shard_map(
        shards, mesh=fine, in_specs=in_specs, out_specs=P(None, ROW + COL), check_vma=False
    )
```

time: 1050 us -> 320 us (0.30)
  waiting for transfers between devices: 563 us -> 135 us
  blocking collectives: 341 us -> 104 us
  other arithmetic: 39.8 us -> 5.43 us
  matrix products: 31.9 us -> 0 us
  loops' own time: 31.1 us -> 0 us
  starting transfers between devices: 0.17 us -> 29.6 us
  Pallas kernels: 0 us -> 27.1 us
  local copies, waits for them, and re-layouts: 30 us -> 3.91 us
    psum x5 -> x0, blocking collectives: 341 us -> none  [the longest x2 136 us: shards(): lax.psum((local_top, local_total), ('row', 'col'))]
    reduce_scatter x2 -> x0, waiting for transfers between devices: 247 us -> none  [shards(): lax.psum_scatter(running, 'col', scatter_dimension=1, tiled=True)]
    all_gather x3 -> x1, waiting for transfers between devices: 316 us -> 108 us  [shards(): column = lax.all_gather(own, ROW, axis=0)]
    all_to_all x0 -> x5, blocking collectives: none -> 104 us  [the longest x4 83.9 us: share(): lax.all_to_all(jnp.broadcast_to(value[None], (size,) + value.shape), axes...]
    another operation x3 -> x0, loops' own time: 31.1 us -> none  [the longest x2 17.2 us: shards(): running = lax.fori_loop(0, live_count, add_slot, running)]
    pallas_call x0 -> x7, Pallas kernels: none -> 27.1 us  [the longest x2 12.7 us: orthonormalize(): pl.pallas_call(functools.partial(orthonormalize_kernel, scale), out_shape...]
    dot_general x16 -> x0, matrix products: 26.9 us -> none  [the longest x8 11 us: add_slot(): lax.dot_general(vec_piece, tile_store[position], (((1,), (1,)), ((), ()))...]
    another operation x10 -> x0, other arithmetic: 24.1 us -> none  [the longest x6 13 us: shards(): cholesky_factor = jnp.linalg.cholesky(gram_matrix)]
  transfers between devices with their start and end apart: 5 -> 9, of which waited for: 5 -> 9; matrix products, arithmetic and copies ran while one was open for 1% -> 2% of each run, Pallas kernels for 0% -> 0%
where the time goes in v1:
time: 320 us
  waiting for transfers between devices  135 us (42%)
  blocking collectives  104 us (32%)
  starting transfers between devices  29.6 us (9%)
  Pallas kernels  27.1 us (8%)
  between operations  14.2 us (4%)
  other arithmetic  5.43 us (2%)
  local copies, waits for them, and re-layouts  3.91 us (1%)
    all_gather x1, waiting for transfers between devices, shards(): column = lax.all_gather(own, ROW, axis=0)  108 us
    all_to_all x4, blocking collectives, share(): lax.all_to_all(jnp.broadcast_to(value[None], (size,) + value.shape), axes...  83.9 us
    all_to_all x1, blocking collectives, shards(): parts = lax.all_to_all(running, COL, 0, 0, tiled=True)  20.1 us
    all_to_all x1, waiting for transfers between devices, shards(): parts = lax.all_to_all(running, COL, 0, 0, tiled=True)  16.2 us
    all_to_all x1, starting transfers between devices, shards(): lax.all_to_all(partial_degree.reshape(SLAB_TILES, 1, TILE), COL, 0, 0, ti...  13.6 us
    pallas_call x2, Pallas kernels, orthonormalize(): pl.pallas_call(functools.partial(orthonormalize_kernel, scale), out_shape...  12.7 us
    ppermute x6, starting transfers between devices, swap_cores(): return lax.ppermute(value, 'core', [(0, 1), (1, 0)])  11.6 us
    pallas_call x1, Pallas kernels, build(): pl.pallas_call(build_kernel, out_shape=(jax.ShapeDtypeStruct((PAIRS, TILE...  7.65 us
  transfers between devices with their start and end apart: 9, of which 9 were waited for; matrix products, arithmetic and copies ran while one was open for 2% of the time, Pallas kernels for 0%

profile of v1, /device:TPU:1, one launch (start us, length us, event | category | flops | bytes accessed | tf_op | source)
XLA Modules:
  0.0 319.7 jit_solution(11879969818914293283)
XLA Ops:
  6.5 2.3 constant_dynamic-slice_fusion.2
  9.5 5.1 %multiply_reduce_fusion = f32[4096]{0:T(1024)S(1)} fusion(bf16[4096,1024]{1,0:T(8,128)(2,1)} %param.5), kind=kLoop, calls=%fused_computation | loop fusion | flops 12578816 | bytes 8404992 | tf_op jit(solution)/shard_map/reduce_sum | solution.py:326
  14.6 0.8 concatenate.12.info
  15.4 108.4 %all-gather.2.cloned.1.call-done.column = bf16[16,512,1024]{2,1,0:T(8,128)(2,1)} async-done(((bf16[1,512,1024]{2,1,0:T(8,128)(2,1)}), bf16[16,512,1024]{2,1,0:T(8,128)(2,1)}) %all-gather.2.cloned.1.call-update) | async-done | bytes 16777232 | tf_op jit(solution)/shard_map/all_gather | solution.py:325
  123.8 7.7 %build_tiles.1 = (bf16[24,512,512]{2,1,0:T(8,128)(2,1)}, f32[8,512]{1,0:T(8,128)S(1)}) custom-call(s32[56]{0:T(128)S(1)} %concatenate.12.info, bf16[8,512,1024]{2,1,0:T(8,128)(2,1)} %bitcast.34, bf16[16,512,1024]{2,1,0:T(8,128)(2,1)} %all-gather.2.cloned.1.call-done.column, f32[8,512]{1,0:T(8,128)S(1)} %mul.30.half_rows), custom_call_target="tpu_custom_call" | custom-call | tf_op jit(solution)/shard_map/build_tiles/pallas_call | solution.py:107
  131.4 0.6 copy.8
  132.0 13.6 %all-to-all-start = ((f32[8,1,512]{2,1,0:T(1,128)}), f32[8,1,512]{2,1,0:T(1,128)S(1)}, u32[]{:S(2)}, u32[]{:S(2)}) async-start(f32[8,1,512]{2,1,0:T(1,128)} %copy.8), calls=%async_computation | async-start | bytes 32768 | tf_op jit(solution)/shard_map/all_to_all | solution.py:330
  145.7 5.0 %all-to-all-done = f32[8,1,512]{2,1,0:T(1,128)S(1)} async-done(((f32[8,1,512]{2,1,0:T(1,128)}), f32[8,1,512]{2,1,0:T(1,128)S(1)}, u32[]{:S(2)}, u32[]{:S(2)}) %all-to-all-start) | async-done | bytes 16416 | tf_op jit(solution)/shard_map/all_to_all | solution.py:330
  150.8 27.4 %all_to_all.35 = f32[8,2,512]{2,1,0:T(2,128)S(1)} all-to-all(f32[8,2,512]{2,1,0:T(2,128)S(1)} %broadcast_in_dim.11), channel_id=1, replica_groups=mesh['y'=4,'zh'=2,'core'=2,'x'=4,'zl'=2] {'y','zh'}, dimensions={0} | all-to-all | bytes 65536 | tf_op jit(solution)/shard_map/all_to_all | solution.py:294
  178.2 3.4 %collective-permute-start = (f32[8,2,512]{2,1,0:T(2,128)S(1)}, f32[8,2,512]{2,1,0:T(2,128)S(1)}, u32[]{:S(2)}, u32[]{:S(2)}) collective-permute-start(f32[8,2,512]{2,1,0:T(2,128)S(1)} %all_to_all.35), channel_id=1, source_target_pairs={{0,8},{8,0},{1,9},{9,1},{2,10},{10,2},{3,11},{11,3},{4,12},{12,4},... | collective-permute-start | bytes 98312 | tf_op jit(solution)/shard_map/ppermute | solution.py:289
  181.6 0.9 collective-permute-done
  182.6 3.5 %product.2 = f32[8,64,512]{2,1,0:T(8,128)} custom-call(s32[56]{0:T(128)S(1)} %concatenate.12.info, bf16[24,512,512]{2,1,0:T(8,128)(2,1)} %get-tuple-element.11.tiles, s32[16,512]{1,0:T(8,128)S(1)} %get-tuple-element.18.refs_0_, f32[16,512]{1,0:T(8,128)S(1)} %get-tuple-element.17.refs_1_), custom_call_target="tpu_custom_call" | custom-call | tf_op jit(solution)/shard_map/product/pallas_call | solution.py:177
  186.1 4.4 %all-to-all-start.2 = ((f32[8,64,512]{2,1,0:T(8,128)}), f32[8,64,512]{2,1,0:T(8,128)S(1)}, u32[]{:S(2)}, u32[]{:S(2)}) async-start(f32[8,64,512]{2,1,0:T(8,128)} %product.2), calls=%async_computation.2 | async-start | bytes 2097152 | tf_op jit(solution)/shard_map/all_to_all | solution.py:344
  190.5 16.2 %all-to-all-done.2.parts = f32[8,64,512]{2,1,0:T(8,128)S(1)} async-done(((f32[8,64,512]{2,1,0:T(8,128)}), f32[8,64,512]{2,1,0:T(8,128)S(1)}, u32[]{:S(2)}, u32[]{:S(2)}) %all-to-all-start.2) | async-done | bytes 1048608 | tf_op jit(solution)/shard_map/all_to_all | solution.py:344
  206.7 0.4 weigh.2
  207.1 1.4 collective-permute-start.1
  208.5 0.8 collective-permute-done.1
  209.3 21.8 %all_to_all.36 = f32[64,16,128]{2,1,0:T(8,128)S(1)} all-to-all(f32[64,16,128]{2,1,0:T(8,128)S(1)} %broadcast_in_dim.12), channel_id=1, replica_groups=mesh['y'=4,'zh'=2,'core'=2,'x'=4,'zl'=2] {'y','zh','x','zl'}, dimensions={0} | all-to-all | bytes 1048576 | tf_op jit(solution)/shard_map/all_to_all | solution.py:294
  231.2 2.0 collective-permute-start.2
  233.2 0.8 collective-permute-done.2
  234.0 6.0 %orthonormalize.2 = bf16[64,512]{1,0:T(8,128)(2,1)S(1)} custom-call(f32[32,128]{1,0:T(8,128)S(1)} %pad_maximum_fusion.message, f32[64,512]{1,0:T(8,128)S(1)} %get-tuple-element.14.image, f32[1,512]{1,0:T(1,128)S(1)} %bitcast.25, f32[1,512]{1,0:T(1,128)S(1)} %bitcast.29), custom_call_target="tpu_custom_call" | custom-call | tf_op jit(solution)/shard_map/orthonormalize/pallas_call | solution.py:278
  240.1 12.7 %all_to_all.37 = bf16[8,64,512]{2,1,0:T(8,128)(2,1)S(1)} all-to-all(bf16[8,64,512]{2,1,0:T(8,128)(2,1)S(1)} %broadcast_in_dim.13), channel_id=1, replica_groups=mesh['y'=4,'zh'=2,'core'=2,'x'=4,'zl'=2] {'y','zh'}, dimensions={0} | all-to-all | bytes 1048576 | tf_op jit(solution)/shard_map/all_to_all | solution.py:294
  252.8 2.2 collective-permute-start.3
  255.0 1.5 collective-permute-done.3
  256.6 2.5 product.3
  259.1 20.1 %all_to_all.38.parts = f32[8,64,512]{2,1,0:T(8,128)S(1)} all-to-all(f32[8,64,512]{2,1,0:T(8,128)S(1)} %product.3), channel_id=1, replica_groups=mesh['y'=4,'zh'=2,'core'=2,'x'=4,'zl'=2] {'x','zl'}, dimensions={0} | all-to-all | bytes 2097152 | tf_op jit(solution)/shard_map/all_to_all | solution.py:344
  279.7 0.7 collective-permute-start.4
  280.4 0.8 collective-permute-done.4
  281.3 22.1 %all_to_all.39 = f32[64,16,128]{2,1,0:T(8,128)S(1)} all-to-all(f32[64,16,128]{2,1,0:T(8,128)S(1)} %broadcast_in_dim.14), channel_id=1, replica_groups=mesh['y'=4,'zh'=2,'core'=2,'x'=4,'zl'=2] {'y','zh','x','zl'}, dimensions={0} | all-to-all | bytes 1048576 | tf_op jit(solution)/shard_map/all_to_all | solution.py:294
  303.4 2.0 collective-permute-start.5
  305.4 0.8 collective-permute-done.5
  306.2 6.7 %orthonormalize.3 = f32[64,512]{1,0:T(8,128)} custom-call(f32[32,128]{1,0:T(8,128)S(1)} %pad_maximum_fusion.1.message, f32[64,512]{1,0:T(8,128)S(1)} %get-tuple-element.16.image, f32[1,512]{1,0:T(1,128)S(1)} %bitcast.27, f32[1,512]{1,0:T(1,128)S(1)} %bitcast.31), custom_call_target="tpu_custom_call" | custom-call | tf_op jit(solution)/shard_map/orthonormalize/pallas_call | solution.py:278
  (31 shorter events, 1.0 us)
Async XLA Ops:
  6.5 117.2 %all-gather.2.cloned.1.call-start = ((), (), s32[]{:S(2)}) async-start(), calls=%async_computation.7 | async-start | bytes 17825792 | tf_op jit(solution)/shard_map/all_gather | solution.py:325
  15.4 130.3 %copy-start = (s32[512]{0:T(512)S(1)}, s32[512]{0:T(512)}, u32[]{:S(2)}) copy-start(s32[512]{0:T(512)} %param.6) | copy-start | bytes 6148
  132.0 18.7 %all-to-all-start = ((f32[8,1,512]{2,1,0:T(1,128)}), f32[8,1,512]{2,1,0:T(1,128)S(1)}, u32[]{:S(2)}, u32[]{:S(2)}) async-start(f32[8,1,512]{2,1,0:T(1,128)} %copy.8), calls=%async_computation | async-start | bytes 32768 | tf_op jit(solution)/shard_map/all_to_all | solution.py:330
  178.2 4.3 %collective-permute-start = (f32[8,2,512]{2,1,0:T(2,128)S(1)}, f32[8,2,512]{2,1,0:T(2,128)S(1)}, u32[]{:S(2)}, u32[]{:S(2)}) collective-permute-start(f32[8,2,512]{2,1,0:T(2,128)S(1)} %all_to_all.35), channel_id=1, source_target_pairs={{0,8},{8,0},{1,9},{9,1},{2,10},{10,2},{3,11},{11,3},{4,12},{12,4},... | collective-permute-start | bytes 98312 | tf_op jit(solution)/shard_map/ppermute | solution.py:289
  186.1 20.6 %all-to-all-start.2 = ((f32[8,64,512]{2,1,0:T(8,128)}), f32[8,64,512]{2,1,0:T(8,128)S(1)}, u32[]{:S(2)}, u32[]{:S(2)}) async-start(f32[8,64,512]{2,1,0:T(8,128)} %product.2), calls=%async_computation.2 | async-start | bytes 2097152 | tf_op jit(solution)/shard_map/all_to_all | solution.py:344
  207.1 2.2 collective-permute-start.1
  231.2 2.8 collective-permute-start.2
  252.8 3.7 %collective-permute-start.3 = (bf16[8,64,512]{2,1,0:T(8,128)(2,1)S(1)}, bf16[8,64,512]{2,1,0:T(8,128)(2,1)S(1)}, u32[]{:S(2)}, u32[]{:S(2)}) collective-permute-start(bf16[8,64,512]{2,1,0:T(8,128)(2,1)S(1)} %all_to_all.37), channel_id=1, source_target_pairs={{0,8},{8,0},{1,9},{9,1},{2,10},{10,2},{3,11},{11,3},{4,12},{12,4},... | collective-permute-start | bytes 1572872 | tf_op jit(solution)/shard_map/ppermute | solution.py:289
  279.7 1.5 collective-permute-start.4
  303.4 2.8 collective-permute-start.5
Sparse Core Ops, SparseCore 0:
  9.8 113.9 all-gather.1

commit v2 on v1

--- a/solution.py
+++ b/solution.py
@@ -27,106 +27,160 @@
 VMEM_LIMIT = 48 * 1024 * 1024
 
 
-def build_kernel(info, slab, column, half_rows, tiles, degree, left, right, made, sem_in, sem_out):
-    count = info[0]
+def build_kernel(first, arrived, info, slab, half_rows, *refs):
+    columns, refs = refs[:arrived], refs[arrived:]
+    if first:
+        _, old_degree, *refs = refs
+    tiles, degree, order, left, right, made, sem_left, sem_right, sem_out = refs
+    live = info[0]
     slab_index = info[1]
     block_index = info[2]
-    degree[...] = jnp.zeros_like(degree)
-
-    def fetches(position, slot):
-        t = info[8 + position]
-        q = info[8 + PAIRS + position]
-        return (
-            pltpu.make_async_copy(slab.at[t], left.at[slot], sem_in.at[0, slot]),
-            pltpu.make_async_copy(column.at[q], right.at[slot], sem_in.at[1, slot]),
-        )
-
-    def store(position, slot):
-        return pltpu.make_async_copy(made.at[slot], tiles.at[position], sem_out.at[slot])
-
-    for copy in fetches(0, 0):
-        copy.start()
-
-    def step(position, carry):
-        slot = lax.rem(position, 2)
-
-        @pl.when(position + 1 < count)
-        def _():
-            for copy in fetches(position + 1, 1 - slot):
-                copy.start()
-
-        @pl.when(position >= 2)
-        def _():
-            store(position - 2, slot).wait()
-
-        for copy in fetches(position, slot):
-            copy.wait()
-        t = info[8 + position]
-        q = info[8 + PAIRS + position]
-        b = right[slot]
-        bf = b.astype(F32)
-        half_b = 0.5 * jnp.sum(bf * bf, axis=1, keepdims=True)
+    ahead, stores = left.shape[0] - 1, made.shape[0]
+    if first:
+        degree[...] = old_degree[...]
+    else:
+        degree[...] = jnp.zeros_like(degree)
+
+    count = jnp.int32(0)
+    group = jnp.int32(-1)
+    for s in range(arrived):
+        slab_of = info[8 + 2 * PAIRS + first + s]
+
+        def pick(position, carry):
+            count, group, seen = carry
+            hit = jnp.logical_and(position < live, info[8 + PAIRS + position] == slab_of)
+            fresh = jnp.logical_and(hit, jnp.logical_not(seen))
+            group = group + fresh.astype(jnp.int32)
+
+            @pl.when(hit)
+            def _():
+                order[0, count] = position
+                order[1, count] = s
+                order[2, count] = group
+                order[3, count] = fresh.astype(jnp.int32)
+
+            return count + hit.astype(jnp.int32), group, jnp.logical_or(seen, hit)
+
+        count, group, _ = lax.fori_loop(0, PAIRS, pick, (count, group, jnp.bool_(False)))
+
+    def left_copy(entry):
+        slot = lax.rem(entry, ahead + 1)
+        t = info[8 + order[0, entry]]
+        return pltpu.make_async_copy(slab.at[t], left.at[slot], sem_left.at[slot])
+
+    def right_copy(entry, s):
+        slot = lax.rem(order[2, entry], right.shape[0])
+        return pltpu.make_async_copy(columns[s], right.at[slot], sem_right.at[slot])
+
+    def fetch(entry):
+        left_copy(entry).start()
+        for s in range(arrived):
+
+            @pl.when(jnp.logical_and(order[3, entry] == 1, order[1, entry] == s))
+            def _():
+                right_copy(entry, s).start()
+
+    def store(entry):
+        slot = lax.rem(entry, stores)
+        return pltpu.make_async_copy(made.at[slot], tiles.at[order[0, entry]], sem_out.at[slot])
+
+    for entry in range(ahead):
+
+        @pl.when(entry < count)
+        def _():
+            fetch(jnp.int32(entry))
+
+    def step(entry, carry):
+        @pl.when(entry + ahead < count)
+        def _():
+            fetch(entry + ahead)
+
+        @pl.when(entry >= stores)
+        def _():
+            store(entry - stores).wait()
+
+        left_copy(entry).wait()
+
+        @pl.when(order[3, entry] == 1)
+        def _():
+            right_copy(entry, 0).wait()
+
+        a_slot = lax.rem(entry, ahead + 1)
+        b_slot = lax.rem(order[2, entry], right.shape[0])
+        m_slot = lax.rem(entry, stores)
+        t = info[8 + order[0, entry]]
+        b = right[b_slot]
+        wide = b.astype(F32)
+        half_b = 0.5 * jnp.sum(wide * wide, axis=1, keepdims=True)
         sums = []
         for n in range(2):
             lanes = pl.ds(n * 256, 256)
             inner = lax.dot_general(
-                b, left[slot, lanes, :], (((1,), (1,)), ((), ())), preferred_element_type=F32
+                b, left[a_slot, lanes, :], (((1,), (1,)), ((), ())), preferred_element_type=F32
             )
             half_a = half_rows[pl.ds(t, 1), lanes]
             w = jnp.exp2(RATE * ((inner - half_a) - half_b)).astype(BF16)
-            made[slot, :, lanes] = w
+            made[m_slot, :, lanes] = w
             sums.append(jnp.sum(w.astype(F32), axis=0, keepdims=True))
-        on_diagonal = jnp.logical_and(t == block_index, q == slab_index)
         old = degree[pl.ds(t, 1), :]
         degree[pl.ds(t, 1), :] = old + jnp.concatenate(sums, axis=1)
-
-        @pl.when(on_diagonal)
-        def _():
-            w = made[slot]
-            same = lax.broadcasted_iota(jnp.int32, (TILE, TILE), 0) == lax.broadcasted_iota(
-                jnp.int32, (TILE, TILE), 1
-            )
-            w = jnp.where(same, jnp.zeros_like(w), w)
-            made[slot] = w
-            degree[pl.ds(t, 1), :] = old + jnp.sum(w.astype(F32), axis=0, keepdims=True)
-
-        store(position, slot).start()
+        if first == 0:
+            q = info[8 + PAIRS + order[0, entry]]
+
+            @pl.when(jnp.logical_and(t == block_index, q == slab_index))
+            def _():
+                w = made[m_slot]
+                same = lax.broadcasted_iota(jnp.int32, (TILE, TILE), 0) == lax.broadcasted_iota(
+                    jnp.int32, (TILE, TILE), 1
+                )
+                w = jnp.where(same, jnp.zeros_like(w), w)
+                made[m_slot] = w
+                degree[pl.ds(t, 1), :] = old + jnp.sum(w.astype(F32), axis=0, keepdims=True)
+
+        store(entry).start()
         return carry
 
     lax.fori_loop(0, count, step, 0)
-
-    @pl.when(count >= 2)
-    def _():
-        store(count - 2, lax.rem(count, 2)).wait()
-
-    store(count - 1, lax.rem(count - 1, 2)).wait()
-
-
-def build(info, slab, column, half_rows):
+    for back in range(stores):
+
+        @pl.when(count > back)
+        def _():
+            store(count - 1 - back).wait()
+
+
+def build(first, info, slab, half_rows, columns, made):
     any_space = pl.BlockSpec(memory_space=pl.ANY)
+    vmem = pl.BlockSpec(memory_space=pltpu.VMEM)
+    arrived = len(columns)
+    pairs = PAIRS * arrived // BLOCK_TILES
     return pl.pallas_call(
-        build_kernel,
+        functools.partial(build_kernel, first, arrived),
         out_shape=(
             jax.ShapeDtypeStruct((PAIRS, TILE, TILE), BF16),
             jax.ShapeDtypeStruct((SLAB_TILES, TILE), F32),
         ),
-        in_specs=[
-            pl.BlockSpec(memory_space=pltpu.SMEM),
-            any_space,
-            any_space,
-            pl.BlockSpec(memory_space=pltpu.VMEM),
+        in_specs=[pl.BlockSpec(memory_space=pltpu.SMEM), any_space, vmem]
+        + [any_space] * arrived
+        + ([any_space, vmem] if made else []),
+        out_specs=(any_space, vmem),
+        scratch_shapes=[
+            pltpu.SMEM((4, PAIRS), jnp.int32),
+            pltpu.VMEM((3, TILE, WIDTH), BF16),
+            pltpu.VMEM((3, TILE, WIDTH), BF16),
+            pltpu.VMEM((4, TILE, TILE), BF16),
+            pltpu.SemaphoreType.DMA((3,)),
+            pltpu.SemaphoreType.DMA((3,)),
+            pltpu.SemaphoreType.DMA((4,)),
         ],
-        out_specs=(any_space, pl.BlockSpec(memory_space=pltpu.VMEM)),
-        scratch_shapes=[
-            pltpu.VMEM((2, TILE, WIDTH), BF16),
-            pltpu.VMEM((2, TILE, WIDTH), BF16),
-            pltpu.VMEM((2, TILE, TILE), BF16),
-            pltpu.SemaphoreType.DMA((2, 2)),
-            pltpu.SemaphoreType.DMA((2,)),
-        ],
-        compiler_params=pltpu.CompilerParams(vmem_limit_bytes=VMEM_LIMIT),
+        input_output_aliases={3 + arrived: 0} if made else {},
+        compiler_params=pltpu.CompilerParams(vmem_limit_bytes=20 * 1024 * 1024),
+        cost_estimate=pl.CostEstimate(
+            flops=pairs * 2 * TILE * TILE * WIDTH,
+            bytes_accessed=pairs * 5 * TILE * WIDTH,
+            transcendentals=pairs * TILE * TILE,
+        ),
         name="build_tiles",
-    )(info, slab, column, half_rows)
+    )(info, slab, half_rows, *columns, *made)
 
 
 def product_kernel(first, info, tiles, *refs):
@@ -315,25 +369,98 @@
     return jnp.concatenate([jnp.where(first, summed, other), jnp.where(first, other, summed)], 0)
 
 
+def up(value):
+    return lax.ppermute(value, "y", [(i, (i + 1) % 4) for i in range(4)])
+
+
+def down(value):
+    return lax.ppermute(value, "y", [(i, (i + 3) % 4) for i in range(4)])
+
+
+def apart(value):
+    return lax.ppermute(
+        value,
+        ("y", "core"),
+        [(2 * i + k, 2 * ((i + 1 + 2 * k) % 4) + k) for i in range(4) for k in range(2)],
+    )
+
+
+def apart_z(value):
+    moves = []
+    for z in range(4):
+        for k in range(2):
+            to = (z + 1 + 2 * k) % 4
+            moves.append((z // 2 * 4 + k * 2 + z % 2, to // 2 * 4 + k * 2 + to % 2))
+    return lax.ppermute(value, ("zh", "core", "zl"), moves)
+
+
+def cross(value):
+    return lax.ppermute(value, ("zh", "zl"), [(0, 3), (3, 0), (1, 2), (2, 1)])
+
+
 def shards(embeddings, labels, pair_rows, pair_cols, pair_count):
+    y, zh, core = (lax.axis_index(a) for a in ROW)
     slab_index = lax.axis_index(ROW)
     block_index = lax.axis_index(COL)
-    head = jnp.stack([pair_count[0, 0], slab_index, block_index] + [jnp.int32(0)] * 5)
-    info = jnp.concatenate([head, pair_rows[0, 0], pair_cols[0, 0]]).astype(jnp.int32)
+    zero = core == 0
     slab = embeddings.reshape(SLAB_TILES, TILE, WIDTH)
+
+    def of(dy, dz, k):
+        return ((y + dy) % 4 * 2 + (zh + dz) % 2) * 2 + k
+
+    side = lambda k: jnp.where(k == 0, 3, 1)
+    arrivals = []
+    for k in (core, 1 - core):
+        arrivals.append(
+            [
+                of(0, 0, k),
+                of(0, 1, k),
+                of(3, 0, k),
+                of(1, 0, k),
+                of(2, 0, k),
+                of(side(k), 1, k),
+                of(2, 1, k),
+                of(4 - side(k), 1, k),
+            ]
+        )
+    arrivals = [q for both in zip(*arrivals, strict=True) for q in both]
+    head = [pair_count[0, 0], slab_index, block_index] + [jnp.int32(0)] * 5
+    info = jnp.concatenate(
+        [jnp.stack(head), pair_rows[0, 0], pair_cols[0, 0], jnp.stack(arrivals)]
+    ).astype(jnp.int32)
+
     own = lax.dynamic_index_in_dim(slab, block_index, 0, keepdims=False)
-    column = lax.all_gather(own, ROW, axis=0)
+    give = lax.dynamic_index_in_dim(slab, block_index ^ 1, 0, keepdims=False)
+    across = cross(give)
+    below = up(own)
+    above = down(own)
+    beyond = apart(jnp.where(zero, below, above))
+    near = apart(across)
+    far = apart(near)
+    other = apart_z(apart_z(jnp.where(zero, above, below)))
     half_rows = 0.5 * jnp.sum(jnp.square(slab.astype(F32)), axis=2)
-    tiles, partial_degree = build(info, slab, column, half_rows)
-
-    degree = jnp.sum(
-        lax.all_to_all(partial_degree.reshape(SLAB_TILES, 1, TILE), COL, 0, 0, tiled=True), axis=0
-    )
+    column_labels = share_row(labels[None].astype(F32))[:, 0].astype(jnp.int32)
+    made = ()
+    first = 0
+    for stage in ((own,), (across, below, above), (beyond, near), (far, other)):
+        columns = [piece for tile in stage for piece in (tile, swap_cores(tile))]
+        made = build(first, info, slab, half_rows, columns, made)
+        first += len(columns)
+    tiles, partial_degree = made
+
+    spread = jnp.broadcast_to(partial_degree[None, :, None], (8, SLAB_TILES, 1, TILE))
+    got = lax.all_to_all(
+        spread.reshape(8 * SLAB_TILES, 1, TILE), CHIPS, 0, 0, tiled=True
+    )
+    mine = jnp.sum(got.reshape(8, SLAB_TILES, TILE), axis=1)
+    others = swap_cores(mine)
+    column_degree = jnp.where(
+        zero, jnp.stack([mine, others], 1), jnp.stack([others, mine], 1)
+    ).reshape(BLOCK_TILES, TILE)
+    column_inv_root = lax.rsqrt(column_degree)
+    degree = lax.dynamic_slice_in_dim(column_degree, slab_index, 1, 0)
     inv_root = lax.rsqrt(degree)
     root = jnp.sqrt(degree)
-    known = share_row(jnp.concatenate([inv_root, labels.astype(F32)[None]], axis=0))
-    column_inv_root = known[:, 0]
-    column_labels = known[:, 1].astype(jnp.int32)
 
     out = None
     for iteration in range(ITERS):

time: 320 us -> 272 us (0.85)
  waiting for transfers between devices: 135 us -> 59.5 us
  starting transfers between devices: 29.6 us -> 73.6 us
  blocking collectives: 104 us -> 74.6 us
  Pallas kernels: 27.1 us -> 40.2 us
  between operations: 14.2 us -> 1.11 us
  local copies, waits for them, and re-layouts: 3.91 us -> 14.5 us
    all_gather x1 -> x0, waiting for transfers between devices: 108 us -> none  [shards(): column = lax.all_gather(own, ROW, axis=0)]
    ppermute x0 -> x8, waiting for transfers between devices: none -> 28.9 us  [the longest x1 17.6 us: up(): return lax.ppermute(value, 'y', [(i, (i + 1) % 4) for i in range(4)])]
    all_to_all x4 -> x3, blocking collectives: 83.9 us -> 56.4 us  [share(): lax.all_to_all(jnp.broadcast_to(value[None], (size,) + value.shape), axes...]
    ppermute x0 -> x8, starting transfers between devices: none -> 19.7 us  [the longest x2 7.18 us: apart_z(): return lax.ppermute(value, ('zh', 'core', 'zl'), moves)]
    all_to_all x1 -> x2, starting transfers between devices: 13.6 us -> 32.9 us  [the longest x1 27.3 us: shards(): lax.all_to_all(spread.reshape(8 * SLAB_TILES, 1, TILE), CHIPS, 0, 0, tile...]
    pallas_call x1 -> x4, Pallas kernels: 7.65 us -> 17.9 us  [build(): pl.pallas_call(functools.partial(build_kernel, first, arrived), out_shape...]
    unnamed x2 -> x12, local copies, waits for them, and re-layouts: 0.01 us -> 10.1 us
    ppermute x6 -> x15, starting transfers between devices: 11.6 us -> 17.5 us  [swap_cores(): return lax.ppermute(value, 'core', [(0, 1), (1, 0)])]
  transfers between devices with their start and end apart: 9 -> 26, of which waited for: 9 -> 11; matrix products, arithmetic and copies ran while one was open for 2% -> 3% of each run, Pallas kernels for 0% -> 7%
where the time goes in v2:
time: 272 us; the launch traced here: 271 us
  blocking collectives  74.6 us (27%)
  starting transfers between devices  73.6 us (27%)
  waiting for transfers between devices  59.5 us (22%)
  Pallas kernels  40.2 us (15%)
  local copies, waits for them, and re-layouts  14.5 us (5%)
  other arithmetic  7.36 us (3%)
    all_to_all x3, blocking collectives, share(): lax.all_to_all(jnp.broadcast_to(value[None], (size,) + value.shape), axes...  56.4 us
    all_to_all x1, starting transfers between devices, shards(): lax.all_to_all(spread.reshape(8 * SLAB_TILES, 1, TILE), CHIPS, 0, 0, tile...  27.3 us
    all_to_all x1, blocking collectives, shards(): parts = lax.all_to_all(running, COL, 0, 0, tiled=True)  18.1 us
    pallas_call x4, Pallas kernels, build(): pl.pallas_call(functools.partial(build_kernel, first, arrived), out_shape...  17.9 us
    ppermute x1, waiting for transfers between devices, up(): return lax.ppermute(value, 'y', [(i, (i + 1) % 4) for i in range(4)])  17.6 us
    ppermute x15, starting transfers between devices, swap_cores(): return lax.ppermute(value, 'core', [(0, 1), (1, 0)])  17.5 us
    all_to_all x1, waiting for transfers between devices, shards(): parts = lax.all_to_all(running, COL, 0, 0, tiled=True)  17.2 us
    pallas_call x2, Pallas kernels, orthonormalize(): pl.pallas_call(functools.partial(orthonormalize_kernel, scale), out_shape...  12.7 us
  transfers between devices with their start and end apart: 26, of which 11 were waited for; matrix products, arithmetic and copies ran while one was open for 3% of the time, Pallas kernels for 7%

profile of v2, /device:TPU:1, one launch (start us, length us, event | category | flops | bytes accessed | tf_op | source)
XLA Modules:
  0.0 270.9 jit_solution(13766508248752818191)
XLA Ops:
  0.0 2.7 dynamic-slice_bitcast_fusion
  2.7 2.1 collective-permute-start.5
  6.3 3.8 %collective-permute-start = (bf16[512,1024]{1,0:T(8,128)(2,1)}, bf16[512,1024]{1,0:T(8,128)(2,1)}, u32[]{:S(2)}, u32[]{:S(2)}) collective-permute-start(bf16[512,1024]{1,0:T(8,128)(2,1)} %get-tuple-element.30), channel_id=1, source_target_pairs={{0,17},{17,0},{1,16},{16,1},{2,19},{19,2},{3,18},{18,3},{4,21},{21... | collective-permute-start | bytes 3145736 | tf_op jit(solution)/shard_map/ppermute | solution.py:398
  11.5 17.6 %collective-permute-done.5.refs_2_ = bf16[512,1024]{1,0:T(8,128)(2,1)S(1)} collective-permute-done((bf16[512,1024]{1,0:T(8,128)(2,1)S(1)}, bf16[512,1024]{1,0:T(8,128)(2,1)S(1)}, u32[]{:S(2)}, u32[]{:S(2)}) %collective-permute-start.5) | collective-permute-done | bytes 1048608 | tf_op jit(solution)/shard_map/ppermute | solution.py:373
  30.3 3.7 %collective-permute-start.6 = (bf16[512,1024]{1,0:T(8,128)(2,1)S(1)}, bf16[512,1024]{1,0:T(8,128)(2,1)}, u32[]{:S(2)}, u32[]{:S(2)}) collective-permute-start(bf16[512,1024]{1,0:T(8,128)(2,1)S(1)} %get-tuple-element.32), channel_id=1, source_target_pairs={{0,1},{8,25},{1,16},{9,8},{16,17},{24,9},{17,0},{25,24},{2,3},{10,... | collective-permute-start | bytes 3145736 | tf_op jit(solution)/shard_map/ppermute | solution.py:394
  33.9 2.3 collective-permute-start.1
  37.4 8.3 %collective-permute-done.6 = bf16[512,1024]{1,0:T(8,128)(2,1)} collective-permute-done((bf16[512,1024]{1,0:T(8,128)(2,1)S(1)}, bf16[512,1024]{1,0:T(8,128)(2,1)}, u32[]{:S(2)}, u32[]{:S(2)}) %collective-permute-start.6) | collective-permute-done | bytes 1048608 | tf_op jit(solution)/shard_map/ppermute | solution.py:394
  45.7 3.5 %collective-permute-start.7 = (bf16[512,1024]{1,0:T(8,128)(2,1)}, bf16[512,1024]{1,0:T(8,128)(2,1)}, u32[]{:S(2)}, u32[]{:S(2)}) collective-permute-start(bf16[512,1024]{1,0:T(8,128)(2,1)} %collective-permute-done.6), channel_id=1, source_target_pairs={{0,1},{8,25},{1,16},{9,8},{16,17},{24,9},{17,0},{25,24},{2,3},{10,... | collective-permute-start | bytes 3145736 | tf_op jit(solution)/shard_map/ppermute | solution.py:394
  49.2 2.3 collective-permute-start.2
  53.7 5.6 %all-to-all-start = ((f32[8,1,512]{2,1,0:T(1,128)}), f32[8,1,512]{2,1,0:T(1,128)S(1)}, u32[]{:S(2)}, u32[]{:S(2)}) async-start(f32[8,1,512]{2,1,0:T(1,128)} %broadcast_in_dim.12), calls=%async_computation | async-start | bytes 32768 | tf_op jit(solution)/shard_map/all_to_all | solution.py:348
  59.7 2.3 collective-permute-start.10
  62.0 5.1 %multiply_reduce_fusion = f32[4096]{0:T(1024)S(1)} fusion(bf16[4096,1024]{1,0:T(8,128)(2,1)} %param.5), kind=kLoop, calls=%fused_computation | loop fusion | flops 12578816 | bytes 8404992 | tf_op jit(solution)/shard_map/reduce_sum | solution.py:441
  68.0 3.0 %collective-permute-done.2.refs_0_ = bf16[512,1024]{1,0:T(8,128)(2,1)} collective-permute-done((bf16[512,1024]{1,0:T(8,128)(2,1)}, bf16[512,1024]{1,0:T(8,128)(2,1)}, u32[]{:S(2)}, u32[]{:S(2)}) %collective-permute-start.2) | collective-permute-done | bytes 1048608 | tf_op jit(solution)/shard_map/ppermute | solution.py:381
  71.0 2.4 collective-permute-start.3
  73.5 3.4 %copy-done.1 = bf16[4096,1024]{1,0:T(8,128)(2,1)S(1)} copy-done((bf16[4096,1024]{1,0:T(8,128)(2,1)S(1)}, bf16[4096,1024]{1,0:T(8,128)(2,1)}, u32[]{:S(2)}) %copy-start.1) | copy-done | bytes 8388632
  76.9 3.6 %build_tiles.4 = (bf16[24,512,512]{2,1,0:T(8,128)(2,1)S(1)}, f32[8,512]{1,0:T(8,128)S(1)}) custom-call(s32[72]{0:T(128)S(1)} %concatenate.13.info, bf16[8,512,1024]{2,1,0:T(8,128)(2,1)S(1)} %bitcast.37, f32[8,512]{1,0:T(8,128)S(1)} %mul.116.half_rows, bf16[512,1024]{1,0:T(8,128)(2,1)S(1)} %get-tuple-element.29.refs_0_, ...), custom_call_target="tpu_custom_call" | custom-call | flops 1610612736 | bytes 7864320 | tf_op jit(solution)/shard_map/build_tiles/pallas_call | solution.py:156
  81.7 10.2 %build_tiles.5 = (bf16[24,512,512]{2,1,0:T(8,128)(2,1)S(1)}, f32[8,512]{1,0:T(8,128)S(1)}) custom-call(s32[72]{0:T(128)S(1)} %concatenate.13.info, bf16[8,512,1024]{2,1,0:T(8,128)(2,1)S(1)} %bitcast.38, f32[8,512]{1,0:T(8,128)S(1)} %mul.116.half_rows, bf16[512,1024]{1,0:T(8,128)(2,1)} %collective-permute-done.refs_0_, ...), custom_call_target="tpu_custom_call", output_to_operand_aliasing={{0}: (9, {})} | custom-call | flops 4831838208 | bytes 23592960 | tf_op jit(solution)/shard_map/build_tiles/pallas_call | solution.py:156
  94.0 2.1 build_tiles.7
  96.1 4.5 %copy-done = bf16[24,512,512]{2,1,0:T(8,128)(2,1)} copy-done((bf16[24,512,512]{2,1,0:T(8,128)(2,1)}, bf16[24,512,512]{2,1,0:T(8,128)(2,1)S(1)}, u32[]{:S(2)}) %copy-start) | copy-done | bytes 12582936
  101.4 27.3 %all-to-all-start.1 = ((f32[64,1,512]{2,1,0:T(1,128)}), f32[64,1,512]{2,1,0:T(1,128)S(1)}, u32[]{:S(2)}, u32[]{:S(2)}) async-start(f32[64,1,512]{2,1,0:T(1,128)} %broadcast_in_dim.14), calls=%async_computation.1 | async-start | bytes 262144 | tf_op jit(solution)/shard_map/all_to_all | solution.py:452
  129.6 7.8 %all-to-all-done.1 = f32[64,1,512]{2,1,0:T(1,128)S(1)} async-done(((f32[64,1,512]{2,1,0:T(1,128)}), f32[64,1,512]{2,1,0:T(1,128)S(1)}, u32[]{:S(2)}, u32[]{:S(2)}) %all-to-all-start.1) | async-done | bytes 131104 | tf_op jit(solution)/shard_map/all_to_all | solution.py:452
  140.4 4.9 %product.2 = f32[8,64,512]{2,1,0:T(8,128)} custom-call(s32[72]{0:T(128)S(1)} %concatenate.13.info, bf16[24,512,512]{2,1,0:T(8,128)(2,1)} %copy-done, s32[16,512]{1,0:T(8,128)S(1)} %convert_element_type.16.refs_0_, f32[16,512]{1,0:T(8,128)S(1)} %rsqrt.6.refs_1_), custom_call_target="tpu_custom_call" | custom-call | tf_op jit(solution)/shard_map/product/pallas_call | solution.py:231
  145.3 3.6 %all-to-all-start.2 = ((f32[8,64,512]{2,1,0:T(8,128)}), f32[8,64,512]{2,1,0:T(8,128)S(1)}, u32[]{:S(2)}, u32[]{:S(2)}) async-start(f32[8,64,512]{2,1,0:T(8,128)} %product.2), calls=%async_computation.2 | async-start | bytes 2097152 | tf_op jit(solution)/shard_map/all_to_all | solution.py:471
  148.9 17.2 %all-to-all-done.2.parts = f32[8,64,512]{2,1,0:T(8,128)S(1)} async-done(((f32[8,64,512]{2,1,0:T(8,128)}), f32[8,64,512]{2,1,0:T(8,128)S(1)}, u32[]{:S(2)}, u32[]{:S(2)}) %all-to-all-start.2) | async-done | bytes 1048608 | tf_op jit(solution)/shard_map/all_to_all | solution.py:471
  167.9 21.2 %all_to_all.35 = f32[64,16,128]{2,1,0:T(8,128)S(1)} all-to-all(f32[64,16,128]{2,1,0:T(8,128)S(1)} %broadcast_in_dim.15), channel_id=1, replica_groups=mesh['y'=4,'zh'=2,'core'=2,'x'=4,'zl'=2] {'y','zh','x','zl'}, dimensions={0} | all-to-all | bytes 1048576 | tf_op jit(solution)/shard_map/all_to_all | solution.py:348
  192.0 6.0 %orthonormalize.2 = bf16[64,512]{1,0:T(8,128)(2,1)S(1)} custom-call(f32[32,128]{1,0:T(8,128)S(1)} %pad_maximum_fusion.message, f32[64,512]{1,0:T(8,128)S(1)} %get-tuple-element.26.image, f32[1,512]{1,0:T(1,128)S(1)} %get-tuple-element.34.inv_root, f32[1,512]{1,0:T(1,128)S(1)} %get-tuple-element.33.root), custom_call_target="tpu_custom_call" | custom-call | tf_op jit(solution)/shard_map/orthonormalize/pallas_call | solution.py:332
  198.1 12.7 %all_to_all.36 = bf16[8,64,512]{2,1,0:T(8,128)(2,1)S(1)} all-to-all(bf16[8,64,512]{2,1,0:T(8,128)(2,1)S(1)} %broadcast_in_dim.16), channel_id=1, replica_groups=mesh['y'=4,'zh'=2,'core'=2,'x'=4,'zl'=2] {'y','zh'}, dimensions={0} | all-to-all | bytes 1048576 | tf_op jit(solution)/shard_map/all_to_all | solution.py:348
  210.8 2.2 collective-permute-start.20
  214.6 3.8 %product.3 = f32[8,64,512]{2,1,0:T(8,128)S(1)} custom-call(s32[72]{0:T(128)S(1)} %concatenate.13.info, bf16[24,512,512]{2,1,0:T(8,128)(2,1)} %copy-done, bf16[16,64,512]{2,1,0:T(8,128)(2,1)S(1)} %bitcast.41), custom_call_target="tpu_custom_call" | custom-call | tf_op jit(solution)/shard_map/product/pallas_call | solution.py:231
  218.5 18.1 %all_to_all.37.parts = f32[8,64,512]{2,1,0:T(8,128)S(1)} all-to-all(f32[8,64,512]{2,1,0:T(8,128)S(1)} %product.3), channel_id=1, replica_groups=mesh['y'=4,'zh'=2,'core'=2,'x'=4,'zl'=2] {'x','zl'}, dimensions={0} | all-to-all | bytes 2097152 | tf_op jit(solution)/shard_map/all_to_all | solution.py:471
  238.8 22.6 %all_to_all.38 = f32[64,16,128]{2,1,0:T(8,128)S(1)} all-to-all(f32[64,16,128]{2,1,0:T(8,128)S(1)} %broadcast_in_dim.17), channel_id=1, replica_groups=mesh['y'=4,'zh'=2,'core'=2,'x'=4,'zl'=2] {'y','zh','x','zl'}, dimensions={0} | all-to-all | bytes 1048576 | tf_op jit(solution)/shard_map/all_to_all | solution.py:348
  264.2 6.7 %orthonormalize.3 = f32[64,512]{1,0:T(8,128)} custom-call(f32[32,128]{1,0:T(8,128)S(1)} %pad_maximum_fusion.1.message, f32[64,512]{1,0:T(8,128)S(1)} %get-tuple-element.28.image, f32[1,512]{1,0:T(1,128)S(1)} %get-tuple-element.34.inv_root, f32[1,512]{1,0:T(1,128)S(1)} %get-tuple-element.33.root), custom_call_target="tpu_custom_call" | custom-call | tf_op jit(solution)/shard_map/orthonormalize/pallas_call | solution.py:332
  (80 shorter events, 27.3 us)
Async XLA Ops:
  0.0 73.3 %copy-start.4 = (s32[1,1,24]{2,1,0:T(1,128)S(1)}, s32[1,1,24]{2,1,0:T(1,128)}, u32[]{:S(2)}) copy-start(s32[1,1,24]{2,1,0:T(1,128)} %param.7) | copy-start | bytes 292
  0.0 73.4 %copy-start.5 = (s32[1,1,24]{2,1,0:T(1,128)S(1)}, s32[1,1,24]{2,1,0:T(1,128)}, u32[]{:S(2)}) copy-start(s32[1,1,24]{2,1,0:T(1,128)} %param.8) | copy-start | bytes 292
  2.7 26.4 %collective-permute-start.5 = (bf16[512,1024]{1,0:T(8,128)(2,1)S(1)}, bf16[512,1024]{1,0:T(8,128)(2,1)S(1)}, u32[]{:S(2)}, u32[]{:S(2)}) collective-permute-start(bf16[512,1024]{1,0:T(8,128)(2,1)S(1)} %get-tuple-element.29.refs_0_), channel_id=1, source_target_pairs={{0,32},{32,64},{64,96},{96,0},{1,33},{33,65},{65,97},{97,1},{2,34}... | collective-permute-start | bytes 3145736 | tf_op jit(solution)/shard_map/ppermute | solution.py:373
  4.8 24.3 %collective-permute-start.4 = (bf16[512,1024]{1,0:T(8,128)(2,1)S(1)}, bf16[512,1024]{1,0:T(8,128)(2,1)S(1)}, u32[]{:S(2)}, u32[]{:S(2)}) collective-permute-start(bf16[512,1024]{1,0:T(8,128)(2,1)S(1)} %get-tuple-element.29.refs_0_), channel_id=1, source_target_pairs={{0,96},{32,0},{64,32},{96,64},{1,97},{33,1},{65,33},{97,65},{2,98}... | collective-permute-start | bytes 3145736 | tf_op jit(solution)/shard_map/ppermute | solution.py:377
  6.3 27.7 %collective-permute-start = (bf16[512,1024]{1,0:T(8,128)(2,1)}, bf16[512,1024]{1,0:T(8,128)(2,1)}, u32[]{:S(2)}, u32[]{:S(2)}) collective-permute-start(bf16[512,1024]{1,0:T(8,128)(2,1)} %get-tuple-element.30), channel_id=1, source_target_pairs={{0,17},{17,0},{1,16},{16,1},{2,19},{19,2},{3,18},{18,3},{4,21},{21... | collective-permute-start | bytes 3145736 | tf_op jit(solution)/shard_map/ppermute | solution.py:398
  10.0 26.8 %collective-permute-start.15 = (bf16[512,1024]{1,0:T(8,128)(2,1)S(1)}, bf16[512,1024]{1,0:T(8,128)(2,1)}, u32[]{:S(2)}, u32[]{:S(2)}) collective-permute-start(bf16[512,1024]{1,0:T(8,128)(2,1)S(1)} %get-tuple-element.29.refs_0_), channel_id=1, source_target_pairs={{0,8},{8,0},{1,9},{9,1},{2,10},{10,2},{3,11},{11,3},{4,12},{12,4},... | collective-permute-start | bytes 3145736 | tf_op jit(solution)/shard_map/ppermute | solution.py:343
  30.3 15.4 %collective-permute-start.6 = (bf16[512,1024]{1,0:T(8,128)(2,1)S(1)}, bf16[512,1024]{1,0:T(8,128)(2,1)}, u32[]{:S(2)}, u32[]{:S(2)}) collective-permute-start(bf16[512,1024]{1,0:T(8,128)(2,1)S(1)} %get-tuple-element.32), channel_id=1, source_target_pairs={{0,1},{8,25},{1,16},{9,8},{16,17},{24,9},{17,0},{25,24},{2,3},{10,... | collective-permute-start | bytes 3145736 | tf_op jit(solution)/shard_map/ppermute | solution.py:394
  33.9 15.3 %collective-permute-start.1 = (bf16[512,1024]{1,0:T(8,128)(2,1)}, bf16[512,1024]{1,0:T(8,128)(2,1)}, u32[]{:S(2)}, u32[]{:S(2)}) collective-permute-start(bf16[512,1024]{1,0:T(8,128)(2,1)} %collective-permute-done.refs_0_), channel_id=1, source_target_pairs={{0,32},{8,104},{32,64},{40,8},{64,96},{72,40},{96,0},{104,72},{1,3... | collective-permute-start | bytes 3145736 | tf_op jit(solution)/shard_map/ppermute | solution.py:381
  36.3 15.2 %collective-permute-start.13 = (bf16[512,1024]{1,0:T(8,128)(2,1)S(1)}, bf16[512,1024]{1,0:T(8,128)(2,1)S(1)}, u32[]{:S(2)}, u32[]{:S(2)}) collective-permute-start(bf16[512,1024]{1,0:T(8,128)(2,1)S(1)} %collective-permute-done.5.refs_2_), channel_id=1, source_target_pairs={{0,8},{8,0},{1,9},{9,1},{2,10},{10,2},{3,11},{11,3},{4,12},{12,4},... | collective-permute-start | bytes 3145736 | tf_op jit(solution)/shard_map/ppermute | solution.py:343
  36.3 23.1 %collective-permute-start.14 = (bf16[512,1024]{1,0:T(8,128)(2,1)S(1)}, bf16[512,1024]{1,0:T(8,128)(2,1)}, u32[]{:S(2)}, u32[]{:S(2)}) collective-permute-start(bf16[512,1024]{1,0:T(8,128)(2,1)S(1)} %collective-permute-done.4.refs_4_), channel_id=1, source_target_pairs={{0,8},{8,0},{1,9},{9,1},{2,10},{10,2},{3,11},{11,3},{4,12},{12,4},... | collective-permute-start | bytes 3145736 | tf_op jit(solution)/shard_map/ppermute | solution.py:343
  36.8 22.9 %collective-permute-start.9 = (bf16[512,1024]{1,0:T(8,128)(2,1)}, bf16[512,1024]{1,0:T(8,128)(2,1)}, u32[]{:S(2)}, u32[]{:S(2)}) collective-permute-start(bf16[512,1024]{1,0:T(8,128)(2,1)} %get-tuple-element.31), channel_id=1, source_target_pairs={{0,32},{8,104},{32,64},{40,8},{64,96},{72,40},{96,0},{104,72},{1,3... | collective-permute-start | bytes 3145736 | tf_op jit(solution)/shard_map/ppermute | solution.py:381
  45.7 22.2 %collective-permute-start.7 = (bf16[512,1024]{1,0:T(8,128)(2,1)}, bf16[512,1024]{1,0:T(8,128)(2,1)}, u32[]{:S(2)}, u32[]{:S(2)}) collective-permute-start(bf16[512,1024]{1,0:T(8,128)(2,1)} %collective-permute-done.6), channel_id=1, source_target_pairs={{0,1},{8,25},{1,16},{9,8},{16,17},{24,9},{17,0},{25,24},{2,3},{10,... | collective-permute-start | bytes 3145736 | tf_op jit(solution)/shard_map/ppermute | solution.py:394
  49.2 21.8 %collective-permute-start.2 = (bf16[512,1024]{1,0:T(8,128)(2,1)}, bf16[512,1024]{1,0:T(8,128)(2,1)}, u32[]{:S(2)}, u32[]{:S(2)}) collective-permute-start(bf16[512,1024]{1,0:T(8,128)(2,1)} %collective-permute-done.1.refs_2_), channel_id=1, source_target_pairs={{0,32},{8,104},{32,64},{40,8},{64,96},{72,40},{96,0},{104,72},{1,3... | collective-permute-start | bytes 3145736 | tf_op jit(solution)/shard_map/ppermute | solution.py:381
  51.5 1.0 copy-start.2
  52.4 28.1 %collective-permute-start.12 = (bf16[512,1024]{1,0:T(8,128)(2,1)}, bf16[512,1024]{1,0:T(8,128)(2,1)}, u32[]{:S(2)}, u32[]{:S(2)}) collective-permute-start(bf16[512,1024]{1,0:T(8,128)(2,1)} %collective-permute-done.refs_0_), channel_id=1, source_target_pairs={{0,8},{8,0},{1,9},{9,1},{2,10},{10,2},{3,11},{11,3},{4,12},{12,4},... | collective-permute-start | bytes 3145736 | tf_op jit(solution)/shard_map/ppermute | solution.py:343
  53.7 47.7 %all-to-all-start = ((f32[8,1,512]{2,1,0:T(1,128)}), f32[8,1,512]{2,1,0:T(1,128)S(1)}, u32[]{:S(2)}, u32[]{:S(2)}) async-start(f32[8,1,512]{2,1,0:T(1,128)} %broadcast_in_dim.12), calls=%async_computation | async-start | bytes 32768 | tf_op jit(solution)/shard_map/all_to_all | solution.py:348
  59.3 32.7 %collective-permute-start.11 = (bf16[512,1024]{1,0:T(8,128)(2,1)}, bf16[512,1024]{1,0:T(8,128)(2,1)}, u32[]{:S(2)}, u32[]{:S(2)}) collective-permute-start(bf16[512,1024]{1,0:T(8,128)(2,1)} %collective-permute-done.1.refs_2_), channel_id=1, source_target_pairs={{0,8},{8,0},{1,9},{9,1},{2,10},{10,2},{3,11},{11,3},{4,12},{12,4},... | collective-permute-start | bytes 3145736 | tf_op jit(solution)/shard_map/ppermute | solution.py:343
  59.7 32.3 %collective-permute-start.10 = (bf16[512,1024]{1,0:T(8,128)(2,1)}, bf16[512,1024]{1,0:T(8,128)(2,1)}, u32[]{:S(2)}, u32[]{:S(2)}) collective-permute-start(bf16[512,1024]{1,0:T(8,128)(2,1)} %collective-permute-done.9.refs_0_), channel_id=1, source_target_pairs={{0,8},{8,0},{1,9},{9,1},{2,10},{10,2},{3,11},{11,3},{4,12},{12,4},... | collective-permute-start | bytes 3145736 | tf_op jit(solution)/shard_map/ppermute | solution.py:343
  67.9 26.1 %collective-permute-start.8 = (bf16[512,1024]{1,0:T(8,128)(2,1)}, bf16[512,1024]{1,0:T(8,128)(2,1)}, u32[]{:S(2)}, u32[]{:S(2)}) collective-permute-start(bf16[512,1024]{1,0:T(8,128)(2,1)} %collective-permute-done.7.refs_2_), channel_id=1, source_target_pairs={{0,8},{8,0},{1,9},{9,1},{2,10},{10,2},{3,11},{11,3},{4,12},{12,4},... | collective-permute-start | bytes 3145736 | tf_op jit(solution)/shard_map/ppermute | solution.py:343
  71.0 23.0 %collective-permute-start.3 = (bf16[512,1024]{1,0:T(8,128)(2,1)}, bf16[512,1024]{1,0:T(8,128)(2,1)}, u32[]{:S(2)}, u32[]{:S(2)}) collective-permute-start(bf16[512,1024]{1,0:T(8,128)(2,1)} %collective-permute-done.2.refs_0_), channel_id=1, source_target_pairs={{0,8},{8,0},{1,9},{9,1},{2,10},{10,2},{3,11},{11,3},{4,12},{12,4},... | collective-permute-start | bytes 3145736 | tf_op jit(solution)/shard_map/ppermute | solution.py:343
  73.5 3.4 %copy-start.1 = (bf16[4096,1024]{1,0:T(8,128)(2,1)S(1)}, bf16[4096,1024]{1,0:T(8,128)(2,1)}, u32[]{:S(2)}) copy-start(bf16[4096,1024]{1,0:T(8,128)(2,1)} %param.5) | copy-start | bytes 25165828
  80.5 1.2 copy-start.3
  96.1 4.5 %copy-start = (bf16[24,512,512]{2,1,0:T(8,128)(2,1)}, bf16[24,512,512]{2,1,0:T(8,128)(2,1)S(1)}, u32[]{:S(2)}) copy-start(bf16[24,512,512]{2,1,0:T(8,128)(2,1)S(1)} %get-tuple-element.23.tiles) | copy-start | bytes 37748740
  101.4 36.0 %all-to-all-start.1 = ((f32[64,1,512]{2,1,0:T(1,128)}), f32[64,1,512]{2,1,0:T(1,128)S(1)}, u32[]{:S(2)}, u32[]{:S(2)}) async-start(f32[64,1,512]{2,1,0:T(1,128)} %broadcast_in_dim.14), calls=%async_computation.1 | async-start | bytes 262144 | tf_op jit(solution)/shard_map/all_to_all | solution.py:452
  128.7 10.8 %collective-permute-start.16 = (f32[8,1,512]{2,1,0:T(1,128)S(1)}, f32[8,1,512]{2,1,0:T(1,128)S(1)}, u32[]{:S(2)}, u32[]{:S(2)}) collective-permute-start(f32[8,1,512]{2,1,0:T(1,128)S(1)} %all-to-all-done), channel_id=1, source_target_pairs={{0,8},{8,0},{1,9},{9,1},{2,10},{10,2},{3,11},{11,3},{4,12},{12,4},... | collective-permute-start | bytes 49160 | tf_op jit(solution)/shard_map/ppermute | solution.py:343
  137.4 2.9 %collective-permute-start.17 = (f32[8,512]{1,0:T(8,128)S(1)}, f32[8,512]{1,0:T(8,128)S(1)}, u32[]{:S(2)}, u32[]{:S(2)}) collective-permute-start(f32[8,512]{1,0:T(8,128)S(1)} %bitcast_reduce_fusion), channel_id=1, source_target_pairs={{0,8},{8,0},{1,9},{9,1},{2,10},{10,2},{3,11},{11,3},{4,12},{12,4},... | collective-permute-start | bytes 49160 | tf_op jit(solution)/shard_map/ppermute | solution.py:343
  145.3 20.8 %all-to-all-start.2 = ((f32[8,64,512]{2,1,0:T(8,128)}), f32[8,64,512]{2,1,0:T(8,128)S(1)}, u32[]{:S(2)}, u32[]{:S(2)}) async-start(f32[8,64,512]{2,1,0:T(8,128)} %product.2), calls=%async_computation.2 | async-start | bytes 2097152 | tf_op jit(solution)/shard_map/all_to_all | solution.py:471
  166.6 1.3 collective-permute-start.18
  189.2 2.8 %collective-permute-start.19 = (f32[16,128]{1,0:T(8,128)S(1)}, f32[16,128]{1,0:T(8,128)S(1)}, u32[]{:S(2)}, u32[]{:S(2)}) collective-permute-start(f32[16,128]{1,0:T(8,128)S(1)} %reduce_sum.38), channel_id=1, source_target_pairs={{0,8},{8,0},{1,9},{9,1},{2,10},{10,2},{3,11},{11,3},{4,12},{12,4},... | collective-permute-start | bytes 24584 | tf_op jit(solution)/shard_map/ppermute | solution.py:343
  210.8 3.7 %collective-permute-start.20 = (bf16[8,64,512]{2,1,0:T(8,128)(2,1)S(1)}, bf16[8,64,512]{2,1,0:T(8,128)(2,1)S(1)}, u32[]{:S(2)}, u32[]{:S(2)}) collective-permute-start(bf16[8,64,512]{2,1,0:T(8,128)(2,1)S(1)} %all_to_all.36), channel_id=1, source_target_pairs={{0,8},{8,0},{1,9},{9,1},{2,10},{10,2},{3,11},{11,3},{4,12},{12,4},... | collective-permute-start | bytes 1572872 | tf_op jit(solution)/shard_map/ppermute | solution.py:343
  237.0 1.7 collective-permute-start.21
  261.4 2.8 %collective-permute-start.22 = (f32[16,128]{1,0:T(8,128)S(1)}, f32[16,128]{1,0:T(8,128)S(1)}, u32[]{:S(2)}, u32[]{:S(2)}) collective-permute-start(f32[16,128]{1,0:T(8,128)S(1)} %reduce_sum.39), channel_id=1, source_target_pairs={{0,8},{8,0},{1,9},{9,1},{2,10},{10,2},{3,11},{11,3},{4,12},{12,4},... | collective-permute-start | bytes 24584 | tf_op jit(solution)/shard_map/ppermute | solution.py:343

commit v3 on v2

--- a/solution.py
+++ b/solution.py
@@ -24,91 +24,73 @@
 CHIPS = ("y", "zh", "x", "zl")
 SLAB_TILES = 8
 BLOCK_TILES = 16
-VMEM_LIMIT = 48 * 1024 * 1024
+VMEM_LIMIT = 10 * 1024 * 1024
+ROWS, SLABS, RANKS, GROUPS, STARTS = (8 + PAIRS * i for i in range(5))
 
 
 def build_kernel(first, arrived, info, slab, half_rows, *refs):
     columns, refs = refs[:arrived], refs[arrived:]
     if first:
         _, old_degree, *refs = refs
-    tiles, degree, order, left, right, made, sem_left, sem_right, sem_out = refs
-    live = info[0]
-    slab_index = info[1]
-    block_index = info[2]
+    tiles, degree, left, right, made, sem_left, sem_right, sem_out = refs
+    block_index = info[1]
     ahead, stores = left.shape[0] - 1, made.shape[0]
     if first:
         degree[...] = old_degree[...]
     else:
         degree[...] = jnp.zeros_like(degree)
 
-    count = jnp.int32(0)
-    group = jnp.int32(-1)
-    for s in range(arrived):
-        slab_of = info[8 + 2 * PAIRS + first + s]
-
-        def pick(position, carry):
-            count, group, seen = carry
-            hit = jnp.logical_and(position < live, info[8 + PAIRS + position] == slab_of)
-            fresh = jnp.logical_and(hit, jnp.logical_not(seen))
-            group = group + fresh.astype(jnp.int32)
-
-            @pl.when(hit)
-            def _():
-                order[0, count] = position
-                order[1, count] = s
-                order[2, count] = group
-                order[3, count] = fresh.astype(jnp.int32)
-
-            return count + hit.astype(jnp.int32), group, jnp.logical_or(seen, hit)
-
-        count, group, _ = lax.fori_loop(0, PAIRS, pick, (count, group, jnp.bool_(False)))
+    begin, end = info[STARTS + first], info[STARTS + first + arrived]
 
     def left_copy(entry):
         slot = lax.rem(entry, ahead + 1)
-        t = info[8 + order[0, entry]]
+        t = info[ROWS + entry]
         return pltpu.make_async_copy(slab.at[t], left.at[slot], sem_left.at[slot])
 
     def right_copy(entry, s):
-        slot = lax.rem(order[2, entry], right.shape[0])
+        slot = lax.rem(info[GROUPS + entry], right.shape[0])
         return pltpu.make_async_copy(columns[s], right.at[slot], sem_right.at[slot])
+
+    def fresh(entry):
+        return jnp.logical_or(entry == begin, info[GROUPS + entry] != info[GROUPS + entry - 1])
 
     def fetch(entry):
         left_copy(entry).start()
         for s in range(arrived):
 
-            @pl.when(jnp.logical_and(order[3, entry] == 1, order[1, entry] == s))
+            @pl.when(jnp.logical_and(fresh(entry), info[RANKS + entry] == first + s))
             def _():
                 right_copy(entry, s).start()
 
     def store(entry):
         slot = lax.rem(entry, stores)
-        return pltpu.make_async_copy(made.at[slot], tiles.at[order[0, entry]], sem_out.at[slot])
+        return pltpu.make_async_copy(made.at[slot], tiles.at[entry], sem_out.at[slot])
 
     for entry in range(ahead):
 
-        @pl.when(entry < count)
-        def _():
-            fetch(jnp.int32(entry))
+        @pl.when(begin + entry < end)
+        def _():
+            fetch(begin + entry)
 
     def step(entry, carry):
-        @pl.when(entry + ahead < count)
+        @pl.when(entry + ahead < end)
         def _():
             fetch(entry + ahead)
 
-        @pl.when(entry >= stores)
+        @pl.when(entry - begin >= stores)
         def _():
             store(entry - stores).wait()
 
         left_copy(entry).wait()
 
-        @pl.when(order[3, entry] == 1)
+        @pl.when(fresh(entry))
         def _():
             right_copy(entry, 0).wait()
 
         a_slot = lax.rem(entry, ahead + 1)
-        b_slot = lax.rem(order[2, entry], right.shape[0])
+        b_slot = lax.rem(info[GROUPS + entry], right.shape[0])
         m_slot = lax.rem(entry, stores)
-        t = info[8 + order[0, entry]]
+        t = info[ROWS + entry]
         b = right[b_slot]
         wide = b.astype(F32)
         half_b = 0.5 * jnp.sum(wide * wide, axis=1, keepdims=True)
@@ -125,9 +107,7 @@
         old = degree[pl.ds(t, 1), :]
         degree[pl.ds(t, 1), :] = old + jnp.concatenate(sums, axis=1)
         if first == 0:
-            q = info[8 + PAIRS + order[0, entry]]
-
-            @pl.when(jnp.logical_and(t == block_index, q == slab_index))
+            @pl.when(jnp.logical_and(t == block_index, info[RANKS + entry] == 0))
             def _():
                 w = made[m_slot]
                 same = lax.broadcasted_iota(jnp.int32, (TILE, TILE), 0) == lax.broadcasted_iota(
@@ -140,12 +120,12 @@
         store(entry).start()
         return carry
 
-    lax.fori_loop(0, count, step, 0)
+    lax.fori_loop(begin, end, step, 0)
     for back in range(stores):
 
-        @pl.when(count > back)
-        def _():
-            store(count - 1 - back).wait()
+        @pl.when(end - begin > back)
+        def _():
+            store(end - 1 - back).wait()
 
 
 def build(first, info, slab, half_rows, columns, made):
@@ -164,7 +144,6 @@
         + ([any_space, vmem] if made else []),
         out_specs=(any_space, vmem),
         scratch_shapes=[
-            pltpu.SMEM((4, PAIRS), jnp.int32),
             pltpu.VMEM((3, TILE, WIDTH), BF16),
             pltpu.VMEM((3, TILE, WIDTH), BF16),
             pltpu.VMEM((4, TILE, TILE), BF16),
@@ -207,8 +186,8 @@
         def _():
             fetch(position + depth - 1).start()
 
-        t = info[8 + position]
-        q = info[8 + PAIRS + position]
+        t = info[ROWS + position]
+        q = info[SLABS + position]
         if first:
             label = labels[pl.ds(q, 1), :]
             value = inv_root[pl.ds(q, 1), :]
@@ -398,6 +377,27 @@
     return lax.ppermute(value, ("zh", "zl"), [(0, 3), (3, 0), (1, 2), (2, 1)])
 
 
+def pair_list(count, block_index, rows, slabs, arrivals):
+    slot = jnp.arange(PAIRS, dtype=jnp.int32)
+    rank = jnp.sum(
+        jnp.where(slabs[:, None] == arrivals[None, :], jnp.arange(BLOCK_TILES, dtype=jnp.int32), 0), 1
+    )
+    key = jnp.where(slot < count, rank * PAIRS + slot, BLOCK_TILES * PAIRS + slot)
+    place = jnp.sum((key[None, :] < key[:, None]).astype(jnp.int32), axis=1)
+    at = place[None, :] == slot[:, None]
+
+    def ordered(value):
+        return jnp.sum(jnp.where(at, value[None, :], 0), axis=1)
+
+    ranks = ordered(rank)
+    fresh = jnp.concatenate([jnp.zeros(1, bool), ranks[1:] != ranks[:-1]])
+    groups = jnp.sum(jnp.where(slot[None, :] <= slot[:, None], fresh[None, :], False).astype(jnp.int32), 1)
+    limit = jnp.arange(BLOCK_TILES + 1, dtype=jnp.int32) * PAIRS
+    starts = jnp.sum((key[None, :] < limit[:, None]).astype(jnp.int32), axis=1)
+    head = jnp.stack([count, block_index] + [jnp.int32(0)] * 6)
+    return jnp.concatenate([head, ordered(rows), ordered(slabs), ranks, groups, starts]).astype(jnp.int32)
+
+
 def shards(embeddings, labels, pair_rows, pair_cols, pair_count):
     y, zh, core = (lax.axis_index(a) for a in ROW)
     slab_index = lax.axis_index(ROW)
@@ -423,29 +423,39 @@
                 of(4 - side(k), 1, k),
             ]
         )
-    arrivals = [q for both in zip(*arrivals, strict=True) for q in both]
-    head = [pair_count[0, 0], slab_index, block_index] + [jnp.int32(0)] * 5
-    info = jnp.concatenate(
-        [jnp.stack(head), pair_rows[0, 0], pair_cols[0, 0], jnp.stack(arrivals)]
-    ).astype(jnp.int32)
+    first, second = arrivals
+    arrivals = [q for both in zip(first[:6], second[:6], strict=True) for q in both]
+    arrivals = jnp.stack(arrivals + first[6:] + second[6:])
+    info = pair_list(pair_count[0, 0], block_index, pair_rows[0, 0], pair_cols[0, 0], arrivals)
 
     own = lax.dynamic_index_in_dim(slab, block_index, 0, keepdims=False)
     give = lax.dynamic_index_in_dim(slab, block_index ^ 1, 0, keepdims=False)
     across = cross(give)
     below = up(own)
     above = down(own)
-    beyond = apart(jnp.where(zero, below, above))
-    near = apart(across)
-    far = apart(near)
-    other = apart_z(apart_z(jnp.where(zero, above, below)))
     half_rows = 0.5 * jnp.sum(jnp.square(slab.astype(F32)), axis=2)
     column_labels = share_row(labels[None].astype(F32))[:, 0].astype(jnp.int32)
-    made = ()
-    first = 0
-    for stage in ((own,), (across, below, above), (beyond, near), (far, other)):
-        columns = [piece for tile in stage for piece in (tile, swap_cores(tile))]
-        made = build(first, info, slab, half_rows, columns, made)
-        first += len(columns)
+
+    def both(*pieces):
+        return [each for piece in pieces for each in (piece, swap_cores(piece))]
+
+    def after(made, *pieces):
+        tied = lax.optimization_barrier((made[1], column_labels) + pieces)
+        return (made[0], tied[0]), tied[2:]
+
+    made = build(0, info, slab, half_rows, both(own), ())
+    made, (across, below, above) = after(made, across, below, above)
+    near = apart(across)
+    beyond = apart(jnp.where(zero, below, above))
+    other = apart_z(jnp.where(zero, above, below))
+    made = build(2, info, slab, half_rows, both(across, below), made)
+    made, (near, beyond, other) = after(made, near, beyond, other)
+    far = apart(near)
+    other = apart_z(other)
+    made = build(6, info, slab, half_rows, both(above, beyond, near), made)
+    made, last = after(made, far, other)
+    made = build(12, info, slab, half_rows, last, made)
+    made = build(14, info, slab, half_rows, [swap_cores(piece) for piece in last], made)
     tiles, partial_degree = made
 
     spread = jnp.broadcast_to(partial_degree[None, :, None], (8, SLAB_TILES, 1, TILE))

time: 272 us -> 262 us (0.963)
  starting transfers between devices: 73.6 us -> 40 us
  blocking collectives: 74.6 us -> 91.8 us
  local copies, waits for them, and re-layouts: 14.5 us -> 20.9 us
  waiting for transfers between devices: 59.5 us -> 64.9 us
  Pallas kernels: 40.2 us -> 35.3 us
    all_to_all x1 -> x0, starting transfers between devices: 27.3 us -> none  [shards(): lax.all_to_all(spread.reshape(8 * SLAB_TILES, 1, TILE), CHIPS, 0, 0, tile...]
    all_to_all x0 -> x1, blocking collectives: none -> 20.7 us  [shards(): lax.all_to_all(spread.reshape(8 * SLAB_TILES, 1, TILE), CHIPS, 0, 0, tile...]
    ppermute x1, waiting for transfers between devices: 17.6 us -> 0.01 us  [up(): return lax.ppermute(value, 'y', [(i, (i + 1) % 4) for i in range(4)])]
    ppermute x3, waiting for transfers between devices: 3 us -> 19.3 us  [apart(): lax.ppermute(value, ('y', 'core'), [(2 * i + k, 2 * ((i + 1 + 2 * k) % 4)...]
    all_to_all x1, waiting for transfers between devices: 0.01 us -> 12.3 us  [share(): lax.all_to_all(jnp.broadcast_to(value[None], (size,) + value.shape), axes...]
    all_to_all x1 -> x0, waiting for transfers between devices: 7.81 us -> none  [shards(): lax.all_to_all(spread.reshape(8 * SLAB_TILES, 1, TILE), CHIPS, 0, 0, tile...]
    unnamed x12, local copies, waits for them, and re-layouts: 10.1 us -> 17 us
    ppermute x15, waiting for transfers between devices: 5.59 us -> 10.9 us  [swap_cores(): return lax.ppermute(value, 'core', [(0, 1), (1, 0)])]
  transfers between devices with their start and end apart: 26 -> 25, of which waited for: 11 -> 17; matrix products, arithmetic and copies ran while one was open for 3% -> 3% of each run, Pallas kernels for 7% -> 4%
where the time goes in v3:
time: 262 us; the launch traced here: 261 us
  blocking collectives  91.8 us (35%)
  waiting for transfers between devices  64.9 us (25%)
  starting transfers between devices  40 us (15%)
  Pallas kernels  35.3 us (13%)
  local copies, waits for them, and re-layouts  20.9 us (8%)
  other arithmetic  7.2 us (3%)
    all_to_all x3, blocking collectives, share(): lax.all_to_all(jnp.broadcast_to(value[None], (size,) + value.shape), axes...  53.2 us
    ppermute x15, starting transfers between devices, swap_cores(): return lax.ppermute(value, 'core', [(0, 1), (1, 0)])  20.7 us
    all_to_all x1, blocking collectives, shards(): lax.all_to_all(spread.reshape(8 * SLAB_TILES, 1, TILE), CHIPS, 0, 0, tile...  20.7 us
    ppermute x3, waiting for transfers between devices, apart(): lax.ppermute(value, ('y', 'core'), [(2 * i + k, 2 * ((i + 1 + 2 * k) % 4)...  19.3 us
    all_to_all x1, blocking collectives, shards(): parts = lax.all_to_all(running, COL, 0, 0, tiled=True)  17.9 us
    all_to_all x1, waiting for transfers between devices, shards(): parts = lax.all_to_all(running, COL, 0, 0, tiled=True)  17.6 us
    unnamed x12, local copies, waits for them, and re-layouts  17 us
    pallas_call x5, Pallas kernels, build(): pl.pallas_call(functools.partial(build_kernel, first, arrived), out_shape...  14.7 us
  transfers between devices with their start and end apart: 25, of which 17 were waited for; matrix products, arithmetic and copies ran while one was open for 3% of the time, Pallas kernels for 4%

profile of v3, /device:TPU:1, one launch (start us, length us, event | category | flops | bytes accessed | tf_op | source)
XLA Modules:
  0.0 261.3 jit_solution(5237701357122964990)
XLA Ops:
  0.0 2.7 %dynamic-slice_bitcast_fusion = (bf16[512,1024]{1,0:T(8,128)(2,1)}, bf16[512,1024]{1,0:T(8,128)(2,1)S(1)}) fusion(bf16[8,512,1024]{2,1,0:T(8,128)(2,1)} %bitcast.37, s32[]{:T(128)S(6)} %select_n.234, s32[]{:T(128)S(6)} %select_n.231), kind=kLoop, calls=%fused_computation.2 | loop fusion | bytes 4194312 | tf_op jit(solution)/shard_map/jit(dynamic_index_in_dim)/squeeze | solution.py:432
  7.0 3.8 %collective-permute-start.2 = (bf16[512,1024]{1,0:T(8,128)(2,1)}, bf16[512,1024]{1,0:T(8,128)(2,1)}, u32[]{:S(2)}, u32[]{:S(2)}) collective-permute-start(bf16[512,1024]{1,0:T(8,128)(2,1)} %get-tuple-element.58), channel_id=1, source_target_pairs={{0,17},{17,0},{1,16},{16,1},{2,19},{19,2},{3,18},{18,3},{4,21},{21... | collective-permute-start | bytes 3145736 | tf_op jit(solution)/shard_map/ppermute | solution.py:377
  12.0 3.3 %all-to-all-start = ((f32[8,1,512]{2,1,0:T(1,128)}), f32[8,1,512]{2,1,0:T(1,128)S(1)}, u32[]{:S(2)}, u32[]{:S(2)}) async-start(f32[8,1,512]{2,1,0:T(1,128)} %broadcast_in_dim.99), calls=%async_computation | async-start | bytes 32768 | tf_op jit(solution)/shard_map/all_to_all | solution.py:327
  15.5 5.1 %multiply_reduce_fusion = f32[4096]{0:T(1024)S(1)} fusion(bf16[4096,1024]{1,0:T(8,128)(2,1)} %param.5), kind=kLoop, calls=%fused_computation | loop fusion | flops 12578816 | bytes 8404992 | tf_op jit(solution)/shard_map/reduce_sum | solution.py:436
  22.2 12.3 %all-to-all-done = f32[8,1,512]{2,1,0:T(1,128)S(1)} async-done(((f32[8,1,512]{2,1,0:T(1,128)}), f32[8,1,512]{2,1,0:T(1,128)S(1)}, u32[]{:S(2)}, u32[]{:S(2)}) %all-to-all-start) | async-done | bytes 16416 | tf_op jit(solution)/shard_map/all_to_all | solution.py:327
  36.6 3.4 %copy-done.3 = bf16[4096,1024]{1,0:T(8,128)(2,1)S(1)} copy-done((bf16[4096,1024]{1,0:T(8,128)(2,1)S(1)}, bf16[4096,1024]{1,0:T(8,128)(2,1)}, u32[]{:S(2)}) %copy-start.3) | copy-done | bytes 8388632
  43.7 2.8 %collective-permute-start.10 = (bf16[512,1024]{1,0:T(8,128)(2,1)S(1)}, bf16[512,1024]{1,0:T(8,128)(2,1)S(1)}, u32[]{:S(2)}, u32[]{:S(2)}) collective-permute-start(bf16[512,1024]{1,0:T(8,128)(2,1)S(1)} %get-tuple-element.60), channel_id=1, source_target_pairs={{0,1},{8,25},{1,16},{9,8},{16,17},{24,9},{17,0},{25,24},{2,3},{10,... | collective-permute-start | bytes 3145736 | tf_op jit(solution)/shard_map/ppermute | solution.py:373
  48.9 4.9 %build_tiles.6 = (bf16[24,512,512]{2,1,0:T(8,128)(2,1)S(1)}, f32[8,512]{1,0:T(8,128)S(1)}) custom-call(s32[121]{0:T(128)S(1)} %concatenate.17.info, bf16[8,512,1024]{2,1,0:T(8,128)(2,1)S(1)} %bitcast.39, f32[8,512]{1,0:T(8,128)S(1)} %mul.134.half_rows, bf16[512,1024]{1,0:T(8,128)(2,1)} %collective-permute-done.2.refs_0_, ...), custom_call_target="tpu_custom_call", output_to_operand_aliasing={{0}: (7, {})} | custom-call | flops 3221225472 | bytes 15728640 | tf_op jit(solution)/shard_map/build_tiles/pallas_call | solution.py:136
  53.8 4.4 %collective-permute-done.10 = bf16[512,1024]{1,0:T(8,128)(2,1)S(1)} collective-permute-done((bf16[512,1024]{1,0:T(8,128)(2,1)S(1)}, bf16[512,1024]{1,0:T(8,128)(2,1)S(1)}, u32[]{:S(2)}, u32[]{:S(2)}) %collective-permute-start.10) | collective-permute-done | bytes 1048608 | tf_op jit(solution)/shard_map/ppermute | solution.py:373
  58.3 2.2 collective-permute-done.9.refs_2_
  60.5 11.2 %collective-permute-done.8.refs_4_ = bf16[512,1024]{1,0:T(8,128)(2,1)S(1)} collective-permute-done((bf16[512,1024]{1,0:T(8,128)(2,1)}, bf16[512,1024]{1,0:T(8,128)(2,1)S(1)}, u32[]{:S(2)}, u32[]{:S(2)}) %collective-permute-start.8) | collective-permute-done | bytes 1048608 | tf_op jit(solution)/shard_map/ppermute | solution.py:360
  77.4 4.3 %build_tiles.7 = (bf16[24,512,512]{2,1,0:T(8,128)(2,1)S(1)}, f32[8,512]{1,0:T(8,128)S(1)}) custom-call(s32[121]{0:T(128)S(1)} %concatenate.17.info, bf16[8,512,1024]{2,1,0:T(8,128)(2,1)S(1)} %bitcast.40, f32[8,512]{1,0:T(8,128)S(1)} %mul.134.half_rows, bf16[512,1024]{1,0:T(8,128)(2,1)S(1)} %collective-permute-done.4.refs_0_, ...), custom_call_target="tpu_custom_call", output_to_operand_aliasing={{0}: (9, {})} | custom-call | flops 4831838208 | bytes 23592960 | tf_op jit(solution)/shard_map/build_tiles/pallas_call | solution.py:136
  81.6 5.9 %collective-permute-done.13.refs_0_ = bf16[512,1024]{1,0:T(8,128)(2,1)S(1)} collective-permute-done((bf16[512,1024]{1,0:T(8,128)(2,1)S(1)}, bf16[512,1024]{1,0:T(8,128)(2,1)S(1)}, u32[]{:S(2)}, u32[]{:S(2)}) %collective-permute-start.13) | collective-permute-done | bytes 1048608 | tf_op jit(solution)/shard_map/ppermute | solution.py:360
  87.9 2.2 collective-permute-start.15
  93.9 3.0 %build_tiles.9 = (bf16[24,512,512]{2,1,0:T(8,128)(2,1)S(1)}, f32[8,512]{1,0:T(8,128)S(1)}) custom-call(s32[121]{0:T(128)S(1)} %concatenate.17.info, bf16[8,512,1024]{2,1,0:T(8,128)(2,1)S(1)} %bitcast.42, f32[8,512]{1,0:T(8,128)S(1)} %mul.134.half_rows, bf16[512,1024]{1,0:T(8,128)(2,1)S(1)} %collective-permute-done.15.refs_0_, ...), custom_call_target="tpu_custom_call", output_to_operand_aliasing={{0}: (5, {})} | custom-call | flops 1610612736 | bytes 7864320 | tf_op jit(solution)/shard_map/build_tiles/pallas_call | solution.py:136
  96.9 4.5 %copy-done = bf16[24,512,512]{2,1,0:T(8,128)(2,1)} copy-done((bf16[24,512,512]{2,1,0:T(8,128)(2,1)}, bf16[24,512,512]{2,1,0:T(8,128)(2,1)S(1)}, u32[]{:S(2)}) %copy-start) | copy-done | bytes 12582936
  101.6 20.7 %all_to_all.35 = f32[64,1,512]{2,1,0:T(1,128)S(1)} all-to-all(f32[64,1,512]{2,1,0:T(1,128)S(1)} %broadcast_in_dim.101), channel_id=1, replica_groups=mesh['y'=4,'zh'=2,'core'=2,'x'=4,'zl'=2] {'y','zh','x','zl'}, dimensions={0} | all-to-all | bytes 262144 | tf_op jit(solution)/shard_map/all_to_all | solution.py:462
  122.3 3.4 %collective-permute-start.17 = (f32[8,512]{1,0:T(8,128)S(1)}, f32[8,512]{1,0:T(8,128)S(1)}, u32[]{:S(2)}, u32[]{:S(2)}) collective-permute-start(f32[8,512]{1,0:T(8,128)S(1)} %bitcast_reduce_fusion), channel_id=1, source_target_pairs={{0,8},{8,0},{1,9},{9,1},{2,10},{10,2},{3,11},{11,3},{4,12},{12,4},... | collective-permute-start | bytes 49160 | tf_op jit(solution)/shard_map/ppermute | solution.py:322
  126.7 4.6 %copy-done.1 = bf16[24,512,512]{2,1,0:T(8,128)(2,1)S(1)} copy-done((bf16[24,512,512]{2,1,0:T(8,128)(2,1)S(1)}, bf16[24,512,512]{2,1,0:T(8,128)(2,1)}, u32[]{:S(2)}) %copy-start.1) | copy-done | bytes 12582936
  131.2 4.1 %product.2 = f32[8,64,512]{2,1,0:T(8,128)} custom-call(s32[121]{0:T(128)S(1)} %concatenate.17.info, bf16[24,512,512]{2,1,0:T(8,128)(2,1)S(1)} %copy-done.1, s32[16,512]{1,0:T(8,128)S(1)} %convert_element_type.28.refs_0_, f32[16,512]{1,0:T(8,128)S(1)} %rsqrt.6.refs_1_), custom_call_target="tpu_custom_call" | custom-call | tf_op jit(solution)/shard_map/product/pallas_call | solution.py:210
  135.3 3.6 %all-to-all-start.2 = ((f32[8,64,512]{2,1,0:T(8,128)}), f32[8,64,512]{2,1,0:T(8,128)S(1)}, u32[]{:S(2)}, u32[]{:S(2)}) async-start(f32[8,64,512]{2,1,0:T(8,128)} %product.2), calls=%async_computation.2 | async-start | bytes 2097152 | tf_op jit(solution)/shard_map/all_to_all | solution.py:481
  138.9 17.6 %all-to-all-done.2.parts = f32[8,64,512]{2,1,0:T(8,128)S(1)} async-done(((f32[8,64,512]{2,1,0:T(8,128)}), f32[8,64,512]{2,1,0:T(8,128)S(1)}, u32[]{:S(2)}, u32[]{:S(2)}) %all-to-all-start.2) | async-done | bytes 1048608 | tf_op jit(solution)/shard_map/all_to_all | solution.py:481
  158.3 19.2 %all_to_all.36 = f32[64,16,128]{2,1,0:T(8,128)S(1)} all-to-all(f32[64,16,128]{2,1,0:T(8,128)S(1)} %broadcast_in_dim.102), channel_id=1, replica_groups=mesh['y'=4,'zh'=2,'core'=2,'x'=4,'zl'=2] {'y','zh','x','zl'}, dimensions={0} | all-to-all | bytes 1048576 | tf_op jit(solution)/shard_map/all_to_all | solution.py:327
  177.5 2.0 collective-permute-start.19
  180.3 6.0 %orthonormalize.2 = bf16[64,512]{1,0:T(8,128)(2,1)S(1)} custom-call(f32[32,128]{1,0:T(8,128)S(1)} %pad_maximum_fusion.message, f32[64,512]{1,0:T(8,128)S(1)} %get-tuple-element.52.image, f32[1,512]{1,0:T(1,128)S(1)} %get-tuple-element.63.inv_root, f32[1,512]{1,0:T(1,128)S(1)} %get-tuple-element.62.root), custom_call_target="tpu_custom_call" | custom-call | tf_op jit(solution)/shard_map/orthonormalize/pallas_call | solution.py:311
  186.4 12.7 %all_to_all.37 = bf16[8,64,512]{2,1,0:T(8,128)(2,1)S(1)} all-to-all(bf16[8,64,512]{2,1,0:T(8,128)(2,1)S(1)} %broadcast_in_dim.103), channel_id=1, replica_groups=mesh['y'=4,'zh'=2,'core'=2,'x'=4,'zl'=2] {'y','zh'}, dimensions={0} | all-to-all | bytes 1048576 | tf_op jit(solution)/shard_map/all_to_all | solution.py:327
  199.1 2.2 collective-permute-start.20
  203.0 4.6 %copy-done.2 = bf16[24,512,512]{2,1,0:T(8,128)(2,1)S(1)} copy-done((bf16[24,512,512]{2,1,0:T(8,128)(2,1)S(1)}, bf16[24,512,512]{2,1,0:T(8,128)(2,1)}, u32[]{:S(2)}) %copy-start.2) | copy-done | bytes 12582936
  207.5 2.9 %product.3 = f32[8,64,512]{2,1,0:T(8,128)S(1)} custom-call(s32[121]{0:T(128)S(1)} %concatenate.17.info, bf16[24,512,512]{2,1,0:T(8,128)(2,1)S(1)} %copy-done.2, bf16[16,64,512]{2,1,0:T(8,128)(2,1)S(1)} %bitcast.43), custom_call_target="tpu_custom_call" | custom-call | tf_op jit(solution)/shard_map/product/pallas_call | solution.py:210
  210.5 17.9 %all_to_all.38.parts = f32[8,64,512]{2,1,0:T(8,128)S(1)} all-to-all(f32[8,64,512]{2,1,0:T(8,128)S(1)} %product.3), channel_id=1, replica_groups=mesh['y'=4,'zh'=2,'core'=2,'x'=4,'zl'=2] {'x','zl'}, dimensions={0} | all-to-all | bytes 2097152 | tf_op jit(solution)/shard_map/all_to_all | solution.py:481
  230.4 21.3 %all_to_all.39 = f32[64,16,128]{2,1,0:T(8,128)S(1)} all-to-all(f32[64,16,128]{2,1,0:T(8,128)S(1)} %broadcast_in_dim.104), channel_id=1, replica_groups=mesh['y'=4,'zh'=2,'core'=2,'x'=4,'zl'=2] {'y','zh','x','zl'}, dimensions={0} | all-to-all | bytes 1048576 | tf_op jit(solution)/shard_map/all_to_all | solution.py:327
  254.6 6.7 %orthonormalize.3 = f32[64,512]{1,0:T(8,128)} custom-call(f32[32,128]{1,0:T(8,128)S(1)} %pad_maximum_fusion.1.message, f32[64,512]{1,0:T(8,128)S(1)} %get-tuple-element.54.image, f32[1,512]{1,0:T(1,128)S(1)} %get-tuple-element.63.inv_root, f32[1,512]{1,0:T(1,128)S(1)} %get-tuple-element.62.root), custom_call_target="tpu_custom_call" | custom-call | tf_op jit(solution)/shard_map/orthonormalize/pallas_call | solution.py:311
  (91 shorter events, 34.8 us)
Async XLA Ops:
  0.0 21.4 %copy-start.4 = (s32[1,1,24]{2,1,0:T(1,128)S(1)}, s32[1,1,24]{2,1,0:T(1,128)}, u32[]{:S(2)}) copy-start(s32[1,1,24]{2,1,0:T(1,128)} %param.8) | copy-start | bytes 292
  0.0 21.9 %copy-start.5 = (s32[1,1,24]{2,1,0:T(1,128)S(1)}, s32[1,1,24]{2,1,0:T(1,128)}, u32[]{:S(2)}) copy-start(s32[1,1,24]{2,1,0:T(1,128)} %param.7) | copy-start | bytes 292
  2.7 33.9 %collective-permute-start = (bf16[512,1024]{1,0:T(8,128)(2,1)S(1)}, bf16[512,1024]{1,0:T(8,128)(2,1)}, u32[]{:S(2)}, u32[]{:S(2)}) collective-permute-start(bf16[512,1024]{1,0:T(8,128)(2,1)S(1)} %get-tuple-element.59.refs_0_), channel_id=1, source_target_pairs={{0,8},{8,0},{1,9},{9,1},{2,10},{10,2},{3,11},{11,3},{4,12},{12,4},... | collective-permute-start | bytes 3145736 | tf_op jit(solution)/shard_map/ppermute | solution.py:322
  4.1 37.8 %collective-permute-start.3 = (bf16[512,1024]{1,0:T(8,128)(2,1)S(1)}, bf16[512,1024]{1,0:T(8,128)(2,1)S(1)}, u32[]{:S(2)}, u32[]{:S(2)}) collective-permute-start(bf16[512,1024]{1,0:T(8,128)(2,1)S(1)} %get-tuple-element.59.refs_0_), channel_id=1, source_target_pairs={{0,32},{32,64},{64,96},{96,0},{1,33},{33,65},{65,97},{97,1},{2,34}... | collective-permute-start | bytes 3145736 | tf_op jit(solution)/shard_map/ppermute | solution.py:352
  5.5 36.5 %collective-permute-start.4 = (bf16[512,1024]{1,0:T(8,128)(2,1)S(1)}, bf16[512,1024]{1,0:T(8,128)(2,1)S(1)}, u32[]{:S(2)}, u32[]{:S(2)}) collective-permute-start(bf16[512,1024]{1,0:T(8,128)(2,1)S(1)} %get-tuple-element.59.refs_0_), channel_id=1, source_target_pairs={{0,96},{32,0},{64,32},{96,64},{1,97},{33,1},{65,33},{97,65},{2,98}... | collective-permute-start | bytes 3145736 | tf_op jit(solution)/shard_map/ppermute | solution.py:356
  7.0 35.0 %collective-permute-start.2 = (bf16[512,1024]{1,0:T(8,128)(2,1)}, bf16[512,1024]{1,0:T(8,128)(2,1)}, u32[]{:S(2)}, u32[]{:S(2)}) collective-permute-start(bf16[512,1024]{1,0:T(8,128)(2,1)} %get-tuple-element.58), channel_id=1, source_target_pairs={{0,17},{17,0},{1,16},{16,1},{2,19},{19,2},{3,18},{18,3},{4,21},{21... | collective-permute-start | bytes 3145736 | tf_op jit(solution)/shard_map/ppermute | solution.py:377
  12.0 22.5 %all-to-all-start = ((f32[8,1,512]{2,1,0:T(1,128)}), f32[8,1,512]{2,1,0:T(1,128)S(1)}, u32[]{:S(2)}, u32[]{:S(2)}) async-start(f32[8,1,512]{2,1,0:T(1,128)} %broadcast_in_dim.99), calls=%async_computation | async-start | bytes 32768 | tf_op jit(solution)/shard_map/all_to_all | solution.py:327
  34.5 2.0 collective-permute-start.1
  36.6 3.4 %copy-start.3 = (bf16[4096,1024]{1,0:T(8,128)(2,1)S(1)}, bf16[4096,1024]{1,0:T(8,128)(2,1)}, u32[]{:S(2)}) copy-start(bf16[4096,1024]{1,0:T(8,128)(2,1)} %param.5) | copy-start | bytes 25165828
  42.0 5.2 %collective-permute-start.6 = (bf16[512,1024]{1,0:T(8,128)(2,1)}, bf16[512,1024]{1,0:T(8,128)(2,1)S(1)}, u32[]{:S(2)}, u32[]{:S(2)}) collective-permute-start(bf16[512,1024]{1,0:T(8,128)(2,1)} %collective-permute-done.2.refs_0_), channel_id=1, source_target_pairs={{0,8},{8,0},{1,9},{9,1},{2,10},{10,2},{3,11},{11,3},{4,12},{12,4},... | collective-permute-start | bytes 3145736 | tf_op jit(solution)/shard_map/ppermute | solution.py:322
  43.5 5.4 %collective-permute-start.7 = (bf16[512,1024]{1,0:T(8,128)(2,1)S(1)}, bf16[512,1024]{1,0:T(8,128)(2,1)S(1)}, u32[]{:S(2)}, u32[]{:S(2)}) collective-permute-start(bf16[512,1024]{1,0:T(8,128)(2,1)S(1)} %collective-permute-done.3.refs_2_), channel_id=1, source_target_pairs={{0,8},{8,0},{1,9},{9,1},{2,10},{10,2},{3,11},{11,3},{4,12},{12,4},... | collective-permute-start | bytes 3145736 | tf_op jit(solution)/shard_map/ppermute | solution.py:322
  43.7 14.5 %collective-permute-start.10 = (bf16[512,1024]{1,0:T(8,128)(2,1)S(1)}, bf16[512,1024]{1,0:T(8,128)(2,1)S(1)}, u32[]{:S(2)}, u32[]{:S(2)}) collective-permute-start(bf16[512,1024]{1,0:T(8,128)(2,1)S(1)} %get-tuple-element.60), channel_id=1, source_target_pairs={{0,1},{8,25},{1,16},{9,8},{16,17},{24,9},{17,0},{25,24},{2,3},{10,... | collective-permute-start | bytes 3145736 | tf_op jit(solution)/shard_map/ppermute | solution.py:373
  46.5 13.9 %collective-permute-start.9 = (bf16[512,1024]{1,0:T(8,128)(2,1)S(1)}, bf16[512,1024]{1,0:T(8,128)(2,1)S(1)}, u32[]{:S(2)}, u32[]{:S(2)}) collective-permute-start(bf16[512,1024]{1,0:T(8,128)(2,1)S(1)} %get-tuple-element.61), channel_id=1, source_target_pairs={{0,32},{8,104},{32,64},{40,8},{64,96},{72,40},{96,0},{104,72},{1,3... | collective-permute-start | bytes 3145736 | tf_op jit(solution)/shard_map/ppermute | solution.py:360
  47.0 24.7 %collective-permute-start.8 = (bf16[512,1024]{1,0:T(8,128)(2,1)}, bf16[512,1024]{1,0:T(8,128)(2,1)S(1)}, u32[]{:S(2)}, u32[]{:S(2)}) collective-permute-start(bf16[512,1024]{1,0:T(8,128)(2,1)} %collective-permute-done.2.refs_0_), channel_id=1, source_target_pairs={{0,32},{8,104},{32,64},{40,8},{64,96},{72,40},{96,0},{104,72},{1,3... | collective-permute-start | bytes 3145736 | tf_op jit(solution)/shard_map/ppermute | solution.py:360
  47.2 28.7 %collective-permute-start.5 = (bf16[512,1024]{1,0:T(8,128)(2,1)S(1)}, bf16[512,1024]{1,0:T(8,128)(2,1)S(1)}, u32[]{:S(2)}, u32[]{:S(2)}) collective-permute-start(bf16[512,1024]{1,0:T(8,128)(2,1)S(1)} %collective-permute-done.4.refs_0_), channel_id=1, source_target_pairs={{0,8},{8,0},{1,9},{9,1},{2,10},{10,2},{3,11},{11,3},{4,12},{12,4},... | collective-permute-start | bytes 3145736 | tf_op jit(solution)/shard_map/ppermute | solution.py:322
  71.7 4.2 %collective-permute-start.11 = (bf16[512,1024]{1,0:T(8,128)(2,1)S(1)}, bf16[512,1024]{1,0:T(8,128)(2,1)S(1)}, u32[]{:S(2)}, u32[]{:S(2)}) collective-permute-start(bf16[512,1024]{1,0:T(8,128)(2,1)S(1)} %collective-permute-done.9.refs_2_), channel_id=1, source_target_pairs={{0,8},{8,0},{1,9},{9,1},{2,10},{10,2},{3,11},{11,3},{4,12},{12,4},... | collective-permute-start | bytes 3145736 | tf_op jit(solution)/shard_map/ppermute | solution.py:322
  73.6 3.8 %collective-permute-start.12 = (bf16[512,1024]{1,0:T(8,128)(2,1)S(1)}, bf16[512,1024]{1,0:T(8,128)(2,1)S(1)}, u32[]{:S(2)}, u32[]{:S(2)}) collective-permute-start(bf16[512,1024]{1,0:T(8,128)(2,1)S(1)} %collective-permute-done.8.refs_4_), channel_id=1, source_target_pairs={{0,8},{8,0},{1,9},{9,1},{2,10},{10,2},{3,11},{11,3},{4,12},{12,4},... | collective-permute-start | bytes 3145736 | tf_op jit(solution)/shard_map/ppermute | solution.py:322
  73.6 13.9 %collective-permute-start.13 = (bf16[512,1024]{1,0:T(8,128)(2,1)S(1)}, bf16[512,1024]{1,0:T(8,128)(2,1)S(1)}, u32[]{:S(2)}, u32[]{:S(2)}) collective-permute-start(bf16[512,1024]{1,0:T(8,128)(2,1)S(1)} %collective-permute-done.8.refs_4_), channel_id=1, source_target_pairs={{0,32},{8,104},{32,64},{40,8},{64,96},{72,40},{96,0},{104,72},{1,3... | collective-permute-start | bytes 3145736 | tf_op jit(solution)/shard_map/ppermute | solution.py:360
  73.9 13.9 %collective-permute-start.14 = (bf16[512,1024]{1,0:T(8,128)(2,1)S(1)}, bf16[512,1024]{1,0:T(8,128)(2,1)S(1)}, u32[]{:S(2)}, u32[]{:S(2)}) collective-permute-start(bf16[512,1024]{1,0:T(8,128)(2,1)S(1)} %collective-permute-done.10), channel_id=1, source_target_pairs={{0,1},{8,25},{1,16},{9,8},{16,17},{24,9},{17,0},{25,24},{2,3},{10,... | collective-permute-start | bytes 3145736 | tf_op jit(solution)/shard_map/ppermute | solution.py:373
  87.9 4.5 %collective-permute-start.15 = (bf16[512,1024]{1,0:T(8,128)(2,1)S(1)}, bf16[512,1024]{1,0:T(8,128)(2,1)S(1)}, u32[]{:S(2)}, u32[]{:S(2)}) collective-permute-start(bf16[512,1024]{1,0:T(8,128)(2,1)S(1)} %collective-permute-done.13.refs_0_), channel_id=1, source_target_pairs={{0,8},{8,0},{1,9},{9,1},{2,10},{10,2},{3,11},{11,3},{4,12},{12,4},... | collective-permute-start | bytes 3145736 | tf_op jit(solution)/shard_map/ppermute | solution.py:322
  90.1 3.8 %collective-permute-start.16 = (bf16[512,1024]{1,0:T(8,128)(2,1)S(1)}, bf16[512,1024]{1,0:T(8,128)(2,1)S(1)}, u32[]{:S(2)}, u32[]{:S(2)}) collective-permute-start(bf16[512,1024]{1,0:T(8,128)(2,1)S(1)} %collective-permute-done.14.refs_1_), channel_id=1, source_target_pairs={{0,8},{8,0},{1,9},{9,1},{2,10},{10,2},{3,11},{11,3},{4,12},{12,4},... | collective-permute-start | bytes 3145736 | tf_op jit(solution)/shard_map/ppermute | solution.py:322
  96.9 4.5 %copy-start = (bf16[24,512,512]{2,1,0:T(8,128)(2,1)}, bf16[24,512,512]{2,1,0:T(8,128)(2,1)S(1)}, u32[]{:S(2)}) copy-start(bf16[24,512,512]{2,1,0:T(8,128)(2,1)S(1)} %get-tuple-element.49.tiles) | copy-start | bytes 37748740
  122.3 4.2 %collective-permute-start.17 = (f32[8,512]{1,0:T(8,128)S(1)}, f32[8,512]{1,0:T(8,128)S(1)}, u32[]{:S(2)}, u32[]{:S(2)}) collective-permute-start(f32[8,512]{1,0:T(8,128)S(1)} %bitcast_reduce_fusion), channel_id=1, source_target_pairs={{0,8},{8,0},{1,9},{9,1},{2,10},{10,2},{3,11},{11,3},{4,12},{12,4},... | collective-permute-start | bytes 49160 | tf_op jit(solution)/shard_map/ppermute | solution.py:322
  126.7 4.6 %copy-start.1 = (bf16[24,512,512]{2,1,0:T(8,128)(2,1)S(1)}, bf16[24,512,512]{2,1,0:T(8,128)(2,1)}, u32[]{:S(2)}) copy-start(bf16[24,512,512]{2,1,0:T(8,128)(2,1)} %copy-done) | copy-start | bytes 37748740
  135.3 21.2 %all-to-all-start.2 = ((f32[8,64,512]{2,1,0:T(8,128)}), f32[8,64,512]{2,1,0:T(8,128)S(1)}, u32[]{:S(2)}, u32[]{:S(2)}) async-start(f32[8,64,512]{2,1,0:T(8,128)} %product.2), calls=%async_computation.2 | async-start | bytes 2097152 | tf_op jit(solution)/shard_map/all_to_all | solution.py:481
  156.9 1.3 collective-permute-start.18
  177.5 2.8 %collective-permute-start.19 = (f32[16,128]{1,0:T(8,128)S(1)}, f32[16,128]{1,0:T(8,128)S(1)}, u32[]{:S(2)}, u32[]{:S(2)}) collective-permute-start(f32[16,128]{1,0:T(8,128)S(1)} %reduce_sum.108), channel_id=1, source_target_pairs={{0,8},{8,0},{1,9},{9,1},{2,10},{10,2},{3,11},{11,3},{4,12},{12,4},... | collective-permute-start | bytes 24584 | tf_op jit(solution)/shard_map/ppermute | solution.py:322
  199.1 3.7 %collective-permute-start.20 = (bf16[8,64,512]{2,1,0:T(8,128)(2,1)S(1)}, bf16[8,64,512]{2,1,0:T(8,128)(2,1)S(1)}, u32[]{:S(2)}, u32[]{:S(2)}) collective-permute-start(bf16[8,64,512]{2,1,0:T(8,128)(2,1)S(1)} %all_to_all.37), channel_id=1, source_target_pairs={{0,8},{8,0},{1,9},{9,1},{2,10},{10,2},{3,11},{11,3},{4,12},{12,4},... | collective-permute-start | bytes 1572872 | tf_op jit(solution)/shard_map/ppermute | solution.py:322
  202.9 4.6 %copy-start.2 = (bf16[24,512,512]{2,1,0:T(8,128)(2,1)S(1)}, bf16[24,512,512]{2,1,0:T(8,128)(2,1)}, u32[]{:S(2)}) copy-start(bf16[24,512,512]{2,1,0:T(8,128)(2,1)} %copy-done) | copy-start | bytes 37748740
  228.8 1.5 collective-permute-start.21
  251.8 2.8 %collective-permute-start.22 = (f32[16,128]{1,0:T(8,128)S(1)}, f32[16,128]{1,0:T(8,128)S(1)}, u32[]{:S(2)}, u32[]{:S(2)}) collective-permute-start(f32[16,128]{1,0:T(8,128)S(1)} %reduce_sum.109), channel_id=1, source_target_pairs={{0,8},{8,0},{1,9},{9,1},{2,10},{10,2},{3,11},{11,3},{4,12},{12,4},... | collective-permute-start | bytes 24584 | tf_op jit(solution)/shard_map/ppermute | solution.py:322

commit v4 on v3

--- a/solution.py
+++ b/solution.py
@@ -11,7 +11,6 @@
 
 TILE = 512
 K = 64
-ITERS = 2
 PAIRS = 24
 WIDTH = 1024
 KERNEL_SCALE = 0.5
@@ -130,6 +129,7 @@
 
 def build(first, info, slab, half_rows, columns, made):
     any_space = pl.BlockSpec(memory_space=pl.ANY)
+    hbm = pl.BlockSpec(memory_space=pltpu.HBM)
     vmem = pl.BlockSpec(memory_space=pltpu.VMEM)
     arrived = len(columns)
     pairs = PAIRS * arrived // BLOCK_TILES
@@ -139,10 +139,10 @@
             jax.ShapeDtypeStruct((PAIRS, TILE, TILE), BF16),
             jax.ShapeDtypeStruct((SLAB_TILES, TILE), F32),
         ),
-        in_specs=[pl.BlockSpec(memory_space=pltpu.SMEM), any_space, vmem]
+        in_specs=[pl.BlockSpec(memory_space=pltpu.SMEM), hbm, vmem]
         + [any_space] * arrived
-        + ([any_space, vmem] if made else []),
-        out_specs=(any_space, vmem),
+        + ([hbm, vmem] if made else []),
+        out_specs=(hbm, vmem),
         scratch_shapes=[
             pltpu.VMEM((3, TILE, WIDTH), BF16),
             pltpu.VMEM((3, TILE, WIDTH), BF16),
@@ -166,69 +166,91 @@
     if first:
         labels, inv_root, running, held, sem = refs
     else:
-        scaled, running, held, sem = refs
-    count = info[0]
+        mine, others, inv_root, running, held, sem = refs
+    count, core = info[0], info[2]
+    depth = held.shape[0]
     running[...] = jnp.zeros_like(running)
-    depth = held.shape[0]
-
-    def fetch(position):
-        slot = lax.rem(position, depth)
-        return pltpu.make_async_copy(tiles.at[position], held.at[slot], sem.at[slot])
-
-    for ahead in range(depth - 1):
-
-        @pl.when(ahead < count)
-        def _():
-            fetch(ahead).start()
-
-    def step(position, carry):
-        @pl.when(position + depth - 1 < count)
-        def _():
-            fetch(position + depth - 1).start()
-
-        t = info[ROWS + position]
-        q = info[SLABS + position]
+    if not first:
+        rest = jnp.sum(mine[:, K:, :], axis=0) + jnp.sum(others[:, K:, :], axis=0)
+        for t in range(SLAB_TILES):
+            running[t, K:, :] = rest
+
+    def fetch(entry):
+        slot = lax.rem(entry, depth)
+        return pltpu.make_async_copy(tiles.at[entry], held.at[slot], sem.at[slot])
+
+    def piece(entry):
+        q = info[SLABS + entry]
+        value = inv_root[pl.ds(q, 1), :]
         if first:
             label = labels[pl.ds(q, 1), :]
-            value = inv_root[pl.ds(q, 1), :]
             value = jnp.where(label < K, value, -value)
-            mine = (label & (K - 1)) == lax.broadcasted_iota(jnp.int32, (K, TILE), 0)
-            piece = jnp.where(mine, jnp.broadcast_to(value, (K, TILE)), 0.0).astype(BF16)
-        else:
-            piece = scaled[q]
-        fetch(position).wait()
-        running[t] += jnp.dot(
-            piece, held[lax.rem(position, depth)], preferred_element_type=F32
+            same = (label & (K - 1)) == lax.broadcasted_iota(jnp.int32, (K, TILE), 0)
+            return jnp.where(same, jnp.broadcast_to(value, (K, TILE)), 0.0).astype(BF16)
+        chip = q // 2
+        vectors = jnp.where(q % 2 == core, mine[chip, :K, :], others[chip, :K, :]) * value
+        high = vectors.astype(BF16)
+        low = (vectors - high.astype(F32)).astype(BF16)
+        return jnp.concatenate([high, low], axis=0)
+
+    def term(entry):
+        result = jnp.dot(
+            piece(entry), held[lax.rem(entry, depth)], preferred_element_type=F32
         )
+        return result if first else result[:K] + result[K:]
+
+    for entry in range(depth - 2):
+
+        @pl.when(entry < count)
+        def _():
+            fetch(jnp.int32(entry)).start()
+
+    def step(pair, carry):
+        one = 2 * pair
+        two = one + 1
+        for entry in (one, two):
+
+            @pl.when(entry + depth - 2 < count)
+            def _():
+                fetch(entry + depth - 2).start()
+
+        fetch(one).wait()
+
+        @pl.when(two < count)
+        def _():
+            fetch(two).wait()
+
+        one_term, two_term = term(one), term(two)
+        running[info[ROWS + one], :K, :] += one_term
+        running[info[ROWS + two], :K, :] += jnp.where(two < count, two_term, 0.0)
         return carry
 
-    lax.fori_loop(0, count, step, 0)
+    lax.fori_loop(0, (count + 1) // 2, step, 0)
 
 
 def product(info, tiles, *operands):
     vmem = pl.BlockSpec(memory_space=pltpu.VMEM)
+    first = len(operands) == 2
     return pl.pallas_call(
-        functools.partial(product_kernel, len(operands) == 2),
-        out_shape=jax.ShapeDtypeStruct((SLAB_TILES, K, TILE), F32),
+        functools.partial(product_kernel, first),
+        out_shape=jax.ShapeDtypeStruct((SLAB_TILES, K if first else K + 8, TILE), F32),
         in_specs=[
             pl.BlockSpec(memory_space=pltpu.SMEM),
-            pl.BlockSpec(memory_space=pl.ANY),
+            pl.BlockSpec(memory_space=pltpu.HBM),
         ]
         + [vmem] * len(operands),
         out_specs=vmem,
         scratch_shapes=[
-            pltpu.VMEM((4, TILE, TILE), BF16),
-            pltpu.SemaphoreType.DMA((4,)),
+            pltpu.VMEM((8, TILE, TILE), BF16),
+            pltpu.SemaphoreType.DMA((8,)),
         ],
-        compiler_params=pltpu.CompilerParams(vmem_limit_bytes=VMEM_LIMIT),
+        compiler_params=pltpu.CompilerParams(vmem_limit_bytes=20 * 1024 * 1024),
         name="product",
     )(info, tiles, *operands)
 
 
-def weigh_kernel(parts, inv_root, root, image, message):
-    block = jnp.sum(parts[...], axis=0) * inv_root[...]
-    image[...] = block
-    heavy = jnp.concatenate([block, jnp.broadcast_to(root[...], (8, TILE))], axis=0)
+def weights_of(image, root):
+    heavy = jnp.concatenate([image, jnp.broadcast_to(root, (8, TILE))], axis=0)
     weights = lax.dot_general(
         heavy,
         heavy,
@@ -237,7 +259,7 @@
         preferred_element_type=F32,
     )
     half = K // 2
-    message[...] = jnp.concatenate(
+    return jnp.concatenate(
         [
             weights[:half, :half],
             weights[half:K, :half],
@@ -250,24 +272,8 @@
     )
 
 
-def weigh(parts, inv_root, root):
-    vmem = pl.BlockSpec(memory_space=pltpu.VMEM)
-    return pl.pallas_call(
-        weigh_kernel,
-        out_shape=(
-            jax.ShapeDtypeStruct((K, TILE), F32),
-            jax.ShapeDtypeStruct((K // 2, 128), F32),
-        ),
-        in_specs=[vmem] * 3,
-        out_specs=(vmem, vmem),
-        compiler_params=pltpu.CompilerParams(vmem_limit_bytes=VMEM_LIMIT),
-        name="weigh",
-    )(parts, inv_root, root)
-
-
-def orthonormalize_kernel(scale, message, image, inv_root, root, out):
+def factor_of(sums, scale):
     half = K // 2
-    sums = message[...]
     lower = sums[:, half : 2 * half]
     gram = jnp.concatenate(
         [
@@ -295,27 +301,44 @@
             below = jnp.where(index[first:] > j, column[first:], 0.0)
             rest = work[first:] - below * (row / pivot)
             work = jnp.concatenate([work[:first], rest], axis=0) if first else rest
-    inverse = work[:, K:] * lax.rsqrt(pivots)
-    projected = image[...] - top * root[...] / total
-    vectors = jnp.dot(
-        inverse, projected, precision=lax.Precision.HIGHEST, preferred_element_type=F32
-    )
-    if out.dtype == BF16:
-        out[...] = (vectors * inv_root[...]).astype(BF16)
-    else:
-        out[...] = vectors
-
-
-def orthonormalize(message, image, inv_root, root, scale, dtype):
+    return work[:, K:] * lax.rsqrt(pivots), top / total
+
+
+def times(factor, block):
+    return jnp.dot(factor, block, precision=lax.Precision.HIGHEST, preferred_element_type=F32)
+
+
+def weigh_kernel(parts, inv_root, root, out):
+    image = jnp.sum(parts[...], axis=0) * inv_root[...]
+    out[:K, :] = image
+    packed = weights_of(image, root[...])
+    out[K:, :] = jnp.concatenate([packed[8 * i : 8 * i + 8] for i in range(4)], axis=1)
+
+
+def middle_kernel(scale, parts, inv_root, root, image, message):
+    sums = jnp.sum(parts[...], axis=0)
+    packed = jnp.concatenate([sums[K:, 128 * i : 128 * i + 128] for i in range(4)], axis=0)
+    factor, lead = factor_of(packed, scale)
+    block = times(factor, sums[:K] * inv_root[...] - lead * root[...])
+    image[...] = block
+    message[...] = weights_of(block, root[...])
+
+
+def last_kernel(scale, message, image, root, out):
+    factor, lead = factor_of(message[...], scale)
+    out[...] = times(factor, image[...] - lead * root[...])
+
+
+def local(kernel, name, out_shape, *operands):
     vmem = pl.BlockSpec(memory_space=pltpu.VMEM)
     return pl.pallas_call(
-        functools.partial(orthonormalize_kernel, scale),
-        out_shape=jax.ShapeDtypeStruct((K, TILE), dtype),
-        in_specs=[vmem] * 4,
-        out_specs=vmem,
+        kernel,
+        out_shape=jax.tree.map(lambda shape: jax.ShapeDtypeStruct(shape, F32), out_shape, is_leaf=lambda x: isinstance(x[0], int)),
+        in_specs=[vmem] * len(operands),
+        out_specs=jax.tree.map(lambda shape: vmem, out_shape, is_leaf=lambda x: isinstance(x[0], int)),
         compiler_params=pltpu.CompilerParams(vmem_limit_bytes=VMEM_LIMIT),
-        name="orthonormalize",
-    )(message, image, inv_root, root)
+        name=name,
+    )(*operands)
 
 
 def swap_cores(value):
@@ -331,10 +354,7 @@
 
 def share_row(value):
     mine = share(value, ("y", "zh"))
-    other = swap_cores(mine)
-    first = lax.axis_index("core") == 0
-    pair = jnp.where(first, jnp.stack([mine, other], 1), jnp.stack([other, mine], 1))
-    return pair.reshape((BLOCK_TILES,) + value.shape)
+    return mine, swap_cores(mine)
 
 
 def sum_all(message):
@@ -377,7 +397,7 @@
     return lax.ppermute(value, ("zh", "zl"), [(0, 3), (3, 0), (1, 2), (2, 1)])
 
 
-def pair_list(count, block_index, rows, slabs, arrivals):
+def pair_list(count, block_index, core, rows, slabs, arrivals):
     slot = jnp.arange(PAIRS, dtype=jnp.int32)
     rank = jnp.sum(
         jnp.where(slabs[:, None] == arrivals[None, :], jnp.arange(BLOCK_TILES, dtype=jnp.int32), 0), 1
@@ -394,7 +414,7 @@
     groups = jnp.sum(jnp.where(slot[None, :] <= slot[:, None], fresh[None, :], False).astype(jnp.int32), 1)
     limit = jnp.arange(BLOCK_TILES + 1, dtype=jnp.int32) * PAIRS
     starts = jnp.sum((key[None, :] < limit[:, None]).astype(jnp.int32), axis=1)
-    head = jnp.stack([count, block_index] + [jnp.int32(0)] * 6)
+    head = jnp.stack([count, block_index, core] + [jnp.int32(0)] * 5)
     return jnp.concatenate([head, ordered(rows), ordered(slabs), ranks, groups, starts]).astype(jnp.int32)
 
 
@@ -426,7 +446,7 @@
     first, second = arrivals
     arrivals = [q for both in zip(first[:6], second[:6], strict=True) for q in both]
     arrivals = jnp.stack(arrivals + first[6:] + second[6:])
-    info = pair_list(pair_count[0, 0], block_index, pair_rows[0, 0], pair_cols[0, 0], arrivals)
+    info = pair_list(pair_count[0, 0], block_index, core, pair_rows[0, 0], pair_cols[0, 0], arrivals)
 
     own = lax.dynamic_index_in_dim(slab, block_index, 0, keepdims=False)
     give = lax.dynamic_index_in_dim(slab, block_index ^ 1, 0, keepdims=False)
@@ -434,14 +454,14 @@
     below = up(own)
     above = down(own)
     half_rows = 0.5 * jnp.sum(jnp.square(slab.astype(F32)), axis=2)
-    column_labels = share_row(labels[None].astype(F32))[:, 0].astype(jnp.int32)
+    column_labels = lax.all_gather(labels, ROW, axis=0)
 
     def both(*pieces):
         return [each for piece in pieces for each in (piece, swap_cores(piece))]
 
     def after(made, *pieces):
-        tied = lax.optimization_barrier((made[1], column_labels) + pieces)
-        return (made[0], tied[0]), tied[2:]
+        tied = lax.optimization_barrier((made[1],) + pieces)
+        return (made[0], tied[0]), tied[1:]
 
     made = build(0, info, slab, half_rows, both(own), ())
     made, (across, below, above) = after(made, across, below, above)
@@ -449,7 +469,7 @@
     beyond = apart(jnp.where(zero, below, above))
     other = apart_z(jnp.where(zero, above, below))
     made = build(2, info, slab, half_rows, both(across, below), made)
-    made, (near, beyond, other) = after(made, near, beyond, other)
+    made, (near, beyond, other, column_labels) = after(made, near, beyond, other, column_labels)
     far = apart(near)
     other = apart_z(other)
     made = build(6, info, slab, half_rows, both(above, beyond, near), made)
@@ -472,19 +492,18 @@
     inv_root = lax.rsqrt(degree)
     root = jnp.sqrt(degree)
 
-    out = None
-    for iteration in range(ITERS):
-        if iteration == 0:
-            running = product(info, tiles, column_labels, column_inv_root)
-        else:
-            running = product(info, tiles, share_row(out))
-        parts = lax.all_to_all(running, COL, 0, 0, tiled=True)
-        image, message = weigh(parts, inv_root, root)
-        dtype = F32 if iteration == ITERS - 1 else BF16
-        out = orthonormalize(
-            sum_all(message), image, inv_root, root, 1.0 / (BLOCK_TILES * SLAB_TILES * TILE), dtype
-        )
-    return out
+    scale = 1.0 / (BLOCK_TILES * SLAB_TILES * TILE)
+    running = product(info, tiles, column_labels, column_inv_root)
+    parts = lax.all_to_all(running, COL, 0, 0, tiled=True)
+    weighed = local(weigh_kernel, "weigh", (K + 8, TILE), parts, inv_root, root)
+    running = product(info, tiles, *share_row(weighed), column_inv_root)
+    parts = lax.all_to_all(running, COL, 0, 0, tiled=True)
+    image, message = local(
+        functools.partial(middle_kernel, scale), "middle", ((K, TILE), (K // 2, 128)), parts, inv_root, root
+    )
+    return local(
+        functools.partial(last_kernel, scale), "last", (K, TILE), sum_all(message), image, root
+    )
 
 
 def solution(mesh):

time: 262 us -> 265 us (1.011)
  Pallas kernels: 35.3 us -> 58.3 us
  waiting for transfers between devices: 64.9 us -> 42.4 us
  blocking collectives: 91.8 us -> 96.9 us
    all_gather x0 -> x1, blocking collectives: none -> 34.5 us  [shards(): column_labels = lax.all_gather(labels, ROW, axis=0)]
    ppermute x3, waiting for transfers between devices: 19.3 us -> 0.01 us  [apart(): lax.ppermute(value, ('y', 'core'), [(2 * i + k, 2 * ((i + 1 + 2 * k) % 4)...]
    all_to_all x1 -> x0, blocking collectives: 17.9 us -> none  [shards(): parts = lax.all_to_all(running, COL, 0, 0, tiled=True)]
    pallas_call x5, Pallas kernels: 14.7 us -> 31.7 us  [build(): pl.pallas_call(functools.partial(build_kernel, first, arrived), out_shape...]
    all_to_all x1 -> x0, waiting for transfers between devices: 12.3 us -> none  [share(): lax.all_to_all(jnp.broadcast_to(value[None], (size,) + value.shape), axes...]
    all_to_all x1 -> x2, waiting for transfers between devices: 17.6 us -> 27.5 us  [shards(): parts = lax.all_to_all(running, COL, 0, 0, tiled=True)]
    all_to_all x3 -> x2, blocking collectives: 53.2 us -> 44.4 us  [share(): lax.all_to_all(jnp.broadcast_to(value[None], (size,) + value.shape), axes...]
    ppermute x15 -> x12, starting transfers between devices: 20.7 us -> 14.2 us  [swap_cores(): return lax.ppermute(value, 'core', [(0, 1), (1, 0)])]
  transfers between devices with their start and end apart: 25 -> 22, of which waited for: 17 -> 9; matrix products, arithmetic and copies ran while one was open for 3% -> 2% of each run, Pallas kernels for 4% -> 10%
where the time goes in v4:
time: 265 us; the launch traced here: 264 us
  blocking collectives  96.9 us (37%)
  Pallas kernels  58.3 us (22%)
  waiting for transfers between devices  42.4 us (16%)
  starting transfers between devices  39 us (15%)
  local copies, waits for them, and re-layouts  20.4 us (8%)
  other arithmetic  6.28 us (2%)
    all_to_all x2, blocking collectives, share(): lax.all_to_all(jnp.broadcast_to(value[None], (size,) + value.shape), axes...  44.4 us
    all_gather x1, blocking collectives, shards(): column_labels = lax.all_gather(labels, ROW, axis=0)  34.5 us
    pallas_call x5, Pallas kernels, build(): pl.pallas_call(functools.partial(build_kernel, first, arrived), out_shape...  31.7 us
    all_to_all x2, waiting for transfers between devices, shards(): parts = lax.all_to_all(running, COL, 0, 0, tiled=True)  27.5 us
    all_to_all x1, blocking collectives, shards(): lax.all_to_all(spread.reshape(8 * SLAB_TILES, 1, TILE), CHIPS, 0, 0, tile...  18.1 us
    unnamed x15, local copies, waits for them, and re-layouts  17.1 us
    ppermute x12, starting transfers between devices, swap_cores(): return lax.ppermute(value, 'core', [(0, 1), (1, 0)])  14.2 us
    pallas_call x3, Pallas kernels, local(): pl.pallas_call(kernel, out_shape=jax.tree.map(lambda shape: jax.ShapeDtyp...  13.5 us
  transfers between devices with their start and end apart: 22, of which 9 were waited for; matrix products, arithmetic and copies ran while one was open for 2% of the time, Pallas kernels for 10%

profile of v4, /device:TPU:1, one launch (start us, length us, event | category | flops | bytes accessed | tf_op | source)
XLA Modules:
  0.0 264.4 jit_solution(3492744881956359739)
XLA Ops:
  0.0 2.7 %dynamic-slice_bitcast_fusion = (bf16[512,1024]{1,0:T(8,128)(2,1)}, bf16[512,1024]{1,0:T(8,128)(2,1)S(1)}) fusion(bf16[8,512,1024]{2,1,0:T(8,128)(2,1)} %bitcast.35, s32[]{:T(128)S(6)} %select_n.198, s32[]{:T(128)S(6)} %select_n.197), kind=kLoop, calls=%fused_computation.1 | loop fusion | bytes 4194312 | tf_op jit(solution)/shard_map/jit(dynamic_index_in_dim)/squeeze | solution.py:452
  7.0 3.8 %collective-permute-start.1 = (bf16[512,1024]{1,0:T(8,128)(2,1)}, bf16[512,1024]{1,0:T(8,128)(2,1)}, u32[]{:S(2)}, u32[]{:S(2)}) collective-permute-start(bf16[512,1024]{1,0:T(8,128)(2,1)} %get-tuple-element.56), channel_id=1, source_target_pairs={{0,17},{17,0},{1,16},{16,1},{2,19},{19,2},{3,18},{18,3},{4,21},{21... | collective-permute-start | bytes 3145736 | tf_op jit(solution)/shard_map/ppermute | solution.py:397
  10.7 5.1 %multiply_reduce_fusion = f32[4096]{0:T(1024)S(1)} fusion(bf16[4096,1024]{1,0:T(8,128)(2,1)} %param.5), kind=kLoop, calls=%fused_computation | loop fusion | flops 12578816 | bytes 8404992 | tf_op jit(solution)/shard_map/reduce_sum | solution.py:456
  17.7 3.4 %copy-done.3 = bf16[4096,1024]{1,0:T(8,128)(2,1)S(1)} copy-done((bf16[4096,1024]{1,0:T(8,128)(2,1)S(1)}, bf16[4096,1024]{1,0:T(8,128)(2,1)}, u32[]{:S(2)}) %copy-start.3) | copy-done | bytes 8388632
  21.0 6.3 %build_tiles.5 = (bf16[24,512,512]{2,1,0:T(8,128)(2,1)S(1)}, f32[8,512]{1,0:T(8,128)S(1)}) custom-call(s32[121]{0:T(128)S(1)} %concatenate.10.info, bf16[8,512,1024]{2,1,0:T(8,128)(2,1)S(1)} %bitcast.36, f32[8,512]{1,0:T(8,128)S(1)} %mul.132.half_rows, bf16[512,1024]{1,0:T(8,128)(2,1)S(1)} %get-tuple-element.57.refs_0_, ...), custom_call_target="tpu_custom_call" | custom-call | flops 1610612736 | bytes 7864320 | tf_op jit(solution)/shard_map/build_tiles/pallas_call | solution.py:136
  27.4 3.1 %collective-permute-done.2.refs_2_ = bf16[512,1024]{1,0:T(8,128)(2,1)S(1)} collective-permute-done((bf16[512,1024]{1,0:T(8,128)(2,1)S(1)}, bf16[512,1024]{1,0:T(8,128)(2,1)S(1)}, u32[]{:S(2)}, u32[]{:S(2)}) %collective-permute-start.2) | collective-permute-done | bytes 1048608 | tf_op jit(solution)/shard_map/ppermute | solution.py:372
  30.5 3.7 %collective-permute-done.1.refs_0_ = bf16[512,1024]{1,0:T(8,128)(2,1)} collective-permute-done((bf16[512,1024]{1,0:T(8,128)(2,1)}, bf16[512,1024]{1,0:T(8,128)(2,1)}, u32[]{:S(2)}, u32[]{:S(2)}) %collective-permute-start.1) | collective-permute-done | bytes 1048608 | tf_op jit(solution)/shard_map/ppermute | solution.py:397
  36.8 2.7 %collective-permute-start.9 = (bf16[512,1024]{1,0:T(8,128)(2,1)S(1)}, bf16[512,1024]{1,0:T(8,128)(2,1)S(1)}, u32[]{:S(2)}, u32[]{:S(2)}) collective-permute-start(bf16[512,1024]{1,0:T(8,128)(2,1)S(1)} %get-tuple-element.58), channel_id=1, source_target_pairs={{0,1},{8,25},{1,16},{9,8},{16,17},{24,9},{17,0},{25,24},{2,3},{10,... | collective-permute-start | bytes 3145736 | tf_op jit(solution)/shard_map/ppermute | solution.py:393
  40.0 34.5 %all-gather.1 = s32[16,1,512]{2,1,0:T(1,128)S(1)} all-gather(s32[1,1,512]{2,1,0:T(1,128)S(1)} %bitcast.42), channel_id=2, replica_groups=mesh['y'=4,'zh'=2,'core'=2,'x'=4,'zl'=2] {'y','zh','core'}, dimensions={0}, use_global_device_ids=true | all-gather | bytes 34816 | tf_op jit(solution)/shard_map/all_gather | solution.py:457
  74.8 7.2 %build_tiles.6 = (bf16[24,512,512]{2,1,0:T(8,128)(2,1)S(1)}, f32[8,512]{1,0:T(8,128)S(1)}) custom-call(s32[121]{0:T(128)S(1)} %concatenate.10.info, bf16[8,512,1024]{2,1,0:T(8,128)(2,1)S(1)} %bitcast.37, f32[8,512]{1,0:T(8,128)S(1)} %mul.132.half_rows, bf16[512,1024]{1,0:T(8,128)(2,1)} %collective-permute-done.1.refs_0_, ...), custom_call_target="tpu_custom_call", output_to_operand_aliasing={{0}: (7, {})} | custom-call | flops 3221225472 | bytes 15728640 | tf_op jit(solution)/shard_map/build_tiles/pallas_call | solution.py:136
  83.7 5.4 %collective-permute-start.13 = (bf16[512,1024]{1,0:T(8,128)(2,1)S(1)}, bf16[512,1024]{1,0:T(8,128)(2,1)S(1)}, u32[]{:S(2)}, u32[]{:S(2)}) collective-permute-start(bf16[512,1024]{1,0:T(8,128)(2,1)S(1)} %collective-permute-done.9), channel_id=1, source_target_pairs={{0,1},{8,25},{1,16},{9,8},{16,17},{24,9},{17,0},{25,24},{2,3},{10,... | collective-permute-start | bytes 3145736 | tf_op jit(solution)/shard_map/ppermute | solution.py:393
  89.2 8.9 %build_tiles.7 = (bf16[24,512,512]{2,1,0:T(8,128)(2,1)S(1)}, f32[8,512]{1,0:T(8,128)S(1)}) custom-call(s32[121]{0:T(128)S(1)} %concatenate.10.info, bf16[8,512,1024]{2,1,0:T(8,128)(2,1)S(1)} %bitcast.38, f32[8,512]{1,0:T(8,128)S(1)} %mul.132.half_rows, bf16[512,1024]{1,0:T(8,128)(2,1)S(1)} %collective-permute-done.3.refs_0_, ...), custom_call_target="tpu_custom_call", output_to_operand_aliasing={{0}: (9, {})} | custom-call | flops 4831838208 | bytes 23592960 | tf_op jit(solution)/shard_map/build_tiles/pallas_call | solution.py:136
  98.1 2.8 %collective-permute-done.13.refs_1_ = bf16[512,1024]{1,0:T(8,128)(2,1)S(1)} collective-permute-done((bf16[512,1024]{1,0:T(8,128)(2,1)S(1)}, bf16[512,1024]{1,0:T(8,128)(2,1)S(1)}, u32[]{:S(2)}, u32[]{:S(2)}) %collective-permute-start.13) | collective-permute-done | bytes 1048608 | tf_op jit(solution)/shard_map/ppermute | solution.py:393
  101.4 5.1 %build_tiles.8 = (bf16[24,512,512]{2,1,0:T(8,128)(2,1)S(1)}, f32[8,512]{1,0:T(8,128)S(1)}) custom-call(s32[121]{0:T(128)S(1)} %concatenate.10.info, bf16[8,512,1024]{2,1,0:T(8,128)(2,1)S(1)} %bitcast.39, f32[8,512]{1,0:T(8,128)S(1)} %mul.132.half_rows, bf16[512,1024]{1,0:T(8,128)(2,1)S(1)} %collective-permute-done.12.refs_0_, ...), custom_call_target="tpu_custom_call", output_to_operand_aliasing={{0}: (5, {})} | custom-call | flops 1610612736 | bytes 7864320 | tf_op jit(solution)/shard_map/build_tiles/pallas_call | solution.py:136
  106.6 4.1 %build_tiles.9 = (bf16[24,512,512]{2,1,0:T(8,128)(2,1)S(1)}, f32[8,512]{1,0:T(8,128)S(1)}) custom-call(s32[121]{0:T(128)S(1)} %concatenate.10.info, bf16[8,512,1024]{2,1,0:T(8,128)(2,1)S(1)} %bitcast.40, f32[8,512]{1,0:T(8,128)S(1)} %mul.132.half_rows, bf16[512,1024]{1,0:T(8,128)(2,1)S(1)} %collective-permute-done.14.refs_0_, ...), custom_call_target="tpu_custom_call", output_to_operand_aliasing={{0}: (5, {})} | custom-call | flops 1610612736 | bytes 7864320 | tf_op jit(solution)/shard_map/build_tiles/pallas_call | solution.py:136
  110.6 4.5 %copy-done = bf16[24,512,512]{2,1,0:T(8,128)(2,1)} copy-done((bf16[24,512,512]{2,1,0:T(8,128)(2,1)}, bf16[24,512,512]{2,1,0:T(8,128)(2,1)S(1)}, u32[]{:S(2)}) %copy-start) | copy-done | bytes 12582936
  115.3 18.1 %all_to_all.25 = f32[64,1,512]{2,1,0:T(1,128)S(1)} all-to-all(f32[64,1,512]{2,1,0:T(1,128)S(1)} %broadcast_in_dim.87), channel_id=1, replica_groups=mesh['y'=4,'zh'=2,'core'=2,'x'=4,'zl'=2] {'y','zh','x','zl'}, dimensions={0} | all-to-all | bytes 262144 | tf_op jit(solution)/shard_map/all_to_all | solution.py:482
  133.5 6.0 %collective-permute-start.16 = (f32[8,512]{1,0:T(8,128)S(1)}, f32[8,512]{1,0:T(8,128)S(1)}, u32[]{:S(2)}, u32[]{:S(2)}) collective-permute-start(f32[8,512]{1,0:T(8,128)S(1)} %bitcast_reduce_fusion), channel_id=1, source_target_pairs={{0,8},{8,0},{1,9},{9,1},{2,10},{10,2},{3,11},{11,3},{4,12},{12,4},... | collective-permute-start | bytes 49160 | tf_op jit(solution)/shard_map/ppermute | solution.py:345
  140.5 4.6 %copy-done.1 = bf16[24,512,512]{2,1,0:T(8,128)(2,1)S(1)} copy-done((bf16[24,512,512]{2,1,0:T(8,128)(2,1)S(1)}, bf16[24,512,512]{2,1,0:T(8,128)(2,1)}, u32[]{:S(2)}) %copy-start.1) | copy-done | bytes 12582936
  145.1 6.4 %product.2 = f32[8,64,512]{2,1,0:T(8,128)} custom-call(s32[121]{0:T(128)S(1)} %concatenate.10.info, bf16[24,512,512]{2,1,0:T(8,128)(2,1)S(1)} %copy-done.1, s32[16,512]{1,0:T(8,128)S(1)} %bitcast.41, f32[16,512]{1,0:T(8,128)S(1)} %rsqrt.6.refs_1_.refs_2_), custom_call_target="tpu_custom_call" | custom-call | tf_op jit(solution)/shard_map/product/pallas_call | solution.py:234
  151.5 3.6 %all-to-all-start.1 = ((f32[8,64,512]{2,1,0:T(8,128)}), f32[8,64,512]{2,1,0:T(8,128)S(1)}, u32[]{:S(2)}, u32[]{:S(2)}) async-start(f32[8,64,512]{2,1,0:T(8,128)} %product.2), calls=%async_computation.1 | async-start | bytes 2097152 | tf_op jit(solution)/shard_map/all_to_all | solution.py:497
  155.1 13.0 %all-to-all-done.1.parts = f32[8,64,512]{2,1,0:T(8,128)S(1)} async-done(((f32[8,64,512]{2,1,0:T(8,128)}), f32[8,64,512]{2,1,0:T(8,128)S(1)}, u32[]{:S(2)}, u32[]{:S(2)}) %all-to-all-start.1) | async-done | bytes 1048608 | tf_op jit(solution)/shard_map/all_to_all | solution.py:497
  168.7 23.7 %all_to_all.26.refs_0_ = f32[8,72,512]{2,1,0:T(8,128)S(1)} all-to-all(f32[8,72,512]{2,1,0:T(8,128)S(1)} %broadcast_in_dim.88), channel_id=1, replica_groups=mesh['y'=4,'zh'=2,'core'=2,'x'=4,'zl'=2] {'y','zh'}, dimensions={0} | all-to-all | bytes 2359296 | tf_op jit(solution)/shard_map/all_to_all | solution.py:350
  192.5 2.2 collective-permute-start.17
  194.7 2.5 collective-permute-done.17.refs_1_
  197.1 4.6 %copy-done.2 = bf16[24,512,512]{2,1,0:T(8,128)(2,1)S(1)} copy-done((bf16[24,512,512]{2,1,0:T(8,128)(2,1)S(1)}, bf16[24,512,512]{2,1,0:T(8,128)(2,1)}, u32[]{:S(2)}) %copy-start.2) | copy-done | bytes 12582936
  201.7 6.7 %product.3 = f32[8,72,512]{2,1,0:T(8,128)} custom-call(s32[121]{0:T(128)S(1)} %concatenate.10.info, bf16[24,512,512]{2,1,0:T(8,128)(2,1)S(1)} %copy-done.2, f32[8,72,512]{2,1,0:T(8,128)S(1)} %all_to_all.26.refs_0_, f32[8,72,512]{2,1,0:T(8,128)S(1)} %collective-permute-done.17.refs_1_, f32[16,512]{1,0:T(8,128)S(1)} %rsqrt.6.refs_1_.refs_2_), custom_call_target="tpu_custom_call" | custom-call | tf_op jit(solution)/shard_map/product/pallas_call | solution.py:234
  208.4 3.6 %all-to-all-start.3 = ((f32[8,72,512]{2,1,0:T(8,128)}), f32[8,72,512]{2,1,0:T(8,128)S(1)}, u32[]{:S(2)}, u32[]{:S(2)}) async-start(f32[8,72,512]{2,1,0:T(8,128)} %product.3), calls=%async_computation.3 | async-start | bytes 2359296 | tf_op jit(solution)/shard_map/all_to_all | solution.py:500
  212.0 14.5 %all-to-all-done.3.parts = f32[8,72,512]{2,1,0:T(8,128)S(1)} async-done(((f32[8,72,512]{2,1,0:T(8,128)}), f32[8,72,512]{2,1,0:T(8,128)S(1)}, u32[]{:S(2)}, u32[]{:S(2)}) %all-to-all-start.3) | async-done | bytes 1179680 | tf_op jit(solution)/shard_map/all_to_all | solution.py:500
  226.4 6.4 %middle.1 = (f32[64,512]{1,0:T(8,128)S(1)}, f32[32,128]{1,0:T(8,128)S(1)}) custom-call(f32[8,72,512]{2,1,0:T(8,128)S(1)} %all-to-all-done.3.parts, f32[1,512]{1,0:T(1,128)S(1)} %get-tuple-element.61.inv_root, f32[1,512]{1,0:T(1,128)S(1)} %get-tuple-element.60.root), custom_call_target="tpu_custom_call" | custom-call | tf_op jit(solution)/shard_map/middle/pallas_call | solution.py:334
  234.2 20.6 %all_to_all.27 = f32[64,16,128]{2,1,0:T(8,128)S(1)} all-to-all(f32[64,16,128]{2,1,0:T(8,128)S(1)} %broadcast_in_dim.89), channel_id=1, replica_groups=mesh['y'=4,'zh'=2,'core'=2,'x'=4,'zl'=2] {'y','zh','x','zl'}, dimensions={0} | all-to-all | bytes 1048576 | tf_op jit(solution)/shard_map/all_to_all | solution.py:350
  257.7 6.7 %last.1 = f32[64,512]{1,0:T(8,128)} custom-call(f32[32,128]{1,0:T(8,128)S(1)} %pad_maximum_fusion.message, f32[64,512]{1,0:T(8,128)S(1)} %get-tuple-element.52.image, f32[1,512]{1,0:T(1,128)S(1)} %get-tuple-element.60.root), custom_call_target="tpu_custom_call" | custom-call | tf_op jit(solution)/shard_map/last/pallas_call | solution.py:334
  (74 shorter events, 16.9 us)
Async XLA Ops:
  0.0 16.6 %copy-start.5 = (s32[1,1,24]{2,1,0:T(1,128)S(1)}, s32[1,1,24]{2,1,0:T(1,128)}, u32[]{:S(2)}) copy-start(s32[1,1,24]{2,1,0:T(1,128)} %param.8) | copy-start | bytes 292
  0.0 16.9 %copy-start.6 = (s32[1,1,24]{2,1,0:T(1,128)S(1)}, s32[1,1,24]{2,1,0:T(1,128)}, u32[]{:S(2)}) copy-start(s32[1,1,24]{2,1,0:T(1,128)} %param.7) | copy-start | bytes 292
  2.7 14.9 %collective-permute-start = (bf16[512,1024]{1,0:T(8,128)(2,1)S(1)}, bf16[512,1024]{1,0:T(8,128)(2,1)}, u32[]{:S(2)}, u32[]{:S(2)}) collective-permute-start(bf16[512,1024]{1,0:T(8,128)(2,1)S(1)} %get-tuple-element.57.refs_0_), channel_id=1, source_target_pairs={{0,8},{8,0},{1,9},{9,1},{2,10},{10,2},{3,11},{11,3},{4,12},{12,4},... | collective-permute-start | bytes 3145736 | tf_op jit(solution)/shard_map/ppermute | solution.py:345
  4.1 26.3 %collective-permute-start.2 = (bf16[512,1024]{1,0:T(8,128)(2,1)S(1)}, bf16[512,1024]{1,0:T(8,128)(2,1)S(1)}, u32[]{:S(2)}, u32[]{:S(2)}) collective-permute-start(bf16[512,1024]{1,0:T(8,128)(2,1)S(1)} %get-tuple-element.57.refs_0_), channel_id=1, source_target_pairs={{0,32},{32,64},{64,96},{96,0},{1,33},{33,65},{65,97},{97,1},{2,34}... | collective-permute-start | bytes 3145736 | tf_op jit(solution)/shard_map/ppermute | solution.py:372
  5.5 24.9 %collective-permute-start.3 = (bf16[512,1024]{1,0:T(8,128)(2,1)S(1)}, bf16[512,1024]{1,0:T(8,128)(2,1)S(1)}, u32[]{:S(2)}, u32[]{:S(2)}) collective-permute-start(bf16[512,1024]{1,0:T(8,128)(2,1)S(1)} %get-tuple-element.57.refs_0_), channel_id=1, source_target_pairs={{0,96},{32,0},{64,32},{96,64},{1,97},{33,1},{65,33},{97,65},{2,98}... | collective-permute-start | bytes 3145736 | tf_op jit(solution)/shard_map/ppermute | solution.py:376
  7.0 27.2 %collective-permute-start.1 = (bf16[512,1024]{1,0:T(8,128)(2,1)}, bf16[512,1024]{1,0:T(8,128)(2,1)}, u32[]{:S(2)}, u32[]{:S(2)}) collective-permute-start(bf16[512,1024]{1,0:T(8,128)(2,1)} %get-tuple-element.56), channel_id=1, source_target_pairs={{0,17},{17,0},{1,16},{16,1},{2,19},{19,2},{3,18},{18,3},{4,21},{21... | collective-permute-start | bytes 3145736 | tf_op jit(solution)/shard_map/ppermute | solution.py:397
  15.8 24.2 %copy-start.4 = (s32[512]{0:T(512)S(1)}, s32[512]{0:T(512)}, u32[]{:S(2)}) copy-start(s32[512]{0:T(512)} %param.6) | copy-start | bytes 6148
  17.7 3.4 %copy-start.3 = (bf16[4096,1024]{1,0:T(8,128)(2,1)S(1)}, bf16[4096,1024]{1,0:T(8,128)(2,1)}, u32[]{:S(2)}) copy-start(bf16[4096,1024]{1,0:T(8,128)(2,1)} %param.5) | copy-start | bytes 25165828
  34.1 40.3 %collective-permute-start.5 = (bf16[512,1024]{1,0:T(8,128)(2,1)}, bf16[512,1024]{1,0:T(8,128)(2,1)S(1)}, u32[]{:S(2)}, u32[]{:S(2)}) collective-permute-start(bf16[512,1024]{1,0:T(8,128)(2,1)} %collective-permute-done.1.refs_0_), channel_id=1, source_target_pairs={{0,8},{8,0},{1,9},{9,1},{2,10},{10,2},{3,11},{11,3},{4,12},{12,4},... | collective-permute-start | bytes 3145736 | tf_op jit(solution)/shard_map/ppermute | solution.py:345
  35.1 39.6 %collective-permute-start.6 = (bf16[512,1024]{1,0:T(8,128)(2,1)S(1)}, bf16[512,1024]{1,0:T(8,128)(2,1)S(1)}, u32[]{:S(2)}, u32[]{:S(2)}) collective-permute-start(bf16[512,1024]{1,0:T(8,128)(2,1)S(1)} %collective-permute-done.2.refs_2_), channel_id=1, source_target_pairs={{0,8},{8,0},{1,9},{9,1},{2,10},{10,2},{3,11},{11,3},{4,12},{12,4},... | collective-permute-start | bytes 3145736 | tf_op jit(solution)/shard_map/ppermute | solution.py:345
  35.3 46.7 %collective-permute-start.8 = (bf16[512,1024]{1,0:T(8,128)(2,1)S(1)}, bf16[512,1024]{1,0:T(8,128)(2,1)S(1)}, u32[]{:S(2)}, u32[]{:S(2)}) collective-permute-start(bf16[512,1024]{1,0:T(8,128)(2,1)S(1)} %get-tuple-element.59), channel_id=1, source_target_pairs={{0,32},{8,104},{32,64},{40,8},{64,96},{72,40},{96,0},{104,72},{1,3... | collective-permute-start | bytes 3145736 | tf_op jit(solution)/shard_map/ppermute | solution.py:380
  36.8 45.2 %collective-permute-start.9 = (bf16[512,1024]{1,0:T(8,128)(2,1)S(1)}, bf16[512,1024]{1,0:T(8,128)(2,1)S(1)}, u32[]{:S(2)}, u32[]{:S(2)}) collective-permute-start(bf16[512,1024]{1,0:T(8,128)(2,1)S(1)} %get-tuple-element.58), channel_id=1, source_target_pairs={{0,1},{8,25},{1,16},{9,8},{16,17},{24,9},{17,0},{25,24},{2,3},{10,... | collective-permute-start | bytes 3145736 | tf_op jit(solution)/shard_map/ppermute | solution.py:393
  39.5 42.5 %collective-permute-start.7 = (bf16[512,1024]{1,0:T(8,128)(2,1)}, bf16[512,1024]{1,0:T(8,128)(2,1)S(1)}, u32[]{:S(2)}, u32[]{:S(2)}) collective-permute-start(bf16[512,1024]{1,0:T(8,128)(2,1)} %collective-permute-done.1.refs_0_), channel_id=1, source_target_pairs={{0,32},{8,104},{32,64},{40,8},{64,96},{72,40},{96,0},{104,72},{1,3... | collective-permute-start | bytes 3145736 | tf_op jit(solution)/shard_map/ppermute | solution.py:380
  74.4 14.7 %collective-permute-start.4 = (bf16[512,1024]{1,0:T(8,128)(2,1)S(1)}, bf16[512,1024]{1,0:T(8,128)(2,1)S(1)}, u32[]{:S(2)}, u32[]{:S(2)}) collective-permute-start(bf16[512,1024]{1,0:T(8,128)(2,1)S(1)} %collective-permute-done.3.refs_0_), channel_id=1, source_target_pairs={{0,8},{8,0},{1,9},{9,1},{2,10},{10,2},{3,11},{11,3},{4,12},{12,4},... | collective-permute-start | bytes 3145736 | tf_op jit(solution)/shard_map/ppermute | solution.py:345
  82.0 7.1 %collective-permute-start.10 = (bf16[512,1024]{1,0:T(8,128)(2,1)S(1)}, bf16[512,1024]{1,0:T(8,128)(2,1)S(1)}, u32[]{:S(2)}, u32[]{:S(2)}) collective-permute-start(bf16[512,1024]{1,0:T(8,128)(2,1)S(1)} %collective-permute-done.8.refs_2_), channel_id=1, source_target_pairs={{0,8},{8,0},{1,9},{9,1},{2,10},{10,2},{3,11},{11,3},{4,12},{12,4},... | collective-permute-start | bytes 3145736 | tf_op jit(solution)/shard_map/ppermute | solution.py:345
  82.1 7.0 %collective-permute-start.11 = (bf16[512,1024]{1,0:T(8,128)(2,1)S(1)}, bf16[512,1024]{1,0:T(8,128)(2,1)S(1)}, u32[]{:S(2)}, u32[]{:S(2)}) collective-permute-start(bf16[512,1024]{1,0:T(8,128)(2,1)S(1)} %collective-permute-done.7.refs_4_), channel_id=1, source_target_pairs={{0,8},{8,0},{1,9},{9,1},{2,10},{10,2},{3,11},{11,3},{4,12},{12,4},... | collective-permute-start | bytes 3145736 | tf_op jit(solution)/shard_map/ppermute | solution.py:345
  82.6 15.4 %collective-permute-start.12 = (bf16[512,1024]{1,0:T(8,128)(2,1)S(1)}, bf16[512,1024]{1,0:T(8,128)(2,1)S(1)}, u32[]{:S(2)}, u32[]{:S(2)}) collective-permute-start(bf16[512,1024]{1,0:T(8,128)(2,1)S(1)} %collective-permute-done.7.refs_4_), channel_id=1, source_target_pairs={{0,32},{8,104},{32,64},{40,8},{64,96},{72,40},{96,0},{104,72},{1,3... | collective-permute-start | bytes 3145736 | tf_op jit(solution)/shard_map/ppermute | solution.py:380
  83.7 17.2 %collective-permute-start.13 = (bf16[512,1024]{1,0:T(8,128)(2,1)S(1)}, bf16[512,1024]{1,0:T(8,128)(2,1)S(1)}, u32[]{:S(2)}, u32[]{:S(2)}) collective-permute-start(bf16[512,1024]{1,0:T(8,128)(2,1)S(1)} %collective-permute-done.9), channel_id=1, source_target_pairs={{0,1},{8,25},{1,16},{9,8},{16,17},{24,9},{17,0},{25,24},{2,3},{10,... | collective-permute-start | bytes 3145736 | tf_op jit(solution)/shard_map/ppermute | solution.py:393
  100.9 5.7 %collective-permute-start.14 = (bf16[512,1024]{1,0:T(8,128)(2,1)S(1)}, bf16[512,1024]{1,0:T(8,128)(2,1)S(1)}, u32[]{:S(2)}, u32[]{:S(2)}) collective-permute-start(bf16[512,1024]{1,0:T(8,128)(2,1)S(1)} %collective-permute-done.12.refs_0_), channel_id=1, source_target_pairs={{0,8},{8,0},{1,9},{9,1},{2,10},{10,2},{3,11},{11,3},{4,12},{12,4},... | collective-permute-start | bytes 3145736 | tf_op jit(solution)/shard_map/ppermute | solution.py:345
  100.9 5.7 %collective-permute-start.15 = (bf16[512,1024]{1,0:T(8,128)(2,1)S(1)}, bf16[512,1024]{1,0:T(8,128)(2,1)S(1)}, u32[]{:S(2)}, u32[]{:S(2)}) collective-permute-start(bf16[512,1024]{1,0:T(8,128)(2,1)S(1)} %collective-permute-done.13.refs_1_), channel_id=1, source_target_pairs={{0,8},{8,0},{1,9},{9,1},{2,10},{10,2},{3,11},{11,3},{4,12},{12,4},... | collective-permute-start | bytes 3145736 | tf_op jit(solution)/shard_map/ppermute | solution.py:345
  110.6 4.5 %copy-start = (bf16[24,512,512]{2,1,0:T(8,128)(2,1)}, bf16[24,512,512]{2,1,0:T(8,128)(2,1)S(1)}, u32[]{:S(2)}) copy-start(bf16[24,512,512]{2,1,0:T(8,128)(2,1)S(1)} %get-tuple-element.48.tiles) | copy-start | bytes 37748740
  133.5 6.9 %collective-permute-start.16 = (f32[8,512]{1,0:T(8,128)S(1)}, f32[8,512]{1,0:T(8,128)S(1)}, u32[]{:S(2)}, u32[]{:S(2)}) collective-permute-start(f32[8,512]{1,0:T(8,128)S(1)} %bitcast_reduce_fusion), channel_id=1, source_target_pairs={{0,8},{8,0},{1,9},{9,1},{2,10},{10,2},{3,11},{11,3},{4,12},{12,4},... | collective-permute-start | bytes 49160 | tf_op jit(solution)/shard_map/ppermute | solution.py:345
  140.5 4.6 %copy-start.1 = (bf16[24,512,512]{2,1,0:T(8,128)(2,1)S(1)}, bf16[24,512,512]{2,1,0:T(8,128)(2,1)}, u32[]{:S(2)}) copy-start(bf16[24,512,512]{2,1,0:T(8,128)(2,1)} %copy-done) | copy-start | bytes 37748740
  151.5 16.6 %all-to-all-start.1 = ((f32[8,64,512]{2,1,0:T(8,128)}), f32[8,64,512]{2,1,0:T(8,128)S(1)}, u32[]{:S(2)}, u32[]{:S(2)}) async-start(f32[8,64,512]{2,1,0:T(8,128)} %product.2), calls=%async_computation.1 | async-start | bytes 2097152 | tf_op jit(solution)/shard_map/all_to_all | solution.py:497
  192.5 4.7 %collective-permute-start.17 = (f32[8,72,512]{2,1,0:T(8,128)S(1)}, f32[8,72,512]{2,1,0:T(8,128)S(1)}, u32[]{:S(2)}, u32[]{:S(2)}) collective-permute-start(f32[8,72,512]{2,1,0:T(8,128)S(1)} %all_to_all.26.refs_0_), channel_id=1, source_target_pairs={{0,8},{8,0},{1,9},{9,1},{2,10},{10,2},{3,11},{11,3},{4,12},{12,4},... | collective-permute-start | bytes 3538952 | tf_op jit(solution)/shard_map/ppermute | solution.py:345
  197.1 4.6 %copy-start.2 = (bf16[24,512,512]{2,1,0:T(8,128)(2,1)S(1)}, bf16[24,512,512]{2,1,0:T(8,128)(2,1)}, u32[]{:S(2)}) copy-start(bf16[24,512,512]{2,1,0:T(8,128)(2,1)} %copy-done) | copy-start | bytes 37748740
  208.4 18.1 %all-to-all-start.3 = ((f32[8,72,512]{2,1,0:T(8,128)}), f32[8,72,512]{2,1,0:T(8,128)S(1)}, u32[]{:S(2)}, u32[]{:S(2)}) async-start(f32[8,72,512]{2,1,0:T(8,128)} %product.3), calls=%async_computation.3 | async-start | bytes 2359296 | tf_op jit(solution)/shard_map/all_to_all | solution.py:500
  232.9 1.3 collective-permute-start.18
  254.9 2.8 %collective-permute-start.19 = (f32[16,128]{1,0:T(8,128)S(1)}, f32[16,128]{1,0:T(8,128)S(1)}, u32[]{:S(2)}, u32[]{:S(2)}) collective-permute-start(f32[16,128]{1,0:T(8,128)S(1)} %reduce_sum.99), channel_id=1, source_target_pairs={{0,8},{8,0},{1,9},{9,1},{2,10},{10,2},{3,11},{11,3},{4,12},{12,4},... | collective-permute-start | bytes 24584 | tf_op jit(solution)/shard_map/ppermute | solution.py:345

commit v5 on v4

--- a/solution.py
+++ b/solution.py
@@ -127,6 +127,10 @@
             store(end - 1 - back).wait()
 
 
+def in_hbm(value):
+    return pltpu.with_memory_space_constraint(value, pltpu.HBM)
+
+
 def build(first, info, slab, half_rows, columns, made):
     any_space = pl.BlockSpec(memory_space=pl.ANY)
     hbm = pl.BlockSpec(memory_space=pltpu.HBM)
@@ -136,7 +140,7 @@
     return pl.pallas_call(
         functools.partial(build_kernel, first, arrived),
         out_shape=(
-            jax.ShapeDtypeStruct((PAIRS, TILE, TILE), BF16),
+            pltpu.HBM((PAIRS, TILE, TILE), BF16),
             jax.ShapeDtypeStruct((SLAB_TILES, TILE), F32),
         ),
         in_specs=[pl.BlockSpec(memory_space=pltpu.SMEM), hbm, vmem]
@@ -159,7 +163,7 @@
             transcendentals=pairs * TILE * TILE,
         ),
         name="build_tiles",
-    )(info, slab, half_rows, *columns, *made)
+    )(info, in_hbm(slab), half_rows, *columns, *([in_hbm(made[0]), made[1]] if made else []))
 
 
 def product_kernel(first, info, tiles, *refs):
@@ -246,7 +250,7 @@
         ],
         compiler_params=pltpu.CompilerParams(vmem_limit_bytes=20 * 1024 * 1024),
         name="product",
-    )(info, tiles, *operands)
+    )(info, in_hbm(tiles), *operands)
 
 
 def weights_of(image, root):
@@ -454,7 +458,6 @@
     below = up(own)
     above = down(own)
     half_rows = 0.5 * jnp.sum(jnp.square(slab.astype(F32)), axis=2)
-    column_labels = lax.all_gather(labels, ROW, axis=0)
 
     def both(*pieces):
         return [each for piece in pieces for each in (piece, swap_cores(piece))]
@@ -469,7 +472,7 @@
     beyond = apart(jnp.where(zero, below, above))
     other = apart_z(jnp.where(zero, above, below))
     made = build(2, info, slab, half_rows, both(across, below), made)
-    made, (near, beyond, other, column_labels) = after(made, near, beyond, other, column_labels)
+    made, (near, beyond, other) = after(made, near, beyond, other)
     far = apart(near)
     other = apart_z(other)
     made = build(6, info, slab, half_rows, both(above, beyond, near), made)
@@ -478,15 +481,16 @@
     made = build(14, info, slab, half_rows, [swap_cores(piece) for piece in last], made)
     tiles, partial_degree = made
 
-    spread = jnp.broadcast_to(partial_degree[None, :, None], (8, SLAB_TILES, 1, TILE))
+    in_block = jnp.arange(SLAB_TILES)[:, None] == block_index
+    sent = jnp.stack([partial_degree, jnp.where(in_block, labels.astype(F32)[None], 0.0)], axis=1)
     got = lax.all_to_all(
-        spread.reshape(8 * SLAB_TILES, 1, TILE), CHIPS, 0, 0, tiled=True
-    )
-    mine = jnp.sum(got.reshape(8, SLAB_TILES, TILE), axis=1)
+        jnp.broadcast_to(sent[None], (8,) + sent.shape).reshape(8 * SLAB_TILES, 2, TILE), CHIPS, 0, 0, tiled=True
+    )
+    mine = jnp.sum(got.reshape(8, SLAB_TILES, 2, TILE), axis=1)
     others = swap_cores(mine)
-    column_degree = jnp.where(
-        zero, jnp.stack([mine, others], 1), jnp.stack([others, mine], 1)
-    ).reshape(BLOCK_TILES, TILE)
+    known = jnp.where(zero, jnp.stack([mine, others], 1), jnp.stack([others, mine], 1)).reshape(BLOCK_TILES, 2, TILE)
+    column_degree = known[:, 0]
+    column_labels = known[:, 1].astype(jnp.int32)
     column_inv_root = lax.rsqrt(column_degree)
     degree = lax.dynamic_slice_in_dim(column_degree, slab_index, 1, 0)
     inv_root = lax.rsqrt(degree)

time: 265 us -> 231 us (0.87)
  waiting for transfers between devices: 42.4 us -> 79.6 us
  blocking collectives: 96.9 us -> 69.5 us
  Pallas kernels: 58.3 us -> 33.6 us
  local copies, waits for them, and re-layouts: 20.4 us -> 3.31 us
    all_gather x1 -> x0, blocking collectives: 34.5 us -> none  [shards(): column_labels = lax.all_gather(labels, ROW, axis=0)]
    ppermute x3, waiting for transfers between devices: 0.01 us -> 23.6 us  [apart(): lax.ppermute(value, ('y', 'core'), [(2 * i + k, 2 * ((i + 1 + 2 * k) % 4)...]
    pallas_call x5, Pallas kernels: 31.7 us -> 13.1 us  [build(): pl.pallas_call(functools.partial(build_kernel, first, arrived), out_shape...]
    unnamed x15 -> x6, local copies, waits for them, and re-layouts: 17.1 us -> 0.01 us
    all_to_all x2, waiting for transfers between devices: 27.5 us -> 34.6 us  [shards(): parts = lax.all_to_all(running, COL, 0, 0, tiled=True)]
    all_to_all x1, blocking collectives: 18.1 us -> 25.1 us  [shards(): lax.all_to_all(jnp.broadcast_to(sent[None], (8,) + sent.shape).reshape(8...]
    pallas_call x2, Pallas kernels: 13.1 us -> 7.01 us  [product(): pl.pallas_call(functools.partial(product_kernel, first), out_shape=jax.Sh...]
    ppermute x1, waiting for transfers between devices: 3.08 us -> 9.1 us  [up(): return lax.ppermute(value, 'y', [(i, (i + 1) % 4) for i in range(4)])]
  transfers between devices with their start and end apart: 22 -> 22, of which waited for: 9 -> 15; matrix products, arithmetic and copies ran while one was open for 2% -> 3% of each run, Pallas kernels for 10% -> 5%
where the time goes in v5:
time: 231 us; the launch traced here: 233 us
  waiting for transfers between devices  79.6 us (34%)
  blocking collectives  69.5 us (30%)
  starting transfers between devices  39.1 us (17%)
  Pallas kernels  33.6 us (15%)
  other arithmetic  6.38 us (3%)
  local copies, waits for them, and re-layouts  3.31 us (1%)
    all_to_all x2, blocking collectives, share(): lax.all_to_all(jnp.broadcast_to(value[None], (size,) + value.shape), axes...  44.4 us
    all_to_all x2, waiting for transfers between devices, shards(): parts = lax.all_to_all(running, COL, 0, 0, tiled=True)  34.6 us
    all_to_all x1, blocking collectives, shards(): lax.all_to_all(jnp.broadcast_to(sent[None], (8,) + sent.shape).reshape(8...  25.1 us
    ppermute x3, waiting for transfers between devices, apart(): lax.ppermute(value, ('y', 'core'), [(2 * i + k, 2 * ((i + 1 + 2 * k) % 4)...  23.6 us
    ppermute x12, starting transfers between devices, swap_cores(): return lax.ppermute(value, 'core', [(0, 1), (1, 0)])  17.8 us
    pallas_call x3, Pallas kernels, local(): pl.pallas_call(kernel, out_shape=jax.tree.map(lambda shape: jax.ShapeDtyp...  13.5 us
    pallas_call x5, Pallas kernels, build(): pl.pallas_call(functools.partial(build_kernel, first, arrived), out_shape...  13.1 us
    ppermute x1, waiting for transfers between devices, up(): return lax.ppermute(value, 'y', [(i, (i + 1) % 4) for i in range(4)])  9.1 us
  transfers between devices with their start and end apart: 22, of which 15 were waited for; matrix products, arithmetic and copies ran while one was open for 3% of the time, Pallas kernels for 5%

profile of v5, /device:TPU:1, one launch (start us, length us, event | category | flops | bytes accessed | tf_op | source)
XLA Modules:
  0.0 232.5 jit_solution(14968064390377032778)
XLA Ops:
  0.0 2.7 %dynamic-slice_bitcast_fusion = (bf16[512,1024]{1,0:T(8,128)(2,1)}, bf16[512,1024]{1,0:T(8,128)(2,1)S(1)}) fusion(bf16[8,512,1024]{2,1,0:T(8,128)(2,1)} %bitcast.46, s32[]{:T(128)S(6)} %select_n.209, s32[]{:T(128)S(6)} %select_n.208), kind=kLoop, calls=%fused_computation.1 | loop fusion | bytes 4194312 | tf_op jit(solution)/shard_map/jit(dynamic_index_in_dim)/squeeze | solution.py:456
  7.0 3.8 %collective-permute-start.1 = (bf16[512,1024]{1,0:T(8,128)(2,1)}, bf16[512,1024]{1,0:T(8,128)(2,1)}, u32[]{:S(2)}, u32[]{:S(2)}) collective-permute-start(bf16[512,1024]{1,0:T(8,128)(2,1)} %get-tuple-element.54), channel_id=1, source_target_pairs={{0,17},{17,0},{1,16},{16,1},{2,19},{19,2},{3,18},{18,3},{4,21},{21... | collective-permute-start | bytes 3145736 | tf_op jit(solution)/shard_map/ppermute | solution.py:401
  10.7 5.1 %multiply_reduce_fusion = f32[4096]{0:T(1024)S(1)} fusion(bf16[4096,1024]{1,0:T(8,128)(2,1)} %param.5), kind=kLoop, calls=%fused_computation | loop fusion | flops 12578816 | bytes 8404992 | tf_op jit(solution)/shard_map/reduce_sum | solution.py:460
  17.7 3.7 %build_tiles.5 = (bf16[24,512,512]{2,1,0:T(8,128)(2,1)}, f32[8,512]{1,0:T(8,128)S(1)}) custom-call(s32[121]{0:T(128)S(1)} %concatenate.10.info, bf16[8,512,1024]{2,1,0:T(8,128)(2,1)} %bitcast.47, f32[8,512]{1,0:T(8,128)S(1)} %mul.132.half_rows, bf16[512,1024]{1,0:T(8,128)(2,1)S(1)} %get-tuple-element.55.refs_0_, bf16[512,1024]{1,0:T(8,128)(2,1)} %collective-permute-done.refs_1_), custom_call_target="tpu_custom_call" | custom-call | flops 1610612736 | bytes 7864320 | tf_op jit(solution)/shard_map/build_tiles/pallas_call | solution.py:140
  21.4 9.1 %collective-permute-done.2.refs_2_ = bf16[512,1024]{1,0:T(8,128)(2,1)S(1)} collective-permute-done((bf16[512,1024]{1,0:T(8,128)(2,1)S(1)}, bf16[512,1024]{1,0:T(8,128)(2,1)S(1)}, u32[]{:S(2)}, u32[]{:S(2)}) %collective-permute-start.2) | collective-permute-done | bytes 1048608 | tf_op jit(solution)/shard_map/ppermute | solution.py:376
  30.5 3.7 %collective-permute-done.1.refs_0_ = bf16[512,1024]{1,0:T(8,128)(2,1)} collective-permute-done((bf16[512,1024]{1,0:T(8,128)(2,1)}, bf16[512,1024]{1,0:T(8,128)(2,1)}, u32[]{:S(2)}, u32[]{:S(2)}) %collective-permute-start.1) | collective-permute-done | bytes 1048608 | tf_op jit(solution)/shard_map/ppermute | solution.py:401
  35.3 1.5 collective-permute-start.8
  36.8 2.7 %collective-permute-start.9 = (bf16[512,1024]{1,0:T(8,128)(2,1)S(1)}, bf16[512,1024]{1,0:T(8,128)(2,1)S(1)}, u32[]{:S(2)}, u32[]{:S(2)}) collective-permute-start(bf16[512,1024]{1,0:T(8,128)(2,1)S(1)} %get-tuple-element.56), channel_id=1, source_target_pairs={{0,1},{8,25},{1,16},{9,8},{16,17},{24,9},{17,0},{25,24},{2,3},{10,... | collective-permute-start | bytes 3145736 | tf_op jit(solution)/shard_map/ppermute | solution.py:397
  40.7 8.7 %collective-permute-done.8.refs_2_ = bf16[512,1024]{1,0:T(8,128)(2,1)S(1)} collective-permute-done((bf16[512,1024]{1,0:T(8,128)(2,1)S(1)}, bf16[512,1024]{1,0:T(8,128)(2,1)S(1)}, u32[]{:S(2)}, u32[]{:S(2)}) %collective-permute-start.8) | collective-permute-done | bytes 1048608 | tf_op jit(solution)/shard_map/ppermute | solution.py:384
  49.3 1.9 collective-permute-done.9
  51.2 9.3 %collective-permute-done.7.refs_4_ = bf16[512,1024]{1,0:T(8,128)(2,1)S(1)} collective-permute-done((bf16[512,1024]{1,0:T(8,128)(2,1)}, bf16[512,1024]{1,0:T(8,128)(2,1)S(1)}, u32[]{:S(2)}, u32[]{:S(2)}) %collective-permute-start.7) | collective-permute-done | bytes 1048608 | tf_op jit(solution)/shard_map/ppermute | solution.py:384
  60.5 2.6 %collective-permute-start.10 = (bf16[512,1024]{1,0:T(8,128)(2,1)S(1)}, bf16[512,1024]{1,0:T(8,128)(2,1)S(1)}, u32[]{:S(2)}, u32[]{:S(2)}) collective-permute-start(bf16[512,1024]{1,0:T(8,128)(2,1)S(1)} %collective-permute-done.8.refs_2_), channel_id=1, source_target_pairs={{0,8},{8,0},{1,9},{9,1},{2,10},{10,2},{3,11},{11,3},{4,12},{12,4},... | collective-permute-start | bytes 3145736 | tf_op jit(solution)/shard_map/ppermute | solution.py:349
  63.4 2.7 %collective-permute-start.13 = (bf16[512,1024]{1,0:T(8,128)(2,1)S(1)}, bf16[512,1024]{1,0:T(8,128)(2,1)S(1)}, u32[]{:S(2)}, u32[]{:S(2)}) collective-permute-start(bf16[512,1024]{1,0:T(8,128)(2,1)S(1)} %collective-permute-done.9), channel_id=1, source_target_pairs={{0,1},{8,25},{1,16},{9,8},{16,17},{24,9},{17,0},{25,24},{2,3},{10,... | collective-permute-start | bytes 3145736 | tf_op jit(solution)/shard_map/ppermute | solution.py:397
  66.9 4.5 %build_tiles.7 = (bf16[24,512,512]{2,1,0:T(8,128)(2,1)}, f32[8,512]{1,0:T(8,128)S(1)}) custom-call(s32[121]{0:T(128)S(1)} %concatenate.10.info, bf16[8,512,1024]{2,1,0:T(8,128)(2,1)} %bitcast.49, f32[8,512]{1,0:T(8,128)S(1)} %mul.132.half_rows, bf16[512,1024]{1,0:T(8,128)(2,1)S(1)} %collective-permute-done.3.refs_0_, ...), custom_call_target="tpu_custom_call", output_to_operand_aliasing={{0}: (9, {})} | custom-call | flops 4831838208 | bytes 23592960 | tf_op jit(solution)/shard_map/build_tiles/pallas_call | solution.py:140
  71.4 5.6 %collective-permute-done.12.refs_0_ = bf16[512,1024]{1,0:T(8,128)(2,1)S(1)} collective-permute-done((bf16[512,1024]{1,0:T(8,128)(2,1)S(1)}, bf16[512,1024]{1,0:T(8,128)(2,1)S(1)}, u32[]{:S(2)}, u32[]{:S(2)}) %collective-permute-start.12) | collective-permute-done | bytes 1048608 | tf_op jit(solution)/shard_map/ppermute | solution.py:384
  77.9 1.8 collective-permute-start.14
  79.7 3.5 %build_tiles.8 = (bf16[24,512,512]{2,1,0:T(8,128)(2,1)}, f32[8,512]{1,0:T(8,128)S(1)}) custom-call(s32[121]{0:T(128)S(1)} %concatenate.10.info, bf16[8,512,1024]{2,1,0:T(8,128)(2,1)} %bitcast.50, f32[8,512]{1,0:T(8,128)S(1)} %mul.132.half_rows, bf16[512,1024]{1,0:T(8,128)(2,1)S(1)} %collective-permute-done.12.refs_0_, ...), custom_call_target="tpu_custom_call", output_to_operand_aliasing={{0}: (5, {})} | custom-call | flops 1610612736 | bytes 7864320 | tf_op jit(solution)/shard_map/build_tiles/pallas_call | solution.py:140
  84.2 25.1 %all_to_all.25 = f32[64,2,512]{2,1,0:T(2,128)S(1)} all-to-all(f32[64,2,512]{2,1,0:T(2,128)S(1)} %bitcast.52), channel_id=1, replica_groups=mesh['y'=4,'zh'=2,'core'=2,'x'=4,'zl'=2] {'y','zh','x','zl'}, dimensions={0} | all-to-all | bytes 524288 | tf_op jit(solution)/shard_map/all_to_all | solution.py:486
  109.4 5.5 %collective-permute-start.16 = (f32[8,2,512]{2,1,0:T(2,128)S(1)}, f32[8,2,512]{2,1,0:T(2,128)S(1)}, u32[]{:S(2)}, u32[]{:S(2)}) collective-permute-start(f32[8,2,512]{2,1,0:T(2,128)S(1)} %bitcast_reduce_fusion), channel_id=1, source_target_pairs={{0,8},{8,0},{1,9},{9,1},{2,10},{10,2},{3,11},{11,3},{4,12},{12,4},... | collective-permute-start | bytes 98312 | tf_op jit(solution)/shard_map/ppermute | solution.py:349
  115.9 3.5 %product.2 = f32[8,64,512]{2,1,0:T(8,128)} custom-call(s32[121]{0:T(128)S(1)} %concatenate.10.info, bf16[24,512,512]{2,1,0:T(8,128)(2,1)} %get-tuple-element.47.tiles, s32[16,512]{1,0:T(8,128)S(1)} %get-tuple-element.60.refs_0_, f32[16,512]{1,0:T(8,128)S(1)} %get-tuple-element.59.refs_1_.refs_2_), custom_call_target="tpu_custom_call" | custom-call | tf_op jit(solution)/shard_map/product/pallas_call | solution.py:238
  119.4 3.6 %all-to-all-start.1 = ((f32[8,64,512]{2,1,0:T(8,128)}), f32[8,64,512]{2,1,0:T(8,128)S(1)}, u32[]{:S(2)}, u32[]{:S(2)}) async-start(f32[8,64,512]{2,1,0:T(8,128)} %product.2), calls=%async_computation.1 | async-start | bytes 2097152 | tf_op jit(solution)/shard_map/all_to_all | solution.py:501
  123.0 16.3 %all-to-all-done.1.parts = f32[8,64,512]{2,1,0:T(8,128)S(1)} async-done(((f32[8,64,512]{2,1,0:T(8,128)}), f32[8,64,512]{2,1,0:T(8,128)S(1)}, u32[]{:S(2)}, u32[]{:S(2)}) %all-to-all-start.1) | async-done | bytes 1048608 | tf_op jit(solution)/shard_map/all_to_all | solution.py:501
  139.9 24.9 %all_to_all.26.refs_0_ = f32[8,72,512]{2,1,0:T(8,128)S(1)} all-to-all(f32[8,72,512]{2,1,0:T(8,128)S(1)} %broadcast_in_dim.110), channel_id=1, replica_groups=mesh['y'=4,'zh'=2,'core'=2,'x'=4,'zl'=2] {'y','zh'}, dimensions={0} | all-to-all | bytes 2359296 | tf_op jit(solution)/shard_map/all_to_all | solution.py:354
  164.8 2.2 collective-permute-start.17
  167.0 2.5 %collective-permute-done.17.refs_1_ = f32[8,72,512]{2,1,0:T(8,128)S(1)} collective-permute-done((f32[8,72,512]{2,1,0:T(8,128)S(1)}, f32[8,72,512]{2,1,0:T(8,128)S(1)}, u32[]{:S(2)}, u32[]{:S(2)}) %collective-permute-start.17) | collective-permute-done | bytes 1179680 | tf_op jit(solution)/shard_map/ppermute | solution.py:349
  169.5 3.5 %product.3 = f32[8,72,512]{2,1,0:T(8,128)} custom-call(s32[121]{0:T(128)S(1)} %concatenate.10.info, bf16[24,512,512]{2,1,0:T(8,128)(2,1)} %get-tuple-element.47.tiles, f32[8,72,512]{2,1,0:T(8,128)S(1)} %all_to_all.26.refs_0_, f32[8,72,512]{2,1,0:T(8,128)S(1)} %collective-permute-done.17.refs_1_, f32[16,512]{1,0:T(8,128)S(1)} %get-tuple-element.59.refs_1_.refs_2_), custom_call_target="tpu_custom_call" | custom-call | tf_op jit(solution)/shard_map/product/pallas_call | solution.py:238
  173.0 3.6 %all-to-all-start.3 = ((f32[8,72,512]{2,1,0:T(8,128)}), f32[8,72,512]{2,1,0:T(8,128)S(1)}, u32[]{:S(2)}, u32[]{:S(2)}) async-start(f32[8,72,512]{2,1,0:T(8,128)} %product.3), calls=%async_computation.3 | async-start | bytes 2359296 | tf_op jit(solution)/shard_map/all_to_all | solution.py:504
  176.6 18.3 %all-to-all-done.3.parts = f32[8,72,512]{2,1,0:T(8,128)S(1)} async-done(((f32[8,72,512]{2,1,0:T(8,128)}), f32[8,72,512]{2,1,0:T(8,128)S(1)}, u32[]{:S(2)}, u32[]{:S(2)}) %all-to-all-start.3) | async-done | bytes 1179680 | tf_op jit(solution)/shard_map/all_to_all | solution.py:504
  194.9 6.4 %middle.1 = (f32[64,512]{1,0:T(8,128)S(1)}, f32[32,128]{1,0:T(8,128)S(1)}) custom-call(f32[8,72,512]{2,1,0:T(8,128)S(1)} %all-to-all-done.3.parts, f32[1,512]{1,0:T(1,128)S(1)} %get-tuple-element.62.inv_root, f32[1,512]{1,0:T(1,128)S(1)} %get-tuple-element.61.root), custom_call_target="tpu_custom_call" | custom-call | tf_op jit(solution)/shard_map/middle/pallas_call | solution.py:338
  203.5 19.5 %all_to_all.27 = f32[64,16,128]{2,1,0:T(8,128)S(1)} all-to-all(f32[64,16,128]{2,1,0:T(8,128)S(1)} %broadcast_in_dim.111), channel_id=1, replica_groups=mesh['y'=4,'zh'=2,'core'=2,'x'=4,'zl'=2] {'y','zh','x','zl'}, dimensions={0} | all-to-all | bytes 1048576 | tf_op jit(solution)/shard_map/all_to_all | solution.py:354
  223.0 2.0 collective-permute-start.19
  225.8 6.7 %last.1 = f32[64,512]{1,0:T(8,128)} custom-call(f32[32,128]{1,0:T(8,128)S(1)} %pad_maximum_fusion.1.message, f32[64,512]{1,0:T(8,128)S(1)} %get-tuple-element.50.image, f32[1,512]{1,0:T(1,128)S(1)} %get-tuple-element.61.root), custom_call_target="tpu_custom_call" | custom-call | tf_op jit(solution)/shard_map/last/pallas_call | solution.py:338
  (67 shorter events, 15.2 us)
Async XLA Ops:
  0.0 16.6 %copy-start.1 = (s32[1,1,24]{2,1,0:T(1,128)S(1)}, s32[1,1,24]{2,1,0:T(1,128)}, u32[]{:S(2)}) copy-start(s32[1,1,24]{2,1,0:T(1,128)} %param.8) | copy-start | bytes 292
  0.0 16.9 %copy-start.2 = (s32[1,1,24]{2,1,0:T(1,128)S(1)}, s32[1,1,24]{2,1,0:T(1,128)}, u32[]{:S(2)}) copy-start(s32[1,1,24]{2,1,0:T(1,128)} %param.7) | copy-start | bytes 292
  2.7 14.9 %collective-permute-start = (bf16[512,1024]{1,0:T(8,128)(2,1)S(1)}, bf16[512,1024]{1,0:T(8,128)(2,1)}, u32[]{:S(2)}, u32[]{:S(2)}) collective-permute-start(bf16[512,1024]{1,0:T(8,128)(2,1)S(1)} %get-tuple-element.55.refs_0_), channel_id=1, source_target_pairs={{0,8},{8,0},{1,9},{9,1},{2,10},{10,2},{3,11},{11,3},{4,12},{12,4},... | collective-permute-start | bytes 3145736 | tf_op jit(solution)/shard_map/ppermute | solution.py:349
  4.1 26.3 %collective-permute-start.2 = (bf16[512,1024]{1,0:T(8,128)(2,1)S(1)}, bf16[512,1024]{1,0:T(8,128)(2,1)S(1)}, u32[]{:S(2)}, u32[]{:S(2)}) collective-permute-start(bf16[512,1024]{1,0:T(8,128)(2,1)S(1)} %get-tuple-element.55.refs_0_), channel_id=1, source_target_pairs={{0,32},{32,64},{64,96},{96,0},{1,33},{33,65},{65,97},{97,1},{2,34}... | collective-permute-start | bytes 3145736 | tf_op jit(solution)/shard_map/ppermute | solution.py:376
  5.5 24.9 %collective-permute-start.3 = (bf16[512,1024]{1,0:T(8,128)(2,1)S(1)}, bf16[512,1024]{1,0:T(8,128)(2,1)S(1)}, u32[]{:S(2)}, u32[]{:S(2)}) collective-permute-start(bf16[512,1024]{1,0:T(8,128)(2,1)S(1)} %get-tuple-element.55.refs_0_), channel_id=1, source_target_pairs={{0,96},{32,0},{64,32},{96,64},{1,97},{33,1},{65,33},{97,65},{2,98}... | collective-permute-start | bytes 3145736 | tf_op jit(solution)/shard_map/ppermute | solution.py:380
  7.0 27.2 %collective-permute-start.1 = (bf16[512,1024]{1,0:T(8,128)(2,1)}, bf16[512,1024]{1,0:T(8,128)(2,1)}, u32[]{:S(2)}, u32[]{:S(2)}) collective-permute-start(bf16[512,1024]{1,0:T(8,128)(2,1)} %get-tuple-element.54), channel_id=1, source_target_pairs={{0,17},{17,0},{1,16},{16,1},{2,19},{19,2},{3,18},{18,3},{4,21},{21... | collective-permute-start | bytes 3145736 | tf_op jit(solution)/shard_map/ppermute | solution.py:401
  34.1 5.9 %collective-permute-start.5 = (bf16[512,1024]{1,0:T(8,128)(2,1)}, bf16[512,1024]{1,0:T(8,128)(2,1)S(1)}, u32[]{:S(2)}, u32[]{:S(2)}) collective-permute-start(bf16[512,1024]{1,0:T(8,128)(2,1)} %collective-permute-done.1.refs_0_), channel_id=1, source_target_pairs={{0,8},{8,0},{1,9},{9,1},{2,10},{10,2},{3,11},{11,3},{4,12},{12,4},... | collective-permute-start | bytes 3145736 | tf_op jit(solution)/shard_map/ppermute | solution.py:349
  35.2 4.8 %collective-permute-start.6 = (bf16[512,1024]{1,0:T(8,128)(2,1)S(1)}, bf16[512,1024]{1,0:T(8,128)(2,1)S(1)}, u32[]{:S(2)}, u32[]{:S(2)}) collective-permute-start(bf16[512,1024]{1,0:T(8,128)(2,1)S(1)} %collective-permute-done.2.refs_2_), channel_id=1, source_target_pairs={{0,8},{8,0},{1,9},{9,1},{2,10},{10,2},{3,11},{11,3},{4,12},{12,4},... | collective-permute-start | bytes 3145736 | tf_op jit(solution)/shard_map/ppermute | solution.py:349
  35.3 14.0 %collective-permute-start.8 = (bf16[512,1024]{1,0:T(8,128)(2,1)S(1)}, bf16[512,1024]{1,0:T(8,128)(2,1)S(1)}, u32[]{:S(2)}, u32[]{:S(2)}) collective-permute-start(bf16[512,1024]{1,0:T(8,128)(2,1)S(1)} %get-tuple-element.57), channel_id=1, source_target_pairs={{0,32},{8,104},{32,64},{40,8},{64,96},{72,40},{96,0},{104,72},{1,3... | collective-permute-start | bytes 3145736 | tf_op jit(solution)/shard_map/ppermute | solution.py:384
  36.8 14.4 %collective-permute-start.9 = (bf16[512,1024]{1,0:T(8,128)(2,1)S(1)}, bf16[512,1024]{1,0:T(8,128)(2,1)S(1)}, u32[]{:S(2)}, u32[]{:S(2)}) collective-permute-start(bf16[512,1024]{1,0:T(8,128)(2,1)S(1)} %get-tuple-element.56), channel_id=1, source_target_pairs={{0,1},{8,25},{1,16},{9,8},{16,17},{24,9},{17,0},{25,24},{2,3},{10,... | collective-permute-start | bytes 3145736 | tf_op jit(solution)/shard_map/ppermute | solution.py:397
  39.5 21.0 %collective-permute-start.7 = (bf16[512,1024]{1,0:T(8,128)(2,1)}, bf16[512,1024]{1,0:T(8,128)(2,1)S(1)}, u32[]{:S(2)}, u32[]{:S(2)}) collective-permute-start(bf16[512,1024]{1,0:T(8,128)(2,1)} %collective-permute-done.1.refs_0_), channel_id=1, source_target_pairs={{0,32},{8,104},{32,64},{40,8},{64,96},{72,40},{96,0},{104,72},{1,3... | collective-permute-start | bytes 3145736 | tf_op jit(solution)/shard_map/ppermute | solution.py:384
  40.0 26.1 %collective-permute-start.4 = (bf16[512,1024]{1,0:T(8,128)(2,1)S(1)}, bf16[512,1024]{1,0:T(8,128)(2,1)S(1)}, u32[]{:S(2)}, u32[]{:S(2)}) collective-permute-start(bf16[512,1024]{1,0:T(8,128)(2,1)S(1)} %collective-permute-done.3.refs_0_), channel_id=1, source_target_pairs={{0,8},{8,0},{1,9},{9,1},{2,10},{10,2},{3,11},{11,3},{4,12},{12,4},... | collective-permute-start | bytes 3145736 | tf_op jit(solution)/shard_map/ppermute | solution.py:349
  60.5 5.6 %collective-permute-start.10 = (bf16[512,1024]{1,0:T(8,128)(2,1)S(1)}, bf16[512,1024]{1,0:T(8,128)(2,1)S(1)}, u32[]{:S(2)}, u32[]{:S(2)}) collective-permute-start(bf16[512,1024]{1,0:T(8,128)(2,1)S(1)} %collective-permute-done.8.refs_2_), channel_id=1, source_target_pairs={{0,8},{8,0},{1,9},{9,1},{2,10},{10,2},{3,11},{11,3},{4,12},{12,4},... | collective-permute-start | bytes 3145736 | tf_op jit(solution)/shard_map/ppermute | solution.py:349
  63.1 3.8 %collective-permute-start.11 = (bf16[512,1024]{1,0:T(8,128)(2,1)S(1)}, bf16[512,1024]{1,0:T(8,128)(2,1)S(1)}, u32[]{:S(2)}, u32[]{:S(2)}) collective-permute-start(bf16[512,1024]{1,0:T(8,128)(2,1)S(1)} %collective-permute-done.7.refs_4_), channel_id=1, source_target_pairs={{0,8},{8,0},{1,9},{9,1},{2,10},{10,2},{3,11},{11,3},{4,12},{12,4},... | collective-permute-start | bytes 3145736 | tf_op jit(solution)/shard_map/ppermute | solution.py:349
  63.1 13.9 %collective-permute-start.12 = (bf16[512,1024]{1,0:T(8,128)(2,1)S(1)}, bf16[512,1024]{1,0:T(8,128)(2,1)S(1)}, u32[]{:S(2)}, u32[]{:S(2)}) collective-permute-start(bf16[512,1024]{1,0:T(8,128)(2,1)S(1)} %collective-permute-done.7.refs_4_), channel_id=1, source_target_pairs={{0,32},{8,104},{32,64},{40,8},{64,96},{72,40},{96,0},{104,72},{1,3... | collective-permute-start | bytes 3145736 | tf_op jit(solution)/shard_map/ppermute | solution.py:384
  63.4 14.4 %collective-permute-start.13 = (bf16[512,1024]{1,0:T(8,128)(2,1)S(1)}, bf16[512,1024]{1,0:T(8,128)(2,1)S(1)}, u32[]{:S(2)}, u32[]{:S(2)}) collective-permute-start(bf16[512,1024]{1,0:T(8,128)(2,1)S(1)} %collective-permute-done.9), channel_id=1, source_target_pairs={{0,1},{8,25},{1,16},{9,8},{16,17},{24,9},{17,0},{25,24},{2,3},{10,... | collective-permute-start | bytes 3145736 | tf_op jit(solution)/shard_map/ppermute | solution.py:397
  66.9 12.7 %copy-start = (s32[512]{0:T(512)S(1)}, s32[512]{0:T(512)}, u32[]{:S(2)}) copy-start(s32[512]{0:T(512)} %param.6) | copy-start | bytes 6148
  77.9 5.4 %collective-permute-start.14 = (bf16[512,1024]{1,0:T(8,128)(2,1)S(1)}, bf16[512,1024]{1,0:T(8,128)(2,1)S(1)}, u32[]{:S(2)}, u32[]{:S(2)}) collective-permute-start(bf16[512,1024]{1,0:T(8,128)(2,1)S(1)} %collective-permute-done.12.refs_0_), channel_id=1, source_target_pairs={{0,8},{8,0},{1,9},{9,1},{2,10},{10,2},{3,11},{11,3},{4,12},{12,4},... | collective-permute-start | bytes 3145736 | tf_op jit(solution)/shard_map/ppermute | solution.py:349
  79.6 3.8 %collective-permute-start.15 = (bf16[512,1024]{1,0:T(8,128)(2,1)S(1)}, bf16[512,1024]{1,0:T(8,128)(2,1)S(1)}, u32[]{:S(2)}, u32[]{:S(2)}) collective-permute-start(bf16[512,1024]{1,0:T(8,128)(2,1)S(1)} %collective-permute-done.13.refs_1_), channel_id=1, source_target_pairs={{0,8},{8,0},{1,9},{9,1},{2,10},{10,2},{3,11},{11,3},{4,12},{12,4},... | collective-permute-start | bytes 3145736 | tf_op jit(solution)/shard_map/ppermute | solution.py:349
  109.4 6.3 %collective-permute-start.16 = (f32[8,2,512]{2,1,0:T(2,128)S(1)}, f32[8,2,512]{2,1,0:T(2,128)S(1)}, u32[]{:S(2)}, u32[]{:S(2)}) collective-permute-start(f32[8,2,512]{2,1,0:T(2,128)S(1)} %bitcast_reduce_fusion), channel_id=1, source_target_pairs={{0,8},{8,0},{1,9},{9,1},{2,10},{10,2},{3,11},{11,3},{4,12},{12,4},... | collective-permute-start | bytes 98312 | tf_op jit(solution)/shard_map/ppermute | solution.py:349
  119.4 19.9 %all-to-all-start.1 = ((f32[8,64,512]{2,1,0:T(8,128)}), f32[8,64,512]{2,1,0:T(8,128)S(1)}, u32[]{:S(2)}, u32[]{:S(2)}) async-start(f32[8,64,512]{2,1,0:T(8,128)} %product.2), calls=%async_computation.1 | async-start | bytes 2097152 | tf_op jit(solution)/shard_map/all_to_all | solution.py:501
  164.8 4.7 %collective-permute-start.17 = (f32[8,72,512]{2,1,0:T(8,128)S(1)}, f32[8,72,512]{2,1,0:T(8,128)S(1)}, u32[]{:S(2)}, u32[]{:S(2)}) collective-permute-start(f32[8,72,512]{2,1,0:T(8,128)S(1)} %all_to_all.26.refs_0_), channel_id=1, source_target_pairs={{0,8},{8,0},{1,9},{9,1},{2,10},{10,2},{3,11},{11,3},{4,12},{12,4},... | collective-permute-start | bytes 3538952 | tf_op jit(solution)/shard_map/ppermute | solution.py:349
  173.0 21.8 %all-to-all-start.3 = ((f32[8,72,512]{2,1,0:T(8,128)}), f32[8,72,512]{2,1,0:T(8,128)S(1)}, u32[]{:S(2)}, u32[]{:S(2)}) async-start(f32[8,72,512]{2,1,0:T(8,128)} %product.3), calls=%async_computation.3 | async-start | bytes 2359296 | tf_op jit(solution)/shard_map/all_to_all | solution.py:504
  201.3 2.1 collective-permute-start.18
  223.0 2.8 %collective-permute-start.19 = (f32[16,128]{1,0:T(8,128)S(1)}, f32[16,128]{1,0:T(8,128)S(1)}, u32[]{:S(2)}, u32[]{:S(2)}) collective-permute-start(f32[16,128]{1,0:T(8,128)S(1)} %reduce_sum.99), channel_id=1, source_target_pairs={{0,8},{8,0},{1,9},{9,1},{2,10},{10,2},{3,11},{11,3},{4,12},{12,4},... | collective-permute-start | bytes 24584 | tf_op jit(solution)/shard_map/ppermute | solution.py:349

commit v6 on v5

--- a/solution.py
+++ b/solution.py
@@ -168,14 +168,17 @@
 
 def product_kernel(first, info, tiles, *refs):
     if first:
-        labels, inv_root, running, held, sem = refs
+        labels, inv_root, out, running, held, sem = refs
     else:
-        mine, others, inv_root, running, held, sem = refs
+        mine, others, running, held, sem = refs
     count, core = info[0], info[2]
     depth = held.shape[0]
     running[...] = jnp.zeros_like(running)
     if not first:
-        rest = jnp.sum(mine[:, K:, :], axis=0) + jnp.sum(others[:, K:, :], axis=0)
+        rest = jnp.zeros((8, TILE), F32)
+        for known in (mine, others):
+            terms = jnp.sum(known[:, K:, :].astype(F32), axis=0)
+            rest = rest + (terms[:8] + (terms[8:16] + terms[16:24]))
         for t in range(SLAB_TILES):
             running[t, K:, :] = rest
 
@@ -185,23 +188,16 @@
 
     def piece(entry):
         q = info[SLABS + entry]
-        value = inv_root[pl.ds(q, 1), :]
         if first:
+            value = inv_root[pl.ds(q, 1), :]
             label = labels[pl.ds(q, 1), :]
             value = jnp.where(label < K, value, -value)
             same = (label & (K - 1)) == lax.broadcasted_iota(jnp.int32, (K, TILE), 0)
             return jnp.where(same, jnp.broadcast_to(value, (K, TILE)), 0.0).astype(BF16)
-        chip = q // 2
-        vectors = jnp.where(q % 2 == core, mine[chip, :K, :], others[chip, :K, :]) * value
-        high = vectors.astype(BF16)
-        low = (vectors - high.astype(F32)).astype(BF16)
-        return jnp.concatenate([high, low], axis=0)
+        return jnp.where(q % 2 == core, mine[q // 2, :K, :], others[q // 2, :K, :])
 
     def term(entry):
-        result = jnp.dot(
-            piece(entry), held[lax.rem(entry, depth)], preferred_element_type=F32
-        )
-        return result if first else result[:K] + result[K:]
+        return jnp.dot(piece(entry), held[lax.rem(entry, depth)], preferred_element_type=F32)
 
     for entry in range(depth - 2):
 
@@ -230,24 +226,26 @@
         return carry
 
     lax.fori_loop(0, (count + 1) // 2, step, 0)
+    if first:
+        out[...] = running[...].astype(BF16)
 
 
 def product(info, tiles, *operands):
     vmem = pl.BlockSpec(memory_space=pltpu.VMEM)
-    first = len(operands) == 2
+    first = operands[0].dtype == jnp.int32
     return pl.pallas_call(
         functools.partial(product_kernel, first),
-        out_shape=jax.ShapeDtypeStruct((SLAB_TILES, K if first else K + 8, TILE), F32),
+        out_shape=jax.ShapeDtypeStruct(
+            (SLAB_TILES, K if first else K + 8, TILE), BF16 if first else F32
+        ),
         in_specs=[
             pl.BlockSpec(memory_space=pltpu.SMEM),
             pl.BlockSpec(memory_space=pltpu.HBM),
         ]
         + [vmem] * len(operands),
         out_specs=vmem,
-        scratch_shapes=[
-            pltpu.VMEM((8, TILE, TILE), BF16),
-            pltpu.SemaphoreType.DMA((8,)),
-        ],
+        scratch_shapes=([pltpu.VMEM((SLAB_TILES, K, TILE), F32)] if first else [])
+        + [pltpu.VMEM((8, TILE, TILE), BF16), pltpu.SemaphoreType.DMA((8,))],
         compiler_params=pltpu.CompilerParams(vmem_limit_bytes=20 * 1024 * 1024),
         name="product",
     )(info, in_hbm(tiles), *operands)
@@ -293,19 +291,25 @@
     across = jnp.sum(jnp.where(rows == columns, top, 0.0), axis=0, keepdims=True)
     gram = (gram - top * across / total) * scale
     work = jnp.concatenate([gram, (rows == columns).astype(F32)], axis=1)
-    index = lax.broadcasted_iota(jnp.int32, (K, 1), 0)
-    pivots = jnp.ones((K, 1), F32)
-    for j in range(K):
-        row = work[j : j + 1, :]
-        pivot = work[j : j + 1, j : j + 1]
-        column = work[:, j : j + 1]
-        pivots = jnp.where(index == j, pivot, pivots)
-        if j < K - 1:
-            first = j // 8 * 8
-            below = jnp.where(index[first:] > j, column[first:], 0.0)
-            rest = work[first:] - below * (row / pivot)
-            work = jnp.concatenate([work[:first], rest], axis=0) if first else rest
-    return work[:, K:] * lax.rsqrt(pivots), top / total
+    index = lax.broadcasted_iota(jnp.int32, (K, 2 * K), 0)
+    pivots = jnp.ones((K, 2 * K), F32)
+    for start in range(0, K, 8):
+        index = index[-(K - start) :]
+        spread = [
+            jnp.broadcast_to(work[start:, j : j + 1], (K - start, 2 * K)) for j in range(start, start + 8)
+        ]
+        rest = work[start:]
+        below = pivots[start:]
+        for a in range(8):
+            pivot = spread[a][a : a + 1, :]
+            below = jnp.where(index == start + a, pivot, below)
+            ratio = jnp.where(index > start + a, spread[a] / pivot, 0.0)
+            rest = rest - ratio * rest[a : a + 1, :]
+            for b in range(a + 1, 8):
+                spread[b] = spread[b] - ratio * spread[b][a : a + 1, :]
+        work = jnp.concatenate([work[:start], rest], axis=0) if start else rest
+        pivots = jnp.concatenate([pivots[:start], below], axis=0) if start else below
+    return work[:, K:] * lax.rsqrt(pivots[:, K:]), top / total
 
 
 def times(factor, block):
@@ -313,10 +317,14 @@
 
 
 def weigh_kernel(parts, inv_root, root, out):
-    image = jnp.sum(parts[...], axis=0) * inv_root[...]
-    out[:K, :] = image
+    image = jnp.sum(parts[...].astype(F32), axis=0) * inv_root[...]
+    out[:K, :] = (image * inv_root[...]).astype(BF16)
     packed = weights_of(image, root[...])
-    out[K:, :] = jnp.concatenate([packed[8 * i : 8 * i + 8] for i in range(4)], axis=1)
+    sums = jnp.concatenate([packed[8 * i : 8 * i + 8] for i in range(4)], axis=1)
+    high = sums.astype(BF16).astype(F32)
+    middle = (sums - high).astype(BF16).astype(F32)
+    low = (sums - high) - middle
+    out[K:, :] = jnp.concatenate([high, middle, low, jnp.zeros_like(low)], axis=0).astype(BF16)
 
 
 def middle_kernel(scale, parts, inv_root, root, image, message):
@@ -337,9 +345,9 @@
     vmem = pl.BlockSpec(memory_space=pltpu.VMEM)
     return pl.pallas_call(
         kernel,
-        out_shape=jax.tree.map(lambda shape: jax.ShapeDtypeStruct(shape, F32), out_shape, is_leaf=lambda x: isinstance(x[0], int)),
+        out_shape=out_shape,
         in_specs=[vmem] * len(operands),
-        out_specs=jax.tree.map(lambda shape: vmem, out_shape, is_leaf=lambda x: isinstance(x[0], int)),
+        out_specs=jax.tree.map(lambda _: vmem, out_shape),
         compiler_params=pltpu.CompilerParams(vmem_limit_bytes=VMEM_LIMIT),
         name=name,
     )(*operands)
@@ -499,15 +507,17 @@
     scale = 1.0 / (BLOCK_TILES * SLAB_TILES * TILE)
     running = product(info, tiles, column_labels, column_inv_root)
     parts = lax.all_to_all(running, COL, 0, 0, tiled=True)
-    weighed = local(weigh_kernel, "weigh", (K + 8, TILE), parts, inv_root, root)
-    running = product(info, tiles, *share_row(weighed), column_inv_root)
+    weighed = local(
+        weigh_kernel, "weigh", jax.ShapeDtypeStruct((K + 32, TILE), BF16), parts, inv_root, root
+    )
+    running = product(info, tiles, *share_row(weighed))
     parts = lax.all_to_all(running, COL, 0, 0, tiled=True)
+    block = jax.ShapeDtypeStruct((K, TILE), F32)
+    packed = jax.ShapeDtypeStruct((K // 2, 128), F32)
     image, message = local(
-        functools.partial(middle_kernel, scale), "middle", ((K, TILE), (K // 2, 128)), parts, inv_root, root
-    )
-    return local(
-        functools.partial(last_kernel, scale), "last", (K, TILE), sum_all(message), image, root
-    )
+        functools.partial(middle_kernel, scale), "middle", (block, packed), parts, inv_root, root
+    )
+    return local(functools.partial(last_kernel, scale), "last", block, sum_all(message), image, root)
 
 
 def solution(mesh):

time: 231 us -> 210 us (0.909); the launches traced: 233 us -> 209 us
  waiting for transfers between devices: 79.6 us -> 69.5 us
  blocking collectives: 69.5 us -> 63.3 us
  starting transfers between devices: 39.1 us -> 35.1 us
  Pallas kernels: 33.6 us -> 30.1 us
    all_to_all x2, blocking collectives: 44.4 us -> 36.1 us  [share(): lax.all_to_all(jnp.broadcast_to(value[None], (size,) + value.shape), axes...]
    pallas_call x3, Pallas kernels: 13.5 us -> 6.05 us  [local(): pl.pallas_call(kernel, out_shape=out_shape, in_specs=[vmem] * len(operand...]
    all_to_all x2, waiting for transfers between devices: 34.6 us -> 27.9 us  [shards(): parts = lax.all_to_all(running, COL, 0, 0, tiled=True)]
    ppermute x12, starting transfers between devices: 17.8 us -> 13.8 us  [swap_cores(): return lax.ppermute(value, 'core', [(0, 1), (1, 0)])]
    ppermute x1, waiting for transfers between devices: 9.1 us -> 6.22 us  [up(): return lax.ppermute(value, 'y', [(i, (i + 1) % 4) for i in range(4)])]
    pallas_call x5, Pallas kernels: 13.1 us -> 16 us  [build(): pl.pallas_call(functools.partial(build_kernel, first, arrived), out_shape...]
  transfers between devices with their start and end apart: 22 -> 22, of which waited for: 15 -> 15; matrix products, arithmetic and copies ran while one was open for 3% -> 3% of each run, Pallas kernels for 5% -> 7%
where the time goes in v6:
time: 210 us; the launch traced here: 209 us
  waiting for transfers between devices  69.5 us (33%)
  blocking collectives  63.3 us (30%)
  starting transfers between devices  35.1 us (17%)
  Pallas kernels  30.1 us (14%)
  other arithmetic  6.38 us (3%)
  local copies, waits for them, and re-layouts  3.23 us (2%)
    all_to_all x2, blocking collectives, share(): lax.all_to_all(jnp.broadcast_to(value[None], (size,) + value.shape), axes...  36.1 us
    all_to_all x2, waiting for transfers between devices, shards(): parts = lax.all_to_all(running, COL, 0, 0, tiled=True)  27.9 us
    all_to_all x1, blocking collectives, shards(): lax.all_to_all(jnp.broadcast_to(sent[None], (8,) + sent.shape).reshape(8...  27.2 us
    ppermute x3, waiting for transfers between devices, apart(): lax.ppermute(value, ('y', 'core'), [(2 * i + k, 2 * ((i + 1 + 2 * k) % 4)...  23.6 us
    pallas_call x5, Pallas kernels, build(): pl.pallas_call(functools.partial(build_kernel, first, arrived), out_shape...  16 us
    ppermute x12, starting transfers between devices, swap_cores(): return lax.ppermute(value, 'core', [(0, 1), (1, 0)])  13.8 us
    pallas_call x2, Pallas kernels, product(): pl.pallas_call(functools.partial(product_kernel, first), out_shape=jax.Sh...  8.05 us
    all_to_all x2, starting transfers between devices, shards(): parts = lax.all_to_all(running, COL, 0, 0, tiled=True)  7.08 us
  transfers between devices with their start and end apart: 22, of which 15 were waited for; matrix products, arithmetic and copies ran while one was open for 3% of the time, Pallas kernels for 7%

profile of v6, /device:TPU:1, one launch (start us, length us, event | category | flops | bytes accessed | tf_op | source)
XLA Modules:
  0.0 208.6 jit_solution(10527374828104772649)
XLA Ops:
  0.0 2.7 %dynamic-slice_bitcast_fusion = (bf16[512,1024]{1,0:T(8,128)(2,1)}, bf16[512,1024]{1,0:T(8,128)(2,1)S(1)}) fusion(bf16[8,512,1024]{2,1,0:T(8,128)(2,1)} %bitcast.46, s32[]{:T(128)S(6)} %select_n.209, s32[]{:T(128)S(6)} %select_n.208), kind=kLoop, calls=%fused_computation.1 | loop fusion | bytes 4194312 | tf_op jit(solution)/shard_map/jit(dynamic_index_in_dim)/squeeze | solution.py:464
  5.5 1.4 collective-permute-start.3
  7.0 3.8 %collective-permute-start.1 = (bf16[512,1024]{1,0:T(8,128)(2,1)}, bf16[512,1024]{1,0:T(8,128)(2,1)}, u32[]{:S(2)}, u32[]{:S(2)}) collective-permute-start(bf16[512,1024]{1,0:T(8,128)(2,1)} %get-tuple-element.54), channel_id=1, source_target_pairs={{0,17},{17,0},{1,16},{16,1},{2,19},{19,2},{3,18},{18,3},{4,21},{21... | collective-permute-start | bytes 3145736 | tf_op jit(solution)/shard_map/ppermute | solution.py:409
  10.7 5.1 %multiply_reduce_fusion = f32[4096]{0:T(1024)S(1)} fusion(bf16[4096,1024]{1,0:T(8,128)(2,1)} %param.5), kind=kLoop, calls=%fused_computation | loop fusion | flops 12578816 | bytes 8404992 | tf_op jit(solution)/shard_map/reduce_sum | solution.py:468
  17.7 6.6 %build_tiles.5 = (bf16[24,512,512]{2,1,0:T(8,128)(2,1)}, f32[8,512]{1,0:T(8,128)S(1)}) custom-call(s32[121]{0:T(128)S(1)} %concatenate.10.info, bf16[8,512,1024]{2,1,0:T(8,128)(2,1)} %bitcast.47, f32[8,512]{1,0:T(8,128)S(1)} %mul.132.half_rows, bf16[512,1024]{1,0:T(8,128)(2,1)S(1)} %get-tuple-element.55.refs_0_, bf16[512,1024]{1,0:T(8,128)(2,1)} %collective-permute-done.refs_1_), custom_call_target="tpu_custom_call" | custom-call | flops 1610612736 | bytes 7864320 | tf_op jit(solution)/shard_map/build_tiles/pallas_call | solution.py:140
  24.2 6.2 %collective-permute-done.2.refs_2_ = bf16[512,1024]{1,0:T(8,128)(2,1)S(1)} collective-permute-done((bf16[512,1024]{1,0:T(8,128)(2,1)S(1)}, bf16[512,1024]{1,0:T(8,128)(2,1)S(1)}, u32[]{:S(2)}, u32[]{:S(2)}) %collective-permute-start.2) | collective-permute-done | bytes 1048608 | tf_op jit(solution)/shard_map/ppermute | solution.py:384
  30.5 3.7 %collective-permute-done.1.refs_0_ = bf16[512,1024]{1,0:T(8,128)(2,1)} collective-permute-done((bf16[512,1024]{1,0:T(8,128)(2,1)}, bf16[512,1024]{1,0:T(8,128)(2,1)}, u32[]{:S(2)}, u32[]{:S(2)}) %collective-permute-start.1) | collective-permute-done | bytes 1048608 | tf_op jit(solution)/shard_map/ppermute | solution.py:409
  35.3 1.5 collective-permute-start.8
  36.8 2.7 %collective-permute-start.9 = (bf16[512,1024]{1,0:T(8,128)(2,1)S(1)}, bf16[512,1024]{1,0:T(8,128)(2,1)S(1)}, u32[]{:S(2)}, u32[]{:S(2)}) collective-permute-start(bf16[512,1024]{1,0:T(8,128)(2,1)S(1)} %get-tuple-element.56), channel_id=1, source_target_pairs={{0,1},{8,25},{1,16},{9,8},{16,17},{24,9},{17,0},{25,24},{2,3},{10,... | collective-permute-start | bytes 3145736 | tf_op jit(solution)/shard_map/ppermute | solution.py:405
  40.0 4.5 %build_tiles.6 = (bf16[24,512,512]{2,1,0:T(8,128)(2,1)}, f32[8,512]{1,0:T(8,128)S(1)}) custom-call(s32[121]{0:T(128)S(1)} %concatenate.10.info, bf16[8,512,1024]{2,1,0:T(8,128)(2,1)} %bitcast.48, f32[8,512]{1,0:T(8,128)S(1)} %mul.132.half_rows, bf16[512,1024]{1,0:T(8,128)(2,1)} %collective-permute-done.1.refs_0_, ...), custom_call_target="tpu_custom_call", output_to_operand_aliasing={{0}: (7, {})} | custom-call | flops 3221225472 | bytes 15728640 | tf_op jit(solution)/shard_map/build_tiles/pallas_call | solution.py:140
  44.5 4.8 %collective-permute-done.8.refs_2_ = bf16[512,1024]{1,0:T(8,128)(2,1)S(1)} collective-permute-done((bf16[512,1024]{1,0:T(8,128)(2,1)S(1)}, bf16[512,1024]{1,0:T(8,128)(2,1)S(1)}, u32[]{:S(2)}, u32[]{:S(2)}) %collective-permute-start.8) | collective-permute-done | bytes 1048608 | tf_op jit(solution)/shard_map/ppermute | solution.py:392
  49.3 1.9 collective-permute-done.9
  51.2 9.3 %collective-permute-done.7.refs_4_ = bf16[512,1024]{1,0:T(8,128)(2,1)S(1)} collective-permute-done((bf16[512,1024]{1,0:T(8,128)(2,1)}, bf16[512,1024]{1,0:T(8,128)(2,1)S(1)}, u32[]{:S(2)}, u32[]{:S(2)}) %collective-permute-start.7) | collective-permute-done | bytes 1048608 | tf_op jit(solution)/shard_map/ppermute | solution.py:392
  60.5 2.6 %collective-permute-start.10 = (bf16[512,1024]{1,0:T(8,128)(2,1)S(1)}, bf16[512,1024]{1,0:T(8,128)(2,1)S(1)}, u32[]{:S(2)}, u32[]{:S(2)}) collective-permute-start(bf16[512,1024]{1,0:T(8,128)(2,1)S(1)} %collective-permute-done.8.refs_2_), channel_id=1, source_target_pairs={{0,8},{8,0},{1,9},{9,1},{2,10},{10,2},{3,11},{11,3},{4,12},{12,4},... | collective-permute-start | bytes 3145736 | tf_op jit(solution)/shard_map/ppermute | solution.py:357
  63.4 2.7 %collective-permute-start.13 = (bf16[512,1024]{1,0:T(8,128)(2,1)S(1)}, bf16[512,1024]{1,0:T(8,128)(2,1)S(1)}, u32[]{:S(2)}, u32[]{:S(2)}) collective-permute-start(bf16[512,1024]{1,0:T(8,128)(2,1)S(1)} %collective-permute-done.9), channel_id=1, source_target_pairs={{0,1},{8,25},{1,16},{9,8},{16,17},{24,9},{17,0},{25,24},{2,3},{10,... | collective-permute-start | bytes 3145736 | tf_op jit(solution)/shard_map/ppermute | solution.py:405
  67.6 9.5 %collective-permute-done.12.refs_0_ = bf16[512,1024]{1,0:T(8,128)(2,1)S(1)} collective-permute-done((bf16[512,1024]{1,0:T(8,128)(2,1)S(1)}, bf16[512,1024]{1,0:T(8,128)(2,1)S(1)}, u32[]{:S(2)}, u32[]{:S(2)}) %collective-permute-start.12) | collective-permute-done | bytes 1048608 | tf_op jit(solution)/shard_map/ppermute | solution.py:392
  77.9 1.8 collective-permute-start.14
  79.7 3.6 %build_tiles.8 = (bf16[24,512,512]{2,1,0:T(8,128)(2,1)}, f32[8,512]{1,0:T(8,128)S(1)}) custom-call(s32[121]{0:T(128)S(1)} %concatenate.10.info, bf16[8,512,1024]{2,1,0:T(8,128)(2,1)} %bitcast.50, f32[8,512]{1,0:T(8,128)S(1)} %mul.132.half_rows, bf16[512,1024]{1,0:T(8,128)(2,1)S(1)} %collective-permute-done.12.refs_0_, ...), custom_call_target="tpu_custom_call", output_to_operand_aliasing={{0}: (5, {})} | custom-call | flops 1610612736 | bytes 7864320 | tf_op jit(solution)/shard_map/build_tiles/pallas_call | solution.py:140
  84.2 27.2 %all_to_all.25 = f32[64,2,512]{2,1,0:T(2,128)S(1)} all-to-all(f32[64,2,512]{2,1,0:T(2,128)S(1)} %bitcast.52), channel_id=1, replica_groups=mesh['y'=4,'zh'=2,'core'=2,'x'=4,'zl'=2] {'y','zh','x','zl'}, dimensions={0} | all-to-all | bytes 524288 | tf_op jit(solution)/shard_map/all_to_all | solution.py:494
  113.6 3.9 %product.2 = bf16[8,64,512]{2,1,0:T(8,128)(2,1)} custom-call(s32[121]{0:T(128)S(1)} %concatenate.10.info, bf16[24,512,512]{2,1,0:T(8,128)(2,1)} %get-tuple-element.47.tiles, s32[16,512]{1,0:T(8,128)S(1)} %get-tuple-element.60.refs_0_, f32[16,512]{1,0:T(8,128)S(1)} %get-tuple-element.59.refs_1_), custom_call_target="tpu_custom_call" | custom-call | tf_op jit(solution)/shard_map/product/pallas_call | solution.py:236
  117.6 3.5 %all-to-all-start.1 = ((bf16[8,64,512]{2,1,0:T(8,128)(2,1)}), bf16[8,64,512]{2,1,0:T(8,128)(2,1)S(1)}, u32[]{:S(2)}, u32[]{:S(2)}) async-start(bf16[8,64,512]{2,1,0:T(8,128)(2,1)} %product.2), calls=%async_computation.1 | async-start | bytes 1048576 | tf_op jit(solution)/shard_map/all_to_all | solution.py:509
  121.1 9.5 %all-to-all-done.1.parts = bf16[8,64,512]{2,1,0:T(8,128)(2,1)S(1)} async-done(((bf16[8,64,512]{2,1,0:T(8,128)(2,1)}), bf16[8,64,512]{2,1,0:T(8,128)(2,1)S(1)}, u32[]{:S(2)}, u32[]{:S(2)}) %all-to-all-start.1) | async-done | bytes 524320 | tf_op jit(solution)/shard_map/all_to_all | solution.py:509
  131.2 17.2 %all_to_all.26.refs_0_ = bf16[8,96,512]{2,1,0:T(8,128)(2,1)S(1)} all-to-all(bf16[8,96,512]{2,1,0:T(8,128)(2,1)S(1)} %broadcast_in_dim.110), channel_id=1, replica_groups=mesh['y'=4,'zh'=2,'core'=2,'x'=4,'zl'=2] {'y','zh'}, dimensions={0} | all-to-all | bytes 1572864 | tf_op jit(solution)/shard_map/all_to_all | solution.py:362
  148.4 2.7 %collective-permute-start.17 = (bf16[8,96,512]{2,1,0:T(8,128)(2,1)S(1)}, bf16[8,96,512]{2,1,0:T(8,128)(2,1)S(1)}, u32[]{:S(2)}, u32[]{:S(2)}) collective-permute-start(bf16[8,96,512]{2,1,0:T(8,128)(2,1)S(1)} %all_to_all.26.refs_0_), channel_id=1, source_target_pairs={{0,8},{8,0},{1,9},{9,1},{2,10},{10,2},{3,11},{11,3},{4,12},{12,4},... | collective-permute-start | bytes 2359304 | tf_op jit(solution)/shard_map/ppermute | solution.py:357
  151.1 1.9 collective-permute-done.17.refs_1_
  153.0 4.1 %product.3 = f32[8,72,512]{2,1,0:T(8,128)} custom-call(s32[121]{0:T(128)S(1)} %concatenate.10.info, bf16[24,512,512]{2,1,0:T(8,128)(2,1)} %get-tuple-element.47.tiles, bf16[8,96,512]{2,1,0:T(8,128)(2,1)S(1)} %all_to_all.26.refs_0_, bf16[8,96,512]{2,1,0:T(8,128)(2,1)S(1)} %collective-permute-done.17.refs_1_), custom_call_target="tpu_custom_call" | custom-call | tf_op jit(solution)/shard_map/product/pallas_call | solution.py:236
  157.1 3.6 %all-to-all-start.3 = ((f32[8,72,512]{2,1,0:T(8,128)}), f32[8,72,512]{2,1,0:T(8,128)S(1)}, u32[]{:S(2)}, u32[]{:S(2)}) async-start(f32[8,72,512]{2,1,0:T(8,128)} %product.3), calls=%async_computation.3 | async-start | bytes 2359296 | tf_op jit(solution)/shard_map/all_to_all | solution.py:514
  160.7 18.4 %all-to-all-done.3.parts = f32[8,72,512]{2,1,0:T(8,128)S(1)} async-done(((f32[8,72,512]{2,1,0:T(8,128)}), f32[8,72,512]{2,1,0:T(8,128)S(1)}, u32[]{:S(2)}, u32[]{:S(2)}) %all-to-all-start.3) | async-done | bytes 1179680 | tf_op jit(solution)/shard_map/all_to_all | solution.py:514
  179.1 2.7 %middle.1 = (f32[64,512]{1,0:T(8,128)S(1)}, f32[32,128]{1,0:T(8,128)S(1)}) custom-call(f32[8,72,512]{2,1,0:T(8,128)S(1)} %all-to-all-done.3.parts, f32[1,512]{1,0:T(1,128)S(1)} %get-tuple-element.62.inv_root, f32[1,512]{1,0:T(1,128)S(1)} %get-tuple-element.61.root), custom_call_target="tpu_custom_call" | custom-call | tf_op jit(solution)/shard_map/middle/pallas_call | solution.py:346
  183.9 18.9 %all_to_all.27 = f32[64,16,128]{2,1,0:T(8,128)S(1)} all-to-all(f32[64,16,128]{2,1,0:T(8,128)S(1)} %broadcast_in_dim.111), channel_id=1, replica_groups=mesh['y'=4,'zh'=2,'core'=2,'x'=4,'zl'=2] {'y','zh','x','zl'}, dimensions={0} | all-to-all | bytes 1048576 | tf_op jit(solution)/shard_map/all_to_all | solution.py:362
  202.8 2.0 collective-permute-start.19
  205.6 2.9 %last.1 = f32[64,512]{1,0:T(8,128)} custom-call(f32[32,128]{1,0:T(8,128)S(1)} %pad_maximum_fusion.1.message, f32[64,512]{1,0:T(8,128)S(1)} %get-tuple-element.50.image, f32[1,512]{1,0:T(1,128)S(1)} %get-tuple-element.61.root), custom_call_target="tpu_custom_call" | custom-call | tf_op jit(solution)/shard_map/last/pallas_call | solution.py:346
  (67 shorter events, 14.8 us)
Async XLA Ops:
  0.0 16.6 %copy-start.1 = (s32[1,1,24]{2,1,0:T(1,128)S(1)}, s32[1,1,24]{2,1,0:T(1,128)}, u32[]{:S(2)}) copy-start(s32[1,1,24]{2,1,0:T(1,128)} %param.8) | copy-start | bytes 292
  0.0 16.9 %copy-start.2 = (s32[1,1,24]{2,1,0:T(1,128)S(1)}, s32[1,1,24]{2,1,0:T(1,128)}, u32[]{:S(2)}) copy-start(s32[1,1,24]{2,1,0:T(1,128)} %param.7) | copy-start | bytes 292
  2.7 14.9 %collective-permute-start = (bf16[512,1024]{1,0:T(8,128)(2,1)S(1)}, bf16[512,1024]{1,0:T(8,128)(2,1)}, u32[]{:S(2)}, u32[]{:S(2)}) collective-permute-start(bf16[512,1024]{1,0:T(8,128)(2,1)S(1)} %get-tuple-element.55.refs_0_), channel_id=1, source_target_pairs={{0,8},{8,0},{1,9},{9,1},{2,10},{10,2},{3,11},{11,3},{4,12},{12,4},... | collective-permute-start | bytes 3145736 | tf_op jit(solution)/shard_map/ppermute | solution.py:357
  4.1 26.3 %collective-permute-start.2 = (bf16[512,1024]{1,0:T(8,128)(2,1)S(1)}, bf16[512,1024]{1,0:T(8,128)(2,1)S(1)}, u32[]{:S(2)}, u32[]{:S(2)}) collective-permute-start(bf16[512,1024]{1,0:T(8,128)(2,1)S(1)} %get-tuple-element.55.refs_0_), channel_id=1, source_target_pairs={{0,32},{32,64},{64,96},{96,0},{1,33},{33,65},{65,97},{97,1},{2,34}... | collective-permute-start | bytes 3145736 | tf_op jit(solution)/shard_map/ppermute | solution.py:384
  5.5 24.9 %collective-permute-start.3 = (bf16[512,1024]{1,0:T(8,128)(2,1)S(1)}, bf16[512,1024]{1,0:T(8,128)(2,1)S(1)}, u32[]{:S(2)}, u32[]{:S(2)}) collective-permute-start(bf16[512,1024]{1,0:T(8,128)(2,1)S(1)} %get-tuple-element.55.refs_0_), channel_id=1, source_target_pairs={{0,96},{32,0},{64,32},{96,64},{1,97},{33,1},{65,33},{97,65},{2,98}... | collective-permute-start | bytes 3145736 | tf_op jit(solution)/shard_map/ppermute | solution.py:388
  7.0 27.2 %collective-permute-start.1 = (bf16[512,1024]{1,0:T(8,128)(2,1)}, bf16[512,1024]{1,0:T(8,128)(2,1)}, u32[]{:S(2)}, u32[]{:S(2)}) collective-permute-start(bf16[512,1024]{1,0:T(8,128)(2,1)} %get-tuple-element.54), channel_id=1, source_target_pairs={{0,17},{17,0},{1,16},{16,1},{2,19},{19,2},{3,18},{18,3},{4,21},{21... | collective-permute-start | bytes 3145736 | tf_op jit(solution)/shard_map/ppermute | solution.py:409
  34.1 5.9 %collective-permute-start.5 = (bf16[512,1024]{1,0:T(8,128)(2,1)}, bf16[512,1024]{1,0:T(8,128)(2,1)S(1)}, u32[]{:S(2)}, u32[]{:S(2)}) collective-permute-start(bf16[512,1024]{1,0:T(8,128)(2,1)} %collective-permute-done.1.refs_0_), channel_id=1, source_target_pairs={{0,8},{8,0},{1,9},{9,1},{2,10},{10,2},{3,11},{11,3},{4,12},{12,4},... | collective-permute-start | bytes 3145736 | tf_op jit(solution)/shard_map/ppermute | solution.py:357
  35.2 4.8 %collective-permute-start.6 = (bf16[512,1024]{1,0:T(8,128)(2,1)S(1)}, bf16[512,1024]{1,0:T(8,128)(2,1)S(1)}, u32[]{:S(2)}, u32[]{:S(2)}) collective-permute-start(bf16[512,1024]{1,0:T(8,128)(2,1)S(1)} %collective-permute-done.2.refs_2_), channel_id=1, source_target_pairs={{0,8},{8,0},{1,9},{9,1},{2,10},{10,2},{3,11},{11,3},{4,12},{12,4},... | collective-permute-start | bytes 3145736 | tf_op jit(solution)/shard_map/ppermute | solution.py:357
  35.3 14.0 %collective-permute-start.8 = (bf16[512,1024]{1,0:T(8,128)(2,1)S(1)}, bf16[512,1024]{1,0:T(8,128)(2,1)S(1)}, u32[]{:S(2)}, u32[]{:S(2)}) collective-permute-start(bf16[512,1024]{1,0:T(8,128)(2,1)S(1)} %get-tuple-element.57), channel_id=1, source_target_pairs={{0,32},{8,104},{32,64},{40,8},{64,96},{72,40},{96,0},{104,72},{1,3... | collective-permute-start | bytes 3145736 | tf_op jit(solution)/shard_map/ppermute | solution.py:392
  36.8 14.4 %collective-permute-start.9 = (bf16[512,1024]{1,0:T(8,128)(2,1)S(1)}, bf16[512,1024]{1,0:T(8,128)(2,1)S(1)}, u32[]{:S(2)}, u32[]{:S(2)}) collective-permute-start(bf16[512,1024]{1,0:T(8,128)(2,1)S(1)} %get-tuple-element.56), channel_id=1, source_target_pairs={{0,1},{8,25},{1,16},{9,8},{16,17},{24,9},{17,0},{25,24},{2,3},{10,... | collective-permute-start | bytes 3145736 | tf_op jit(solution)/shard_map/ppermute | solution.py:405
  39.5 21.0 %collective-permute-start.7 = (bf16[512,1024]{1,0:T(8,128)(2,1)}, bf16[512,1024]{1,0:T(8,128)(2,1)S(1)}, u32[]{:S(2)}, u32[]{:S(2)}) collective-permute-start(bf16[512,1024]{1,0:T(8,128)(2,1)} %collective-permute-done.1.refs_0_), channel_id=1, source_target_pairs={{0,32},{8,104},{32,64},{40,8},{64,96},{72,40},{96,0},{104,72},{1,3... | collective-permute-start | bytes 3145736 | tf_op jit(solution)/shard_map/ppermute | solution.py:392
  40.0 26.1 %collective-permute-start.4 = (bf16[512,1024]{1,0:T(8,128)(2,1)S(1)}, bf16[512,1024]{1,0:T(8,128)(2,1)S(1)}, u32[]{:S(2)}, u32[]{:S(2)}) collective-permute-start(bf16[512,1024]{1,0:T(8,128)(2,1)S(1)} %collective-permute-done.3.refs_0_), channel_id=1, source_target_pairs={{0,8},{8,0},{1,9},{9,1},{2,10},{10,2},{3,11},{11,3},{4,12},{12,4},... | collective-permute-start | bytes 3145736 | tf_op jit(solution)/shard_map/ppermute | solution.py:357
  60.5 5.6 %collective-permute-start.10 = (bf16[512,1024]{1,0:T(8,128)(2,1)S(1)}, bf16[512,1024]{1,0:T(8,128)(2,1)S(1)}, u32[]{:S(2)}, u32[]{:S(2)}) collective-permute-start(bf16[512,1024]{1,0:T(8,128)(2,1)S(1)} %collective-permute-done.8.refs_2_), channel_id=1, source_target_pairs={{0,8},{8,0},{1,9},{9,1},{2,10},{10,2},{3,11},{11,3},{4,12},{12,4},... | collective-permute-start | bytes 3145736 | tf_op jit(solution)/shard_map/ppermute | solution.py:357
  63.1 3.8 %collective-permute-start.11 = (bf16[512,1024]{1,0:T(8,128)(2,1)S(1)}, bf16[512,1024]{1,0:T(8,128)(2,1)S(1)}, u32[]{:S(2)}, u32[]{:S(2)}) collective-permute-start(bf16[512,1024]{1,0:T(8,128)(2,1)S(1)} %collective-permute-done.7.refs_4_), channel_id=1, source_target_pairs={{0,8},{8,0},{1,9},{9,1},{2,10},{10,2},{3,11},{11,3},{4,12},{12,4},... | collective-permute-start | bytes 3145736 | tf_op jit(solution)/shard_map/ppermute | solution.py:357
  63.1 13.9 %collective-permute-start.12 = (bf16[512,1024]{1,0:T(8,128)(2,1)S(1)}, bf16[512,1024]{1,0:T(8,128)(2,1)S(1)}, u32[]{:S(2)}, u32[]{:S(2)}) collective-permute-start(bf16[512,1024]{1,0:T(8,128)(2,1)S(1)} %collective-permute-done.7.refs_4_), channel_id=1, source_target_pairs={{0,32},{8,104},{32,64},{40,8},{64,96},{72,40},{96,0},{104,72},{1,3... | collective-permute-start | bytes 3145736 | tf_op jit(solution)/shard_map/ppermute | solution.py:392
  63.4 14.4 %collective-permute-start.13 = (bf16[512,1024]{1,0:T(8,128)(2,1)S(1)}, bf16[512,1024]{1,0:T(8,128)(2,1)S(1)}, u32[]{:S(2)}, u32[]{:S(2)}) collective-permute-start(bf16[512,1024]{1,0:T(8,128)(2,1)S(1)} %collective-permute-done.9), channel_id=1, source_target_pairs={{0,1},{8,25},{1,16},{9,8},{16,17},{24,9},{17,0},{25,24},{2,3},{10,... | collective-permute-start | bytes 3145736 | tf_op jit(solution)/shard_map/ppermute | solution.py:405
  66.9 12.7 %copy-start = (s32[512]{0:T(512)S(1)}, s32[512]{0:T(512)}, u32[]{:S(2)}) copy-start(s32[512]{0:T(512)} %param.6) | copy-start | bytes 6148
  77.9 5.5 %collective-permute-start.14 = (bf16[512,1024]{1,0:T(8,128)(2,1)S(1)}, bf16[512,1024]{1,0:T(8,128)(2,1)S(1)}, u32[]{:S(2)}, u32[]{:S(2)}) collective-permute-start(bf16[512,1024]{1,0:T(8,128)(2,1)S(1)} %collective-permute-done.12.refs_0_), channel_id=1, source_target_pairs={{0,8},{8,0},{1,9},{9,1},{2,10},{10,2},{3,11},{11,3},{4,12},{12,4},... | collective-permute-start | bytes 3145736 | tf_op jit(solution)/shard_map/ppermute | solution.py:357
  79.6 3.8 %collective-permute-start.15 = (bf16[512,1024]{1,0:T(8,128)(2,1)S(1)}, bf16[512,1024]{1,0:T(8,128)(2,1)S(1)}, u32[]{:S(2)}, u32[]{:S(2)}) collective-permute-start(bf16[512,1024]{1,0:T(8,128)(2,1)S(1)} %collective-permute-done.13.refs_1_), channel_id=1, source_target_pairs={{0,8},{8,0},{1,9},{9,1},{2,10},{10,2},{3,11},{11,3},{4,12},{12,4},... | collective-permute-start | bytes 3145736 | tf_op jit(solution)/shard_map/ppermute | solution.py:357
  111.5 2.0 collective-permute-start.16
  117.6 13.1 %all-to-all-start.1 = ((bf16[8,64,512]{2,1,0:T(8,128)(2,1)}), bf16[8,64,512]{2,1,0:T(8,128)(2,1)S(1)}, u32[]{:S(2)}, u32[]{:S(2)}) async-start(bf16[8,64,512]{2,1,0:T(8,128)(2,1)} %product.2), calls=%async_computation.1 | async-start | bytes 1048576 | tf_op jit(solution)/shard_map/all_to_all | solution.py:509
  148.4 4.6 %collective-permute-start.17 = (bf16[8,96,512]{2,1,0:T(8,128)(2,1)S(1)}, bf16[8,96,512]{2,1,0:T(8,128)(2,1)S(1)}, u32[]{:S(2)}, u32[]{:S(2)}) collective-permute-start(bf16[8,96,512]{2,1,0:T(8,128)(2,1)S(1)} %all_to_all.26.refs_0_), channel_id=1, source_target_pairs={{0,8},{8,0},{1,9},{9,1},{2,10},{10,2},{3,11},{11,3},{4,12},{12,4},... | collective-permute-start | bytes 2359304 | tf_op jit(solution)/shard_map/ppermute | solution.py:357
  157.1 22.0 %all-to-all-start.3 = ((f32[8,72,512]{2,1,0:T(8,128)}), f32[8,72,512]{2,1,0:T(8,128)S(1)}, u32[]{:S(2)}, u32[]{:S(2)}) async-start(f32[8,72,512]{2,1,0:T(8,128)} %product.3), calls=%async_computation.3 | async-start | bytes 2359296 | tf_op jit(solution)/shard_map/all_to_all | solution.py:514
  181.8 2.0 collective-permute-start.18
  202.8 2.8 %collective-permute-start.19 = (f32[16,128]{1,0:T(8,128)S(1)}, f32[16,128]{1,0:T(8,128)S(1)}, u32[]{:S(2)}, u32[]{:S(2)}) collective-permute-start(f32[16,128]{1,0:T(8,128)S(1)} %reduce_sum.99), channel_id=1, source_target_pairs={{0,8},{8,0},{1,9},{9,1},{2,10},{10,2},{3,11},{11,3},{4,12},{12,4},... | collective-permute-start | bytes 24584 | tf_op jit(solution)/shard_map/ppermute | solution.py:357

commit v7 on v6

--- a/solution.py
+++ b/solution.py
@@ -166,21 +166,32 @@
     )(info, in_hbm(slab), half_rows, *columns, *([in_hbm(made[0]), made[1]] if made else []))
 
 
+def terms_of(value):
+    high = value.astype(BF16).astype(F32)
+    middle = (value - high).astype(BF16).astype(F32)
+    low = (value - high) - middle
+    return jnp.concatenate([high, middle, low, jnp.zeros_like(low)], axis=0).astype(BF16)
+
+
+def sum_of(terms):
+    total = jnp.sum(terms.astype(F32), axis=0)
+    return total[:8] + (total[8:16] + total[16:24])
+
+
 def product_kernel(first, info, tiles, *refs):
     if first:
-        labels, inv_root, out, running, held, sem = refs
+        labels, inv_root, degree, shift, out, running, held, sem = refs
     else:
-        mine, others, running, held, sem = refs
+        mine, others, out, running, held, sem = refs
     count, core = info[0], info[2]
     depth = held.shape[0]
     running[...] = jnp.zeros_like(running)
     if not first:
         rest = jnp.zeros((8, TILE), F32)
         for known in (mine, others):
-            terms = jnp.sum(known[:, K:, :].astype(F32), axis=0)
-            rest = rest + (terms[:8] + (terms[8:16] + terms[16:24]))
+            rest = rest + sum_of(known[:, K:, :])
         for t in range(SLAB_TILES):
-            running[t, K:, :] = rest
+            out[t, K:, :] = terms_of(rest)
 
     def fetch(entry):
         slot = lax.rem(entry, depth)
@@ -221,13 +232,16 @@
             fetch(two).wait()
 
         one_term, two_term = term(one), term(two)
-        running[info[ROWS + one], :K, :] += one_term
-        running[info[ROWS + two], :K, :] += jnp.where(two < count, two_term, 0.0)
+        running[info[ROWS + one]] += one_term
+        running[info[ROWS + two]] += jnp.where(two < count, two_term, 0.0)
         return carry
 
     lax.fori_loop(0, (count + 1) // 2, step, 0)
-    if first:
-        out[...] = running[...].astype(BF16)
+    for t in range(SLAB_TILES):
+        total = running[t]
+        if first:
+            total = total - shift[...] * degree[t : t + 1, :]
+        out[t, :K, :] = total.astype(BF16)
 
 
 def product(info, tiles, *operands):
@@ -236,7 +250,7 @@
     return pl.pallas_call(
         functools.partial(product_kernel, first),
         out_shape=jax.ShapeDtypeStruct(
-            (SLAB_TILES, K if first else K + 8, TILE), BF16 if first else F32
+            (SLAB_TILES, K if first else K + 32, TILE), BF16
         ),
         in_specs=[
             pl.BlockSpec(memory_space=pltpu.SMEM),
@@ -244,8 +258,11 @@
         ]
         + [vmem] * len(operands),
         out_specs=vmem,
-        scratch_shapes=([pltpu.VMEM((SLAB_TILES, K, TILE), F32)] if first else [])
-        + [pltpu.VMEM((8, TILE, TILE), BF16), pltpu.SemaphoreType.DMA((8,))],
+        scratch_shapes=[
+            pltpu.VMEM((SLAB_TILES, K, TILE), F32),
+            pltpu.VMEM((8, TILE, TILE), BF16),
+            pltpu.SemaphoreType.DMA((8,)),
+        ],
         compiler_params=pltpu.CompilerParams(vmem_limit_bytes=20 * 1024 * 1024),
         name="product",
     )(info, in_hbm(tiles), *operands)
@@ -321,17 +338,15 @@
     out[:K, :] = (image * inv_root[...]).astype(BF16)
     packed = weights_of(image, root[...])
     sums = jnp.concatenate([packed[8 * i : 8 * i + 8] for i in range(4)], axis=1)
-    high = sums.astype(BF16).astype(F32)
-    middle = (sums - high).astype(BF16).astype(F32)
-    low = (sums - high) - middle
-    out[K:, :] = jnp.concatenate([high, middle, low, jnp.zeros_like(low)], axis=0).astype(BF16)
+    out[K:, :] = terms_of(sums)
 
 
 def middle_kernel(scale, parts, inv_root, root, image, message):
-    sums = jnp.sum(parts[...], axis=0)
-    packed = jnp.concatenate([sums[K:, 128 * i : 128 * i + 128] for i in range(4)], axis=0)
+    sums = sum_of(parts[:, K:, :])
+    packed = jnp.concatenate([sums[:, 128 * i : 128 * i + 128] for i in range(4)], axis=0)
     factor, lead = factor_of(packed, scale)
-    block = times(factor, sums[:K] * inv_root[...] - lead * root[...])
+    whole = jnp.sum(parts[:, :K, :].astype(F32), axis=0)
+    block = times(factor, whole * inv_root[...] - lead * root[...])
     image[...] = block
     message[...] = weights_of(block, root[...])
 
@@ -440,31 +455,27 @@
     def of(dy, dz, k):
         return ((y + dy) % 4 * 2 + (zh + dz) % 2) * 2 + k
 
-    side = lambda k: jnp.where(k == 0, 3, 1)
-    arrivals = []
-    for k in (core, 1 - core):
-        arrivals.append(
-            [
-                of(0, 0, k),
-                of(0, 1, k),
-                of(3, 0, k),
-                of(1, 0, k),
-                of(2, 0, k),
-                of(side(k), 1, k),
-                of(2, 1, k),
-                of(4 - side(k), 1, k),
-            ]
-        )
-    first, second = arrivals
-    arrivals = [q for both in zip(first[:6], second[:6], strict=True) for q in both]
-    arrivals = jnp.stack(arrivals + first[6:] + second[6:])
+    def side(k):
+        return jnp.where(k == 0, 3, 1)
+
+    def both_of(dy, dz):
+        return [of(dy, dz, core), of(dy, dz, 1 - core)]
+
+    near_q, other_q = (
+        [of(side(k ^ way), 1, k) for k in (core, 1 - core)] for way in (0, 1)
+    )
+    beyond_q, far_q = both_of(2, 0), both_of(2, 1)
+    arrivals = both_of(0, 0) + both_of(0, 1) + both_of(3, 0) + both_of(1, 0) + near_q
+    arrivals += [beyond_q[0], other_q[0], beyond_q[1], other_q[1], far_q[0], far_q[1]]
+    arrivals = jnp.stack(arrivals)
     info = pair_list(pair_count[0, 0], block_index, core, pair_rows[0, 0], pair_cols[0, 0], arrivals)
 
     own = lax.dynamic_index_in_dim(slab, block_index, 0, keepdims=False)
-    give = lax.dynamic_index_in_dim(slab, block_index ^ 1, 0, keepdims=False)
-    across = cross(give)
+    later, own = lax.optimization_barrier((slab, own))
     below = up(own)
     above = down(own)
+    give = lax.dynamic_index_in_dim(later, block_index ^ 1, 0, keepdims=False)
+    across = cross(give)
     half_rows = 0.5 * jnp.sum(jnp.square(slab.astype(F32)), axis=2)
 
     def both(*pieces):
@@ -477,35 +488,51 @@
     made = build(0, info, slab, half_rows, both(own), ())
     made, (across, below, above) = after(made, across, below, above)
     near = apart(across)
+    other = apart_z(jnp.where(zero, above, below))
+    made = build(2, info, slab, half_rows, both(across, below, above), made)
+    made, (near, other, below, above) = after(made, near, other, below, above)
     beyond = apart(jnp.where(zero, below, above))
-    other = apart_z(jnp.where(zero, above, below))
-    made = build(2, info, slab, half_rows, both(across, below), made)
-    made, (near, beyond, other) = after(made, near, beyond, other)
-    far = apart(near)
     other = apart_z(other)
-    made = build(6, info, slab, half_rows, both(above, beyond, near), made)
-    made, last = after(made, far, other)
-    made = build(12, info, slab, half_rows, last, made)
-    made = build(14, info, slab, half_rows, [swap_cores(piece) for piece in last], made)
+    made = build(8, info, slab, half_rows, [near], made)
+    made, (passed,) = after(made, near)
+    far = apart(passed)
+    made = build(9, info, slab, half_rows, [swap_cores(near), beyond, other], made)
+    made, (far,) = after(made, far)
+    made = build(12, info, slab, half_rows, [swap_cores(beyond), swap_cores(other), far], made)
+    made = build(15, info, slab, half_rows, [swap_cores(far)], made)
     tiles, partial_degree = made
 
     in_block = jnp.arange(SLAB_TILES)[:, None] == block_index
-    sent = jnp.stack([partial_degree, jnp.where(in_block, labels.astype(F32)[None], 0.0)], axis=1)
+    counted = jnp.where(labels % K == jnp.arange(K)[:, None], jnp.where(labels < K, 1.0, -1.0), 0.0)
+    facts = jnp.concatenate(
+        [jnp.sum(counted, axis=1), jnp.sum(partial_degree)[None], jnp.zeros(TILE - K - 1, F32)]
+    )
+    sent = jnp.stack(
+        [
+            partial_degree,
+            jnp.where(in_block, labels.astype(F32)[None], 0.0),
+            jnp.broadcast_to(facts[None], (SLAB_TILES, TILE)),
+        ],
+        axis=1,
+    )
     got = lax.all_to_all(
-        jnp.broadcast_to(sent[None], (8,) + sent.shape).reshape(8 * SLAB_TILES, 2, TILE), CHIPS, 0, 0, tiled=True
-    )
-    mine = jnp.sum(got.reshape(8, SLAB_TILES, 2, TILE), axis=1)
+        jnp.broadcast_to(sent[None], (8,) + sent.shape).reshape(8 * SLAB_TILES, 3, TILE), CHIPS, 0, 0, tiled=True
+    )
+    mine = jnp.sum(got.reshape(8, SLAB_TILES, 3, TILE), axis=1)
     others = swap_cores(mine)
-    known = jnp.where(zero, jnp.stack([mine, others], 1), jnp.stack([others, mine], 1)).reshape(BLOCK_TILES, 2, TILE)
+    known = jnp.where(zero, jnp.stack([mine, others], 1), jnp.stack([others, mine], 1)).reshape(BLOCK_TILES, 3, TILE)
     column_degree = known[:, 0]
     column_labels = known[:, 1].astype(jnp.int32)
+    facts = jnp.sum(mine[:, 2], axis=0) + jnp.sum(others[:, 2], axis=0)
+    documents = BLOCK_TILES * SLAB_TILES * TILE
+    shift = facts[:K, None] * lax.rsqrt(facts[K] * documents)
     column_inv_root = lax.rsqrt(column_degree)
     degree = lax.dynamic_slice_in_dim(column_degree, slab_index, 1, 0)
     inv_root = lax.rsqrt(degree)
     root = jnp.sqrt(degree)
 
-    scale = 1.0 / (BLOCK_TILES * SLAB_TILES * TILE)
-    running = product(info, tiles, column_labels, column_inv_root)
+    scale = 1.0 / documents
+    running = product(info, tiles, column_labels, column_inv_root, partial_degree, shift)
     parts = lax.all_to_all(running, COL, 0, 0, tiled=True)
     weighed = local(
         weigh_kernel, "weigh", jax.ShapeDtypeStruct((K + 32, TILE), BF16), parts, inv_root, root

time: 210 us -> 211 us (level)
  waiting for transfers between devices: 69.5 us -> 58.7 us
  starting transfers between devices: 35.1 us -> 44.8 us
    ppermute x3, waiting for transfers between devices: 23.6 us -> 13.3 us  [apart(): lax.ppermute(value, ('y', 'core'), [(2 * i + k, 2 * ((i + 1 + 2 * k) % 4)...]
    ppermute x1, waiting for transfers between devices: 3.66 us -> 12.7 us  [cross(): return lax.ppermute(value, ('zh', 'zl'), [(0, 3), (3, 0), (1, 2), (2, 1)])]
    ppermute x1, waiting for transfers between devices: 6.22 us -> 0.01 us  [up(): return lax.ppermute(value, 'y', [(i, (i + 1) % 4) for i in range(4)])]
    ppermute x12, starting transfers between devices: 13.8 us -> 19.5 us  [swap_cores(): return lax.ppermute(value, 'core', [(0, 1), (1, 0)])]
    all_to_all x2, waiting for transfers between devices: 27.9 us -> 22.5 us  [shards(): parts = lax.all_to_all(running, COL, 0, 0, tiled=True)]
    ppermute x2, starting transfers between devices: 5.35 us -> 8.98 us  [apart_z(): return lax.ppermute(value, ('zh', 'core', 'zl'), moves)]
    all_to_all x1, blocking collectives: 27.2 us -> 24 us  [shards(): lax.all_to_all(jnp.broadcast_to(sent[None], (8,) + sent.shape).reshape(8...]
    pallas_call x5 -> x6, Pallas kernels: 16 us -> 17.2 us  [build(): pl.pallas_call(functools.partial(build_kernel, first, arrived), out_shape...]
  transfers between devices with their start and end apart: 22 -> 22, of which waited for: 15 -> 14; matrix products, arithmetic and copies ran while one was open for 3% -> 4% of each run, Pallas kernels for 7% -> 6%
where the time goes in v7:
time: 211 us; the launch traced here: 210 us
  blocking collectives  61.5 us (29%)
  waiting for transfers between devices  58.7 us (28%)
  starting transfers between devices  44.8 us (21%)
  Pallas kernels  30.7 us (15%)
  other arithmetic  8 us (4%)
  local copies, waits for them, and re-layouts  4.85 us (2%)
    all_to_all x2, blocking collectives, share(): lax.all_to_all(jnp.broadcast_to(value[None], (size,) + value.shape), axes...  37.4 us
    all_to_all x1, blocking collectives, shards(): lax.all_to_all(jnp.broadcast_to(sent[None], (8,) + sent.shape).reshape(8...  24 us
    all_to_all x2, waiting for transfers between devices, shards(): parts = lax.all_to_all(running, COL, 0, 0, tiled=True)  22.5 us
    ppermute x12, starting transfers between devices, swap_cores(): return lax.ppermute(value, 'core', [(0, 1), (1, 0)])  19.5 us
    pallas_call x6, Pallas kernels, build(): pl.pallas_call(functools.partial(build_kernel, first, arrived), out_shape...  17.2 us
    ppermute x3, waiting for transfers between devices, apart(): lax.ppermute(value, ('y', 'core'), [(2 * i + k, 2 * ((i + 1 + 2 * k) % 4)...  13.3 us
    ppermute x1, waiting for transfers between devices, cross(): return lax.ppermute(value, ('zh', 'zl'), [(0, 3), (3, 0), (1, 2), (2, 1)])  12.7 us
    ppermute x2, starting transfers between devices, apart_z(): return lax.ppermute(value, ('zh', 'core', 'zl'), moves)  8.98 us
  transfers between devices with their start and end apart: 22, of which 14 were waited for; matrix products, arithmetic and copies ran while one was open for 4% of the time, Pallas kernels for 6%

profile of v7, /device:TPU:1, one launch (start us, length us, event | category | flops | bytes accessed | tf_op | source)
XLA Modules:
  0.0 210.2 jit_solution(15531110499478855026)
XLA Ops:
  5.7 2.3 %dynamic-slice_bitcast_fusion = bf16[512,1024]{1,0:T(8,128)(2,1)} fusion(bf16[8,512,1024]{2,1,0:T(8,128)(2,1)} %bitcast.51, s32[]{:T(128)S(6)} %select_n.229), kind=kLoop, calls=%fused_computation.1 | loop fusion | bytes 2097156 | tf_op jit(solution)/shard_map/jit(dynamic_index_in_dim)/squeeze | solution.py:477
  7.9 3.8 %collective-permute-start.1 = (bf16[512,1024]{1,0:T(8,128)(2,1)}, bf16[512,1024]{1,0:T(8,128)(2,1)}, u32[]{:S(2)}, u32[]{:S(2)}) collective-permute-start(bf16[512,1024]{1,0:T(8,128)(2,1)} %dynamic-slice_bitcast_fusion), channel_id=1, source_target_pairs={{0,17},{17,0},{1,16},{16,1},{2,19},{19,2},{3,18},{18,3},{4,21},{21... | collective-permute-start | bytes 3145736 | tf_op jit(solution)/shard_map/ppermute | solution.py:424
  11.7 5.1 %multiply_reduce_fusion = f32[4096]{0:T(1024)S(1)} fusion(bf16[4096,1024]{1,0:T(8,128)(2,1)} %param.5), kind=kLoop, calls=%fused_computation | loop fusion | flops 12578816 | bytes 8404992 | tf_op jit(solution)/shard_map/reduce_sum | solution.py:479
  18.6 3.7 %build_tiles.6 = (bf16[24,512,512]{2,1,0:T(8,128)(2,1)}, f32[8,512]{1,0:T(8,128)S(1)}) custom-call(s32[121]{0:T(128)S(1)} %concatenate.13.info, bf16[8,512,1024]{2,1,0:T(8,128)(2,1)} %bitcast.52, f32[8,512]{1,0:T(8,128)S(1)} %mul.144.half_rows, bf16[512,1024]{1,0:T(8,128)(2,1)S(1)} %dynamic-slice_bitcast_fusion.1.refs_0_, ...), custom_call_target="tpu_custom_call" | custom-call | flops 1610612736 | bytes 7864320 | tf_op jit(solution)/shard_map/build_tiles/pallas_call | solution.py:140
  22.3 12.7 %collective-permute-done.1.refs_0_ = bf16[512,1024]{1,0:T(8,128)(2,1)} collective-permute-done((bf16[512,1024]{1,0:T(8,128)(2,1)}, bf16[512,1024]{1,0:T(8,128)(2,1)}, u32[]{:S(2)}, u32[]{:S(2)}) %collective-permute-start.1) | collective-permute-done | bytes 1048608 | tf_op jit(solution)/shard_map/ppermute | solution.py:424
  38.2 2.7 %collective-permute-start.8 = (bf16[512,1024]{1,0:T(8,128)(2,1)S(1)}, bf16[512,1024]{1,0:T(8,128)(2,1)S(1)}, u32[]{:S(2)}, u32[]{:S(2)}) collective-permute-start(bf16[512,1024]{1,0:T(8,128)(2,1)S(1)} %broadcast_select_fusion.1), channel_id=1, source_target_pairs={{0,1},{8,25},{1,16},{9,8},{16,17},{24,9},{17,0},{25,24},{2,3},{10,... | collective-permute-start | bytes 3145736 | tf_op jit(solution)/shard_map/ppermute | solution.py:420
  41.4 4.8 %build_tiles.7 = (bf16[24,512,512]{2,1,0:T(8,128)(2,1)}, f32[8,512]{1,0:T(8,128)S(1)}) custom-call(s32[121]{0:T(128)S(1)} %concatenate.13.info, bf16[8,512,1024]{2,1,0:T(8,128)(2,1)} %bitcast.53, f32[8,512]{1,0:T(8,128)S(1)} %mul.144.half_rows, bf16[512,1024]{1,0:T(8,128)(2,1)} %collective-permute-done.1.refs_0_, ...), custom_call_target="tpu_custom_call", output_to_operand_aliasing={{0}: (9, {})} | custom-call | flops 4831838208 | bytes 23592960 | tf_op jit(solution)/shard_map/build_tiles/pallas_call | solution.py:140
  46.2 4.5 %collective-permute-done.7.refs_0_ = bf16[512,1024]{1,0:T(8,128)(2,1)S(1)} collective-permute-done((bf16[512,1024]{1,0:T(8,128)(2,1)}, bf16[512,1024]{1,0:T(8,128)(2,1)S(1)}, u32[]{:S(2)}, u32[]{:S(2)}) %collective-permute-start.7) | collective-permute-done | bytes 1048608 | tf_op jit(solution)/shard_map/ppermute | solution.py:407
  50.8 1.9 collective-permute-done.8
  53.6 6.2 %collective-permute-start.11 = (bf16[512,1024]{1,0:T(8,128)(2,1)S(1)}, bf16[512,1024]{1,0:T(8,128)(2,1)S(1)}, u32[]{:S(2)}, u32[]{:S(2)}) collective-permute-start(bf16[512,1024]{1,0:T(8,128)(2,1)S(1)} %collective-permute-done.8), channel_id=1, source_target_pairs={{0,1},{8,25},{1,16},{9,8},{16,17},{24,9},{17,0},{25,24},{2,3},{10,... | collective-permute-start | bytes 3145736 | tf_op jit(solution)/shard_map/ppermute | solution.py:420
  59.9 3.6 %build_tiles.8 = (bf16[24,512,512]{2,1,0:T(8,128)(2,1)}, f32[8,512]{1,0:T(8,128)S(1)}) custom-call(s32[121]{0:T(128)S(1)} %concatenate.13.info, bf16[8,512,1024]{2,1,0:T(8,128)(2,1)} %bitcast.54, f32[8,512]{1,0:T(8,128)S(1)} %mul.144.half_rows, bf16[512,1024]{1,0:T(8,128)(2,1)S(1)} %collective-permute-done.7.refs_0_, ...), custom_call_target="tpu_custom_call", output_to_operand_aliasing={{0}: (4, {})} | custom-call | flops 536870912 | bytes 2621440 | tf_op jit(solution)/shard_map/build_tiles/pallas_call | solution.py:140
  63.6 3.3 %collective-permute-done.10.refs_1_ = bf16[512,1024]{1,0:T(8,128)(2,1)S(1)} collective-permute-done((bf16[512,1024]{1,0:T(8,128)(2,1)S(1)}, bf16[512,1024]{1,0:T(8,128)(2,1)S(1)}, u32[]{:S(2)}, u32[]{:S(2)}) %collective-permute-start.10) | collective-permute-done | bytes 1048608 | tf_op jit(solution)/shard_map/ppermute | solution.py:407
  66.8 2.8 %collective-permute-start.14 = (bf16[512,1024]{1,0:T(8,128)(2,1)S(1)}, bf16[512,1024]{1,0:T(8,128)(2,1)S(1)}, u32[]{:S(2)}, u32[]{:S(2)}) collective-permute-start(bf16[512,1024]{1,0:T(8,128)(2,1)S(1)} %collective-permute-done.10.refs_1_), channel_id=1, source_target_pairs={{0,8},{8,0},{1,9},{9,1},{2,10},{10,2},{3,11},{11,3},{4,12},{12,4},... | collective-permute-start | bytes 3145736 | tf_op jit(solution)/shard_map/ppermute | solution.py:372
  69.6 2.0 collective-permute-done.11.refs_2_
  72.5 5.6 %collective-permute-done.12.refs_2_ = bf16[512,1024]{1,0:T(8,128)(2,1)S(1)} collective-permute-done((bf16[512,1024]{1,0:T(8,128)(2,1)S(1)}, bf16[512,1024]{1,0:T(8,128)(2,1)S(1)}, u32[]{:S(2)}, u32[]{:S(2)}) %collective-permute-start.12) | collective-permute-done | bytes 1048608 | tf_op jit(solution)/shard_map/ppermute | solution.py:407
  78.1 2.8 %collective-permute-start.13 = (bf16[512,1024]{1,0:T(8,128)(2,1)S(1)}, bf16[512,1024]{1,0:T(8,128)(2,1)S(1)}, u32[]{:S(2)}, u32[]{:S(2)}) collective-permute-start(bf16[512,1024]{1,0:T(8,128)(2,1)S(1)} %collective-permute-done.12.refs_2_), channel_id=1, source_target_pairs={{0,8},{8,0},{1,9},{9,1},{2,10},{10,2},{3,11},{11,3},{4,12},{12,4},... | collective-permute-start | bytes 3145736 | tf_op jit(solution)/shard_map/ppermute | solution.py:372
  83.1 3.6 %build_tiles.11 = (bf16[24,512,512]{2,1,0:T(8,128)(2,1)}, f32[8,512]{1,0:T(8,128)S(1)}) custom-call(s32[121]{0:T(128)S(1)} %concatenate.13.info, bf16[8,512,1024]{2,1,0:T(8,128)(2,1)} %bitcast.57, f32[8,512]{1,0:T(8,128)S(1)} %mul.144.half_rows, bf16[512,1024]{1,0:T(8,128)(2,1)S(1)} %collective-permute-done.13.refs_0_, ...), custom_call_target="tpu_custom_call", output_to_operand_aliasing={{0}: (4, {})} | custom-call | flops 536870912 | bytes 2621440 | tf_op jit(solution)/shard_map/build_tiles/pallas_call | solution.py:140
  88.2 24.0 %all_to_all.25 = f32[64,3,512]{2,1,0:T(4,128)S(1)} all-to-all(f32[64,3,512]{2,1,0:T(4,128)S(1)} %bitcast.58), channel_id=1, replica_groups=mesh['y'=4,'zh'=2,'core'=2,'x'=4,'zl'=2] {'y','zh','x','zl'}, dimensions={0} | all-to-all | bytes 786432 | tf_op jit(solution)/shard_map/all_to_all | solution.py:518
  112.3 5.2 %collective-permute-start.16 = (f32[8,3,512]{2,1,0:T(4,128)S(1)}, f32[8,3,512]{2,1,0:T(4,128)S(1)}, u32[]{:S(2)}, u32[]{:S(2)}) collective-permute-start(f32[8,3,512]{2,1,0:T(4,128)S(1)} %bitcast_reduce_fusion), channel_id=1, source_target_pairs={{0,8},{8,0},{1,9},{9,1},{2,10},{10,2},{3,11},{11,3},{4,12},{12,4},... | collective-permute-start | bytes 147464 | tf_op jit(solution)/shard_map/ppermute | solution.py:372
  120.0 3.7 %product.2 = bf16[8,64,512]{2,1,0:T(8,128)(2,1)} custom-call(s32[121]{0:T(128)S(1)} %concatenate.13.info, bf16[24,512,512]{2,1,0:T(8,128)(2,1)} %get-tuple-element.59.tiles, s32[16,512]{1,0:T(8,128)S(1)} %get-tuple-element.68.refs_0_, f32[16,512]{1,0:T(8,128)S(1)} %get-tuple-element.67.refs_1_, f32[8,512]{1,0:T(8,128)S(1)} %get-tuple-element.60.refs_2_, ...), custom_call_target="tpu_custom_call" | custom-call | tf_op jit(solution)/shard_map/product/pallas_call | solution.py:250
  123.8 3.5 %all-to-all-start.1 = ((bf16[8,64,512]{2,1,0:T(8,128)(2,1)}), bf16[8,64,512]{2,1,0:T(8,128)(2,1)S(1)}, u32[]{:S(2)}, u32[]{:S(2)}) async-start(bf16[8,64,512]{2,1,0:T(8,128)(2,1)} %product.2), calls=%async_computation.1 | async-start | bytes 1048576 | tf_op jit(solution)/shard_map/all_to_all | solution.py:536
  127.3 9.1 %all-to-all-done.1.parts = bf16[8,64,512]{2,1,0:T(8,128)(2,1)S(1)} async-done(((bf16[8,64,512]{2,1,0:T(8,128)(2,1)}), bf16[8,64,512]{2,1,0:T(8,128)(2,1)S(1)}, u32[]{:S(2)}, u32[]{:S(2)}) %all-to-all-start.1) | async-done | bytes 524320 | tf_op jit(solution)/shard_map/all_to_all | solution.py:536
  137.0 18.0 %all_to_all.26.refs_0_ = bf16[8,96,512]{2,1,0:T(8,128)(2,1)S(1)} all-to-all(bf16[8,96,512]{2,1,0:T(8,128)(2,1)S(1)} %broadcast_in_dim.142), channel_id=1, replica_groups=mesh['y'=4,'zh'=2,'core'=2,'x'=4,'zl'=2] {'y','zh'}, dimensions={0} | all-to-all | bytes 1572864 | tf_op jit(solution)/shard_map/all_to_all | solution.py:377
  154.9 2.7 %collective-permute-start.17 = (bf16[8,96,512]{2,1,0:T(8,128)(2,1)S(1)}, bf16[8,96,512]{2,1,0:T(8,128)(2,1)S(1)}, u32[]{:S(2)}, u32[]{:S(2)}) collective-permute-start(bf16[8,96,512]{2,1,0:T(8,128)(2,1)S(1)} %all_to_all.26.refs_0_), channel_id=1, source_target_pairs={{0,8},{8,0},{1,9},{9,1},{2,10},{10,2},{3,11},{11,3},{4,12},{12,4},... | collective-permute-start | bytes 2359304 | tf_op jit(solution)/shard_map/ppermute | solution.py:372
  157.6 1.9 collective-permute-done.17.refs_1_
  159.5 3.7 %product.3 = bf16[8,96,512]{2,1,0:T(8,128)(2,1)} custom-call(s32[121]{0:T(128)S(1)} %concatenate.13.info, bf16[24,512,512]{2,1,0:T(8,128)(2,1)} %get-tuple-element.59.tiles, bf16[8,96,512]{2,1,0:T(8,128)(2,1)S(1)} %all_to_all.26.refs_0_, bf16[8,96,512]{2,1,0:T(8,128)(2,1)S(1)} %collective-permute-done.17.refs_1_), custom_call_target="tpu_custom_call" | custom-call | tf_op jit(solution)/shard_map/product/pallas_call | solution.py:250
  163.3 3.8 %all-to-all-start.3 = ((bf16[8,96,512]{2,1,0:T(8,128)(2,1)}), bf16[8,96,512]{2,1,0:T(8,128)(2,1)S(1)}, u32[]{:S(2)}, u32[]{:S(2)}) async-start(bf16[8,96,512]{2,1,0:T(8,128)(2,1)} %product.3), calls=%async_computation.3 | async-start | bytes 1572864 | tf_op jit(solution)/shard_map/all_to_all | solution.py:541
  167.1 13.3 %all-to-all-done.3.parts = bf16[8,96,512]{2,1,0:T(8,128)(2,1)S(1)} async-done(((bf16[8,96,512]{2,1,0:T(8,128)(2,1)}), bf16[8,96,512]{2,1,0:T(8,128)(2,1)S(1)}, u32[]{:S(2)}, u32[]{:S(2)}) %all-to-all-start.3) | async-done | bytes 786464 | tf_op jit(solution)/shard_map/all_to_all | solution.py:541
  180.4 2.7 %middle.1 = (f32[64,512]{1,0:T(8,128)S(1)}, f32[32,128]{1,0:T(8,128)S(1)}) custom-call(bf16[8,96,512]{2,1,0:T(8,128)(2,1)S(1)} %all-to-all-done.3.parts, f32[1,512]{1,0:T(1,128)S(1)} %get-tuple-element.70.inv_root, f32[1,512]{1,0:T(1,128)S(1)} %get-tuple-element.69.root), custom_call_target="tpu_custom_call" | custom-call | tf_op jit(solution)/shard_map/middle/pallas_call | solution.py:361
  184.9 19.5 %all_to_all.27 = f32[64,16,128]{2,1,0:T(8,128)S(1)} all-to-all(f32[64,16,128]{2,1,0:T(8,128)S(1)} %broadcast_in_dim.143), channel_id=1, replica_groups=mesh['y'=4,'zh'=2,'core'=2,'x'=4,'zl'=2] {'y','zh','x','zl'}, dimensions={0} | all-to-all | bytes 1048576 | tf_op jit(solution)/shard_map/all_to_all | solution.py:377
  204.5 2.0 collective-permute-start.19
  207.3 2.9 %last.1 = f32[64,512]{1,0:T(8,128)} custom-call(f32[32,128]{1,0:T(8,128)S(1)} %pad_maximum_fusion.1.message, f32[64,512]{1,0:T(8,128)S(1)} %get-tuple-element.62.image, f32[1,512]{1,0:T(1,128)S(1)} %get-tuple-element.69.root), custom_call_target="tpu_custom_call" | custom-call | tf_op jit(solution)/shard_map/last/pallas_call | solution.py:361
  (82 shorter events, 21.1 us)
Async XLA Ops:
  0.0 17.6 %copy-start.1 = (s32[1,1,24]{2,1,0:T(1,128)S(1)}, s32[1,1,24]{2,1,0:T(1,128)}, u32[]{:S(2)}) copy-start(s32[1,1,24]{2,1,0:T(1,128)} %param.8) | copy-start | bytes 292
  0.0 17.9 %copy-start.2 = (s32[1,1,24]{2,1,0:T(1,128)S(1)}, s32[1,1,24]{2,1,0:T(1,128)}, u32[]{:S(2)}) copy-start(s32[1,1,24]{2,1,0:T(1,128)} %param.7) | copy-start | bytes 292
  1.3 17.3 %collective-permute-start = (bf16[512,1024]{1,0:T(8,128)(2,1)S(1)}, bf16[512,1024]{1,0:T(8,128)(2,1)}, u32[]{:S(2)}, u32[]{:S(2)}) collective-permute-start(bf16[512,1024]{1,0:T(8,128)(2,1)S(1)} %dynamic-slice_bitcast_fusion.1.refs_0_), channel_id=1, source_target_pairs={{0,8},{8,0},{1,9},{9,1},{2,10},{10,2},{3,11},{11,3},{4,12},{12,4},... | collective-permute-start | bytes 3145736 | tf_op jit(solution)/shard_map/ppermute | solution.py:372
  2.8 32.1 %collective-permute-start.2 = (bf16[512,1024]{1,0:T(8,128)(2,1)S(1)}, bf16[512,1024]{1,0:T(8,128)(2,1)S(1)}, u32[]{:S(2)}, u32[]{:S(2)}) collective-permute-start(bf16[512,1024]{1,0:T(8,128)(2,1)S(1)} %dynamic-slice_bitcast_fusion.1.refs_0_), channel_id=1, source_target_pairs={{0,32},{32,64},{64,96},{96,0},{1,33},{33,65},{65,97},{97,1},{2,34}... | collective-permute-start | bytes 3145736 | tf_op jit(solution)/shard_map/ppermute | solution.py:399
  4.2 30.8 %collective-permute-start.3 = (bf16[512,1024]{1,0:T(8,128)(2,1)S(1)}, bf16[512,1024]{1,0:T(8,128)(2,1)S(1)}, u32[]{:S(2)}, u32[]{:S(2)}) collective-permute-start(bf16[512,1024]{1,0:T(8,128)(2,1)S(1)} %dynamic-slice_bitcast_fusion.1.refs_0_), channel_id=1, source_target_pairs={{0,96},{32,0},{64,32},{96,64},{1,97},{33,1},{65,33},{97,65},{2,98}... | collective-permute-start | bytes 3145736 | tf_op jit(solution)/shard_map/ppermute | solution.py:403
  7.9 27.1 %collective-permute-start.1 = (bf16[512,1024]{1,0:T(8,128)(2,1)}, bf16[512,1024]{1,0:T(8,128)(2,1)}, u32[]{:S(2)}, u32[]{:S(2)}) collective-permute-start(bf16[512,1024]{1,0:T(8,128)(2,1)} %dynamic-slice_bitcast_fusion), channel_id=1, source_target_pairs={{0,17},{17,0},{1,16},{16,1},{2,19},{19,2},{3,18},{18,3},{4,21},{21... | collective-permute-start | bytes 3145736 | tf_op jit(solution)/shard_map/ppermute | solution.py:424
  35.0 6.0 %collective-permute-start.4 = (bf16[512,1024]{1,0:T(8,128)(2,1)}, bf16[512,1024]{1,0:T(8,128)(2,1)S(1)}, u32[]{:S(2)}, u32[]{:S(2)}) collective-permute-start(bf16[512,1024]{1,0:T(8,128)(2,1)} %collective-permute-done.1.refs_0_), channel_id=1, source_target_pairs={{0,8},{8,0},{1,9},{9,1},{2,10},{10,2},{3,11},{11,3},{4,12},{12,4},... | collective-permute-start | bytes 3145736 | tf_op jit(solution)/shard_map/ppermute | solution.py:372
  36.1 4.9 %collective-permute-start.5 = (bf16[512,1024]{1,0:T(8,128)(2,1)S(1)}, bf16[512,1024]{1,0:T(8,128)(2,1)S(1)}, u32[]{:S(2)}, u32[]{:S(2)}) collective-permute-start(bf16[512,1024]{1,0:T(8,128)(2,1)S(1)} %collective-permute-done.2.refs_2_), channel_id=1, source_target_pairs={{0,8},{8,0},{1,9},{9,1},{2,10},{10,2},{3,11},{11,3},{4,12},{12,4},... | collective-permute-start | bytes 3145736 | tf_op jit(solution)/shard_map/ppermute | solution.py:372
  36.2 5.2 %collective-permute-start.6 = (bf16[512,1024]{1,0:T(8,128)(2,1)S(1)}, bf16[512,1024]{1,0:T(8,128)(2,1)S(1)}, u32[]{:S(2)}, u32[]{:S(2)}) collective-permute-start(bf16[512,1024]{1,0:T(8,128)(2,1)S(1)} %collective-permute-done.3.refs_4_), channel_id=1, source_target_pairs={{0,8},{8,0},{1,9},{9,1},{2,10},{10,2},{3,11},{11,3},{4,12},{12,4},... | collective-permute-start | bytes 3145736 | tf_op jit(solution)/shard_map/ppermute | solution.py:372
  36.6 14.2 %collective-permute-start.7 = (bf16[512,1024]{1,0:T(8,128)(2,1)}, bf16[512,1024]{1,0:T(8,128)(2,1)S(1)}, u32[]{:S(2)}, u32[]{:S(2)}) collective-permute-start(bf16[512,1024]{1,0:T(8,128)(2,1)} %collective-permute-done.1.refs_0_), channel_id=1, source_target_pairs={{0,32},{8,104},{32,64},{40,8},{64,96},{72,40},{96,0},{104,72},{1,3... | collective-permute-start | bytes 3145736 | tf_op jit(solution)/shard_map/ppermute | solution.py:407
  38.2 14.5 %collective-permute-start.8 = (bf16[512,1024]{1,0:T(8,128)(2,1)S(1)}, bf16[512,1024]{1,0:T(8,128)(2,1)S(1)}, u32[]{:S(2)}, u32[]{:S(2)}) collective-permute-start(bf16[512,1024]{1,0:T(8,128)(2,1)S(1)} %broadcast_select_fusion.1), channel_id=1, source_target_pairs={{0,1},{8,25},{1,16},{9,8},{16,17},{24,9},{17,0},{25,24},{2,3},{10,... | collective-permute-start | bytes 3145736 | tf_op jit(solution)/shard_map/ppermute | solution.py:420
  52.8 14.0 %collective-permute-start.10 = (bf16[512,1024]{1,0:T(8,128)(2,1)S(1)}, bf16[512,1024]{1,0:T(8,128)(2,1)S(1)}, u32[]{:S(2)}, u32[]{:S(2)}) collective-permute-start(bf16[512,1024]{1,0:T(8,128)(2,1)S(1)} %broadcast_select_fusion), channel_id=1, source_target_pairs={{0,32},{8,104},{32,64},{40,8},{64,96},{72,40},{96,0},{104,72},{1,3... | collective-permute-start | bytes 3145736 | tf_op jit(solution)/shard_map/ppermute | solution.py:407
  53.6 18.0 %collective-permute-start.11 = (bf16[512,1024]{1,0:T(8,128)(2,1)S(1)}, bf16[512,1024]{1,0:T(8,128)(2,1)S(1)}, u32[]{:S(2)}, u32[]{:S(2)}) collective-permute-start(bf16[512,1024]{1,0:T(8,128)(2,1)S(1)} %collective-permute-done.8), channel_id=1, source_target_pairs={{0,1},{8,25},{1,16},{9,8},{16,17},{24,9},{17,0},{25,24},{2,3},{10,... | collective-permute-start | bytes 3145736 | tf_op jit(solution)/shard_map/ppermute | solution.py:420
  59.9 11.8 %collective-permute-start.9 = (bf16[512,1024]{1,0:T(8,128)(2,1)S(1)}, bf16[512,1024]{1,0:T(8,128)(2,1)S(1)}, u32[]{:S(2)}, u32[]{:S(2)}) collective-permute-start(bf16[512,1024]{1,0:T(8,128)(2,1)S(1)} %collective-permute-done.7.refs_0_), channel_id=1, source_target_pairs={{0,8},{8,0},{1,9},{9,1},{2,10},{10,2},{3,11},{11,3},{4,12},{12,4},... | collective-permute-start | bytes 3145736 | tf_op jit(solution)/shard_map/ppermute | solution.py:372
  63.5 17.4 %copy-start = (s32[512]{0:T(512)S(1)}, s32[512]{0:T(512)}, u32[]{:S(2)}) copy-start(s32[512]{0:T(512)} %param.6) | copy-start | bytes 6148
  63.5 14.6 %collective-permute-start.12 = (bf16[512,1024]{1,0:T(8,128)(2,1)S(1)}, bf16[512,1024]{1,0:T(8,128)(2,1)S(1)}, u32[]{:S(2)}, u32[]{:S(2)}) collective-permute-start(bf16[512,1024]{1,0:T(8,128)(2,1)S(1)} %collective-permute-done.7.refs_0_), channel_id=1, source_target_pairs={{0,32},{8,104},{32,64},{40,8},{64,96},{72,40},{96,0},{104,72},{1,3... | collective-permute-start | bytes 3145736 | tf_op jit(solution)/shard_map/ppermute | solution.py:407
  66.8 14.2 %collective-permute-start.14 = (bf16[512,1024]{1,0:T(8,128)(2,1)S(1)}, bf16[512,1024]{1,0:T(8,128)(2,1)S(1)}, u32[]{:S(2)}, u32[]{:S(2)}) collective-permute-start(bf16[512,1024]{1,0:T(8,128)(2,1)S(1)} %collective-permute-done.10.refs_1_), channel_id=1, source_target_pairs={{0,8},{8,0},{1,9},{9,1},{2,10},{10,2},{3,11},{11,3},{4,12},{12,4},... | collective-permute-start | bytes 3145736 | tf_op jit(solution)/shard_map/ppermute | solution.py:372
  71.6 9.4 %collective-permute-start.15 = (bf16[512,1024]{1,0:T(8,128)(2,1)S(1)}, bf16[512,1024]{1,0:T(8,128)(2,1)S(1)}, u32[]{:S(2)}, u32[]{:S(2)}) collective-permute-start(bf16[512,1024]{1,0:T(8,128)(2,1)S(1)} %collective-permute-done.11.refs_2_), channel_id=1, source_target_pairs={{0,8},{8,0},{1,9},{9,1},{2,10},{10,2},{3,11},{11,3},{4,12},{12,4},... | collective-permute-start | bytes 3145736 | tf_op jit(solution)/shard_map/ppermute | solution.py:372
  78.1 5.1 %collective-permute-start.13 = (bf16[512,1024]{1,0:T(8,128)(2,1)S(1)}, bf16[512,1024]{1,0:T(8,128)(2,1)S(1)}, u32[]{:S(2)}, u32[]{:S(2)}) collective-permute-start(bf16[512,1024]{1,0:T(8,128)(2,1)S(1)} %collective-permute-done.12.refs_2_), channel_id=1, source_target_pairs={{0,8},{8,0},{1,9},{9,1},{2,10},{10,2},{3,11},{11,3},{4,12},{12,4},... | collective-permute-start | bytes 3145736 | tf_op jit(solution)/shard_map/ppermute | solution.py:372
  112.3 6.1 %collective-permute-start.16 = (f32[8,3,512]{2,1,0:T(4,128)S(1)}, f32[8,3,512]{2,1,0:T(4,128)S(1)}, u32[]{:S(2)}, u32[]{:S(2)}) collective-permute-start(f32[8,3,512]{2,1,0:T(4,128)S(1)} %bitcast_reduce_fusion), channel_id=1, source_target_pairs={{0,8},{8,0},{1,9},{9,1},{2,10},{10,2},{3,11},{11,3},{4,12},{12,4},... | collective-permute-start | bytes 147464 | tf_op jit(solution)/shard_map/ppermute | solution.py:372
  123.8 12.7 %all-to-all-start.1 = ((bf16[8,64,512]{2,1,0:T(8,128)(2,1)}), bf16[8,64,512]{2,1,0:T(8,128)(2,1)S(1)}, u32[]{:S(2)}, u32[]{:S(2)}) async-start(bf16[8,64,512]{2,1,0:T(8,128)(2,1)} %product.2), calls=%async_computation.1 | async-start | bytes 1048576 | tf_op jit(solution)/shard_map/all_to_all | solution.py:536
  154.9 4.6 %collective-permute-start.17 = (bf16[8,96,512]{2,1,0:T(8,128)(2,1)S(1)}, bf16[8,96,512]{2,1,0:T(8,128)(2,1)S(1)}, u32[]{:S(2)}, u32[]{:S(2)}) collective-permute-start(bf16[8,96,512]{2,1,0:T(8,128)(2,1)S(1)} %all_to_all.26.refs_0_), channel_id=1, source_target_pairs={{0,8},{8,0},{1,9},{9,1},{2,10},{10,2},{3,11},{11,3},{4,12},{12,4},... | collective-permute-start | bytes 2359304 | tf_op jit(solution)/shard_map/ppermute | solution.py:372
  163.3 17.1 %all-to-all-start.3 = ((bf16[8,96,512]{2,1,0:T(8,128)(2,1)}), bf16[8,96,512]{2,1,0:T(8,128)(2,1)S(1)}, u32[]{:S(2)}, u32[]{:S(2)}) async-start(bf16[8,96,512]{2,1,0:T(8,128)(2,1)} %product.3), calls=%async_computation.3 | async-start | bytes 1572864 | tf_op jit(solution)/shard_map/all_to_all | solution.py:541
  183.2 1.7 collective-permute-start.18
  204.5 2.8 %collective-permute-start.19 = (f32[16,128]{1,0:T(8,128)S(1)}, f32[16,128]{1,0:T(8,128)S(1)}, u32[]{:S(2)}, u32[]{:S(2)}) collective-permute-start(f32[16,128]{1,0:T(8,128)S(1)} %reduce_sum.139), channel_id=1, source_target_pairs={{0,8},{8,0},{1,9},{9,1},{2,10},{10,2},{3,11},{11,3},{4,12},{12,4},... | collective-permute-start | bytes 24584 | tf_op jit(solution)/shard_map/ppermute | solution.py:372

commit v8 on v7

--- a/solution.py
+++ b/solution.py
@@ -170,28 +170,29 @@
     high = value.astype(BF16).astype(F32)
     middle = (value - high).astype(BF16).astype(F32)
     low = (value - high) - middle
-    return jnp.concatenate([high, middle, low, jnp.zeros_like(low)], axis=0).astype(BF16)
-
-
-def sum_of(terms):
-    total = jnp.sum(terms.astype(F32), axis=0)
-    return total[:8] + (total[8:16] + total[16:24])
+    wide = jnp.concatenate([high, middle, low, jnp.zeros((32, 16), F32)], axis=1)
+    return jnp.concatenate([wide[:16], wide[16:]], axis=1).astype(BF16)
+
+
+def value_of(terms):
+    wide = jnp.concatenate([terms[:, :256], terms[:, 256:]], axis=0)
+    return wide[:, :80] + (wide[:, 80:160] + wide[:, 160:240])
+
+
+def lead_of(sums):
+    total = sums[:1, 67:68]
+    return jnp.concatenate([sums[:, 65:66], sums[:, 66:67]], axis=0) / total, total
 
 
 def product_kernel(first, info, tiles, *refs):
     if first:
-        labels, inv_root, degree, shift, out, running, held, sem = refs
+        labels, mine, others, out, running, held, sem = refs
     else:
-        mine, others, out, running, held, sem = refs
-    count, core = info[0], info[2]
+        mine, others, degree, out, running, held, sem = refs
+    count = info[0]
+    core, zh, y = info[2], info[3], info[4]
     depth = held.shape[0]
     running[...] = jnp.zeros_like(running)
-    if not first:
-        rest = jnp.zeros((8, TILE), F32)
-        for known in (mine, others):
-            rest = rest + sum_of(known[:, K:, :])
-        for t in range(SLAB_TILES):
-            out[t, K:, :] = terms_of(rest)
 
     def fetch(entry):
         slot = lax.rem(entry, depth)
@@ -199,13 +200,17 @@
 
     def piece(entry):
         q = info[SLABS + entry]
+        own = q % 2 == core
         if first:
-            value = inv_root[pl.ds(q, 1), :]
-            label = labels[pl.ds(q, 1), :]
+            index = (q % 2 ^ core) * 8 + ((q // 4 + 4 - y) % 4) * 2 + (q // 2 % 2 ^ zh)
+            label = labels[pl.ds(index, 1), :]
+            chip = pl.ds(q // 2, 1)
+            value = lax.rsqrt(jnp.where(own, mine[chip, :], others[chip, :]))
             value = jnp.where(label < K, value, -value)
-            same = (label & (K - 1)) == lax.broadcasted_iota(jnp.int32, (K, TILE), 0)
+            label = jnp.where(label < K, label, label - K)
+            same = label == lax.broadcasted_iota(jnp.int32, (K, TILE), 0).astype(F32)
             return jnp.where(same, jnp.broadcast_to(value, (K, TILE)), 0.0).astype(BF16)
-        return jnp.where(q % 2 == core, mine[q // 2, :K, :], others[q // 2, :K, :])
+        return jnp.where(own, mine[q // 2, :K, :], others[q // 2, :K, :])
 
     def term(entry):
         return jnp.dot(piece(entry), held[lax.rem(entry, depth)], preferred_element_type=F32)
@@ -237,20 +242,25 @@
         return carry
 
     lax.fori_loop(0, (count + 1) // 2, step, 0)
-    for t in range(SLAB_TILES):
-        total = running[t]
-        if first:
-            total = total - shift[...] * degree[t : t + 1, :]
-        out[t, :K, :] = total.astype(BF16)
+    if first:
+        out[...] = running[...].astype(BF16)
+    else:
+        sums = jnp.sum(mine[:, K:, :].astype(F32), axis=0) + jnp.sum(others[:, K:, :].astype(F32), axis=0)
+        sums = value_of(sums)
+        lead, _ = lead_of(sums)
+        terms = terms_of(sums)
+        for t in range(SLAB_TILES):
+            out[t, :K, :] = (running[t] - lead * degree[t : t + 1, :]).astype(BF16)
+            out[t, K:, :] = terms
 
 
 def product(info, tiles, *operands):
     vmem = pl.BlockSpec(memory_space=pltpu.VMEM)
-    first = operands[0].dtype == jnp.int32
+    first = operands[0].dtype == F32
     return pl.pallas_call(
         functools.partial(product_kernel, first),
         out_shape=jax.ShapeDtypeStruct(
-            (SLAB_TILES, K if first else K + 32, TILE), BF16
+            (SLAB_TILES, K if first else K + 16, TILE), BF16
         ),
         in_specs=[
             pl.BlockSpec(memory_space=pltpu.SMEM),
@@ -278,14 +288,18 @@
         preferred_element_type=F32,
     )
     half = K // 2
+    rows = lax.broadcasted_iota(jnp.int32, (half, half), 0)
+    columns = lax.broadcasted_iota(jnp.int32, (half, half), 1)
+    corner = weights[half:K, half:K]
     return jnp.concatenate(
         [
-            weights[:half, :half],
             weights[half:K, :half],
-            weights[half:K, half:K],
-            weights[:half, K : K + 8],
-            weights[half:K, K : K + 8],
-            jnp.broadcast_to(weights[K : K + 1, K : K + 1], (half, 16)),
+            jnp.where(rows >= columns, weights[:half, :half], corner),
+            jnp.sum(jnp.where(rows == columns, corner, 0.0), axis=1, keepdims=True),
+            weights[:half, K : K + 1],
+            weights[half:K, K : K + 1],
+            jnp.broadcast_to(weights[K : K + 1, K : K + 1], (half, 1)),
+            jnp.zeros((half, 12), F32),
         ],
         axis=1,
     )
@@ -293,20 +307,22 @@
 
 def factor_of(sums, scale):
     half = K // 2
-    lower = sums[:, half : 2 * half]
+    rows = lax.broadcasted_iota(jnp.int32, (half, half), 0)
+    columns = lax.broadcasted_iota(jnp.int32, (half, half), 1)
+    lower, mixed = sums[:, :half], sums[:, half:K]
+    strict = jnp.where(rows > columns, mixed, 0.0)
+    upper = jnp.where(rows < columns, mixed, 0.0)
+    diagonal = rows == columns
+    left = strict + strict.T + jnp.where(diagonal, mixed, 0.0)
+    right = upper + upper.T + jnp.where(diagonal, sums[:, K : K + 1], 0.0)
     gram = jnp.concatenate(
-        [
-            jnp.concatenate([sums[:, :half], lower.T], axis=1),
-            jnp.concatenate([lower, sums[:, 2 * half : 3 * half]], axis=1),
-        ],
-        axis=0,
-    )
-    top = jnp.concatenate([sums[:, 96:97], sums[:, 104:105]], axis=0)
-    total = sums[:1, 112:113]
+        [jnp.concatenate([left, lower.T], axis=1), jnp.concatenate([lower, right], axis=1)], axis=0
+    )
+    lead, total = lead_of(sums)
     rows = lax.broadcasted_iota(jnp.int32, (K, K), 0)
     columns = lax.broadcasted_iota(jnp.int32, (K, K), 1)
-    across = jnp.sum(jnp.where(rows == columns, top, 0.0), axis=0, keepdims=True)
-    gram = (gram - top * across / total) * scale
+    across = jnp.sum(jnp.where(rows == columns, lead, 0.0), axis=0, keepdims=True)
+    gram = (gram - lead * across * total) * scale
     work = jnp.concatenate([gram, (rows == columns).astype(F32)], axis=1)
     index = lax.broadcasted_iota(jnp.int32, (K, 2 * K), 0)
     pivots = jnp.ones((K, 2 * K), F32)
@@ -326,46 +342,55 @@
                 spread[b] = spread[b] - ratio * spread[b][a : a + 1, :]
         work = jnp.concatenate([work[:start], rest], axis=0) if start else rest
         pivots = jnp.concatenate([pivots[:start], below], axis=0) if start else below
-    return work[:, K:] * lax.rsqrt(pivots[:, K:]), top / total
+    return work[:, K:] * lax.rsqrt(pivots[:, K:]), lead
 
 
 def times(factor, block):
     return jnp.dot(factor, block, precision=lax.Precision.HIGHEST, preferred_element_type=F32)
 
 
-def weigh_kernel(parts, inv_root, root, out):
-    image = jnp.sum(parts[...].astype(F32), axis=0) * inv_root[...]
-    out[:K, :] = (image * inv_root[...]).astype(BF16)
-    packed = weights_of(image, root[...])
-    sums = jnp.concatenate([packed[8 * i : 8 * i + 8] for i in range(4)], axis=1)
-    out[K:, :] = terms_of(sums)
-
-
-def middle_kernel(scale, parts, inv_root, root, image, message):
-    sums = sum_of(parts[:, K:, :])
-    packed = jnp.concatenate([sums[:, 128 * i : 128 * i + 128] for i in range(4)], axis=0)
-    factor, lead = factor_of(packed, scale)
+def roots_of(info, degrees):
+    degree = degrees[pl.ds(info[5], 1), :]
+    return lax.rsqrt(degree), jnp.sqrt(degree)
+
+
+def weigh_kernel(info, parts, degrees, out):
+    inv_root, root = roots_of(info, degrees)
+    image = jnp.sum(parts[...].astype(F32), axis=0) * inv_root
+    out[:K, :] = (image * inv_root).astype(BF16)
+    out[K:, :] = terms_of(weights_of(image, root))
+
+
+def middle_kernel(scale, info, parts, degrees, by_column, image, message):
+    inv_root, root = roots_of(info, degrees)
+    own = by_column[info[5]]
+    columns = [value_of(parts[c, K:, :].astype(F32)) for c in range(SLAB_TILES)]
+    factor, lead = factor_of(sum(columns), scale)
     whole = jnp.sum(parts[:, :K, :].astype(F32), axis=0)
-    block = times(factor, whole * inv_root[...] - lead * root[...])
+    for c in range(SLAB_TILES):
+        whole = whole + (lead_of(columns[c])[0] - lead) * own[c : c + 1, :]
+    block = times(factor, whole * inv_root)
     image[...] = block
-    message[...] = weights_of(block, root[...])
-
-
-def last_kernel(scale, message, image, root, out):
-    factor, lead = factor_of(message[...], scale)
-    out[...] = times(factor, image[...] - lead * root[...])
-
-
-def local(kernel, name, out_shape, *operands):
+    message[:, :80] = weights_of(block, root)
+    message[:, 80:] = jnp.zeros((K // 2, 48), F32)
+
+
+def last_kernel(scale, info, message, image, degrees, out):
+    _, root = roots_of(info, degrees)
+    factor, lead = factor_of(message[:, :80], scale)
+    out[...] = times(factor, image[...] - lead * root)
+
+
+def local(kernel, name, out_shape, info, *operands):
     vmem = pl.BlockSpec(memory_space=pltpu.VMEM)
     return pl.pallas_call(
         kernel,
         out_shape=out_shape,
-        in_specs=[vmem] * len(operands),
+        in_specs=[pl.BlockSpec(memory_space=pltpu.SMEM)] + [vmem] * len(operands),
         out_specs=jax.tree.map(lambda _: vmem, out_shape),
         compiler_params=pltpu.CompilerParams(vmem_limit_bytes=VMEM_LIMIT),
         name=name,
-    )(*operands)
+    )(info, *operands)
 
 
 def swap_cores(value):
@@ -424,7 +449,8 @@
     return lax.ppermute(value, ("zh", "zl"), [(0, 3), (3, 0), (1, 2), (2, 1)])
 
 
-def pair_list(count, block_index, core, rows, slabs, arrivals):
+def pair_list(head, rows, slabs, arrivals):
+    count = head[0]
     slot = jnp.arange(PAIRS, dtype=jnp.int32)
     rank = jnp.sum(
         jnp.where(slabs[:, None] == arrivals[None, :], jnp.arange(BLOCK_TILES, dtype=jnp.int32), 0), 1
@@ -441,7 +467,7 @@
     groups = jnp.sum(jnp.where(slot[None, :] <= slot[:, None], fresh[None, :], False).astype(jnp.int32), 1)
     limit = jnp.arange(BLOCK_TILES + 1, dtype=jnp.int32) * PAIRS
     starts = jnp.sum((key[None, :] < limit[:, None]).astype(jnp.int32), axis=1)
-    head = jnp.stack([count, block_index, core] + [jnp.int32(0)] * 5)
+    head = jnp.stack(head + [jnp.int32(0)] * (8 - len(head)))
     return jnp.concatenate([head, ordered(rows), ordered(slabs), ranks, groups, starts]).astype(jnp.int32)
 
 
@@ -465,10 +491,13 @@
         [of(side(k ^ way), 1, k) for k in (core, 1 - core)] for way in (0, 1)
     )
     beyond_q, far_q = both_of(2, 0), both_of(2, 1)
-    arrivals = both_of(0, 0) + both_of(0, 1) + both_of(3, 0) + both_of(1, 0) + near_q
+    arrivals = both_of(0, 0)
+    arrivals += [near_by[k] for k in (0, 1) for near_by in (both_of(0, 1), both_of(3, 0), both_of(1, 0))]
+    arrivals += near_q
     arrivals += [beyond_q[0], other_q[0], beyond_q[1], other_q[1], far_q[0], far_q[1]]
     arrivals = jnp.stack(arrivals)
-    info = pair_list(pair_count[0, 0], block_index, core, pair_rows[0, 0], pair_cols[0, 0], arrivals)
+    head = [pair_count[0, 0], block_index, core, zh, y, slab_index // 2]
+    info = pair_list(head, pair_rows[0, 0], pair_cols[0, 0], arrivals)
 
     own = lax.dynamic_index_in_dim(slab, block_index, 0, keepdims=False)
     later, own = lax.optimization_barrier((slab, own))
@@ -477,6 +506,8 @@
     give = lax.dynamic_index_in_dim(later, block_index ^ 1, 0, keepdims=False)
     across = cross(give)
     half_rows = 0.5 * jnp.sum(jnp.square(slab.astype(F32)), axis=2)
+    seeds = labels.astype(F32)[None]
+    seeds = jnp.concatenate([seeds, lax.ppermute(seeds, "zh", [(0, 1), (1, 0)])], axis=0)
 
     def both(*pieces):
         return [each for piece in pieces for each in (piece, swap_cores(piece))]
@@ -486,10 +517,15 @@
         return (made[0], tied[0]), tied[1:]
 
     made = build(0, info, slab, half_rows, both(own), ())
-    made, (across, below, above) = after(made, across, below, above)
+    made, (across, below, above, seeds) = after(made, across, below, above, seeds)
     near = apart(across)
     other = apart_z(jnp.where(zero, above, below))
-    made = build(2, info, slab, half_rows, both(across, below, above), made)
+    seeds = [seeds, down(seeds), lax.ppermute(seeds, "y", [(i, (i + 2) % 4) for i in range(4)]), up(seeds)]
+    made = build(2, info, slab, half_rows, [across, below, above], made)
+    made, seeds = after(made, *seeds)
+    seeds = jnp.concatenate(seeds, axis=0)
+    seeds = jnp.concatenate([seeds, swap_cores(seeds)], axis=0)
+    made = build(5, info, slab, half_rows, [swap_cores(piece) for piece in (across, below, above)], made)
     made, (near, other, below, above) = after(made, near, other, below, above)
     beyond = apart(jnp.where(zero, below, above))
     other = apart_z(other)
@@ -497,54 +533,41 @@
     made, (passed,) = after(made, near)
     far = apart(passed)
     made = build(9, info, slab, half_rows, [swap_cores(near), beyond, other], made)
-    made, (far,) = after(made, far)
+    made, (far, seeds) = after(made, far, seeds)
     made = build(12, info, slab, half_rows, [swap_cores(beyond), swap_cores(other), far], made)
     made = build(15, info, slab, half_rows, [swap_cores(far)], made)
     tiles, partial_degree = made
 
-    in_block = jnp.arange(SLAB_TILES)[:, None] == block_index
-    counted = jnp.where(labels % K == jnp.arange(K)[:, None], jnp.where(labels < K, 1.0, -1.0), 0.0)
-    facts = jnp.concatenate(
-        [jnp.sum(counted, axis=1), jnp.sum(partial_degree)[None], jnp.zeros(TILE - K - 1, F32)]
-    )
-    sent = jnp.stack(
-        [
-            partial_degree,
-            jnp.where(in_block, labels.astype(F32)[None], 0.0),
-            jnp.broadcast_to(facts[None], (SLAB_TILES, TILE)),
-        ],
-        axis=1,
-    )
-    got = lax.all_to_all(
-        jnp.broadcast_to(sent[None], (8,) + sent.shape).reshape(8 * SLAB_TILES, 3, TILE), CHIPS, 0, 0, tiled=True
-    )
-    mine = jnp.sum(got.reshape(8, SLAB_TILES, 3, TILE), axis=1)
-    others = swap_cores(mine)
-    known = jnp.where(zero, jnp.stack([mine, others], 1), jnp.stack([others, mine], 1)).reshape(BLOCK_TILES, 3, TILE)
-    column_degree = known[:, 0]
-    column_labels = known[:, 1].astype(jnp.int32)
-    facts = jnp.sum(mine[:, 2], axis=0) + jnp.sum(others[:, 2], axis=0)
-    documents = BLOCK_TILES * SLAB_TILES * TILE
-    shift = facts[:K, None] * lax.rsqrt(facts[K] * documents)
-    column_inv_root = lax.rsqrt(column_degree)
-    degree = lax.dynamic_slice_in_dim(column_degree, slab_index, 1, 0)
-    inv_root = lax.rsqrt(degree)
-    root = jnp.sqrt(degree)
-
-    scale = 1.0 / documents
-    running = product(info, tiles, column_labels, column_inv_root, partial_degree, shift)
+    by_column = lax.all_to_all(
+        jnp.broadcast_to(partial_degree[None, :, None], (8, SLAB_TILES, 1, TILE)).reshape(8 * SLAB_TILES, 1, TILE),
+        CHIPS,
+        0,
+        0,
+        tiled=True,
+    ).reshape(8, SLAB_TILES, TILE)
+    degrees = jnp.sum(by_column, axis=1)
+
+    scale = 1.0 / (BLOCK_TILES * SLAB_TILES * TILE)
+    block = jax.ShapeDtypeStruct((K, TILE), F32)
+    running = product(info, tiles, seeds, degrees, swap_cores(degrees))
     parts = lax.all_to_all(running, COL, 0, 0, tiled=True)
     weighed = local(
-        weigh_kernel, "weigh", jax.ShapeDtypeStruct((K + 32, TILE), BF16), parts, inv_root, root
-    )
-    running = product(info, tiles, *share_row(weighed))
+        weigh_kernel, "weigh", jax.ShapeDtypeStruct((K + 16, TILE), BF16), info, parts, degrees
+    )
+    running = product(info, tiles, *share_row(weighed), partial_degree)
     parts = lax.all_to_all(running, COL, 0, 0, tiled=True)
-    block = jax.ShapeDtypeStruct((K, TILE), F32)
-    packed = jax.ShapeDtypeStruct((K // 2, 128), F32)
     image, message = local(
-        functools.partial(middle_kernel, scale), "middle", (block, packed), parts, inv_root, root
-    )
-    return local(functools.partial(last_kernel, scale), "last", block, sum_all(message), image, root)
+        functools.partial(middle_kernel, scale),
+        "middle",
+        (block, jax.ShapeDtypeStruct((K // 2, 128), F32)),
+        info,
+        parts,
+        degrees,
+        by_column,
+    )
+    return local(
+        functools.partial(last_kernel, scale), "last", block, info, sum_all(message), image, degrees
+    )
 
 
 def solution(mesh):

time: 211 us -> 211 us (level)
  waiting for transfers between devices: 58.7 us -> 41.8 us
  Pallas kernels: 30.7 us -> 43.9 us
  blocking collectives: 61.5 us -> 69.2 us
  starting transfers between devices: 44.8 us -> 41.5 us
    all_to_all x2 -> x1, waiting for transfers between devices: 22.5 us -> 11.6 us  [shards(): parts = lax.all_to_all(running, COL, 0, 0, tiled=True)]
    all_to_all x1 -> x2, blocking collectives: 24 us -> 33.8 us  [the longest x1 21.3 us: shards(): lax.all_to_all(jnp.broadcast_to(partial_degree[None, :, None], (8, SLAB_T...]
    pallas_call x6 -> x7, Pallas kernels: 17.2 us -> 26.8 us  [build(): pl.pallas_call(functools.partial(build_kernel, first, arrived), out_shape...]
    ppermute x2, starting transfers between devices: 8.98 us -> 3.66 us  [apart_z(): return lax.ppermute(value, ('zh', 'core', 'zl'), moves)]
    ppermute x3, starting transfers between devices: 2.39 us -> 6.67 us  [apart(): lax.ppermute(value, ('y', 'core'), [(2 * i + k, 2 * ((i + 1 + 2 * k) % 4)...]
    ppermute x1, waiting for transfers between devices: 12.7 us -> 8.72 us  [cross(): return lax.ppermute(value, ('zh', 'zl'), [(0, 3), (3, 0), (1, 2), (2, 1)])]
    all_to_all x2 -> x1, starting transfers between devices: 7.32 us -> 3.55 us  [shards(): parts = lax.all_to_all(running, COL, 0, 0, tiled=True)]
    pallas_call x3, Pallas kernels: 6.12 us -> 8.27 us  [local(): pl.pallas_call(kernel, out_shape=out_shape, in_specs=[pl.BlockSpec(memory...]
  transfers between devices with their start and end apart: 22 -> 26, of which waited for: 14 -> 12; matrix products, arithmetic and copies ran while one was open for 4% -> 5% of each run, Pallas kernels for 6% -> 11%
where the time goes in v8:
time: 211 us
  blocking collectives  69.2 us (33%)
  Pallas kernels  43.9 us (21%)
  waiting for transfers between devices  41.8 us (20%)
  starting transfers between devices  41.5 us (20%)
  other arithmetic  9.32 us (4%)
  local copies, waits for them, and re-layouts  4.07 us (2%)
    all_to_all x2, blocking collectives, share(): lax.all_to_all(jnp.broadcast_to(value[None], (size,) + value.shape), axes...  35.4 us
    pallas_call x7, Pallas kernels, build(): pl.pallas_call(functools.partial(build_kernel, first, arrived), out_shape...  26.8 us
    all_to_all x1, blocking collectives, shards(): lax.all_to_all(jnp.broadcast_to(partial_degree[None, :, None], (8, SLAB_T...  21.3 us
    ppermute x13, starting transfers between devices, swap_cores(): return lax.ppermute(value, 'core', [(0, 1), (1, 0)])  18.5 us
    ppermute x3, waiting for transfers between devices, apart(): lax.ppermute(value, ('y', 'core'), [(2 * i + k, 2 * ((i + 1 + 2 * k) % 4)...  13.7 us
    all_to_all x1, blocking collectives, shards(): parts = lax.all_to_all(running, COL, 0, 0, tiled=True)  12.5 us
    all_to_all x1, waiting for transfers between devices, shards(): parts = lax.all_to_all(running, COL, 0, 0, tiled=True)  11.6 us
    pallas_call x2, Pallas kernels, product(): pl.pallas_call(functools.partial(product_kernel, first), out_shape=jax.Sh...  8.86 us
  transfers between devices with their start and end apart: 26, of which 12 were waited for; matrix products, arithmetic and copies ran while one was open for 5% of the time, Pallas kernels for 11%

profile of v8, /device:TPU:1, one launch (start us, length us, event | category | flops | bytes accessed | tf_op | source)
XLA Modules:
  0.0 210.7 jit_solution(9433956151590573047)
XLA Ops:
  5.6 2.3 %dynamic-slice_bitcast_fusion = bf16[512,1024]{1,0:T(8,128)(2,1)} fusion(bf16[8,512,1024]{2,1,0:T(8,128)(2,1)} %bitcast.40, s32[]{:T(128)S(6)} %select_n.194), kind=kLoop, calls=%fused_computation.1 | loop fusion | bytes 2097156 | tf_op jit(solution)/shard_map/jit(dynamic_index_in_dim)/squeeze | solution.py:506
  7.9 3.8 %collective-permute-start.1 = (bf16[512,1024]{1,0:T(8,128)(2,1)}, bf16[512,1024]{1,0:T(8,128)(2,1)}, u32[]{:S(2)}, u32[]{:S(2)}) collective-permute-start(bf16[512,1024]{1,0:T(8,128)(2,1)} %dynamic-slice_bitcast_fusion), channel_id=1, source_target_pairs={{0,17},{17,0},{1,16},{16,1},{2,19},{19,2},{3,18},{18,3},{4,21},{21... | collective-permute-start | bytes 3145736 | tf_op jit(solution)/shard_map/ppermute | solution.py:449
  15.3 5.1 %multiply_reduce_fusion = f32[4096]{0:T(1024)S(1)} fusion(bf16[4096,1024]{1,0:T(8,128)(2,1)} %param.5), kind=kLoop, calls=%fused_computation | loop fusion | flops 12578816 | bytes 8404992 | tf_op jit(solution)/shard_map/reduce_sum | solution.py:508
  20.7 5.6 %build_tiles.7 = (bf16[24,512,512]{2,1,0:T(8,128)(2,1)}, f32[8,512]{1,0:T(8,128)S(1)}) custom-call(s32[121]{0:T(128)S(1)} %concatenate.20.info, bf16[8,512,1024]{2,1,0:T(8,128)(2,1)} %bitcast.41, f32[8,512]{1,0:T(8,128)S(1)} %mul.134.half_rows, bf16[512,1024]{1,0:T(8,128)(2,1)S(1)} %dynamic-slice_bitcast_fusion.1.refs_0_, ...), custom_call_target="tpu_custom_call" | custom-call | flops 1610612736 | bytes 7864320 | tf_op jit(solution)/shard_map/build_tiles/pallas_call | solution.py:140
  26.3 8.7 %collective-permute-done.1.refs_0_ = bf16[512,1024]{1,0:T(8,128)(2,1)} collective-permute-done((bf16[512,1024]{1,0:T(8,128)(2,1)}, bf16[512,1024]{1,0:T(8,128)(2,1)}, u32[]{:S(2)}, u32[]{:S(2)}) %collective-permute-start.1) | collective-permute-done | bytes 1048608 | tf_op jit(solution)/shard_map/ppermute | solution.py:449
  37.5 2.0 collective-permute-start.5
  40.4 2.2 %collective-permute-start.11 = (bf16[512,1024]{1,0:T(8,128)(2,1)}, bf16[512,1024]{1,0:T(8,128)(2,1)S(1)}, u32[]{:S(2)}, u32[]{:S(2)}) collective-permute-start(bf16[512,1024]{1,0:T(8,128)(2,1)} %collective-permute-done.1.refs_0_), channel_id=1, source_target_pairs={{0,32},{8,104},{32,64},{40,8},{64,96},{72,40},{96,0},{104,72},{1,3... | collective-permute-start | bytes 3145736 | tf_op jit(solution)/shard_map/ppermute | solution.py:432
  42.6 2.7 %collective-permute-start.12 = (bf16[512,1024]{1,0:T(8,128)(2,1)S(1)}, bf16[512,1024]{1,0:T(8,128)(2,1)}, u32[]{:S(2)}, u32[]{:S(2)}) collective-permute-start(bf16[512,1024]{1,0:T(8,128)(2,1)S(1)} %broadcast_select_fusion.1), channel_id=1, source_target_pairs={{0,1},{8,25},{1,16},{9,8},{16,17},{24,9},{17,0},{25,24},{2,3},{10,... | collective-permute-start | bytes 3145736 | tf_op jit(solution)/shard_map/ppermute | solution.py:445
  45.3 3.9 %build_tiles.8 = (bf16[24,512,512]{2,1,0:T(8,128)(2,1)}, f32[8,512]{1,0:T(8,128)S(1)}) custom-call(s32[121]{0:T(128)S(1)} %concatenate.20.info, bf16[8,512,1024]{2,1,0:T(8,128)(2,1)} %bitcast.42, f32[8,512]{1,0:T(8,128)S(1)} %mul.134.half_rows, bf16[512,1024]{1,0:T(8,128)(2,1)} %collective-permute-done.1.refs_0_, ...), custom_call_target="tpu_custom_call", output_to_operand_aliasing={{0}: (6, {})} | custom-call | flops 2147483648 | bytes 10485760 | tf_op jit(solution)/shard_map/build_tiles/pallas_call | solution.py:140
  49.2 3.6 %build_tiles.9 = (bf16[24,512,512]{2,1,0:T(8,128)(2,1)}, f32[8,512]{1,0:T(8,128)S(1)}) custom-call(s32[121]{0:T(128)S(1)} %concatenate.20.info, bf16[8,512,1024]{2,1,0:T(8,128)(2,1)} %bitcast.43, f32[8,512]{1,0:T(8,128)S(1)} %mul.134.half_rows, bf16[512,1024]{1,0:T(8,128)(2,1)S(1)} %collective-permute-done.5.refs_0_, ...), custom_call_target="tpu_custom_call", output_to_operand_aliasing={{0}: (6, {})} | custom-call | flops 2147483648 | bytes 10485760 | tf_op jit(solution)/shard_map/build_tiles/pallas_call | solution.py:140
  54.7 2.4 %collective-permute-done.12 = bf16[512,1024]{1,0:T(8,128)(2,1)} collective-permute-done((bf16[512,1024]{1,0:T(8,128)(2,1)S(1)}, bf16[512,1024]{1,0:T(8,128)(2,1)}, u32[]{:S(2)}, u32[]{:S(2)}) %collective-permute-start.12) | collective-permute-done | bytes 1048608 | tf_op jit(solution)/shard_map/ppermute | solution.py:445
  58.1 3.9 %collective-permute-start.14 = (bf16[512,1024]{1,0:T(8,128)(2,1)}, bf16[512,1024]{1,0:T(8,128)(2,1)S(1)}, u32[]{:S(2)}, u32[]{:S(2)}) collective-permute-start(bf16[512,1024]{1,0:T(8,128)(2,1)} %broadcast_select_fusion), channel_id=1, source_target_pairs={{0,32},{8,104},{32,64},{40,8},{64,96},{72,40},{96,0},{104,72},{1,3... | collective-permute-start | bytes 3145736 | tf_op jit(solution)/shard_map/ppermute | solution.py:432
  65.8 8.4 %collective-permute-done.14.refs_1_ = bf16[512,1024]{1,0:T(8,128)(2,1)S(1)} collective-permute-done((bf16[512,1024]{1,0:T(8,128)(2,1)}, bf16[512,1024]{1,0:T(8,128)(2,1)S(1)}, u32[]{:S(2)}, u32[]{:S(2)}) %collective-permute-start.14) | collective-permute-done | bytes 1048608 | tf_op jit(solution)/shard_map/ppermute | solution.py:432
  74.1 2.6 %collective-permute-start.19 = (bf16[512,1024]{1,0:T(8,128)(2,1)S(1)}, bf16[512,1024]{1,0:T(8,128)(2,1)S(1)}, u32[]{:S(2)}, u32[]{:S(2)}) collective-permute-start(bf16[512,1024]{1,0:T(8,128)(2,1)S(1)} %collective-permute-done.14.refs_1_), channel_id=1, source_target_pairs={{0,8},{8,0},{1,9},{9,1},{2,10},{10,2},{3,11},{11,3},{4,12},{12,4},... | collective-permute-start | bytes 3145736 | tf_op jit(solution)/shard_map/ppermute | solution.py:397
  77.0 4.8 %build_tiles.11 = (bf16[24,512,512]{2,1,0:T(8,128)(2,1)}, f32[8,512]{1,0:T(8,128)S(1)}) custom-call(s32[121]{0:T(128)S(1)} %concatenate.20.info, bf16[8,512,1024]{2,1,0:T(8,128)(2,1)} %bitcast.45, f32[8,512]{1,0:T(8,128)S(1)} %mul.134.half_rows, bf16[512,1024]{1,0:T(8,128)(2,1)} %collective-permute-done.13.refs_0_, ...), custom_call_target="tpu_custom_call", output_to_operand_aliasing={{0}: (6, {})} | custom-call | flops 2147483648 | bytes 10485760 | tf_op jit(solution)/shard_map/build_tiles/pallas_call | solution.py:140
  81.8 3.4 %collective-permute-done.16.refs_2_ = bf16[512,1024]{1,0:T(8,128)(2,1)} collective-permute-done((bf16[512,1024]{1,0:T(8,128)(2,1)S(1)}, bf16[512,1024]{1,0:T(8,128)(2,1)}, u32[]{:S(2)}, u32[]{:S(2)}) %collective-permute-start.16) | collective-permute-done | bytes 1048608 | tf_op jit(solution)/shard_map/ppermute | solution.py:432
  85.3 2.9 %collective-permute-start.18 = (bf16[512,1024]{1,0:T(8,128)(2,1)}, bf16[512,1024]{1,0:T(8,128)(2,1)S(1)}, u32[]{:S(2)}, u32[]{:S(2)}) collective-permute-start(bf16[512,1024]{1,0:T(8,128)(2,1)} %collective-permute-done.16.refs_2_), channel_id=1, source_target_pairs={{0,8},{8,0},{1,9},{9,1},{2,10},{10,2},{3,11},{11,3},{4,12},{12,4},... | collective-permute-start | bytes 3145736 | tf_op jit(solution)/shard_map/ppermute | solution.py:397
  88.1 4.5 %build_tiles.12 = (bf16[24,512,512]{2,1,0:T(8,128)(2,1)}, f32[8,512]{1,0:T(8,128)S(1)}) custom-call(s32[121]{0:T(128)S(1)} %concatenate.20.info, bf16[8,512,1024]{2,1,0:T(8,128)(2,1)} %bitcast.46, f32[8,512]{1,0:T(8,128)S(1)} %mul.134.half_rows, bf16[512,1024]{1,0:T(8,128)(2,1)S(1)} %collective-permute-done.19.refs_0_, ...), custom_call_target="tpu_custom_call", output_to_operand_aliasing={{0}: (6, {})} | custom-call | flops 2147483648 | bytes 10485760 | tf_op jit(solution)/shard_map/build_tiles/pallas_call | solution.py:140
  92.6 3.6 %build_tiles.13 = (bf16[24,512,512]{2,1,0:T(8,128)(2,1)}, f32[8,512]{1,0:T(8,128)S(1)}) custom-call(s32[121]{0:T(128)S(1)} %concatenate.20.info, bf16[8,512,1024]{2,1,0:T(8,128)(2,1)} %bitcast.47, f32[8,512]{1,0:T(8,128)S(1)} %mul.134.half_rows, bf16[512,1024]{1,0:T(8,128)(2,1)S(1)} %collective-permute-done.18.refs_0_, ...), custom_call_target="tpu_custom_call", output_to_operand_aliasing={{0}: (4, {})} | custom-call | flops 536870912 | bytes 2621440 | tf_op jit(solution)/shard_map/build_tiles/pallas_call | solution.py:140
  96.4 21.3 %all_to_all.25 = f32[64,1,512]{2,1,0:T(1,128)S(1)} all-to-all(f32[64,1,512]{2,1,0:T(1,128)S(1)} %broadcast_in_dim.91), channel_id=1, replica_groups=mesh['y'=4,'zh'=2,'core'=2,'x'=4,'zl'=2] {'y','zh','x','zl'}, dimensions={0} | all-to-all | bytes 262144 | tf_op jit(solution)/shard_map/all_to_all | solution.py:541
  117.8 3.0 %collective-permute-start.21 = (f32[8,512]{1,0:T(8,128)S(1)}, f32[8,512]{1,0:T(8,128)S(1)}, u32[]{:S(2)}, u32[]{:S(2)}) collective-permute-start(f32[8,512]{1,0:T(8,128)S(1)} %fusion.1.refs_1_.degrees), channel_id=1, source_target_pairs={{0,8},{8,0},{1,9},{9,1},{2,10},{10,2},{3,11},{11,3},{4,12},{12,4},... | collective-permute-start | bytes 49160 | tf_op jit(solution)/shard_map/ppermute | solution.py:397
  121.6 3.8 %product.2 = bf16[8,64,512]{2,1,0:T(8,128)(2,1)S(1)} custom-call(s32[121]{0:T(128)S(1)} %concatenate.20.info, bf16[24,512,512]{2,1,0:T(8,128)(2,1)} %get-tuple-element.76.tiles, f32[16,512]{1,0:T(8,128)S(1)} %concatenate.23.refs_0_, f32[8,512]{1,0:T(8,128)S(1)} %fusion.1.refs_1_.degrees, f32[8,512]{1,0:T(8,128)S(1)} %collective-permute-done.21.refs_2_), custom_call_target="tpu_custom_call" | custom-call | tf_op jit(solution)/shard_map/product/pallas_call | solution.py:260
  125.5 12.5 %all_to_all.26.parts = bf16[8,64,512]{2,1,0:T(8,128)(2,1)S(1)} all-to-all(bf16[8,64,512]{2,1,0:T(8,128)(2,1)S(1)} %product.2), channel_id=1, replica_groups=mesh['y'=4,'zh'=2,'core'=2,'x'=4,'zl'=2] {'x','zl'}, dimensions={0} | all-to-all | bytes 1048576 | tf_op jit(solution)/shard_map/all_to_all | solution.py:553
  139.1 16.2 %all_to_all.27.refs_0_ = bf16[8,80,512]{2,1,0:T(8,128)(2,1)S(1)} all-to-all(bf16[8,80,512]{2,1,0:T(8,128)(2,1)S(1)} %broadcast_in_dim.92), channel_id=1, replica_groups=mesh['y'=4,'zh'=2,'core'=2,'x'=4,'zl'=2] {'y','zh'}, dimensions={0} | all-to-all | bytes 1310720 | tf_op jit(solution)/shard_map/all_to_all | solution.py:402
  155.3 2.9 %collective-permute-start.22 = (bf16[8,80,512]{2,1,0:T(8,128)(2,1)S(1)}, bf16[8,80,512]{2,1,0:T(8,128)(2,1)S(1)}, u32[]{:S(2)}, u32[]{:S(2)}) collective-permute-start(bf16[8,80,512]{2,1,0:T(8,128)(2,1)S(1)} %all_to_all.27.refs_0_), channel_id=1, source_target_pairs={{0,8},{8,0},{1,9},{9,1},{2,10},{10,2},{3,11},{11,3},{4,12},{12,4},... | collective-permute-start | bytes 1966088 | tf_op jit(solution)/shard_map/ppermute | solution.py:397
  160.0 5.0 %product.3 = bf16[8,80,512]{2,1,0:T(8,128)(2,1)} custom-call(s32[121]{0:T(128)S(1)} %concatenate.20.info, bf16[24,512,512]{2,1,0:T(8,128)(2,1)} %get-tuple-element.76.tiles, bf16[8,80,512]{2,1,0:T(8,128)(2,1)S(1)} %all_to_all.27.refs_0_, bf16[8,80,512]{2,1,0:T(8,128)(2,1)S(1)} %collective-permute-done.22.refs_1_, f32[8,512]{1,0:T(8,128)S(1)} %get-tuple-element.78.refs_2_), custom_call_target="tpu_custom_call" | custom-call | tf_op jit(solution)/shard_map/product/pallas_call | solution.py:260
  165.0 3.6 %all-to-all-start.3 = ((bf16[8,80,512]{2,1,0:T(8,128)(2,1)}), bf16[8,80,512]{2,1,0:T(8,128)(2,1)S(1)}, u32[]{:S(2)}, u32[]{:S(2)}) async-start(bf16[8,80,512]{2,1,0:T(8,128)(2,1)} %product.3), calls=%async_computation.3 | async-start | bytes 1310720 | tf_op jit(solution)/shard_map/all_to_all | solution.py:558
  168.6 11.6 %all-to-all-done.3.parts = bf16[8,80,512]{2,1,0:T(8,128)(2,1)S(1)} async-done(((bf16[8,80,512]{2,1,0:T(8,128)(2,1)}), bf16[8,80,512]{2,1,0:T(8,128)(2,1)S(1)}, u32[]{:S(2)}, u32[]{:S(2)}) %all-to-all-start.3) | async-done | bytes 655392 | tf_op jit(solution)/shard_map/all_to_all | solution.py:558
  180.2 3.6 %middle.1 = (f32[64,512]{1,0:T(8,128)S(1)}, f32[32,128]{1,0:T(8,128)S(1)}) custom-call(s32[121]{0:T(128)S(1)} %concatenate.20.info, bf16[8,80,512]{2,1,0:T(8,128)(2,1)S(1)} %all-to-all-done.3.parts, f32[8,512]{1,0:T(8,128)S(1)} %fusion.1.refs_1_.degrees, f32[8,8,512]{2,1,0:T(8,128)S(1)} %bitcast.38), custom_call_target="tpu_custom_call" | custom-call | tf_op jit(solution)/shard_map/middle/pallas_call | solution.py:386
  185.1 19.2 %all_to_all.28 = f32[64,16,128]{2,1,0:T(8,128)S(1)} all-to-all(f32[64,16,128]{2,1,0:T(8,128)S(1)} %broadcast_in_dim.93), channel_id=1, replica_groups=mesh['y'=4,'zh'=2,'core'=2,'x'=4,'zl'=2] {'y','zh','x','zl'}, dimensions={0} | all-to-all | bytes 1048576 | tf_op jit(solution)/shard_map/all_to_all | solution.py:402
  204.4 2.0 collective-permute-start.24
  207.2 3.6 %last.1 = f32[64,512]{1,0:T(8,128)} custom-call(s32[121]{0:T(128)S(1)} %concatenate.20.info, f32[32,128]{1,0:T(8,128)S(1)} %pad_maximum_fusion.1.message, f32[64,512]{1,0:T(8,128)S(1)} %get-tuple-element.80.image, f32[8,512]{1,0:T(8,128)S(1)} %fusion.1.refs_1_.degrees), custom_call_target="tpu_custom_call" | custom-call | tf_op jit(solution)/shard_map/last/pallas_call | solution.py:386
  (70 shorter events, 25.3 us)
Async XLA Ops:
  1.3 19.3 %collective-permute-start = (bf16[512,1024]{1,0:T(8,128)(2,1)S(1)}, bf16[512,1024]{1,0:T(8,128)(2,1)}, u32[]{:S(2)}, u32[]{:S(2)}) collective-permute-start(bf16[512,1024]{1,0:T(8,128)(2,1)S(1)} %dynamic-slice_bitcast_fusion.1.refs_0_), channel_id=1, source_target_pairs={{0,8},{8,0},{1,9},{9,1},{2,10},{10,2},{3,11},{11,3},{4,12},{12,4},... | collective-permute-start | bytes 3145736 | tf_op jit(solution)/shard_map/ppermute | solution.py:397
  2.8 32.2 %collective-permute-start.2 = (bf16[512,1024]{1,0:T(8,128)(2,1)S(1)}, bf16[512,1024]{1,0:T(8,128)(2,1)S(1)}, u32[]{:S(2)}, u32[]{:S(2)}) collective-permute-start(bf16[512,1024]{1,0:T(8,128)(2,1)S(1)} %dynamic-slice_bitcast_fusion.1.refs_0_), channel_id=1, source_target_pairs={{0,32},{32,64},{64,96},{96,0},{1,33},{33,65},{65,97},{97,1},{2,34}... | collective-permute-start | bytes 3145736 | tf_op jit(solution)/shard_map/ppermute | solution.py:424
  4.2 30.8 %collective-permute-start.3 = (bf16[512,1024]{1,0:T(8,128)(2,1)S(1)}, bf16[512,1024]{1,0:T(8,128)(2,1)S(1)}, u32[]{:S(2)}, u32[]{:S(2)}) collective-permute-start(bf16[512,1024]{1,0:T(8,128)(2,1)S(1)} %dynamic-slice_bitcast_fusion.1.refs_0_), channel_id=1, source_target_pairs={{0,96},{32,0},{64,32},{96,64},{1,97},{33,1},{65,33},{97,65},{2,98}... | collective-permute-start | bytes 3145736 | tf_op jit(solution)/shard_map/ppermute | solution.py:428
  7.9 27.1 %collective-permute-start.1 = (bf16[512,1024]{1,0:T(8,128)(2,1)}, bf16[512,1024]{1,0:T(8,128)(2,1)}, u32[]{:S(2)}, u32[]{:S(2)}) collective-permute-start(bf16[512,1024]{1,0:T(8,128)(2,1)} %dynamic-slice_bitcast_fusion), channel_id=1, source_target_pairs={{0,17},{17,0},{1,16},{16,1},{2,19},{19,2},{3,18},{18,3},{4,21},{21... | collective-permute-start | bytes 3145736 | tf_op jit(solution)/shard_map/ppermute | solution.py:449
  12.3 8.3 %collective-permute-start.4 = (f32[1,512]{1,0:T(1,128)S(1)}, f32[1,512]{1,0:T(1,128)S(1)}, u32[]{:S(2)}, u32[]{:S(2)}) collective-permute-start(f32[1,512]{1,0:T(1,128)S(1)} %bitcast.48), channel_id=1, source_target_pairs={{0,16},{16,0},{1,17},{17,1},{2,18},{18,2},{3,19},{19,3},{4,20},{20... | collective-permute-start | bytes 6152 | tf_op jit(solution)/shard_map/ppermute | solution.py:510
  35.0 4.5 %collective-permute-start.8 = (f32[2,512]{1,0:T(2,128)S(1)}, f32[2,512]{1,0:T(2,128)S(1)}, u32[]{:S(2)}, u32[]{:S(2)}) collective-permute-start(f32[2,512]{1,0:T(2,128)S(1)} %pad_maximum_fusion.2), channel_id=1, source_target_pairs={{0,96},{32,0},{64,32},{96,64},{1,97},{33,1},{65,33},{97,65},{2,98}... | collective-permute-start | bytes 12296 | tf_op jit(solution)/shard_map/ppermute | solution.py:428
  36.4 4.0 %collective-permute-start.9 = (f32[2,512]{1,0:T(2,128)S(1)}, f32[2,512]{1,0:T(2,128)S(1)}, u32[]{:S(2)}, u32[]{:S(2)}) collective-permute-start(f32[2,512]{1,0:T(2,128)S(1)} %pad_maximum_fusion.2), channel_id=1, source_target_pairs={{0,64},{32,96},{64,0},{96,32},{1,65},{33,97},{65,1},{97,33},{2,66}... | collective-permute-start | bytes 12296 | tf_op jit(solution)/shard_map/ppermute | solution.py:523
  36.8 5.8 %collective-permute-start.10 = (f32[2,512]{1,0:T(2,128)S(1)}, f32[2,512]{1,0:T(2,128)S(1)}, u32[]{:S(2)}, u32[]{:S(2)}) collective-permute-start(f32[2,512]{1,0:T(2,128)S(1)} %pad_maximum_fusion.2), channel_id=1, source_target_pairs={{0,32},{32,64},{64,96},{96,0},{1,33},{33,65},{65,97},{97,1},{2,34}... | collective-permute-start | bytes 12296 | tf_op jit(solution)/shard_map/ppermute | solution.py:424
  37.5 11.7 %collective-permute-start.5 = (bf16[512,1024]{1,0:T(8,128)(2,1)}, bf16[512,1024]{1,0:T(8,128)(2,1)S(1)}, u32[]{:S(2)}, u32[]{:S(2)}) collective-permute-start(bf16[512,1024]{1,0:T(8,128)(2,1)} %collective-permute-done.1.refs_0_), channel_id=1, source_target_pairs={{0,8},{8,0},{1,9},{9,1},{2,10},{10,2},{3,11},{11,3},{4,12},{12,4},... | collective-permute-start | bytes 3145736 | tf_op jit(solution)/shard_map/ppermute | solution.py:397
  39.5 9.7 %collective-permute-start.6 = (bf16[512,1024]{1,0:T(8,128)(2,1)S(1)}, bf16[512,1024]{1,0:T(8,128)(2,1)S(1)}, u32[]{:S(2)}, u32[]{:S(2)}) collective-permute-start(bf16[512,1024]{1,0:T(8,128)(2,1)S(1)} %collective-permute-done.2.refs_1_), channel_id=1, source_target_pairs={{0,8},{8,0},{1,9},{9,1},{2,10},{10,2},{3,11},{11,3},{4,12},{12,4},... | collective-permute-start | bytes 3145736 | tf_op jit(solution)/shard_map/ppermute | solution.py:397
  39.5 9.7 %collective-permute-start.7 = (bf16[512,1024]{1,0:T(8,128)(2,1)S(1)}, bf16[512,1024]{1,0:T(8,128)(2,1)S(1)}, u32[]{:S(2)}, u32[]{:S(2)}) collective-permute-start(bf16[512,1024]{1,0:T(8,128)(2,1)S(1)} %collective-permute-done.3.refs_2_), channel_id=1, source_target_pairs={{0,8},{8,0},{1,9},{9,1},{2,10},{10,2},{3,11},{11,3},{4,12},{12,4},... | collective-permute-start | bytes 3145736 | tf_op jit(solution)/shard_map/ppermute | solution.py:397
  40.4 14.3 %collective-permute-start.11 = (bf16[512,1024]{1,0:T(8,128)(2,1)}, bf16[512,1024]{1,0:T(8,128)(2,1)S(1)}, u32[]{:S(2)}, u32[]{:S(2)}) collective-permute-start(bf16[512,1024]{1,0:T(8,128)(2,1)} %collective-permute-done.1.refs_0_), channel_id=1, source_target_pairs={{0,32},{8,104},{32,64},{40,8},{64,96},{72,40},{96,0},{104,72},{1,3... | collective-permute-start | bytes 3145736 | tf_op jit(solution)/shard_map/ppermute | solution.py:432
  42.6 14.4 %collective-permute-start.12 = (bf16[512,1024]{1,0:T(8,128)(2,1)S(1)}, bf16[512,1024]{1,0:T(8,128)(2,1)}, u32[]{:S(2)}, u32[]{:S(2)}) collective-permute-start(bf16[512,1024]{1,0:T(8,128)(2,1)S(1)} %broadcast_select_fusion.1), channel_id=1, source_target_pairs={{0,1},{8,25},{1,16},{9,8},{16,17},{24,9},{17,0},{25,24},{2,3},{10,... | collective-permute-start | bytes 3145736 | tf_op jit(solution)/shard_map/ppermute | solution.py:445
  58.1 16.0 %collective-permute-start.14 = (bf16[512,1024]{1,0:T(8,128)(2,1)}, bf16[512,1024]{1,0:T(8,128)(2,1)S(1)}, u32[]{:S(2)}, u32[]{:S(2)}) collective-permute-start(bf16[512,1024]{1,0:T(8,128)(2,1)} %broadcast_select_fusion), channel_id=1, source_target_pairs={{0,32},{8,104},{32,64},{40,8},{64,96},{72,40},{96,0},{104,72},{1,3... | collective-permute-start | bytes 3145736 | tf_op jit(solution)/shard_map/ppermute | solution.py:432
  62.1 14.7 %collective-permute-start.15 = (bf16[512,1024]{1,0:T(8,128)(2,1)}, bf16[512,1024]{1,0:T(8,128)(2,1)S(1)}, u32[]{:S(2)}, u32[]{:S(2)}) collective-permute-start(bf16[512,1024]{1,0:T(8,128)(2,1)} %collective-permute-done.12), channel_id=1, source_target_pairs={{0,1},{8,25},{1,16},{9,8},{16,17},{24,9},{17,0},{25,24},{2,3},{10,... | collective-permute-start | bytes 3145736 | tf_op jit(solution)/shard_map/ppermute | solution.py:445
  63.1 14.0 %collective-permute-start.13 = (bf16[512,1024]{1,0:T(8,128)(2,1)S(1)}, bf16[512,1024]{1,0:T(8,128)(2,1)}, u32[]{:S(2)}, u32[]{:S(2)}) collective-permute-start(bf16[512,1024]{1,0:T(8,128)(2,1)S(1)} %collective-permute-done.11.refs_0_), channel_id=1, source_target_pairs={{0,8},{8,0},{1,9},{9,1},{2,10},{10,2},{3,11},{11,3},{4,12},{12,4},... | collective-permute-start | bytes 3145736 | tf_op jit(solution)/shard_map/ppermute | solution.py:397
  63.9 21.3 %collective-permute-start.16 = (bf16[512,1024]{1,0:T(8,128)(2,1)S(1)}, bf16[512,1024]{1,0:T(8,128)(2,1)}, u32[]{:S(2)}, u32[]{:S(2)}) collective-permute-start(bf16[512,1024]{1,0:T(8,128)(2,1)S(1)} %collective-permute-done.11.refs_0_), channel_id=1, source_target_pairs={{0,32},{8,104},{32,64},{40,8},{64,96},{72,40},{96,0},{104,72},{1,3... | collective-permute-start | bytes 3145736 | tf_op jit(solution)/shard_map/ppermute | solution.py:432
  64.4 1.3 collective-permute-start.17
  74.1 14.0 %collective-permute-start.19 = (bf16[512,1024]{1,0:T(8,128)(2,1)S(1)}, bf16[512,1024]{1,0:T(8,128)(2,1)S(1)}, u32[]{:S(2)}, u32[]{:S(2)}) collective-permute-start(bf16[512,1024]{1,0:T(8,128)(2,1)S(1)} %collective-permute-done.14.refs_1_), channel_id=1, source_target_pairs={{0,8},{8,0},{1,9},{9,1},{2,10},{10,2},{3,11},{11,3},{4,12},{12,4},... | collective-permute-start | bytes 3145736 | tf_op jit(solution)/shard_map/ppermute | solution.py:397
  76.8 11.3 %collective-permute-start.20 = (bf16[512,1024]{1,0:T(8,128)(2,1)S(1)}, bf16[512,1024]{1,0:T(8,128)(2,1)S(1)}, u32[]{:S(2)}, u32[]{:S(2)}) collective-permute-start(bf16[512,1024]{1,0:T(8,128)(2,1)S(1)} %collective-permute-done.15.refs_2_), channel_id=1, source_target_pairs={{0,8},{8,0},{1,9},{9,1},{2,10},{10,2},{3,11},{11,3},{4,12},{12,4},... | collective-permute-start | bytes 3145736 | tf_op jit(solution)/shard_map/ppermute | solution.py:397
  85.3 7.4 %collective-permute-start.18 = (bf16[512,1024]{1,0:T(8,128)(2,1)}, bf16[512,1024]{1,0:T(8,128)(2,1)S(1)}, u32[]{:S(2)}, u32[]{:S(2)}) collective-permute-start(bf16[512,1024]{1,0:T(8,128)(2,1)} %collective-permute-done.16.refs_2_), channel_id=1, source_target_pairs={{0,8},{8,0},{1,9},{9,1},{2,10},{10,2},{3,11},{11,3},{4,12},{12,4},... | collective-permute-start | bytes 3145736 | tf_op jit(solution)/shard_map/ppermute | solution.py:397
  117.8 3.9 %collective-permute-start.21 = (f32[8,512]{1,0:T(8,128)S(1)}, f32[8,512]{1,0:T(8,128)S(1)}, u32[]{:S(2)}, u32[]{:S(2)}) collective-permute-start(f32[8,512]{1,0:T(8,128)S(1)} %fusion.1.refs_1_.degrees), channel_id=1, source_target_pairs={{0,8},{8,0},{1,9},{9,1},{2,10},{10,2},{3,11},{11,3},{4,12},{12,4},... | collective-permute-start | bytes 49160 | tf_op jit(solution)/shard_map/ppermute | solution.py:397
  155.3 4.6 %collective-permute-start.22 = (bf16[8,80,512]{2,1,0:T(8,128)(2,1)S(1)}, bf16[8,80,512]{2,1,0:T(8,128)(2,1)S(1)}, u32[]{:S(2)}, u32[]{:S(2)}) collective-permute-start(bf16[8,80,512]{2,1,0:T(8,128)(2,1)S(1)} %all_to_all.27.refs_0_), channel_id=1, source_target_pairs={{0,8},{8,0},{1,9},{9,1},{2,10},{10,2},{3,11},{11,3},{4,12},{12,4},... | collective-permute-start | bytes 1966088 | tf_op jit(solution)/shard_map/ppermute | solution.py:397
  165.0 15.2 %all-to-all-start.3 = ((bf16[8,80,512]{2,1,0:T(8,128)(2,1)}), bf16[8,80,512]{2,1,0:T(8,128)(2,1)S(1)}, u32[]{:S(2)}, u32[]{:S(2)}) async-start(bf16[8,80,512]{2,1,0:T(8,128)(2,1)} %product.3), calls=%async_computation.3 | async-start | bytes 1310720 | tf_op jit(solution)/shard_map/all_to_all | solution.py:558
  183.8 1.3 collective-permute-start.23
  204.4 2.8 %collective-permute-start.24 = (f32[16,128]{1,0:T(8,128)S(1)}, f32[16,128]{1,0:T(8,128)S(1)}, u32[]{:S(2)}, u32[]{:S(2)}) collective-permute-start(f32[16,128]{1,0:T(8,128)S(1)} %reduce_sum.99), channel_id=1, source_target_pairs={{0,8},{8,0},{1,9},{9,1},{2,10},{10,2},{3,11},{11,3},{4,12},{12,4},... | collective-permute-start | bytes 24584 | tf_op jit(solution)/shard_map/ppermute | solution.py:397

commit v9 on v8

--- a/solution.py
+++ b/solution.py
@@ -31,9 +31,9 @@
     columns, refs = refs[:arrived], refs[arrived:]
     if first:
         _, old_degree, *refs = refs
-    tiles, degree, left, right, made, sem_left, sem_right, sem_out = refs
+    tiles, degree, half_column, made, sem_out = refs
     block_index = info[1]
-    ahead, stores = left.shape[0] - 1, made.shape[0]
+    stores = made.shape[0]
     if first:
         degree[...] = old_degree[...]
     else:
@@ -41,85 +41,54 @@
 
     begin, end = info[STARTS + first], info[STARTS + first + arrived]
 
-    def left_copy(entry):
-        slot = lax.rem(entry, ahead + 1)
-        t = info[ROWS + entry]
-        return pltpu.make_async_copy(slab.at[t], left.at[slot], sem_left.at[slot])
-
-    def right_copy(entry, s):
-        slot = lax.rem(info[GROUPS + entry], right.shape[0])
-        return pltpu.make_async_copy(columns[s], right.at[slot], sem_right.at[slot])
-
-    def fresh(entry):
-        return jnp.logical_or(entry == begin, info[GROUPS + entry] != info[GROUPS + entry - 1])
-
-    def fetch(entry):
-        left_copy(entry).start()
-        for s in range(arrived):
-
-            @pl.when(jnp.logical_and(fresh(entry), info[RANKS + entry] == first + s))
-            def _():
-                right_copy(entry, s).start()
-
     def store(entry):
         slot = lax.rem(entry, stores)
         return pltpu.make_async_copy(made.at[slot], tiles.at[entry], sem_out.at[slot])
 
-    for entry in range(ahead):
-
-        @pl.when(begin + entry < end)
-        def _():
-            fetch(begin + entry)
-
-    def step(entry, carry):
-        @pl.when(entry + ahead < end)
-        def _():
-            fetch(entry + ahead)
-
+    def step(column, own, entry, carry):
         @pl.when(entry - begin >= stores)
         def _():
             store(entry - stores).wait()
 
-        left_copy(entry).wait()
-
-        @pl.when(fresh(entry))
-        def _():
-            right_copy(entry, 0).wait()
-
-        a_slot = lax.rem(entry, ahead + 1)
-        b_slot = lax.rem(info[GROUPS + entry], right.shape[0])
-        m_slot = lax.rem(entry, stores)
+        slot = lax.rem(entry, stores)
         t = info[ROWS + entry]
-        b = right[b_slot]
-        wide = b.astype(F32)
-        half_b = 0.5 * jnp.sum(wide * wide, axis=1, keepdims=True)
         sums = []
         for n in range(2):
             lanes = pl.ds(n * 256, 256)
             inner = lax.dot_general(
-                b, left[a_slot, lanes, :], (((1,), (1,)), ((), ())), preferred_element_type=F32
+                column[...], slab[t, lanes, :], (((1,), (1,)), ((), ())), preferred_element_type=F32
             )
-            half_a = half_rows[pl.ds(t, 1), lanes]
-            w = jnp.exp2(RATE * ((inner - half_a) - half_b)).astype(BF16)
-            made[m_slot, :, lanes] = w
+            half_row = half_rows[pl.ds(t, 1), lanes]
+            w = jnp.exp2(RATE * ((inner - half_row) - half_column[...])).astype(BF16)
+            made[slot, :, lanes] = w
             sums.append(jnp.sum(w.astype(F32), axis=0, keepdims=True))
         old = degree[pl.ds(t, 1), :]
         degree[pl.ds(t, 1), :] = old + jnp.concatenate(sums, axis=1)
-        if first == 0:
-            @pl.when(jnp.logical_and(t == block_index, info[RANKS + entry] == 0))
+        if own:
+            @pl.when(t == block_index)
             def _():
-                w = made[m_slot]
+                w = made[slot]
                 same = lax.broadcasted_iota(jnp.int32, (TILE, TILE), 0) == lax.broadcasted_iota(
                     jnp.int32, (TILE, TILE), 1
                 )
                 w = jnp.where(same, jnp.zeros_like(w), w)
-                made[m_slot] = w
+                made[slot] = w
                 degree[pl.ds(t, 1), :] = old + jnp.sum(w.astype(F32), axis=0, keepdims=True)
 
         store(entry).start()
         return carry
 
-    lax.fori_loop(begin, end, step, 0)
+    for s, column in enumerate(columns):
+        low, high = info[STARTS + first + s], info[STARTS + first + s + 1]
+
+        @pl.when(low < high)
+        def _(column=column):
+            wide = column[...].astype(F32)
+            half_column[...] = jnp.broadcast_to(
+                0.5 * jnp.sum(wide * wide, axis=1, keepdims=True), half_column.shape
+            )
+
+        lax.fori_loop(low, high, functools.partial(step, column, first + s == 0), 0)
     for back in range(stores):
 
         @pl.when(end - begin > back)
@@ -131,39 +100,45 @@
     return pltpu.with_memory_space_constraint(value, pltpu.HBM)
 
 
+def in_vmem(value):
+    return pltpu.with_memory_space_constraint(value, pltpu.VMEM)
+
+
 def build(first, info, slab, half_rows, columns, made):
-    any_space = pl.BlockSpec(memory_space=pl.ANY)
     hbm = pl.BlockSpec(memory_space=pltpu.HBM)
     vmem = pl.BlockSpec(memory_space=pltpu.VMEM)
     arrived = len(columns)
-    pairs = PAIRS * arrived // BLOCK_TILES
+    pairs = max(1, PAIRS * arrived // BLOCK_TILES)
     return pl.pallas_call(
         functools.partial(build_kernel, first, arrived),
         out_shape=(
             pltpu.HBM((PAIRS, TILE, TILE), BF16),
             jax.ShapeDtypeStruct((SLAB_TILES, TILE), F32),
         ),
-        in_specs=[pl.BlockSpec(memory_space=pltpu.SMEM), hbm, vmem]
-        + [any_space] * arrived
+        in_specs=[pl.BlockSpec(memory_space=pltpu.SMEM), vmem, vmem]
+        + [vmem] * arrived
         + ([hbm, vmem] if made else []),
         out_specs=(hbm, vmem),
         scratch_shapes=[
-            pltpu.VMEM((3, TILE, WIDTH), BF16),
-            pltpu.VMEM((3, TILE, WIDTH), BF16),
+            pltpu.VMEM((TILE, 256), F32),
             pltpu.VMEM((4, TILE, TILE), BF16),
-            pltpu.SemaphoreType.DMA((3,)),
-            pltpu.SemaphoreType.DMA((3,)),
             pltpu.SemaphoreType.DMA((4,)),
         ],
         input_output_aliases={3 + arrived: 0} if made else {},
-        compiler_params=pltpu.CompilerParams(vmem_limit_bytes=20 * 1024 * 1024),
+        compiler_params=pltpu.CompilerParams(vmem_limit_bytes=16 * 1024 * 1024),
         cost_estimate=pl.CostEstimate(
             flops=pairs * 2 * TILE * TILE * WIDTH,
             bytes_accessed=pairs * 5 * TILE * WIDTH,
             transcendentals=pairs * TILE * TILE,
         ),
         name="build_tiles",
-    )(info, in_hbm(slab), half_rows, *columns, *([in_hbm(made[0]), made[1]] if made else []))
+    )(
+        info,
+        in_vmem(slab),
+        half_rows,
+        *(in_vmem(column) for column in columns),
+        *([in_hbm(made[0]), made[1]] if made else []),
+    )
 
 
 def terms_of(value):
@@ -184,13 +159,17 @@
     return jnp.concatenate([sums[:, 65:66], sums[:, 66:67]], axis=0) / total, total
 
 
+def row_of(rows, start):
+    return jnp.concatenate([rows[start + i : start + i + 1] for i in range(4)], axis=1)
+
+
 def product_kernel(first, info, tiles, *refs):
     if first:
-        labels, mine, others, out, running, held, sem = refs
+        mine, others, out, running, held, sem = refs
     else:
         mine, others, degree, out, running, held, sem = refs
     count = info[0]
-    core, zh, y = info[2], info[3], info[4]
+    core = info[2]
     depth = held.shape[0]
     running[...] = jnp.zeros_like(running)
 
@@ -202,10 +181,8 @@
         q = info[SLABS + entry]
         own = q % 2 == core
         if first:
-            index = (q % 2 ^ core) * 8 + ((q // 4 + 4 - y) % 4) * 2 + (q // 2 % 2 ^ zh)
-            label = labels[pl.ds(index, 1), :]
-            chip = pl.ds(q // 2, 1)
-            value = lax.rsqrt(jnp.where(own, mine[chip, :], others[chip, :]))
+            known = jnp.where(own, mine[q // 2], others[q // 2])
+            value, label = lax.rsqrt(row_of(known, 0)), row_of(known, 4)
             value = jnp.where(label < K, value, -value)
             label = jnp.where(label < K, label, label - K)
             same = label == lax.broadcasted_iota(jnp.int32, (K, TILE), 0).astype(F32)
@@ -256,7 +233,7 @@
 
 def product(info, tiles, *operands):
     vmem = pl.BlockSpec(memory_space=pltpu.VMEM)
-    first = operands[0].dtype == F32
+    first = len(operands) == 2
     return pl.pallas_call(
         functools.partial(product_kernel, first),
         out_shape=jax.ShapeDtypeStruct(
@@ -349,34 +326,34 @@
     return jnp.dot(factor, block, precision=lax.Precision.HIGHEST, preferred_element_type=F32)
 
 
-def roots_of(info, degrees):
-    degree = degrees[pl.ds(info[5], 1), :]
+def roots_of(info, known):
+    degree = row_of(known[info[3]], 0)
     return lax.rsqrt(degree), jnp.sqrt(degree)
 
 
-def weigh_kernel(info, parts, degrees, out):
-    inv_root, root = roots_of(info, degrees)
+def weigh_kernel(info, parts, known, out):
+    inv_root, root = roots_of(info, known)
     image = jnp.sum(parts[...].astype(F32), axis=0) * inv_root
     out[:K, :] = (image * inv_root).astype(BF16)
     out[K:, :] = terms_of(weights_of(image, root))
 
 
-def middle_kernel(scale, info, parts, degrees, by_column, image, message):
-    inv_root, root = roots_of(info, degrees)
-    own = by_column[info[5]]
+def middle_kernel(scale, info, parts, known, by_column, image, message):
+    inv_root, root = roots_of(info, known)
+    own = by_column[info[3]]
     columns = [value_of(parts[c, K:, :].astype(F32)) for c in range(SLAB_TILES)]
     factor, lead = factor_of(sum(columns), scale)
     whole = jnp.sum(parts[:, :K, :].astype(F32), axis=0)
     for c in range(SLAB_TILES):
-        whole = whole + (lead_of(columns[c])[0] - lead) * own[c : c + 1, :]
+        whole = whole + (lead_of(columns[c])[0] - lead) * row_of(own[c], 0)
     block = times(factor, whole * inv_root)
     image[...] = block
     message[:, :80] = weights_of(block, root)
     message[:, 80:] = jnp.zeros((K // 2, 48), F32)
 
 
-def last_kernel(scale, info, message, image, degrees, out):
-    _, root = roots_of(info, degrees)
+def last_kernel(scale, info, message, image, known, out):
+    _, root = roots_of(info, known)
     factor, lead = factor_of(message[:, :80], scale)
     out[...] = times(factor, image[...] - lead * root)
 
@@ -496,7 +473,7 @@
     arrivals += near_q
     arrivals += [beyond_q[0], other_q[0], beyond_q[1], other_q[1], far_q[0], far_q[1]]
     arrivals = jnp.stack(arrivals)
-    head = [pair_count[0, 0], block_index, core, zh, y, slab_index // 2]
+    head = [pair_count[0, 0], block_index, core, slab_index // 2]
     info = pair_list(head, pair_rows[0, 0], pair_cols[0, 0], arrivals)
 
     own = lax.dynamic_index_in_dim(slab, block_index, 0, keepdims=False)
@@ -506,9 +483,6 @@
     give = lax.dynamic_index_in_dim(later, block_index ^ 1, 0, keepdims=False)
     across = cross(give)
     half_rows = 0.5 * jnp.sum(jnp.square(slab.astype(F32)), axis=2)
-    seeds = labels.astype(F32)[None]
-    seeds = jnp.concatenate([seeds, lax.ppermute(seeds, "zh", [(0, 1), (1, 0)])], axis=0)
-
     def both(*pieces):
         return [each for piece in pieces for each in (piece, swap_cores(piece))]
 
@@ -517,14 +491,10 @@
         return (made[0], tied[0]), tied[1:]
 
     made = build(0, info, slab, half_rows, both(own), ())
-    made, (across, below, above, seeds) = after(made, across, below, above, seeds)
+    made, (across, below, above) = after(made, across, below, above)
     near = apart(across)
     other = apart_z(jnp.where(zero, above, below))
-    seeds = [seeds, down(seeds), lax.ppermute(seeds, "y", [(i, (i + 2) % 4) for i in range(4)]), up(seeds)]
     made = build(2, info, slab, half_rows, [across, below, above], made)
-    made, seeds = after(made, *seeds)
-    seeds = jnp.concatenate(seeds, axis=0)
-    seeds = jnp.concatenate([seeds, swap_cores(seeds)], axis=0)
     made = build(5, info, slab, half_rows, [swap_cores(piece) for piece in (across, below, above)], made)
     made, (near, other, below, above) = after(made, near, other, below, above)
     beyond = apart(jnp.where(zero, below, above))
@@ -533,26 +503,25 @@
     made, (passed,) = after(made, near)
     far = apart(passed)
     made = build(9, info, slab, half_rows, [swap_cores(near), beyond, other], made)
-    made, (far, seeds) = after(made, far, seeds)
+    made, (far,) = after(made, far)
     made = build(12, info, slab, half_rows, [swap_cores(beyond), swap_cores(other), far], made)
     made = build(15, info, slab, half_rows, [swap_cores(far)], made)
     tiles, partial_degree = made
 
+    in_block = (jnp.arange(SLAB_TILES) == block_index)[:, None, None]
+    seeds = jnp.where(in_block, labels.astype(F32).reshape(1, 4, 128), 0.0)
+    sent = jnp.concatenate([partial_degree.reshape(SLAB_TILES, 4, 128), seeds], axis=1)
     by_column = lax.all_to_all(
-        jnp.broadcast_to(partial_degree[None, :, None], (8, SLAB_TILES, 1, TILE)).reshape(8 * SLAB_TILES, 1, TILE),
-        CHIPS,
-        0,
-        0,
-        tiled=True,
-    ).reshape(8, SLAB_TILES, TILE)
-    degrees = jnp.sum(by_column, axis=1)
+        jnp.broadcast_to(sent[None], (8,) + sent.shape).reshape(8 * SLAB_TILES, 8, 128), CHIPS, 0, 0, tiled=True
+    ).reshape(8, SLAB_TILES, 8, 128)
+    known = jnp.sum(by_column, axis=1)
 
     scale = 1.0 / (BLOCK_TILES * SLAB_TILES * TILE)
     block = jax.ShapeDtypeStruct((K, TILE), F32)
-    running = product(info, tiles, seeds, degrees, swap_cores(degrees))
+    running = product(info, tiles, known, swap_cores(known))
     parts = lax.all_to_all(running, COL, 0, 0, tiled=True)
     weighed = local(
-        weigh_kernel, "weigh", jax.ShapeDtypeStruct((K + 16, TILE), BF16), info, parts, degrees
+        weigh_kernel, "weigh", jax.ShapeDtypeStruct((K + 16, TILE), BF16), info, parts, known
     )
     running = product(info, tiles, *share_row(weighed), partial_degree)
     parts = lax.all_to_all(running, COL, 0, 0, tiled=True)
@@ -562,11 +531,11 @@
         (block, jax.ShapeDtypeStruct((K // 2, 128), F32)),
         info,
         parts,
-        degrees,
+        known,
         by_column,
     )
     return local(
-        functools.partial(last_kernel, scale), "last", block, info, sum_all(message), image, degrees
+        functools.partial(last_kernel, scale), "last", block, info, sum_all(message), image, known
     )
 
 

time: 211 us -> 200 us (0.948)
  Pallas kernels: 43.9 us -> 32.8 us
  starting transfers between devices: 41.5 us -> 37.1 us
  blocking collectives: 69.2 us -> 72.7 us
  local copies, waits for them, and re-layouts: 4.07 us -> 7.31 us
  other arithmetic: 9.32 us -> 6.37 us
    pallas_call x7, Pallas kernels: 26.8 us -> 17.1 us  [build(): pl.pallas_call(functools.partial(build_kernel, first, arrived), out_shape...]
    ppermute x13 -> x12, starting transfers between devices: 18.5 us -> 14.7 us  [swap_cores(): return lax.ppermute(value, 'core', [(0, 1), (1, 0)])]
    all_to_all x2, blocking collectives: 35.4 us -> 38.8 us  [share(): lax.all_to_all(jnp.broadcast_to(value[None], (size,) + value.shape), axes...]
    unnamed x1 -> x10, local copies, waits for them, and re-layouts: 0.01 us -> 3.4 us
    all_to_all x1, waiting for transfers between devices: 11.6 us -> 8.35 us  [shards(): parts = lax.all_to_all(running, COL, 0, 0, tiled=True)]
    ppermute x3, starting transfers between devices: 6.67 us -> 9.43 us  [apart(): lax.ppermute(value, ('y', 'core'), [(2 * i + k, 2 * ((i + 1 + 2 * k) % 4)...]
    all_to_all x1, blocking collectives: 21.3 us -> 24.1 us  [shards(): lax.all_to_all(jnp.broadcast_to(sent[None], (8,) + sent.shape).reshape(8...]
    ppermute x3, waiting for transfers between devices: 13.7 us -> 16.3 us  [apart(): lax.ppermute(value, ('y', 'core'), [(2 * i + k, 2 * ((i + 1 + 2 * k) % 4)...]
  transfers between devices with their start and end apart: 26 -> 21, of which waited for: 12 -> 11; matrix products, arithmetic and copies ran while one was open for 5% -> 4% of each run, Pallas kernels for 11% -> 8%
where the time goes in v9:
time: 200 us; the launch traced here: 199 us
  blocking collectives  72.7 us (36%)
  waiting for transfers between devices  41.6 us (21%)
  starting transfers between devices  37.1 us (19%)
  Pallas kernels  32.8 us (16%)
  local copies, waits for them, and re-layouts  7.31 us (4%)
  other arithmetic  6.37 us (3%)
    all_to_all x2, blocking collectives, share(): lax.all_to_all(jnp.broadcast_to(value[None], (size,) + value.shape), axes...  38.8 us
    all_to_all x1, blocking collectives, shards(): lax.all_to_all(jnp.broadcast_to(sent[None], (8,) + sent.shape).reshape(8...  24.1 us
    pallas_call x7, Pallas kernels, build(): pl.pallas_call(functools.partial(build_kernel, first, arrived), out_shape...  17.1 us
    ppermute x3, waiting for transfers between devices, apart(): lax.ppermute(value, ('y', 'core'), [(2 * i + k, 2 * ((i + 1 + 2 * k) % 4)...  16.3 us
    ppermute x12, starting transfers between devices, swap_cores(): return lax.ppermute(value, 'core', [(0, 1), (1, 0)])  14.7 us
    all_to_all x1, blocking collectives, shards(): parts = lax.all_to_all(running, COL, 0, 0, tiled=True)  9.87 us
    ppermute x3, starting transfers between devices, apart(): lax.ppermute(value, ('y', 'core'), [(2 * i + k, 2 * ((i + 1 + 2 * k) % 4)...  9.43 us
    all_to_all x1, waiting for transfers between devices, shards(): parts = lax.all_to_all(running, COL, 0, 0, tiled=True)  8.35 us
  transfers between devices with their start and end apart: 21, of which 11 were waited for; matrix products, arithmetic and copies ran while one was open for 4% of the time, Pallas kernels for 8%

profile of v9, /device:TPU:1, one launch (start us, length us, event | category | flops | bytes accessed | tf_op | source)
XLA Modules:
  0.0 198.9 jit_solution(5905582521900583792)
XLA Ops:
  1.3 1.5 collective-permute-start
  5.7 2.3 %dynamic-slice_bitcast_fusion = bf16[512,1024]{1,0:T(8,128)(2,1)} fusion(bf16[8,512,1024]{2,1,0:T(8,128)(2,1)} %bitcast.37, s32[]{:T(128)S(6)} %select_n.198), kind=kLoop, calls=%fused_computation.1 | loop fusion | bytes 2097156 | tf_op jit(solution)/shard_map/jit(dynamic_index_in_dim)/squeeze | solution.py:483
  7.9 3.8 %collective-permute-start.1 = (bf16[512,1024]{1,0:T(8,128)(2,1)}, bf16[512,1024]{1,0:T(8,128)(2,1)}, u32[]{:S(2)}, u32[]{:S(2)}) collective-permute-start(bf16[512,1024]{1,0:T(8,128)(2,1)} %dynamic-slice_bitcast_fusion), channel_id=1, source_target_pairs={{0,17},{17,0},{1,16},{16,1},{2,19},{19,2},{3,18},{18,3},{4,21},{21... | collective-permute-start | bytes 3145736 | tf_op jit(solution)/shard_map/ppermute | solution.py:426
  11.7 5.1 %multiply_reduce_fusion = f32[4096]{0:T(1024)S(1)} fusion(bf16[4096,1024]{1,0:T(8,128)(2,1)} %param.5), kind=kLoop, calls=%fused_computation | loop fusion | flops 12578816 | bytes 8404992 | tf_op jit(solution)/shard_map/reduce_sum | solution.py:485
  18.6 3.4 %copy-done = bf16[4096,1024]{1,0:T(8,128)(2,1)S(1)} copy-done((bf16[4096,1024]{1,0:T(8,128)(2,1)S(1)}, bf16[4096,1024]{1,0:T(8,128)(2,1)}, u32[]{:S(2)}) %copy-start) | copy-done | bytes 8388632
  22.0 5.5 %build_tiles.7 = (bf16[24,512,512]{2,1,0:T(8,128)(2,1)}, f32[8,512]{1,0:T(8,128)S(1)}) custom-call(s32[121]{0:T(128)S(1)} %concatenate.13.info, bf16[8,512,1024]{2,1,0:T(8,128)(2,1)S(1)} %bitcast.38, f32[8,512]{1,0:T(8,128)S(1)} %mul.134.half_rows, bf16[512,1024]{1,0:T(8,128)(2,1)S(1)} %dynamic-slice_bitcast_fusion.1.refs_0_, ...), custom_call_target="tpu_custom_call" | custom-call | flops 1610612736 | bytes 7864320 | tf_op jit(solution)/shard_map/build_tiles/pallas_call | solution.py:112
  27.5 7.4 %collective-permute-done.1.refs_0_ = bf16[512,1024]{1,0:T(8,128)(2,1)} collective-permute-done((bf16[512,1024]{1,0:T(8,128)(2,1)}, bf16[512,1024]{1,0:T(8,128)(2,1)}, u32[]{:S(2)}, u32[]{:S(2)}) %collective-permute-start.1) | collective-permute-done | bytes 1048608 | tf_op jit(solution)/shard_map/ppermute | solution.py:426
  36.8 2.7 %collective-permute-start.8 = (bf16[512,1024]{1,0:T(8,128)(2,1)S(1)}, bf16[512,1024]{1,0:T(8,128)(2,1)S(1)}, u32[]{:S(2)}, u32[]{:S(2)}) collective-permute-start(bf16[512,1024]{1,0:T(8,128)(2,1)S(1)} %broadcast_select_fusion.1), channel_id=1, source_target_pairs={{0,1},{8,25},{1,16},{9,8},{16,17},{24,9},{17,0},{25,24},{2,3},{10,... | collective-permute-start | bytes 3145736 | tf_op jit(solution)/shard_map/ppermute | solution.py:422
  39.5 1.5 collective-permute-start.7
  41.0 5.3 %build_tiles.8 = (bf16[24,512,512]{2,1,0:T(8,128)(2,1)}, f32[8,512]{1,0:T(8,128)S(1)}) custom-call(s32[121]{0:T(128)S(1)} %concatenate.13.info, bf16[8,512,1024]{2,1,0:T(8,128)(2,1)S(1)} %bitcast.39, f32[8,512]{1,0:T(8,128)S(1)} %mul.134.half_rows, bf16[512,1024]{1,0:T(8,128)(2,1)} %collective-permute-done.1.refs_0_, ...), custom_call_target="tpu_custom_call", output_to_operand_aliasing={{0}: (6, {})} | custom-call | flops 2147483648 | bytes 10485760 | tf_op jit(solution)/shard_map/build_tiles/pallas_call | solution.py:112
  47.1 4.1 %collective-permute-done.8 = bf16[512,1024]{1,0:T(8,128)(2,1)S(1)} collective-permute-done((bf16[512,1024]{1,0:T(8,128)(2,1)S(1)}, bf16[512,1024]{1,0:T(8,128)(2,1)S(1)}, u32[]{:S(2)}, u32[]{:S(2)}) %collective-permute-start.8) | collective-permute-done | bytes 1048608 | tf_op jit(solution)/shard_map/ppermute | solution.py:422
  51.2 2.1 %collective-permute-done.7.refs_0_ = bf16[512,1024]{1,0:T(8,128)(2,1)S(1)} collective-permute-done((bf16[512,1024]{1,0:T(8,128)(2,1)}, bf16[512,1024]{1,0:T(8,128)(2,1)S(1)}, u32[]{:S(2)}, u32[]{:S(2)}) %collective-permute-start.7) | collective-permute-done | bytes 1048608 | tf_op jit(solution)/shard_map/ppermute | solution.py:409
  53.5 2.8 %collective-permute-start.10 = (bf16[512,1024]{1,0:T(8,128)(2,1)S(1)}, bf16[512,1024]{1,0:T(8,128)(2,1)S(1)}, u32[]{:S(2)}, u32[]{:S(2)}) collective-permute-start(bf16[512,1024]{1,0:T(8,128)(2,1)S(1)} %broadcast_select_fusion), channel_id=1, source_target_pairs={{0,32},{8,104},{32,64},{40,8},{64,96},{72,40},{96,0},{104,72},{1,3... | collective-permute-start | bytes 3145736 | tf_op jit(solution)/shard_map/ppermute | solution.py:409
  57.0 5.2 %collective-permute-start.12 = (bf16[512,1024]{1,0:T(8,128)(2,1)S(1)}, bf16[512,1024]{1,0:T(8,128)(2,1)S(1)}, u32[]{:S(2)}, u32[]{:S(2)}) collective-permute-start(bf16[512,1024]{1,0:T(8,128)(2,1)S(1)} %collective-permute-done.7.refs_0_), channel_id=1, source_target_pairs={{0,32},{8,104},{32,64},{40,8},{64,96},{72,40},{96,0},{104,72},{1,3... | collective-permute-start | bytes 3145736 | tf_op jit(solution)/shard_map/ppermute | solution.py:409
  62.2 5.8 %collective-permute-done.10.refs_1_ = bf16[512,1024]{1,0:T(8,128)(2,1)S(1)} collective-permute-done((bf16[512,1024]{1,0:T(8,128)(2,1)S(1)}, bf16[512,1024]{1,0:T(8,128)(2,1)S(1)}, u32[]{:S(2)}, u32[]{:S(2)}) %collective-permute-start.10) | collective-permute-done | bytes 1048608 | tf_op jit(solution)/shard_map/ppermute | solution.py:409
  68.0 1.4 collective-permute-start.14
  70.8 8.4 %collective-permute-done.12.refs_2_ = bf16[512,1024]{1,0:T(8,128)(2,1)S(1)} collective-permute-done((bf16[512,1024]{1,0:T(8,128)(2,1)S(1)}, bf16[512,1024]{1,0:T(8,128)(2,1)S(1)}, u32[]{:S(2)}, u32[]{:S(2)}) %collective-permute-start.12) | collective-permute-done | bytes 1048608 | tf_op jit(solution)/shard_map/ppermute | solution.py:409
  80.7 3.6 %build_tiles.12 = (bf16[24,512,512]{2,1,0:T(8,128)(2,1)}, f32[8,512]{1,0:T(8,128)S(1)}) custom-call(s32[121]{0:T(128)S(1)} %concatenate.13.info, bf16[8,512,1024]{2,1,0:T(8,128)(2,1)S(1)} %bitcast.43, f32[8,512]{1,0:T(8,128)S(1)} %mul.134.half_rows, bf16[512,1024]{1,0:T(8,128)(2,1)S(1)} %collective-permute-done.14.refs_0_, ...), custom_call_target="tpu_custom_call", output_to_operand_aliasing={{0}: (6, {})} | custom-call | flops 2147483648 | bytes 10485760 | tf_op jit(solution)/shard_map/build_tiles/pallas_call | solution.py:112
  85.1 24.1 %all_to_all.25 = f32[64,8,128]{2,1,0:T(8,128)S(1)} all-to-all(f32[64,8,128]{2,1,0:T(8,128)S(1)} %bitcast.47), channel_id=1, replica_groups=mesh['y'=4,'zh'=2,'core'=2,'x'=4,'zl'=2] {'y','zh','x','zl'}, dimensions={0} | all-to-all | bytes 524288 | tf_op jit(solution)/shard_map/all_to_all | solution.py:514
  110.4 3.1 %product.2 = bf16[8,64,512]{2,1,0:T(8,128)(2,1)S(1)} custom-call(s32[121]{0:T(128)S(1)} %concatenate.13.info, bf16[24,512,512]{2,1,0:T(8,128)(2,1)} %get-tuple-element.63.tiles, f32[8,8,128]{2,1,0:T(8,128)S(1)} %bitcast_reduce_fusion.refs_0_.known, f32[8,8,128]{2,1,0:T(8,128)S(1)} %collective-permute-done.16.refs_1_), custom_call_target="tpu_custom_call" | custom-call | tf_op jit(solution)/shard_map/product/pallas_call | solution.py:237
  113.6 9.9 %all_to_all.26.parts = bf16[8,64,512]{2,1,0:T(8,128)(2,1)S(1)} all-to-all(bf16[8,64,512]{2,1,0:T(8,128)(2,1)S(1)} %product.2), channel_id=1, replica_groups=mesh['y'=4,'zh'=2,'core'=2,'x'=4,'zl'=2] {'x','zl'}, dimensions={0} | all-to-all | bytes 1048576 | tf_op jit(solution)/shard_map/all_to_all | solution.py:522
  124.6 19.1 %all_to_all.27.refs_0_ = bf16[8,80,512]{2,1,0:T(8,128)(2,1)S(1)} all-to-all(bf16[8,80,512]{2,1,0:T(8,128)(2,1)S(1)} %broadcast_in_dim.112), channel_id=1, replica_groups=mesh['y'=4,'zh'=2,'core'=2,'x'=4,'zl'=2] {'y','zh'}, dimensions={0} | all-to-all | bytes 1310720 | tf_op jit(solution)/shard_map/all_to_all | solution.py:379
  143.7 3.0 %collective-permute-start.17 = (bf16[8,80,512]{2,1,0:T(8,128)(2,1)S(1)}, bf16[8,80,512]{2,1,0:T(8,128)(2,1)S(1)}, u32[]{:S(2)}, u32[]{:S(2)}) collective-permute-start(bf16[8,80,512]{2,1,0:T(8,128)(2,1)S(1)} %all_to_all.27.refs_0_), channel_id=1, source_target_pairs={{0,8},{8,0},{1,9},{9,1},{2,10},{10,2},{3,11},{11,3},{4,12},{12,4},... | collective-permute-start | bytes 1966088 | tf_op jit(solution)/shard_map/ppermute | solution.py:374
  146.7 1.7 collective-permute-done.17.refs_1_
  148.5 4.3 %product.3 = bf16[8,80,512]{2,1,0:T(8,128)(2,1)} custom-call(s32[121]{0:T(128)S(1)} %concatenate.13.info, bf16[24,512,512]{2,1,0:T(8,128)(2,1)} %get-tuple-element.63.tiles, bf16[8,80,512]{2,1,0:T(8,128)(2,1)S(1)} %all_to_all.27.refs_0_, bf16[8,80,512]{2,1,0:T(8,128)(2,1)S(1)} %collective-permute-done.17.refs_1_, f32[8,512]{1,0:T(8,128)S(1)} %get-tuple-element.64.refs_2_), custom_call_target="tpu_custom_call" | custom-call | tf_op jit(solution)/shard_map/product/pallas_call | solution.py:237
  152.8 3.6 %all-to-all-start.3 = ((bf16[8,80,512]{2,1,0:T(8,128)(2,1)}), bf16[8,80,512]{2,1,0:T(8,128)(2,1)S(1)}, u32[]{:S(2)}, u32[]{:S(2)}) async-start(bf16[8,80,512]{2,1,0:T(8,128)(2,1)} %product.3), calls=%async_computation.3 | async-start | bytes 1310720 | tf_op jit(solution)/shard_map/all_to_all | solution.py:527
  156.4 8.4 %all-to-all-done.3.parts = bf16[8,80,512]{2,1,0:T(8,128)(2,1)S(1)} async-done(((bf16[8,80,512]{2,1,0:T(8,128)(2,1)}), bf16[8,80,512]{2,1,0:T(8,128)(2,1)S(1)}, u32[]{:S(2)}, u32[]{:S(2)}) %all-to-all-start.3) | async-done | bytes 655392 | tf_op jit(solution)/shard_map/all_to_all | solution.py:527
  164.7 3.6 %middle.1 = (f32[64,512]{1,0:T(8,128)S(1)}, f32[32,128]{1,0:T(8,128)S(1)}) custom-call(s32[121]{0:T(128)S(1)} %concatenate.13.info, bf16[8,80,512]{2,1,0:T(8,128)(2,1)S(1)} %all-to-all-done.3.parts, f32[8,8,128]{2,1,0:T(8,128)S(1)} %bitcast_reduce_fusion.refs_0_.known, f32[8,8,8,128]{3,2,1,0:T(8,128)S(1)} %bitcast.45), custom_call_target="tpu_custom_call" | custom-call | tf_op jit(solution)/shard_map/middle/pallas_call | solution.py:363
  168.3 3.6 %collective-permute-start.18 = (f32[16,128]{1,0:T(8,128)S(1)}, f32[16,128]{1,0:T(8,128)S(1)}, u32[]{:S(2)}, u32[]{:S(2)}) collective-permute-start(f32[16,128]{1,0:T(8,128)S(1)} %constant_dynamic-slice_fusion), channel_id=1, source_target_pairs={{0,8},{8,0},{1,9},{9,1},{2,10},{10,2},{3,11},{11,3},{4,12},{12,4},... | collective-permute-start | bytes 24584 | tf_op jit(solution)/shard_map/ppermute | solution.py:374
  172.8 19.7 %all_to_all.28 = f32[64,16,128]{2,1,0:T(8,128)S(1)} all-to-all(f32[64,16,128]{2,1,0:T(8,128)S(1)} %broadcast_in_dim.113), channel_id=1, replica_groups=mesh['y'=4,'zh'=2,'core'=2,'x'=4,'zl'=2] {'y','zh','x','zl'}, dimensions={0} | all-to-all | bytes 1048576 | tf_op jit(solution)/shard_map/all_to_all | solution.py:379
  192.6 2.0 collective-permute-start.19
  195.4 3.5 %last.1 = f32[64,512]{1,0:T(8,128)} custom-call(s32[121]{0:T(128)S(1)} %concatenate.13.info, f32[32,128]{1,0:T(8,128)S(1)} %pad_maximum_fusion.1.message, f32[64,512]{1,0:T(8,128)S(1)} %get-tuple-element.66.image, f32[8,8,128]{2,1,0:T(8,128)S(1)} %bitcast_reduce_fusion.refs_0_.known), custom_call_target="tpu_custom_call" | custom-call | tf_op jit(solution)/shard_map/last/pallas_call | solution.py:363
  (69 shorter events, 16.5 us)
Async XLA Ops:
  0.0 17.6 %copy-start.3 = (s32[1,1,24]{2,1,0:T(1,128)S(1)}, s32[1,1,24]{2,1,0:T(1,128)}, u32[]{:S(2)}) copy-start(s32[1,1,24]{2,1,0:T(1,128)} %param.8) | copy-start | bytes 292
  0.0 17.9 %copy-start.4 = (s32[1,1,24]{2,1,0:T(1,128)S(1)}, s32[1,1,24]{2,1,0:T(1,128)}, u32[]{:S(2)}) copy-start(s32[1,1,24]{2,1,0:T(1,128)} %param.7) | copy-start | bytes 292
  1.3 17.3 %collective-permute-start = (bf16[512,1024]{1,0:T(8,128)(2,1)S(1)}, bf16[512,1024]{1,0:T(8,128)(2,1)}, u32[]{:S(2)}, u32[]{:S(2)}) collective-permute-start(bf16[512,1024]{1,0:T(8,128)(2,1)S(1)} %dynamic-slice_bitcast_fusion.1.refs_0_), channel_id=1, source_target_pairs={{0,8},{8,0},{1,9},{9,1},{2,10},{10,2},{3,11},{11,3},{4,12},{12,4},... | collective-permute-start | bytes 3145736 | tf_op jit(solution)/shard_map/ppermute | solution.py:374
  2.8 32.2 %collective-permute-start.2 = (bf16[512,1024]{1,0:T(8,128)(2,1)S(1)}, bf16[512,1024]{1,0:T(8,128)(2,1)S(1)}, u32[]{:S(2)}, u32[]{:S(2)}) collective-permute-start(bf16[512,1024]{1,0:T(8,128)(2,1)S(1)} %dynamic-slice_bitcast_fusion.1.refs_0_), channel_id=1, source_target_pairs={{0,32},{32,64},{64,96},{96,0},{1,33},{33,65},{65,97},{97,1},{2,34}... | collective-permute-start | bytes 3145736 | tf_op jit(solution)/shard_map/ppermute | solution.py:401
  4.2 30.8 %collective-permute-start.3 = (bf16[512,1024]{1,0:T(8,128)(2,1)S(1)}, bf16[512,1024]{1,0:T(8,128)(2,1)S(1)}, u32[]{:S(2)}, u32[]{:S(2)}) collective-permute-start(bf16[512,1024]{1,0:T(8,128)(2,1)S(1)} %dynamic-slice_bitcast_fusion.1.refs_0_), channel_id=1, source_target_pairs={{0,96},{32,0},{64,32},{96,64},{1,97},{33,1},{65,33},{97,65},{2,98}... | collective-permute-start | bytes 3145736 | tf_op jit(solution)/shard_map/ppermute | solution.py:405
  7.9 27.1 %collective-permute-start.1 = (bf16[512,1024]{1,0:T(8,128)(2,1)}, bf16[512,1024]{1,0:T(8,128)(2,1)}, u32[]{:S(2)}, u32[]{:S(2)}) collective-permute-start(bf16[512,1024]{1,0:T(8,128)(2,1)} %dynamic-slice_bitcast_fusion), channel_id=1, source_target_pairs={{0,17},{17,0},{1,16},{16,1},{2,19},{19,2},{3,18},{18,3},{4,21},{21... | collective-permute-start | bytes 3145736 | tf_op jit(solution)/shard_map/ppermute | solution.py:426
  18.6 3.4 %copy-start = (bf16[4096,1024]{1,0:T(8,128)(2,1)S(1)}, bf16[4096,1024]{1,0:T(8,128)(2,1)}, u32[]{:S(2)}) copy-start(bf16[4096,1024]{1,0:T(8,128)(2,1)} %param.5) | copy-start | bytes 25165828
  22.0 19.0 %copy-start.1 = (bf16[4096,1024]{1,0:T(8,128)(2,1)S(1)}, bf16[4096,1024]{1,0:T(8,128)(2,1)}, u32[]{:S(2)}) copy-start(bf16[4096,1024]{1,0:T(8,128)(2,1)} %param.5) | copy-start | bytes 25165828
  35.0 11.3 %collective-permute-start.4 = (bf16[512,1024]{1,0:T(8,128)(2,1)}, bf16[512,1024]{1,0:T(8,128)(2,1)S(1)}, u32[]{:S(2)}, u32[]{:S(2)}) collective-permute-start(bf16[512,1024]{1,0:T(8,128)(2,1)} %collective-permute-done.1.refs_0_), channel_id=1, source_target_pairs={{0,8},{8,0},{1,9},{9,1},{2,10},{10,2},{3,11},{11,3},{4,12},{12,4},... | collective-permute-start | bytes 3145736 | tf_op jit(solution)/shard_map/ppermute | solution.py:374
  36.1 10.1 %collective-permute-start.5 = (bf16[512,1024]{1,0:T(8,128)(2,1)S(1)}, bf16[512,1024]{1,0:T(8,128)(2,1)S(1)}, u32[]{:S(2)}, u32[]{:S(2)}) collective-permute-start(bf16[512,1024]{1,0:T(8,128)(2,1)S(1)} %collective-permute-done.2.refs_1_), channel_id=1, source_target_pairs={{0,8},{8,0},{1,9},{9,1},{2,10},{10,2},{3,11},{11,3},{4,12},{12,4},... | collective-permute-start | bytes 3145736 | tf_op jit(solution)/shard_map/ppermute | solution.py:374
  36.2 10.1 %collective-permute-start.6 = (bf16[512,1024]{1,0:T(8,128)(2,1)S(1)}, bf16[512,1024]{1,0:T(8,128)(2,1)S(1)}, u32[]{:S(2)}, u32[]{:S(2)}) collective-permute-start(bf16[512,1024]{1,0:T(8,128)(2,1)S(1)} %collective-permute-done.3.refs_2_), channel_id=1, source_target_pairs={{0,8},{8,0},{1,9},{9,1},{2,10},{10,2},{3,11},{11,3},{4,12},{12,4},... | collective-permute-start | bytes 3145736 | tf_op jit(solution)/shard_map/ppermute | solution.py:374
  36.8 14.5 %collective-permute-start.8 = (bf16[512,1024]{1,0:T(8,128)(2,1)S(1)}, bf16[512,1024]{1,0:T(8,128)(2,1)S(1)}, u32[]{:S(2)}, u32[]{:S(2)}) collective-permute-start(bf16[512,1024]{1,0:T(8,128)(2,1)S(1)} %broadcast_select_fusion.1), channel_id=1, source_target_pairs={{0,1},{8,25},{1,16},{9,8},{16,17},{24,9},{17,0},{25,24},{2,3},{10,... | collective-permute-start | bytes 3145736 | tf_op jit(solution)/shard_map/ppermute | solution.py:422
  39.5 13.9 %collective-permute-start.7 = (bf16[512,1024]{1,0:T(8,128)(2,1)}, bf16[512,1024]{1,0:T(8,128)(2,1)S(1)}, u32[]{:S(2)}, u32[]{:S(2)}) collective-permute-start(bf16[512,1024]{1,0:T(8,128)(2,1)} %collective-permute-done.1.refs_0_), channel_id=1, source_target_pairs={{0,32},{8,104},{32,64},{40,8},{64,96},{72,40},{96,0},{104,72},{1,3... | collective-permute-start | bytes 3145736 | tf_op jit(solution)/shard_map/ppermute | solution.py:409
  53.5 14.5 %collective-permute-start.10 = (bf16[512,1024]{1,0:T(8,128)(2,1)S(1)}, bf16[512,1024]{1,0:T(8,128)(2,1)S(1)}, u32[]{:S(2)}, u32[]{:S(2)}) collective-permute-start(bf16[512,1024]{1,0:T(8,128)(2,1)S(1)} %broadcast_select_fusion), channel_id=1, source_target_pairs={{0,32},{8,104},{32,64},{40,8},{64,96},{72,40},{96,0},{104,72},{1,3... | collective-permute-start | bytes 3145736 | tf_op jit(solution)/shard_map/ppermute | solution.py:409
  56.2 13.9 %collective-permute-start.11 = (bf16[512,1024]{1,0:T(8,128)(2,1)S(1)}, bf16[512,1024]{1,0:T(8,128)(2,1)S(1)}, u32[]{:S(2)}, u32[]{:S(2)}) collective-permute-start(bf16[512,1024]{1,0:T(8,128)(2,1)S(1)} %collective-permute-done.8), channel_id=1, source_target_pairs={{0,1},{8,25},{1,16},{9,8},{16,17},{24,9},{17,0},{25,24},{2,3},{10,... | collective-permute-start | bytes 3145736 | tf_op jit(solution)/shard_map/ppermute | solution.py:422
  56.3 13.8 %collective-permute-start.9 = (bf16[512,1024]{1,0:T(8,128)(2,1)S(1)}, bf16[512,1024]{1,0:T(8,128)(2,1)S(1)}, u32[]{:S(2)}, u32[]{:S(2)}) collective-permute-start(bf16[512,1024]{1,0:T(8,128)(2,1)S(1)} %collective-permute-done.7.refs_0_), channel_id=1, source_target_pairs={{0,8},{8,0},{1,9},{9,1},{2,10},{10,2},{3,11},{11,3},{4,12},{12,4},... | collective-permute-start | bytes 3145736 | tf_op jit(solution)/shard_map/ppermute | solution.py:374
  57.0 23.7 %copy-start.2 = (s32[512]{0:T(512)S(1)}, s32[512]{0:T(512)}, u32[]{:S(2)}) copy-start(s32[512]{0:T(512)} %param.6) | copy-start | bytes 6148
  57.0 22.2 %collective-permute-start.12 = (bf16[512,1024]{1,0:T(8,128)(2,1)S(1)}, bf16[512,1024]{1,0:T(8,128)(2,1)S(1)}, u32[]{:S(2)}, u32[]{:S(2)}) collective-permute-start(bf16[512,1024]{1,0:T(8,128)(2,1)S(1)} %collective-permute-done.7.refs_0_), channel_id=1, source_target_pairs={{0,32},{8,104},{32,64},{40,8},{64,96},{72,40},{96,0},{104,72},{1,3... | collective-permute-start | bytes 3145736 | tf_op jit(solution)/shard_map/ppermute | solution.py:409
  68.0 12.8 %collective-permute-start.14 = (bf16[512,1024]{1,0:T(8,128)(2,1)S(1)}, bf16[512,1024]{1,0:T(8,128)(2,1)S(1)}, u32[]{:S(2)}, u32[]{:S(2)}) collective-permute-start(bf16[512,1024]{1,0:T(8,128)(2,1)S(1)} %collective-permute-done.10.refs_1_), channel_id=1, source_target_pairs={{0,8},{8,0},{1,9},{9,1},{2,10},{10,2},{3,11},{11,3},{4,12},{12,4},... | collective-permute-start | bytes 3145736 | tf_op jit(solution)/shard_map/ppermute | solution.py:374
  70.2 10.6 %collective-permute-start.15 = (bf16[512,1024]{1,0:T(8,128)(2,1)S(1)}, bf16[512,1024]{1,0:T(8,128)(2,1)S(1)}, u32[]{:S(2)}, u32[]{:S(2)}) collective-permute-start(bf16[512,1024]{1,0:T(8,128)(2,1)S(1)} %collective-permute-done.11.refs_2_), channel_id=1, source_target_pairs={{0,8},{8,0},{1,9},{9,1},{2,10},{10,2},{3,11},{11,3},{4,12},{12,4},... | collective-permute-start | bytes 3145736 | tf_op jit(solution)/shard_map/ppermute | solution.py:374
  79.2 5.2 %collective-permute-start.13 = (bf16[512,1024]{1,0:T(8,128)(2,1)S(1)}, bf16[512,1024]{1,0:T(8,128)(2,1)S(1)}, u32[]{:S(2)}, u32[]{:S(2)}) collective-permute-start(bf16[512,1024]{1,0:T(8,128)(2,1)S(1)} %collective-permute-done.12.refs_2_), channel_id=1, source_target_pairs={{0,8},{8,0},{1,9},{9,1},{2,10},{10,2},{3,11},{11,3},{4,12},{12,4},... | collective-permute-start | bytes 3145736 | tf_op jit(solution)/shard_map/ppermute | solution.py:374
  109.2 1.3 collective-permute-start.16
  143.7 4.7 %collective-permute-start.17 = (bf16[8,80,512]{2,1,0:T(8,128)(2,1)S(1)}, bf16[8,80,512]{2,1,0:T(8,128)(2,1)S(1)}, u32[]{:S(2)}, u32[]{:S(2)}) collective-permute-start(bf16[8,80,512]{2,1,0:T(8,128)(2,1)S(1)} %all_to_all.27.refs_0_), channel_id=1, source_target_pairs={{0,8},{8,0},{1,9},{9,1},{2,10},{10,2},{3,11},{11,3},{4,12},{12,4},... | collective-permute-start | bytes 1966088 | tf_op jit(solution)/shard_map/ppermute | solution.py:374
  152.8 11.9 %all-to-all-start.3 = ((bf16[8,80,512]{2,1,0:T(8,128)(2,1)}), bf16[8,80,512]{2,1,0:T(8,128)(2,1)S(1)}, u32[]{:S(2)}, u32[]{:S(2)}) async-start(bf16[8,80,512]{2,1,0:T(8,128)(2,1)} %product.3), calls=%async_computation.3 | async-start | bytes 1310720 | tf_op jit(solution)/shard_map/all_to_all | solution.py:527
  168.3 4.4 %collective-permute-start.18 = (f32[16,128]{1,0:T(8,128)S(1)}, f32[16,128]{1,0:T(8,128)S(1)}, u32[]{:S(2)}, u32[]{:S(2)}) collective-permute-start(f32[16,128]{1,0:T(8,128)S(1)} %constant_dynamic-slice_fusion), channel_id=1, source_target_pairs={{0,8},{8,0},{1,9},{9,1},{2,10},{10,2},{3,11},{11,3},{4,12},{12,4},... | collective-permute-start | bytes 24584 | tf_op jit(solution)/shard_map/ppermute | solution.py:374
  192.6 2.8 %collective-permute-start.19 = (f32[16,128]{1,0:T(8,128)S(1)}, f32[16,128]{1,0:T(8,128)S(1)}, u32[]{:S(2)}, u32[]{:S(2)}) collective-permute-start(f32[16,128]{1,0:T(8,128)S(1)} %reduce_sum.99), channel_id=1, source_target_pairs={{0,8},{8,0},{1,9},{9,1},{2,10},{10,2},{3,11},{11,3},{4,12},{12,4},... | collective-permute-start | bytes 24584 | tf_op jit(solution)/shard_map/ppermute | solution.py:374

commit v10 on v9

--- a/solution.py
+++ b/solution.py
@@ -495,14 +495,13 @@
     near = apart(across)
     other = apart_z(jnp.where(zero, above, below))
     made = build(2, info, slab, half_rows, [across, below, above], made)
+    made, (passed,) = after(made, jnp.where(zero, below, above))
+    beyond = apart(passed)
     made = build(5, info, slab, half_rows, [swap_cores(piece) for piece in (across, below, above)], made)
-    made, (near, other, below, above) = after(made, near, other, below, above)
-    beyond = apart(jnp.where(zero, below, above))
+    made, (near, other) = after(made, near, other)
+    far = apart(near)
     other = apart_z(other)
-    made = build(8, info, slab, half_rows, [near], made)
-    made, (passed,) = after(made, near)
-    far = apart(passed)
-    made = build(9, info, slab, half_rows, [swap_cores(near), beyond, other], made)
+    made = build(8, info, slab, half_rows, [near, swap_cores(near), beyond, other], made)
     made, (far,) = after(made, far)
     made = build(12, info, slab, half_rows, [swap_cores(beyond), swap_cores(other), far], made)
     made = build(15, info, slab, half_rows, [swap_cores(far)], made)

time: 200 us -> 197 us (0.985)
  Pallas kernels: 32.8 us -> 26.9 us
  blocking collectives: 72.7 us -> 77.5 us
    pallas_call x7 -> x6, Pallas kernels: 17.1 us -> 12.4 us  [build(): pl.pallas_call(functools.partial(build_kernel, first, arrived), out_shape...]
    ppermute x12, starting transfers between devices: 14.7 us -> 11.1 us  [swap_cores(): return lax.ppermute(value, 'core', [(0, 1), (1, 0)])]
    all_to_all x1, blocking collectives: 24.1 us -> 27.5 us  [shards(): lax.all_to_all(jnp.broadcast_to(sent[None], (8,) + sent.shape).reshape(8...]
    all_to_all x1, blocking collectives: 9.87 us -> 12.7 us  [shards(): parts = lax.all_to_all(running, COL, 0, 0, tiled=True)]
    all_to_all x1, waiting for transfers between devices: 8.35 us -> 10.6 us  [shards(): parts = lax.all_to_all(running, COL, 0, 0, tiled=True)]
    ppermute x2, waiting for transfers between devices: 4.91 us -> 2.71 us  [apart_z(): return lax.ppermute(value, ('zh', 'core', 'zl'), moves)]
  transfers between devices with their start and end apart: 21 -> 21, of which waited for: 11 -> 10; matrix products, arithmetic and copies ran while one was open for 4% -> 4% of each run, Pallas kernels for 8% -> 6%
where the time goes in v10:
time: 197 us; the launch traced here: 196 us
  blocking collectives  77.5 us (39%)
  waiting for transfers between devices  41.8 us (21%)
  starting transfers between devices  35.6 us (18%)
  Pallas kernels  26.9 us (14%)
  local copies, waits for them, and re-layouts  7.31 us (4%)
  other arithmetic  6.29 us (3%)
    all_to_all x2, blocking collectives, share(): lax.all_to_all(jnp.broadcast_to(value[None], (size,) + value.shape), axes...  37.3 us
    all_to_all x1, blocking collectives, shards(): lax.all_to_all(jnp.broadcast_to(sent[None], (8,) + sent.shape).reshape(8...  27.5 us
    ppermute x3, waiting for transfers between devices, apart(): lax.ppermute(value, ('y', 'core'), [(2 * i + k, 2 * ((i + 1 + 2 * k) % 4)...  15.5 us
    all_to_all x1, blocking collectives, shards(): parts = lax.all_to_all(running, COL, 0, 0, tiled=True)  12.7 us
    pallas_call x6, Pallas kernels, build(): pl.pallas_call(functools.partial(build_kernel, first, arrived), out_shape...  12.4 us
    ppermute x12, starting transfers between devices, swap_cores(): return lax.ppermute(value, 'core', [(0, 1), (1, 0)])  11.1 us
    ppermute x3, starting transfers between devices, apart(): lax.ppermute(value, ('y', 'core'), [(2 * i + k, 2 * ((i + 1 + 2 * k) % 4)...  10.7 us
    all_to_all x1, waiting for transfers between devices, shards(): parts = lax.all_to_all(running, COL, 0, 0, tiled=True)  10.6 us
  transfers between devices with their start and end apart: 21, of which 10 were waited for; matrix products, arithmetic and copies ran while one was open for 4% of the time, Pallas kernels for 6%

profile of v10, /device:TPU:1, one launch (start us, length us, event | category | flops | bytes accessed | tf_op | source)
XLA Modules:
  0.0 196.4 jit_solution(774023084526118961)
XLA Ops:
  1.3 1.5 collective-permute-start
  4.2 1.4 collective-permute-start.3
  5.7 2.3 %dynamic-slice_bitcast_fusion = bf16[512,1024]{1,0:T(8,128)(2,1)} fusion(bf16[8,512,1024]{2,1,0:T(8,128)(2,1)} %bitcast.37, s32[]{:T(128)S(6)} %select_n.198), kind=kLoop, calls=%fused_computation.1 | loop fusion | bytes 2097156 | tf_op jit(solution)/shard_map/jit(dynamic_index_in_dim)/squeeze | solution.py:483
  7.9 3.8 %collective-permute-start.1 = (bf16[512,1024]{1,0:T(8,128)(2,1)}, bf16[512,1024]{1,0:T(8,128)(2,1)}, u32[]{:S(2)}, u32[]{:S(2)}) collective-permute-start(bf16[512,1024]{1,0:T(8,128)(2,1)} %dynamic-slice_bitcast_fusion), channel_id=1, source_target_pairs={{0,17},{17,0},{1,16},{16,1},{2,19},{19,2},{3,18},{18,3},{4,21},{21... | collective-permute-start | bytes 3145736 | tf_op jit(solution)/shard_map/ppermute | solution.py:426
  11.7 5.1 %multiply_reduce_fusion = f32[4096]{0:T(1024)S(1)} fusion(bf16[4096,1024]{1,0:T(8,128)(2,1)} %param.5), kind=kLoop, calls=%fused_computation | loop fusion | flops 12578816 | bytes 8404992 | tf_op jit(solution)/shard_map/reduce_sum | solution.py:485
  18.6 3.4 %copy-done = bf16[4096,1024]{1,0:T(8,128)(2,1)S(1)} copy-done((bf16[4096,1024]{1,0:T(8,128)(2,1)S(1)}, bf16[4096,1024]{1,0:T(8,128)(2,1)}, u32[]{:S(2)}) %copy-start) | copy-done | bytes 8388632
  22.0 4.6 %build_tiles.6 = (bf16[24,512,512]{2,1,0:T(8,128)(2,1)}, f32[8,512]{1,0:T(8,128)S(1)}) custom-call(s32[121]{0:T(128)S(1)} %concatenate.13.info, bf16[8,512,1024]{2,1,0:T(8,128)(2,1)S(1)} %bitcast.38, f32[8,512]{1,0:T(8,128)S(1)} %mul.134.half_rows, bf16[512,1024]{1,0:T(8,128)(2,1)S(1)} %dynamic-slice_bitcast_fusion.1.refs_0_, ...), custom_call_target="tpu_custom_call" | custom-call | flops 1610612736 | bytes 7864320 | tf_op jit(solution)/shard_map/build_tiles/pallas_call | solution.py:112
  26.6 8.3 %collective-permute-done.1.refs_0_ = bf16[512,1024]{1,0:T(8,128)(2,1)} collective-permute-done((bf16[512,1024]{1,0:T(8,128)(2,1)}, bf16[512,1024]{1,0:T(8,128)(2,1)}, u32[]{:S(2)}, u32[]{:S(2)}) %collective-permute-start.1) | collective-permute-done | bytes 1048608 | tf_op jit(solution)/shard_map/ppermute | solution.py:426
  36.8 2.7 %collective-permute-start.8 = (bf16[512,1024]{1,0:T(8,128)(2,1)S(1)}, bf16[512,1024]{1,0:T(8,128)(2,1)S(1)}, u32[]{:S(2)}, u32[]{:S(2)}) collective-permute-start(bf16[512,1024]{1,0:T(8,128)(2,1)S(1)} %get-tuple-element.62), channel_id=1, source_target_pairs={{0,1},{8,25},{1,16},{9,8},{16,17},{24,9},{17,0},{25,24},{2,3},{10,... | collective-permute-start | bytes 3145736 | tf_op jit(solution)/shard_map/ppermute | solution.py:422
  39.5 1.5 collective-permute-start.7
  42.4 6.2 %collective-permute-start.10 = (bf16[512,1024]{1,0:T(8,128)(2,1)S(1)}, bf16[512,1024]{1,0:T(8,128)(2,1)S(1)}, u32[]{:S(2)}, u32[]{:S(2)}) collective-permute-start(bf16[512,1024]{1,0:T(8,128)(2,1)S(1)} %get-tuple-element.45), channel_id=1, source_target_pairs={{0,32},{8,104},{32,64},{40,8},{64,96},{72,40},{96,0},{104,72},{1,3... | collective-permute-start | bytes 3145736 | tf_op jit(solution)/shard_map/ppermute | solution.py:409
  48.6 2.7 %build_tiles.8 = (bf16[24,512,512]{2,1,0:T(8,128)(2,1)}, f32[8,512]{1,0:T(8,128)S(1)}) custom-call(s32[121]{0:T(128)S(1)} %concatenate.13.info, bf16[8,512,1024]{2,1,0:T(8,128)(2,1)S(1)} %bitcast.40, f32[8,512]{1,0:T(8,128)S(1)} %mul.134.half_rows, bf16[512,1024]{1,0:T(8,128)(2,1)S(1)} %collective-permute-done.4.refs_0_, ...), custom_call_target="tpu_custom_call", output_to_operand_aliasing={{0}: (6, {})} | custom-call | flops 2147483648 | bytes 10485760 | tf_op jit(solution)/shard_map/build_tiles/pallas_call | solution.py:112
  51.3 2.4 %collective-permute-done.7.refs_0_ = bf16[512,1024]{1,0:T(8,128)(2,1)S(1)} collective-permute-done((bf16[512,1024]{1,0:T(8,128)(2,1)}, bf16[512,1024]{1,0:T(8,128)(2,1)S(1)}, u32[]{:S(2)}, u32[]{:S(2)}) %collective-permute-start.7) | collective-permute-done | bytes 1048608 | tf_op jit(solution)/shard_map/ppermute | solution.py:409
  54.7 3.0 %collective-permute-start.12 = (bf16[512,1024]{1,0:T(8,128)(2,1)S(1)}, bf16[512,1024]{1,0:T(8,128)(2,1)S(1)}, u32[]{:S(2)}, u32[]{:S(2)}) collective-permute-start(bf16[512,1024]{1,0:T(8,128)(2,1)S(1)} %collective-permute-done.7.refs_0_), channel_id=1, source_target_pairs={{0,32},{8,104},{32,64},{40,8},{64,96},{72,40},{96,0},{104,72},{1,3... | collective-permute-start | bytes 3145736 | tf_op jit(solution)/shard_map/ppermute | solution.py:409
  57.7 7.2 %collective-permute-done.10.refs_2_ = bf16[512,1024]{1,0:T(8,128)(2,1)S(1)} collective-permute-done((bf16[512,1024]{1,0:T(8,128)(2,1)S(1)}, bf16[512,1024]{1,0:T(8,128)(2,1)S(1)}, u32[]{:S(2)}, u32[]{:S(2)}) %collective-permute-start.10) | collective-permute-done | bytes 1048608 | tf_op jit(solution)/shard_map/ppermute | solution.py:409
  64.9 2.7 %collective-permute-done.11.refs_3_ = bf16[512,1024]{1,0:T(8,128)(2,1)S(1)} collective-permute-done((bf16[512,1024]{1,0:T(8,128)(2,1)S(1)}, bf16[512,1024]{1,0:T(8,128)(2,1)S(1)}, u32[]{:S(2)}, u32[]{:S(2)}) %collective-permute-start.11) | collective-permute-done | bytes 1048608 | tf_op jit(solution)/shard_map/ppermute | solution.py:422
  67.6 1.6 collective-permute-start.15
  69.9 6.0 %collective-permute-done.12.refs_2_ = bf16[512,1024]{1,0:T(8,128)(2,1)S(1)} collective-permute-done((bf16[512,1024]{1,0:T(8,128)(2,1)S(1)}, bf16[512,1024]{1,0:T(8,128)(2,1)S(1)}, u32[]{:S(2)}, u32[]{:S(2)}) %collective-permute-start.12) | collective-permute-done | bytes 1048608 | tf_op jit(solution)/shard_map/ppermute | solution.py:409
  76.0 2.5 %build_tiles.10 = (bf16[24,512,512]{2,1,0:T(8,128)(2,1)}, f32[8,512]{1,0:T(8,128)S(1)}) custom-call(s32[121]{0:T(128)S(1)} %concatenate.13.info, bf16[8,512,1024]{2,1,0:T(8,128)(2,1)S(1)} %bitcast.42, f32[8,512]{1,0:T(8,128)S(1)} %mul.134.half_rows, bf16[512,1024]{1,0:T(8,128)(2,1)S(1)} %collective-permute-done.14.refs_0_, ...), custom_call_target="tpu_custom_call", output_to_operand_aliasing={{0}: (6, {})} | custom-call | flops 2147483648 | bytes 10485760 | tf_op jit(solution)/shard_map/build_tiles/pallas_call | solution.py:112
  79.2 27.5 %all_to_all.25 = f32[64,8,128]{2,1,0:T(8,128)S(1)} all-to-all(f32[64,8,128]{2,1,0:T(8,128)S(1)} %bitcast.46), channel_id=1, replica_groups=mesh['y'=4,'zh'=2,'core'=2,'x'=4,'zl'=2] {'y','zh','x','zl'}, dimensions={0} | all-to-all | bytes 524288 | tf_op jit(solution)/shard_map/all_to_all | solution.py:513
  108.0 2.5 %product.2 = bf16[8,64,512]{2,1,0:T(8,128)(2,1)S(1)} custom-call(s32[121]{0:T(128)S(1)} %concatenate.13.info, bf16[24,512,512]{2,1,0:T(8,128)(2,1)} %get-tuple-element.55.tiles, f32[8,8,128]{2,1,0:T(8,128)S(1)} %bitcast_reduce_fusion.refs_0_.known, f32[8,8,128]{2,1,0:T(8,128)S(1)} %collective-permute-done.16.refs_1_), custom_call_target="tpu_custom_call" | custom-call | tf_op jit(solution)/shard_map/product/pallas_call | solution.py:237
  110.5 12.7 %all_to_all.26.parts = bf16[8,64,512]{2,1,0:T(8,128)(2,1)S(1)} all-to-all(bf16[8,64,512]{2,1,0:T(8,128)(2,1)S(1)} %product.2), channel_id=1, replica_groups=mesh['y'=4,'zh'=2,'core'=2,'x'=4,'zl'=2] {'x','zl'}, dimensions={0} | all-to-all | bytes 1048576 | tf_op jit(solution)/shard_map/all_to_all | solution.py:521
  124.4 16.6 %all_to_all.27.refs_0_ = bf16[8,80,512]{2,1,0:T(8,128)(2,1)S(1)} all-to-all(bf16[8,80,512]{2,1,0:T(8,128)(2,1)S(1)} %broadcast_in_dim.112), channel_id=1, replica_groups=mesh['y'=4,'zh'=2,'core'=2,'x'=4,'zl'=2] {'y','zh'}, dimensions={0} | all-to-all | bytes 1310720 | tf_op jit(solution)/shard_map/all_to_all | solution.py:379
  141.0 2.9 %collective-permute-start.17 = (bf16[8,80,512]{2,1,0:T(8,128)(2,1)S(1)}, bf16[8,80,512]{2,1,0:T(8,128)(2,1)S(1)}, u32[]{:S(2)}, u32[]{:S(2)}) collective-permute-start(bf16[8,80,512]{2,1,0:T(8,128)(2,1)S(1)} %all_to_all.27.refs_0_), channel_id=1, source_target_pairs={{0,8},{8,0},{1,9},{9,1},{2,10},{10,2},{3,11},{11,3},{4,12},{12,4},... | collective-permute-start | bytes 1966088 | tf_op jit(solution)/shard_map/ppermute | solution.py:374
  143.9 1.7 collective-permute-done.17.refs_1_
  145.6 3.7 %product.3 = bf16[8,80,512]{2,1,0:T(8,128)(2,1)} custom-call(s32[121]{0:T(128)S(1)} %concatenate.13.info, bf16[24,512,512]{2,1,0:T(8,128)(2,1)} %get-tuple-element.55.tiles, bf16[8,80,512]{2,1,0:T(8,128)(2,1)S(1)} %all_to_all.27.refs_0_, bf16[8,80,512]{2,1,0:T(8,128)(2,1)S(1)} %collective-permute-done.17.refs_1_, f32[8,512]{1,0:T(8,128)S(1)} %get-tuple-element.56.refs_2_), custom_call_target="tpu_custom_call" | custom-call | tf_op jit(solution)/shard_map/product/pallas_call | solution.py:237
  149.3 3.6 %all-to-all-start.3 = ((bf16[8,80,512]{2,1,0:T(8,128)(2,1)}), bf16[8,80,512]{2,1,0:T(8,128)(2,1)S(1)}, u32[]{:S(2)}, u32[]{:S(2)}) async-start(bf16[8,80,512]{2,1,0:T(8,128)(2,1)} %product.3), calls=%async_computation.3 | async-start | bytes 1310720 | tf_op jit(solution)/shard_map/all_to_all | solution.py:526
  152.9 10.6 %all-to-all-done.3.parts = bf16[8,80,512]{2,1,0:T(8,128)(2,1)S(1)} async-done(((bf16[8,80,512]{2,1,0:T(8,128)(2,1)}), bf16[8,80,512]{2,1,0:T(8,128)(2,1)S(1)}, u32[]{:S(2)}, u32[]{:S(2)}) %all-to-all-start.3) | async-done | bytes 655392 | tf_op jit(solution)/shard_map/all_to_all | solution.py:526
  163.5 3.6 %middle.1 = (f32[64,512]{1,0:T(8,128)S(1)}, f32[32,128]{1,0:T(8,128)S(1)}) custom-call(s32[121]{0:T(128)S(1)} %concatenate.13.info, bf16[8,80,512]{2,1,0:T(8,128)(2,1)S(1)} %all-to-all-done.3.parts, f32[8,8,128]{2,1,0:T(8,128)S(1)} %bitcast_reduce_fusion.refs_0_.known, f32[8,8,8,128]{3,2,1,0:T(8,128)S(1)} %bitcast.44), custom_call_target="tpu_custom_call" | custom-call | tf_op jit(solution)/shard_map/middle/pallas_call | solution.py:363
  169.3 20.7 %all_to_all.28 = f32[64,16,128]{2,1,0:T(8,128)S(1)} all-to-all(f32[64,16,128]{2,1,0:T(8,128)S(1)} %broadcast_in_dim.113), channel_id=1, replica_groups=mesh['y'=4,'zh'=2,'core'=2,'x'=4,'zl'=2] {'y','zh','x','zl'}, dimensions={0} | all-to-all | bytes 1048576 | tf_op jit(solution)/shard_map/all_to_all | solution.py:379
  190.0 2.0 collective-permute-start.19
  192.8 3.6 %last.1 = f32[64,512]{1,0:T(8,128)} custom-call(s32[121]{0:T(128)S(1)} %concatenate.13.info, f32[32,128]{1,0:T(8,128)S(1)} %pad_maximum_fusion.1.message, f32[64,512]{1,0:T(8,128)S(1)} %get-tuple-element.58.image, f32[8,8,128]{2,1,0:T(8,128)S(1)} %bitcast_reduce_fusion.refs_0_.known), custom_call_target="tpu_custom_call" | custom-call | tf_op jit(solution)/shard_map/last/pallas_call | solution.py:363
  (67 shorter events, 14.9 us)
Async XLA Ops:
  0.0 17.6 %copy-start.3 = (s32[1,1,24]{2,1,0:T(1,128)S(1)}, s32[1,1,24]{2,1,0:T(1,128)}, u32[]{:S(2)}) copy-start(s32[1,1,24]{2,1,0:T(1,128)} %param.8) | copy-start | bytes 292
  0.0 17.9 %copy-start.4 = (s32[1,1,24]{2,1,0:T(1,128)S(1)}, s32[1,1,24]{2,1,0:T(1,128)}, u32[]{:S(2)}) copy-start(s32[1,1,24]{2,1,0:T(1,128)} %param.7) | copy-start | bytes 292
  1.3 17.3 %collective-permute-start = (bf16[512,1024]{1,0:T(8,128)(2,1)S(1)}, bf16[512,1024]{1,0:T(8,128)(2,1)}, u32[]{:S(2)}, u32[]{:S(2)}) collective-permute-start(bf16[512,1024]{1,0:T(8,128)(2,1)S(1)} %dynamic-slice_bitcast_fusion.1.refs_0_), channel_id=1, source_target_pairs={{0,8},{8,0},{1,9},{9,1},{2,10},{10,2},{3,11},{11,3},{4,12},{12,4},... | collective-permute-start | bytes 3145736 | tf_op jit(solution)/shard_map/ppermute | solution.py:374
  2.8 32.2 %collective-permute-start.2 = (bf16[512,1024]{1,0:T(8,128)(2,1)S(1)}, bf16[512,1024]{1,0:T(8,128)(2,1)S(1)}, u32[]{:S(2)}, u32[]{:S(2)}) collective-permute-start(bf16[512,1024]{1,0:T(8,128)(2,1)S(1)} %dynamic-slice_bitcast_fusion.1.refs_0_), channel_id=1, source_target_pairs={{0,32},{32,64},{64,96},{96,0},{1,33},{33,65},{65,97},{97,1},{2,34}... | collective-permute-start | bytes 3145736 | tf_op jit(solution)/shard_map/ppermute | solution.py:401
  4.2 30.8 %collective-permute-start.3 = (bf16[512,1024]{1,0:T(8,128)(2,1)S(1)}, bf16[512,1024]{1,0:T(8,128)(2,1)S(1)}, u32[]{:S(2)}, u32[]{:S(2)}) collective-permute-start(bf16[512,1024]{1,0:T(8,128)(2,1)S(1)} %dynamic-slice_bitcast_fusion.1.refs_0_), channel_id=1, source_target_pairs={{0,96},{32,0},{64,32},{96,64},{1,97},{33,1},{65,33},{97,65},{2,98}... | collective-permute-start | bytes 3145736 | tf_op jit(solution)/shard_map/ppermute | solution.py:405
  7.9 27.1 %collective-permute-start.1 = (bf16[512,1024]{1,0:T(8,128)(2,1)}, bf16[512,1024]{1,0:T(8,128)(2,1)}, u32[]{:S(2)}, u32[]{:S(2)}) collective-permute-start(bf16[512,1024]{1,0:T(8,128)(2,1)} %dynamic-slice_bitcast_fusion), channel_id=1, source_target_pairs={{0,17},{17,0},{1,16},{16,1},{2,19},{19,2},{3,18},{18,3},{4,21},{21... | collective-permute-start | bytes 3145736 | tf_op jit(solution)/shard_map/ppermute | solution.py:426
  18.6 3.4 %copy-start = (bf16[4096,1024]{1,0:T(8,128)(2,1)S(1)}, bf16[4096,1024]{1,0:T(8,128)(2,1)}, u32[]{:S(2)}) copy-start(bf16[4096,1024]{1,0:T(8,128)(2,1)} %param.5) | copy-start | bytes 25165828
  22.0 19.0 %copy-start.1 = (bf16[4096,1024]{1,0:T(8,128)(2,1)S(1)}, bf16[4096,1024]{1,0:T(8,128)(2,1)}, u32[]{:S(2)}) copy-start(bf16[4096,1024]{1,0:T(8,128)(2,1)} %param.5) | copy-start | bytes 25165828
  35.0 7.4 %collective-permute-start.4 = (bf16[512,1024]{1,0:T(8,128)(2,1)}, bf16[512,1024]{1,0:T(8,128)(2,1)S(1)}, u32[]{:S(2)}, u32[]{:S(2)}) collective-permute-start(bf16[512,1024]{1,0:T(8,128)(2,1)} %collective-permute-done.1.refs_0_), channel_id=1, source_target_pairs={{0,8},{8,0},{1,9},{9,1},{2,10},{10,2},{3,11},{11,3},{4,12},{12,4},... | collective-permute-start | bytes 3145736 | tf_op jit(solution)/shard_map/ppermute | solution.py:374
  36.1 12.4 %collective-permute-start.5 = (bf16[512,1024]{1,0:T(8,128)(2,1)S(1)}, bf16[512,1024]{1,0:T(8,128)(2,1)S(1)}, u32[]{:S(2)}, u32[]{:S(2)}) collective-permute-start(bf16[512,1024]{1,0:T(8,128)(2,1)S(1)} %collective-permute-done.2.refs_1_), channel_id=1, source_target_pairs={{0,8},{8,0},{1,9},{9,1},{2,10},{10,2},{3,11},{11,3},{4,12},{12,4},... | collective-permute-start | bytes 3145736 | tf_op jit(solution)/shard_map/ppermute | solution.py:374
  36.2 12.3 %collective-permute-start.6 = (bf16[512,1024]{1,0:T(8,128)(2,1)S(1)}, bf16[512,1024]{1,0:T(8,128)(2,1)S(1)}, u32[]{:S(2)}, u32[]{:S(2)}) collective-permute-start(bf16[512,1024]{1,0:T(8,128)(2,1)S(1)} %collective-permute-done.3.refs_2_), channel_id=1, source_target_pairs={{0,8},{8,0},{1,9},{9,1},{2,10},{10,2},{3,11},{11,3},{4,12},{12,4},... | collective-permute-start | bytes 3145736 | tf_op jit(solution)/shard_map/ppermute | solution.py:374
  36.8 14.5 %collective-permute-start.8 = (bf16[512,1024]{1,0:T(8,128)(2,1)S(1)}, bf16[512,1024]{1,0:T(8,128)(2,1)S(1)}, u32[]{:S(2)}, u32[]{:S(2)}) collective-permute-start(bf16[512,1024]{1,0:T(8,128)(2,1)S(1)} %get-tuple-element.62), channel_id=1, source_target_pairs={{0,1},{8,25},{1,16},{9,8},{16,17},{24,9},{17,0},{25,24},{2,3},{10,... | collective-permute-start | bytes 3145736 | tf_op jit(solution)/shard_map/ppermute | solution.py:422
  39.5 14.2 %collective-permute-start.7 = (bf16[512,1024]{1,0:T(8,128)(2,1)}, bf16[512,1024]{1,0:T(8,128)(2,1)S(1)}, u32[]{:S(2)}, u32[]{:S(2)}) collective-permute-start(bf16[512,1024]{1,0:T(8,128)(2,1)} %collective-permute-done.1.refs_0_), channel_id=1, source_target_pairs={{0,32},{8,104},{32,64},{40,8},{64,96},{72,40},{96,0},{104,72},{1,3... | collective-permute-start | bytes 3145736 | tf_op jit(solution)/shard_map/ppermute | solution.py:409
  42.4 22.5 %collective-permute-start.10 = (bf16[512,1024]{1,0:T(8,128)(2,1)S(1)}, bf16[512,1024]{1,0:T(8,128)(2,1)S(1)}, u32[]{:S(2)}, u32[]{:S(2)}) collective-permute-start(bf16[512,1024]{1,0:T(8,128)(2,1)S(1)} %get-tuple-element.45), channel_id=1, source_target_pairs={{0,32},{8,104},{32,64},{40,8},{64,96},{72,40},{96,0},{104,72},{1,3... | collective-permute-start | bytes 3145736 | tf_op jit(solution)/shard_map/ppermute | solution.py:409
  53.7 13.9 %collective-permute-start.11 = (bf16[512,1024]{1,0:T(8,128)(2,1)S(1)}, bf16[512,1024]{1,0:T(8,128)(2,1)S(1)}, u32[]{:S(2)}, u32[]{:S(2)}) collective-permute-start(bf16[512,1024]{1,0:T(8,128)(2,1)S(1)} %collective-permute-done.8), channel_id=1, source_target_pairs={{0,1},{8,25},{1,16},{9,8},{16,17},{24,9},{17,0},{25,24},{2,3},{10,... | collective-permute-start | bytes 3145736 | tf_op jit(solution)/shard_map/ppermute | solution.py:422
  54.7 14.6 %collective-permute-start.9 = (bf16[512,1024]{1,0:T(8,128)(2,1)S(1)}, bf16[512,1024]{1,0:T(8,128)(2,1)S(1)}, u32[]{:S(2)}, u32[]{:S(2)}) collective-permute-start(bf16[512,1024]{1,0:T(8,128)(2,1)S(1)} %collective-permute-done.7.refs_0_), channel_id=1, source_target_pairs={{0,8},{8,0},{1,9},{9,1},{2,10},{10,2},{3,11},{11,3},{4,12},{12,4},... | collective-permute-start | bytes 3145736 | tf_op jit(solution)/shard_map/ppermute | solution.py:374
  54.7 21.2 %collective-permute-start.12 = (bf16[512,1024]{1,0:T(8,128)(2,1)S(1)}, bf16[512,1024]{1,0:T(8,128)(2,1)S(1)}, u32[]{:S(2)}, u32[]{:S(2)}) collective-permute-start(bf16[512,1024]{1,0:T(8,128)(2,1)S(1)} %collective-permute-done.7.refs_0_), channel_id=1, source_target_pairs={{0,32},{8,104},{32,64},{40,8},{64,96},{72,40},{96,0},{104,72},{1,3... | collective-permute-start | bytes 3145736 | tf_op jit(solution)/shard_map/ppermute | solution.py:409
  64.9 11.0 %collective-permute-start.14 = (bf16[512,1024]{1,0:T(8,128)(2,1)S(1)}, bf16[512,1024]{1,0:T(8,128)(2,1)S(1)}, u32[]{:S(2)}, u32[]{:S(2)}) collective-permute-start(bf16[512,1024]{1,0:T(8,128)(2,1)S(1)} %collective-permute-done.10.refs_2_), channel_id=1, source_target_pairs={{0,8},{8,0},{1,9},{9,1},{2,10},{10,2},{3,11},{11,3},{4,12},{12,4},... | collective-permute-start | bytes 3145736 | tf_op jit(solution)/shard_map/ppermute | solution.py:374
  67.6 8.3 %collective-permute-start.15 = (bf16[512,1024]{1,0:T(8,128)(2,1)S(1)}, bf16[512,1024]{1,0:T(8,128)(2,1)S(1)}, u32[]{:S(2)}, u32[]{:S(2)}) collective-permute-start(bf16[512,1024]{1,0:T(8,128)(2,1)S(1)} %collective-permute-done.11.refs_3_), channel_id=1, source_target_pairs={{0,8},{8,0},{1,9},{9,1},{2,10},{10,2},{3,11},{11,3},{4,12},{12,4},... | collective-permute-start | bytes 3145736 | tf_op jit(solution)/shard_map/ppermute | solution.py:374
  69.3 6.6 %copy-start.2 = (s32[512]{0:T(512)S(1)}, s32[512]{0:T(512)}, u32[]{:S(2)}) copy-start(s32[512]{0:T(512)} %param.6) | copy-start | bytes 6148
  75.9 2.7 %collective-permute-start.13 = (bf16[512,1024]{1,0:T(8,128)(2,1)S(1)}, bf16[512,1024]{1,0:T(8,128)(2,1)S(1)}, u32[]{:S(2)}, u32[]{:S(2)}) collective-permute-start(bf16[512,1024]{1,0:T(8,128)(2,1)S(1)} %collective-permute-done.12.refs_2_), channel_id=1, source_target_pairs={{0,8},{8,0},{1,9},{9,1},{2,10},{10,2},{3,11},{11,3},{4,12},{12,4},... | collective-permute-start | bytes 3145736 | tf_op jit(solution)/shard_map/ppermute | solution.py:374
  106.7 1.3 collective-permute-start.16
  141.0 4.7 %collective-permute-start.17 = (bf16[8,80,512]{2,1,0:T(8,128)(2,1)S(1)}, bf16[8,80,512]{2,1,0:T(8,128)(2,1)S(1)}, u32[]{:S(2)}, u32[]{:S(2)}) collective-permute-start(bf16[8,80,512]{2,1,0:T(8,128)(2,1)S(1)} %all_to_all.27.refs_0_), channel_id=1, source_target_pairs={{0,8},{8,0},{1,9},{9,1},{2,10},{10,2},{3,11},{11,3},{4,12},{12,4},... | collective-permute-start | bytes 1966088 | tf_op jit(solution)/shard_map/ppermute | solution.py:374
  149.3 14.2 %all-to-all-start.3 = ((bf16[8,80,512]{2,1,0:T(8,128)(2,1)}), bf16[8,80,512]{2,1,0:T(8,128)(2,1)S(1)}, u32[]{:S(2)}, u32[]{:S(2)}) async-start(bf16[8,80,512]{2,1,0:T(8,128)(2,1)} %product.3), calls=%async_computation.3 | async-start | bytes 1310720 | tf_op jit(solution)/shard_map/all_to_all | solution.py:526
  167.1 2.1 %collective-permute-start.18 = (f32[16,128]{1,0:T(8,128)S(1)}, f32[16,128]{1,0:T(8,128)S(1)}, u32[]{:S(2)}, u32[]{:S(2)}) collective-permute-start(f32[16,128]{1,0:T(8,128)S(1)} %constant_dynamic-slice_fusion), channel_id=1, source_target_pairs={{0,8},{8,0},{1,9},{9,1},{2,10},{10,2},{3,11},{11,3},{4,12},{12,4},... | collective-permute-start | bytes 24584 | tf_op jit(solution)/shard_map/ppermute | solution.py:374
  190.0 2.8 %collective-permute-start.19 = (f32[16,128]{1,0:T(8,128)S(1)}, f32[16,128]{1,0:T(8,128)S(1)}, u32[]{:S(2)}, u32[]{:S(2)}) collective-permute-start(f32[16,128]{1,0:T(8,128)S(1)} %reduce_sum.99), channel_id=1, source_target_pairs={{0,8},{8,0},{1,9},{9,1},{2,10},{10,2},{3,11},{11,3},{4,12},{12,4},... | collective-permute-start | bytes 24584 | tf_op jit(solution)/shard_map/ppermute | solution.py:374

commit v11 on v10

--- a/solution.py
+++ b/solution.py
@@ -192,33 +192,32 @@
     def term(entry):
         return jnp.dot(piece(entry), held[lax.rem(entry, depth)], preferred_element_type=F32)
 
-    for entry in range(depth - 2):
+    for entry in range(depth - 4):
 
         @pl.when(entry < count)
         def _():
             fetch(jnp.int32(entry)).start()
 
-    def step(pair, carry):
-        one = 2 * pair
-        two = one + 1
-        for entry in (one, two):
-
-            @pl.when(entry + depth - 2 < count)
-            def _():
-                fetch(entry + depth - 2).start()
-
-        fetch(one).wait()
-
-        @pl.when(two < count)
-        def _():
-            fetch(two).wait()
-
-        one_term, two_term = term(one), term(two)
-        running[info[ROWS + one]] += one_term
-        running[info[ROWS + two]] += jnp.where(two < count, two_term, 0.0)
+    def step(turn, carry):
+        entries = [4 * turn + i for i in range(4)]
+        for entry in entries:
+
+            @pl.when(entry + depth - 4 < count)
+            def _(entry=entry):
+                fetch(entry + depth - 4).start()
+
+        for entry in entries:
+
+            @pl.when(entry < count)
+            def _(entry=entry):
+                fetch(entry).wait()
+
+        terms = [term(entry) for entry in entries]
+        for entry, value in zip(entries, terms, strict=True):
+            running[info[ROWS + entry]] += jnp.where(entry < count, value, 0.0)
         return carry
 
-    lax.fori_loop(0, (count + 1) // 2, step, 0)
+    lax.fori_loop(0, (count + 3) // 4, step, 0)
     if first:
         out[...] = running[...].astype(BF16)
     else:
@@ -247,8 +246,8 @@
         out_specs=vmem,
         scratch_shapes=[
             pltpu.VMEM((SLAB_TILES, K, TILE), F32),
-            pltpu.VMEM((8, TILE, TILE), BF16),
-            pltpu.SemaphoreType.DMA((8,)),
+            pltpu.VMEM((PAIRS, TILE, TILE), BF16),
+            pltpu.SemaphoreType.DMA((PAIRS,)),
         ],
         compiler_params=pltpu.CompilerParams(vmem_limit_bytes=20 * 1024 * 1024),
         name="product",
@@ -313,7 +312,7 @@
         for a in range(8):
             pivot = spread[a][a : a + 1, :]
             below = jnp.where(index == start + a, pivot, below)
-            ratio = jnp.where(index > start + a, spread[a] / pivot, 0.0)
+            ratio = jnp.where(index > start + a, spread[a] * (1.0 / pivot), 0.0)
             rest = rest - ratio * rest[a : a + 1, :]
             for b in range(a + 1, 8):
                 spread[b] = spread[b] - ratio * spread[b][a : a + 1, :]

time: 197 us -> 198 us (level)
  waiting for transfers between devices: 41.8 us -> 46.5 us
  blocking collectives: 77.5 us -> 73 us
  starting transfers between devices: 35.6 us -> 33.1 us
    ppermute x2, waiting for transfers between devices: 2.71 us -> 7.48 us  [apart_z(): return lax.ppermute(value, ('zh', 'core', 'zl'), moves)]
    ppermute x3, starting transfers between devices: 10.7 us -> 6.23 us  [apart(): lax.ppermute(value, ('y', 'core'), [(2 * i + k, 2 * ((i + 1 + 2 * k) % 4)...]
    all_to_all x1, blocking collectives: 27.5 us -> 25.3 us  [shards(): lax.all_to_all(jnp.broadcast_to(sent[None], (8,) + sent.shape).reshape(8...]
  transfers between devices with their start and end apart: 21 -> 21, of which waited for: 10 -> 11; matrix products, arithmetic and copies ran while one was open for 4% -> 4% of each run, Pallas kernels for 6% -> 6%
where the time goes in v11:
time: 198 us; the launch traced here: 196 us
  blocking collectives  73 us (37%)
  waiting for transfers between devices  46.5 us (23%)
  starting transfers between devices  33.1 us (17%)
  Pallas kernels  28.6 us (14%)
  local copies, waits for them, and re-layouts  7.31 us (4%)
  other arithmetic  6.29 us (3%)
    all_to_all x2, blocking collectives, share(): lax.all_to_all(jnp.broadcast_to(value[None], (size,) + value.shape), axes...  36.5 us
    all_to_all x1, blocking collectives, shards(): lax.all_to_all(jnp.broadcast_to(sent[None], (8,) + sent.shape).reshape(8...  25.3 us
    ppermute x3, waiting for transfers between devices, apart(): lax.ppermute(value, ('y', 'core'), [(2 * i + k, 2 * ((i + 1 + 2 * k) % 4)...  17.1 us
    ppermute x12, starting transfers between devices, swap_cores(): return lax.ppermute(value, 'core', [(0, 1), (1, 0)])  13 us
    pallas_call x6, Pallas kernels, build(): pl.pallas_call(functools.partial(build_kernel, first, arrived), out_shape...  12.6 us
    all_to_all x1, blocking collectives, shards(): parts = lax.all_to_all(running, COL, 0, 0, tiled=True)  11.2 us
    all_to_all x1, waiting for transfers between devices, shards(): parts = lax.all_to_all(running, COL, 0, 0, tiled=True)  10.2 us
    pallas_call x3, Pallas kernels, local(): pl.pallas_call(kernel, out_shape=out_shape, in_specs=[pl.BlockSpec(memory...  8.1 us
  transfers between devices with their start and end apart: 21, of which 11 were waited for; matrix products, arithmetic and copies ran while one was open for 4% of the time, Pallas kernels for 6%

profile of v11, /device:TPU:1, one launch (start us, length us, event | category | flops | bytes accessed | tf_op | source)
XLA Modules:
  0.0 195.8 jit_solution(11246565869308144557)
XLA Ops:
  1.3 1.5 collective-permute-start
  5.7 2.3 %dynamic-slice_bitcast_fusion = bf16[512,1024]{1,0:T(8,128)(2,1)} fusion(bf16[8,512,1024]{2,1,0:T(8,128)(2,1)} %bitcast.37, s32[]{:T(128)S(6)} %select_n.198), kind=kLoop, calls=%fused_computation.1 | loop fusion | bytes 2097156 | tf_op jit(solution)/shard_map/jit(dynamic_index_in_dim)/squeeze | solution.py:482
  7.9 3.8 %collective-permute-start.1 = (bf16[512,1024]{1,0:T(8,128)(2,1)}, bf16[512,1024]{1,0:T(8,128)(2,1)}, u32[]{:S(2)}, u32[]{:S(2)}) collective-permute-start(bf16[512,1024]{1,0:T(8,128)(2,1)} %dynamic-slice_bitcast_fusion), channel_id=1, source_target_pairs={{0,17},{17,0},{1,16},{16,1},{2,19},{19,2},{3,18},{18,3},{4,21},{21... | collective-permute-start | bytes 3145736 | tf_op jit(solution)/shard_map/ppermute | solution.py:425
  11.7 5.1 %multiply_reduce_fusion = f32[4096]{0:T(1024)S(1)} fusion(bf16[4096,1024]{1,0:T(8,128)(2,1)} %param.5), kind=kLoop, calls=%fused_computation | loop fusion | flops 12578816 | bytes 8404992 | tf_op jit(solution)/shard_map/reduce_sum | solution.py:484
  18.6 3.4 %copy-done = bf16[4096,1024]{1,0:T(8,128)(2,1)S(1)} copy-done((bf16[4096,1024]{1,0:T(8,128)(2,1)S(1)}, bf16[4096,1024]{1,0:T(8,128)(2,1)}, u32[]{:S(2)}) %copy-start) | copy-done | bytes 8388632
  22.0 5.5 %build_tiles.6 = (bf16[24,512,512]{2,1,0:T(8,128)(2,1)}, f32[8,512]{1,0:T(8,128)S(1)}) custom-call(s32[121]{0:T(128)S(1)} %concatenate.13.info, bf16[8,512,1024]{2,1,0:T(8,128)(2,1)S(1)} %bitcast.38, f32[8,512]{1,0:T(8,128)S(1)} %mul.134.half_rows, bf16[512,1024]{1,0:T(8,128)(2,1)S(1)} %dynamic-slice_bitcast_fusion.1.refs_0_, ...), custom_call_target="tpu_custom_call" | custom-call | flops 1610612736 | bytes 7864320 | tf_op jit(solution)/shard_map/build_tiles/pallas_call | solution.py:112
  27.5 7.5 %collective-permute-done.1.refs_0_ = bf16[512,1024]{1,0:T(8,128)(2,1)} collective-permute-done((bf16[512,1024]{1,0:T(8,128)(2,1)}, bf16[512,1024]{1,0:T(8,128)(2,1)}, u32[]{:S(2)}, u32[]{:S(2)}) %collective-permute-start.1) | collective-permute-done | bytes 1048608 | tf_op jit(solution)/shard_map/ppermute | solution.py:425
  36.8 2.7 %collective-permute-start.8 = (bf16[512,1024]{1,0:T(8,128)(2,1)S(1)}, bf16[512,1024]{1,0:T(8,128)(2,1)S(1)}, u32[]{:S(2)}, u32[]{:S(2)}) collective-permute-start(bf16[512,1024]{1,0:T(8,128)(2,1)S(1)} %get-tuple-element.62), channel_id=1, source_target_pairs={{0,1},{8,25},{1,16},{9,8},{16,17},{24,9},{17,0},{25,24},{2,3},{10,... | collective-permute-start | bytes 3145736 | tf_op jit(solution)/shard_map/ppermute | solution.py:421
  39.5 1.5 collective-permute-start.7
  42.4 3.3 %collective-permute-start.10 = (bf16[512,1024]{1,0:T(8,128)(2,1)S(1)}, bf16[512,1024]{1,0:T(8,128)(2,1)S(1)}, u32[]{:S(2)}, u32[]{:S(2)}) collective-permute-start(bf16[512,1024]{1,0:T(8,128)(2,1)S(1)} %get-tuple-element.45), channel_id=1, source_target_pairs={{0,32},{8,104},{32,64},{40,8},{64,96},{72,40},{96,0},{104,72},{1,3... | collective-permute-start | bytes 3145736 | tf_op jit(solution)/shard_map/ppermute | solution.py:408
  46.5 4.8 %collective-permute-done.8 = bf16[512,1024]{1,0:T(8,128)(2,1)S(1)} collective-permute-done((bf16[512,1024]{1,0:T(8,128)(2,1)S(1)}, bf16[512,1024]{1,0:T(8,128)(2,1)S(1)}, u32[]{:S(2)}, u32[]{:S(2)}) %collective-permute-start.8) | collective-permute-done | bytes 1048608 | tf_op jit(solution)/shard_map/ppermute | solution.py:421
  51.3 2.4 %collective-permute-done.7.refs_0_ = bf16[512,1024]{1,0:T(8,128)(2,1)S(1)} collective-permute-done((bf16[512,1024]{1,0:T(8,128)(2,1)}, bf16[512,1024]{1,0:T(8,128)(2,1)S(1)}, u32[]{:S(2)}, u32[]{:S(2)}) %collective-permute-start.7) | collective-permute-done | bytes 1048608 | tf_op jit(solution)/shard_map/ppermute | solution.py:408
  56.2 8.8 %collective-permute-done.10.refs_2_ = bf16[512,1024]{1,0:T(8,128)(2,1)S(1)} collective-permute-done((bf16[512,1024]{1,0:T(8,128)(2,1)S(1)}, bf16[512,1024]{1,0:T(8,128)(2,1)S(1)}, u32[]{:S(2)}, u32[]{:S(2)}) %collective-permute-start.10) | collective-permute-done | bytes 1048608 | tf_op jit(solution)/shard_map/ppermute | solution.py:408
  64.9 2.7 %collective-permute-done.11.refs_3_ = bf16[512,1024]{1,0:T(8,128)(2,1)S(1)} collective-permute-done((bf16[512,1024]{1,0:T(8,128)(2,1)S(1)}, bf16[512,1024]{1,0:T(8,128)(2,1)S(1)}, u32[]{:S(2)}, u32[]{:S(2)}) %collective-permute-start.11) | collective-permute-done | bytes 1048608 | tf_op jit(solution)/shard_map/ppermute | solution.py:421
  67.6 1.6 collective-permute-start.15
  69.9 6.0 %collective-permute-done.12.refs_2_ = bf16[512,1024]{1,0:T(8,128)(2,1)S(1)} collective-permute-done((bf16[512,1024]{1,0:T(8,128)(2,1)S(1)}, bf16[512,1024]{1,0:T(8,128)(2,1)S(1)}, u32[]{:S(2)}, u32[]{:S(2)}) %collective-permute-start.12) | collective-permute-done | bytes 1048608 | tf_op jit(solution)/shard_map/ppermute | solution.py:408
  76.0 3.7 %build_tiles.10 = (bf16[24,512,512]{2,1,0:T(8,128)(2,1)}, f32[8,512]{1,0:T(8,128)S(1)}) custom-call(s32[121]{0:T(128)S(1)} %concatenate.13.info, bf16[8,512,1024]{2,1,0:T(8,128)(2,1)S(1)} %bitcast.42, f32[8,512]{1,0:T(8,128)S(1)} %mul.134.half_rows, bf16[512,1024]{1,0:T(8,128)(2,1)S(1)} %collective-permute-done.14.refs_0_, ...), custom_call_target="tpu_custom_call", output_to_operand_aliasing={{0}: (6, {})} | custom-call | flops 2147483648 | bytes 10485760 | tf_op jit(solution)/shard_map/build_tiles/pallas_call | solution.py:112
  80.3 25.3 %all_to_all.25 = f32[64,8,128]{2,1,0:T(8,128)S(1)} all-to-all(f32[64,8,128]{2,1,0:T(8,128)S(1)} %bitcast.46), channel_id=1, replica_groups=mesh['y'=4,'zh'=2,'core'=2,'x'=4,'zl'=2] {'y','zh','x','zl'}, dimensions={0} | all-to-all | bytes 524288 | tf_op jit(solution)/shard_map/all_to_all | solution.py:512
  105.6 1.7 collective-permute-start.16
  108.2 3.3 %product.2 = bf16[8,64,512]{2,1,0:T(8,128)(2,1)S(1)} custom-call(s32[121]{0:T(128)S(1)} %concatenate.13.info, bf16[24,512,512]{2,1,0:T(8,128)(2,1)} %get-tuple-element.55.tiles, f32[8,8,128]{2,1,0:T(8,128)S(1)} %bitcast_reduce_fusion.refs_0_.known, f32[8,8,128]{2,1,0:T(8,128)S(1)} %collective-permute-done.16.refs_1_), custom_call_target="tpu_custom_call" | custom-call | tf_op jit(solution)/shard_map/product/pallas_call | solution.py:236
  111.6 11.2 %all_to_all.26.parts = bf16[8,64,512]{2,1,0:T(8,128)(2,1)S(1)} all-to-all(bf16[8,64,512]{2,1,0:T(8,128)(2,1)S(1)} %product.2), channel_id=1, replica_groups=mesh['y'=4,'zh'=2,'core'=2,'x'=4,'zl'=2] {'x','zl'}, dimensions={0} | all-to-all | bytes 1048576 | tf_op jit(solution)/shard_map/all_to_all | solution.py:520
  123.9 17.3 %all_to_all.27.refs_0_ = bf16[8,80,512]{2,1,0:T(8,128)(2,1)S(1)} all-to-all(bf16[8,80,512]{2,1,0:T(8,128)(2,1)S(1)} %broadcast_in_dim.112), channel_id=1, replica_groups=mesh['y'=4,'zh'=2,'core'=2,'x'=4,'zl'=2] {'y','zh'}, dimensions={0} | all-to-all | bytes 1310720 | tf_op jit(solution)/shard_map/all_to_all | solution.py:378
  141.2 2.9 %collective-permute-start.17 = (bf16[8,80,512]{2,1,0:T(8,128)(2,1)S(1)}, bf16[8,80,512]{2,1,0:T(8,128)(2,1)S(1)}, u32[]{:S(2)}, u32[]{:S(2)}) collective-permute-start(bf16[8,80,512]{2,1,0:T(8,128)(2,1)S(1)} %all_to_all.27.refs_0_), channel_id=1, source_target_pairs={{0,8},{8,0},{1,9},{9,1},{2,10},{10,2},{3,11},{11,3},{4,12},{12,4},... | collective-permute-start | bytes 1966088 | tf_op jit(solution)/shard_map/ppermute | solution.py:373
  144.1 1.7 collective-permute-done.17.refs_1_
  145.8 4.5 %product.3 = bf16[8,80,512]{2,1,0:T(8,128)(2,1)} custom-call(s32[121]{0:T(128)S(1)} %concatenate.13.info, bf16[24,512,512]{2,1,0:T(8,128)(2,1)} %get-tuple-element.55.tiles, bf16[8,80,512]{2,1,0:T(8,128)(2,1)S(1)} %all_to_all.27.refs_0_, bf16[8,80,512]{2,1,0:T(8,128)(2,1)S(1)} %collective-permute-done.17.refs_1_, f32[8,512]{1,0:T(8,128)S(1)} %get-tuple-element.56.refs_2_), custom_call_target="tpu_custom_call" | custom-call | tf_op jit(solution)/shard_map/product/pallas_call | solution.py:236
  150.4 3.6 %all-to-all-start.3 = ((bf16[8,80,512]{2,1,0:T(8,128)(2,1)}), bf16[8,80,512]{2,1,0:T(8,128)(2,1)S(1)}, u32[]{:S(2)}, u32[]{:S(2)}) async-start(bf16[8,80,512]{2,1,0:T(8,128)(2,1)} %product.3), calls=%async_computation.3 | async-start | bytes 1310720 | tf_op jit(solution)/shard_map/all_to_all | solution.py:525
  153.9 10.2 %all-to-all-done.3.parts = bf16[8,80,512]{2,1,0:T(8,128)(2,1)S(1)} async-done(((bf16[8,80,512]{2,1,0:T(8,128)(2,1)}), bf16[8,80,512]{2,1,0:T(8,128)(2,1)S(1)}, u32[]{:S(2)}, u32[]{:S(2)}) %all-to-all-start.3) | async-done | bytes 655392 | tf_op jit(solution)/shard_map/all_to_all | solution.py:525
  164.1 3.5 %middle.1 = (f32[64,512]{1,0:T(8,128)S(1)}, f32[32,128]{1,0:T(8,128)S(1)}) custom-call(s32[121]{0:T(128)S(1)} %concatenate.13.info, bf16[8,80,512]{2,1,0:T(8,128)(2,1)S(1)} %all-to-all-done.3.parts, f32[8,8,128]{2,1,0:T(8,128)S(1)} %bitcast_reduce_fusion.refs_0_.known, f32[8,8,8,128]{3,2,1,0:T(8,128)S(1)} %bitcast.44), custom_call_target="tpu_custom_call" | custom-call | tf_op jit(solution)/shard_map/middle/pallas_call | solution.py:362
  167.6 1.7 collective-permute-start.18
  170.2 19.3 %all_to_all.28 = f32[64,16,128]{2,1,0:T(8,128)S(1)} all-to-all(f32[64,16,128]{2,1,0:T(8,128)S(1)} %broadcast_in_dim.113), channel_id=1, replica_groups=mesh['y'=4,'zh'=2,'core'=2,'x'=4,'zl'=2] {'y','zh','x','zl'}, dimensions={0} | all-to-all | bytes 1048576 | tf_op jit(solution)/shard_map/all_to_all | solution.py:378
  189.5 2.0 collective-permute-start.19
  192.3 3.5 %last.1 = f32[64,512]{1,0:T(8,128)} custom-call(s32[121]{0:T(128)S(1)} %concatenate.13.info, f32[32,128]{1,0:T(8,128)S(1)} %pad_maximum_fusion.1.message, f32[64,512]{1,0:T(8,128)S(1)} %get-tuple-element.58.image, f32[8,8,128]{2,1,0:T(8,128)S(1)} %bitcast_reduce_fusion.refs_0_.known), custom_call_target="tpu_custom_call" | custom-call | tf_op jit(solution)/shard_map/last/pallas_call | solution.py:362
  (67 shorter events, 16.9 us)
Async XLA Ops:
  0.0 17.6 %copy-start.3 = (s32[1,1,24]{2,1,0:T(1,128)S(1)}, s32[1,1,24]{2,1,0:T(1,128)}, u32[]{:S(2)}) copy-start(s32[1,1,24]{2,1,0:T(1,128)} %param.8) | copy-start | bytes 292
  0.0 17.9 %copy-start.4 = (s32[1,1,24]{2,1,0:T(1,128)S(1)}, s32[1,1,24]{2,1,0:T(1,128)}, u32[]{:S(2)}) copy-start(s32[1,1,24]{2,1,0:T(1,128)} %param.7) | copy-start | bytes 292
  1.3 17.3 %collective-permute-start = (bf16[512,1024]{1,0:T(8,128)(2,1)S(1)}, bf16[512,1024]{1,0:T(8,128)(2,1)}, u32[]{:S(2)}, u32[]{:S(2)}) collective-permute-start(bf16[512,1024]{1,0:T(8,128)(2,1)S(1)} %dynamic-slice_bitcast_fusion.1.refs_0_), channel_id=1, source_target_pairs={{0,8},{8,0},{1,9},{9,1},{2,10},{10,2},{3,11},{11,3},{4,12},{12,4},... | collective-permute-start | bytes 3145736 | tf_op jit(solution)/shard_map/ppermute | solution.py:373
  2.8 32.2 %collective-permute-start.2 = (bf16[512,1024]{1,0:T(8,128)(2,1)S(1)}, bf16[512,1024]{1,0:T(8,128)(2,1)S(1)}, u32[]{:S(2)}, u32[]{:S(2)}) collective-permute-start(bf16[512,1024]{1,0:T(8,128)(2,1)S(1)} %dynamic-slice_bitcast_fusion.1.refs_0_), channel_id=1, source_target_pairs={{0,32},{32,64},{64,96},{96,0},{1,33},{33,65},{65,97},{97,1},{2,34}... | collective-permute-start | bytes 3145736 | tf_op jit(solution)/shard_map/ppermute | solution.py:400
  4.2 30.8 %collective-permute-start.3 = (bf16[512,1024]{1,0:T(8,128)(2,1)S(1)}, bf16[512,1024]{1,0:T(8,128)(2,1)S(1)}, u32[]{:S(2)}, u32[]{:S(2)}) collective-permute-start(bf16[512,1024]{1,0:T(8,128)(2,1)S(1)} %dynamic-slice_bitcast_fusion.1.refs_0_), channel_id=1, source_target_pairs={{0,96},{32,0},{64,32},{96,64},{1,97},{33,1},{65,33},{97,65},{2,98}... | collective-permute-start | bytes 3145736 | tf_op jit(solution)/shard_map/ppermute | solution.py:404
  7.9 27.1 %collective-permute-start.1 = (bf16[512,1024]{1,0:T(8,128)(2,1)}, bf16[512,1024]{1,0:T(8,128)(2,1)}, u32[]{:S(2)}, u32[]{:S(2)}) collective-permute-start(bf16[512,1024]{1,0:T(8,128)(2,1)} %dynamic-slice_bitcast_fusion), channel_id=1, source_target_pairs={{0,17},{17,0},{1,16},{16,1},{2,19},{19,2},{3,18},{18,3},{4,21},{21... | collective-permute-start | bytes 3145736 | tf_op jit(solution)/shard_map/ppermute | solution.py:425
  18.6 3.4 %copy-start = (bf16[4096,1024]{1,0:T(8,128)(2,1)S(1)}, bf16[4096,1024]{1,0:T(8,128)(2,1)}, u32[]{:S(2)}) copy-start(bf16[4096,1024]{1,0:T(8,128)(2,1)} %param.5) | copy-start | bytes 25165828
  22.0 19.0 %copy-start.1 = (bf16[4096,1024]{1,0:T(8,128)(2,1)S(1)}, bf16[4096,1024]{1,0:T(8,128)(2,1)}, u32[]{:S(2)}) copy-start(bf16[4096,1024]{1,0:T(8,128)(2,1)} %param.5) | copy-start | bytes 25165828
  35.0 7.4 %collective-permute-start.4 = (bf16[512,1024]{1,0:T(8,128)(2,1)}, bf16[512,1024]{1,0:T(8,128)(2,1)S(1)}, u32[]{:S(2)}, u32[]{:S(2)}) collective-permute-start(bf16[512,1024]{1,0:T(8,128)(2,1)} %collective-permute-done.1.refs_0_), channel_id=1, source_target_pairs={{0,8},{8,0},{1,9},{9,1},{2,10},{10,2},{3,11},{11,3},{4,12},{12,4},... | collective-permute-start | bytes 3145736 | tf_op jit(solution)/shard_map/ppermute | solution.py:373
  36.1 9.5 %collective-permute-start.5 = (bf16[512,1024]{1,0:T(8,128)(2,1)S(1)}, bf16[512,1024]{1,0:T(8,128)(2,1)S(1)}, u32[]{:S(2)}, u32[]{:S(2)}) collective-permute-start(bf16[512,1024]{1,0:T(8,128)(2,1)S(1)} %collective-permute-done.2.refs_1_), channel_id=1, source_target_pairs={{0,8},{8,0},{1,9},{9,1},{2,10},{10,2},{3,11},{11,3},{4,12},{12,4},... | collective-permute-start | bytes 3145736 | tf_op jit(solution)/shard_map/ppermute | solution.py:373
  36.2 9.5 %collective-permute-start.6 = (bf16[512,1024]{1,0:T(8,128)(2,1)S(1)}, bf16[512,1024]{1,0:T(8,128)(2,1)S(1)}, u32[]{:S(2)}, u32[]{:S(2)}) collective-permute-start(bf16[512,1024]{1,0:T(8,128)(2,1)S(1)} %collective-permute-done.3.refs_2_), channel_id=1, source_target_pairs={{0,8},{8,0},{1,9},{9,1},{2,10},{10,2},{3,11},{11,3},{4,12},{12,4},... | collective-permute-start | bytes 3145736 | tf_op jit(solution)/shard_map/ppermute | solution.py:373
  36.8 14.5 %collective-permute-start.8 = (bf16[512,1024]{1,0:T(8,128)(2,1)S(1)}, bf16[512,1024]{1,0:T(8,128)(2,1)S(1)}, u32[]{:S(2)}, u32[]{:S(2)}) collective-permute-start(bf16[512,1024]{1,0:T(8,128)(2,1)S(1)} %get-tuple-element.62), channel_id=1, source_target_pairs={{0,1},{8,25},{1,16},{9,8},{16,17},{24,9},{17,0},{25,24},{2,3},{10,... | collective-permute-start | bytes 3145736 | tf_op jit(solution)/shard_map/ppermute | solution.py:421
  39.5 14.2 %collective-permute-start.7 = (bf16[512,1024]{1,0:T(8,128)(2,1)}, bf16[512,1024]{1,0:T(8,128)(2,1)S(1)}, u32[]{:S(2)}, u32[]{:S(2)}) collective-permute-start(bf16[512,1024]{1,0:T(8,128)(2,1)} %collective-permute-done.1.refs_0_), channel_id=1, source_target_pairs={{0,32},{8,104},{32,64},{40,8},{64,96},{72,40},{96,0},{104,72},{1,3... | collective-permute-start | bytes 3145736 | tf_op jit(solution)/shard_map/ppermute | solution.py:408
  42.4 22.5 %collective-permute-start.10 = (bf16[512,1024]{1,0:T(8,128)(2,1)S(1)}, bf16[512,1024]{1,0:T(8,128)(2,1)S(1)}, u32[]{:S(2)}, u32[]{:S(2)}) collective-permute-start(bf16[512,1024]{1,0:T(8,128)(2,1)S(1)} %get-tuple-element.45), channel_id=1, source_target_pairs={{0,32},{8,104},{32,64},{40,8},{64,96},{72,40},{96,0},{104,72},{1,3... | collective-permute-start | bytes 3145736 | tf_op jit(solution)/shard_map/ppermute | solution.py:408
  53.7 13.9 %collective-permute-start.11 = (bf16[512,1024]{1,0:T(8,128)(2,1)S(1)}, bf16[512,1024]{1,0:T(8,128)(2,1)S(1)}, u32[]{:S(2)}, u32[]{:S(2)}) collective-permute-start(bf16[512,1024]{1,0:T(8,128)(2,1)S(1)} %collective-permute-done.8), channel_id=1, source_target_pairs={{0,1},{8,25},{1,16},{9,8},{16,17},{24,9},{17,0},{25,24},{2,3},{10,... | collective-permute-start | bytes 3145736 | tf_op jit(solution)/shard_map/ppermute | solution.py:421
  54.7 14.6 %collective-permute-start.9 = (bf16[512,1024]{1,0:T(8,128)(2,1)S(1)}, bf16[512,1024]{1,0:T(8,128)(2,1)S(1)}, u32[]{:S(2)}, u32[]{:S(2)}) collective-permute-start(bf16[512,1024]{1,0:T(8,128)(2,1)S(1)} %collective-permute-done.7.refs_0_), channel_id=1, source_target_pairs={{0,8},{8,0},{1,9},{9,1},{2,10},{10,2},{3,11},{11,3},{4,12},{12,4},... | collective-permute-start | bytes 3145736 | tf_op jit(solution)/shard_map/ppermute | solution.py:373
  54.7 21.2 %collective-permute-start.12 = (bf16[512,1024]{1,0:T(8,128)(2,1)S(1)}, bf16[512,1024]{1,0:T(8,128)(2,1)S(1)}, u32[]{:S(2)}, u32[]{:S(2)}) collective-permute-start(bf16[512,1024]{1,0:T(8,128)(2,1)S(1)} %collective-permute-done.7.refs_0_), channel_id=1, source_target_pairs={{0,32},{8,104},{32,64},{40,8},{64,96},{72,40},{96,0},{104,72},{1,3... | collective-permute-start | bytes 3145736 | tf_op jit(solution)/shard_map/ppermute | solution.py:408
  64.9 11.0 %collective-permute-start.14 = (bf16[512,1024]{1,0:T(8,128)(2,1)S(1)}, bf16[512,1024]{1,0:T(8,128)(2,1)S(1)}, u32[]{:S(2)}, u32[]{:S(2)}) collective-permute-start(bf16[512,1024]{1,0:T(8,128)(2,1)S(1)} %collective-permute-done.10.refs_2_), channel_id=1, source_target_pairs={{0,8},{8,0},{1,9},{9,1},{2,10},{10,2},{3,11},{11,3},{4,12},{12,4},... | collective-permute-start | bytes 3145736 | tf_op jit(solution)/shard_map/ppermute | solution.py:373
  67.6 8.3 %collective-permute-start.15 = (bf16[512,1024]{1,0:T(8,128)(2,1)S(1)}, bf16[512,1024]{1,0:T(8,128)(2,1)S(1)}, u32[]{:S(2)}, u32[]{:S(2)}) collective-permute-start(bf16[512,1024]{1,0:T(8,128)(2,1)S(1)} %collective-permute-done.11.refs_3_), channel_id=1, source_target_pairs={{0,8},{8,0},{1,9},{9,1},{2,10},{10,2},{3,11},{11,3},{4,12},{12,4},... | collective-permute-start | bytes 3145736 | tf_op jit(solution)/shard_map/ppermute | solution.py:373
  69.3 6.6 %copy-start.2 = (s32[512]{0:T(512)S(1)}, s32[512]{0:T(512)}, u32[]{:S(2)}) copy-start(s32[512]{0:T(512)} %param.6) | copy-start | bytes 6148
  75.9 3.8 %collective-permute-start.13 = (bf16[512,1024]{1,0:T(8,128)(2,1)S(1)}, bf16[512,1024]{1,0:T(8,128)(2,1)S(1)}, u32[]{:S(2)}, u32[]{:S(2)}) collective-permute-start(bf16[512,1024]{1,0:T(8,128)(2,1)S(1)} %collective-permute-done.12.refs_2_), channel_id=1, source_target_pairs={{0,8},{8,0},{1,9},{9,1},{2,10},{10,2},{3,11},{11,3},{4,12},{12,4},... | collective-permute-start | bytes 3145736 | tf_op jit(solution)/shard_map/ppermute | solution.py:373
  105.6 2.6 %collective-permute-start.16 = (f32[8,8,128]{2,1,0:T(8,128)S(1)}, f32[8,8,128]{2,1,0:T(8,128)S(1)}, u32[]{:S(2)}, u32[]{:S(2)}) collective-permute-start(f32[8,8,128]{2,1,0:T(8,128)S(1)} %bitcast_reduce_fusion.refs_0_.known), channel_id=1, source_target_pairs={{0,8},{8,0},{1,9},{9,1},{2,10},{10,2},{3,11},{11,3},{4,12},{12,4},... | collective-permute-start | bytes 98312 | tf_op jit(solution)/shard_map/ppermute | solution.py:373
  141.2 4.6 %collective-permute-start.17 = (bf16[8,80,512]{2,1,0:T(8,128)(2,1)S(1)}, bf16[8,80,512]{2,1,0:T(8,128)(2,1)S(1)}, u32[]{:S(2)}, u32[]{:S(2)}) collective-permute-start(bf16[8,80,512]{2,1,0:T(8,128)(2,1)S(1)} %all_to_all.27.refs_0_), channel_id=1, source_target_pairs={{0,8},{8,0},{1,9},{9,1},{2,10},{10,2},{3,11},{11,3},{4,12},{12,4},... | collective-permute-start | bytes 1966088 | tf_op jit(solution)/shard_map/ppermute | solution.py:373
  150.4 13.7 %all-to-all-start.3 = ((bf16[8,80,512]{2,1,0:T(8,128)(2,1)}), bf16[8,80,512]{2,1,0:T(8,128)(2,1)S(1)}, u32[]{:S(2)}, u32[]{:S(2)}) async-start(bf16[8,80,512]{2,1,0:T(8,128)(2,1)} %product.3), calls=%async_computation.3 | async-start | bytes 1310720 | tf_op jit(solution)/shard_map/all_to_all | solution.py:525
  167.6 2.5 %collective-permute-start.18 = (f32[16,128]{1,0:T(8,128)S(1)}, f32[16,128]{1,0:T(8,128)S(1)}, u32[]{:S(2)}, u32[]{:S(2)}) collective-permute-start(f32[16,128]{1,0:T(8,128)S(1)} %constant_dynamic-slice_fusion), channel_id=1, source_target_pairs={{0,8},{8,0},{1,9},{9,1},{2,10},{10,2},{3,11},{11,3},{4,12},{12,4},... | collective-permute-start | bytes 24584 | tf_op jit(solution)/shard_map/ppermute | solution.py:373
  189.5 2.8 %collective-permute-start.19 = (f32[16,128]{1,0:T(8,128)S(1)}, f32[16,128]{1,0:T(8,128)S(1)}, u32[]{:S(2)}, u32[]{:S(2)}) collective-permute-start(f32[16,128]{1,0:T(8,128)S(1)} %reduce_sum.99), channel_id=1, source_target_pairs={{0,8},{8,0},{1,9},{9,1},{2,10},{10,2},{3,11},{11,3},{4,12},{12,4},... | collective-permute-start | bytes 24584 | tf_op jit(solution)/shard_map/ppermute | solution.py:373

commit v12 on v11

--- a/solution.py
+++ b/solution.py
@@ -31,7 +31,7 @@
     columns, refs = refs[:arrived], refs[arrived:]
     if first:
         _, old_degree, *refs = refs
-    tiles, degree, half_column, made, sem_out = refs
+    tiles, degree, made, sem_out = refs
     block_index = info[1]
     stores = made.shape[0]
     if first:
@@ -52,6 +52,8 @@
 
         slot = lax.rem(entry, stores)
         t = info[ROWS + entry]
+        wide = column[...].astype(F32)
+        half_column = 0.5 * jnp.sum(wide * wide, axis=1, keepdims=True)
         sums = []
         for n in range(2):
             lanes = pl.ds(n * 256, 256)
@@ -59,7 +61,7 @@
                 column[...], slab[t, lanes, :], (((1,), (1,)), ((), ())), preferred_element_type=F32
             )
             half_row = half_rows[pl.ds(t, 1), lanes]
-            w = jnp.exp2(RATE * ((inner - half_row) - half_column[...])).astype(BF16)
+            w = jnp.exp2(RATE * ((inner - half_row) - half_column)).astype(BF16)
             made[slot, :, lanes] = w
             sums.append(jnp.sum(w.astype(F32), axis=0, keepdims=True))
         old = degree[pl.ds(t, 1), :]
@@ -80,14 +82,6 @@
 
     for s, column in enumerate(columns):
         low, high = info[STARTS + first + s], info[STARTS + first + s + 1]
-
-        @pl.when(low < high)
-        def _(column=column):
-            wide = column[...].astype(F32)
-            half_column[...] = jnp.broadcast_to(
-                0.5 * jnp.sum(wide * wide, axis=1, keepdims=True), half_column.shape
-            )
-
         lax.fori_loop(low, high, functools.partial(step, column, first + s == 0), 0)
     for back in range(stores):
 
@@ -120,7 +114,6 @@
         + ([hbm, vmem] if made else []),
         out_specs=(hbm, vmem),
         scratch_shapes=[
-            pltpu.VMEM((TILE, 256), F32),
             pltpu.VMEM((4, TILE, TILE), BF16),
             pltpu.SemaphoreType.DMA((4,)),
         ],
@@ -171,7 +164,6 @@
     count = info[0]
     core = info[2]
     depth = held.shape[0]
-    running[...] = jnp.zeros_like(running)
 
     def fetch(entry):
         slot = lax.rem(entry, depth)
@@ -198,6 +190,14 @@
         def _():
             fetch(jnp.int32(entry)).start()
 
+    running[...] = jnp.zeros_like(running)
+    if not first:
+        sums = jnp.sum(mine[:, K:, :].astype(F32), axis=0) + jnp.sum(others[:, K:, :].astype(F32), axis=0)
+        sums = value_of(sums)
+        terms = terms_of(sums)
+        for t in range(SLAB_TILES):
+            out[t, K:, :] = terms
+
     def step(turn, carry):
         entries = [4 * turn + i for i in range(4)]
         for entry in entries:
@@ -221,13 +221,9 @@
     if first:
         out[...] = running[...].astype(BF16)
     else:
-        sums = jnp.sum(mine[:, K:, :].astype(F32), axis=0) + jnp.sum(others[:, K:, :].astype(F32), axis=0)
-        sums = value_of(sums)
         lead, _ = lead_of(sums)
-        terms = terms_of(sums)
         for t in range(SLAB_TILES):
             out[t, :K, :] = (running[t] - lead * degree[t : t + 1, :]).astype(BF16)
-            out[t, K:, :] = terms
 
 
 def product(info, tiles, *operands):

time: 198 us -> 196 us (0.990)
    ppermute x2, waiting for transfers between devices: 7.48 us -> 4.95 us  [apart_z(): return lax.ppermute(value, ('zh', 'core', 'zl'), moves)]
    ppermute x3, starting transfers between devices: 6.23 us -> 3.85 us  [apart(): lax.ppermute(value, ('y', 'core'), [(2 * i + k, 2 * ((i + 1 + 2 * k) % 4)...]
    ppermute x12, starting transfers between devices: 13 us -> 15.4 us  [swap_cores(): return lax.ppermute(value, 'core', [(0, 1), (1, 0)])]
    ppermute x1, waiting for transfers between devices: 7.45 us -> 9.71 us  [cross(): return lax.ppermute(value, ('zh', 'zl'), [(0, 3), (3, 0), (1, 2), (2, 1)])]
  transfers between devices with their start and end apart: 21 -> 21, of which waited for: 11 -> 12; matrix products, arithmetic and copies ran while one was open for 4% -> 4% of each run, Pallas kernels for 6% -> 6%
where the time goes in v12:
time: 196 us
  blocking collectives  74.1 us (38%)
  waiting for transfers between devices  45.6 us (23%)
  starting transfers between devices  33.1 us (17%)
  Pallas kernels  28.2 us (14%)
  local copies, waits for them, and re-layouts  7.31 us (4%)
  other arithmetic  6.29 us (3%)
    all_to_all x2, blocking collectives, share(): lax.all_to_all(jnp.broadcast_to(value[None], (size,) + value.shape), axes...  37.9 us
    all_to_all x1, blocking collectives, shards(): lax.all_to_all(jnp.broadcast_to(sent[None], (8,) + sent.shape).reshape(8...  26.4 us
    ppermute x3, waiting for transfers between devices, apart(): lax.ppermute(value, ('y', 'core'), [(2 * i + k, 2 * ((i + 1 + 2 * k) % 4)...  16.9 us
    ppermute x12, starting transfers between devices, swap_cores(): return lax.ppermute(value, 'core', [(0, 1), (1, 0)])  15.4 us
    pallas_call x6, Pallas kernels, build(): pl.pallas_call(functools.partial(build_kernel, first, arrived), out_shape...  12.4 us
    all_to_all x1, blocking collectives, shards(): parts = lax.all_to_all(running, COL, 0, 0, tiled=True)  9.81 us
    ppermute x1, waiting for transfers between devices, cross(): return lax.ppermute(value, ('zh', 'zl'), [(0, 3), (3, 0), (1, 2), (2, 1)])  9.71 us
    all_to_all x1, waiting for transfers between devices, shards(): parts = lax.all_to_all(running, COL, 0, 0, tiled=True)  9.57 us
  transfers between devices with their start and end apart: 21, of which 12 were waited for; matrix products, arithmetic and copies ran while one was open for 4% of the time, Pallas kernels for 6%

profile of v12, /device:TPU:1, one launch (start us, length us, event | category | flops | bytes accessed | tf_op | source)
XLA Modules:
  0.0 195.6 jit_solution(15497148100421929105)
XLA Ops:
  5.7 2.3 %dynamic-slice_bitcast_fusion = bf16[512,1024]{1,0:T(8,128)(2,1)} fusion(bf16[8,512,1024]{2,1,0:T(8,128)(2,1)} %bitcast.37, s32[]{:T(128)S(6)} %select_n.198), kind=kLoop, calls=%fused_computation.1 | loop fusion | bytes 2097156 | tf_op jit(solution)/shard_map/jit(dynamic_index_in_dim)/squeeze | solution.py:478
  7.9 3.8 %collective-permute-start.1 = (bf16[512,1024]{1,0:T(8,128)(2,1)}, bf16[512,1024]{1,0:T(8,128)(2,1)}, u32[]{:S(2)}, u32[]{:S(2)}) collective-permute-start(bf16[512,1024]{1,0:T(8,128)(2,1)} %dynamic-slice_bitcast_fusion), channel_id=1, source_target_pairs={{0,17},{17,0},{1,16},{16,1},{2,19},{19,2},{3,18},{18,3},{4,21},{21... | collective-permute-start | bytes 3145736 | tf_op jit(solution)/shard_map/ppermute | solution.py:421
  11.7 5.1 %multiply_reduce_fusion = f32[4096]{0:T(1024)S(1)} fusion(bf16[4096,1024]{1,0:T(8,128)(2,1)} %param.5), kind=kLoop, calls=%fused_computation | loop fusion | flops 12578816 | bytes 8404992 | tf_op jit(solution)/shard_map/reduce_sum | solution.py:480
  18.6 3.4 %copy-done = bf16[4096,1024]{1,0:T(8,128)(2,1)S(1)} copy-done((bf16[4096,1024]{1,0:T(8,128)(2,1)S(1)}, bf16[4096,1024]{1,0:T(8,128)(2,1)}, u32[]{:S(2)}) %copy-start) | copy-done | bytes 8388632
  22.0 3.2 %build_tiles.6 = (bf16[24,512,512]{2,1,0:T(8,128)(2,1)}, f32[8,512]{1,0:T(8,128)S(1)}) custom-call(s32[121]{0:T(128)S(1)} %concatenate.13.info, bf16[8,512,1024]{2,1,0:T(8,128)(2,1)S(1)} %bitcast.38, f32[8,512]{1,0:T(8,128)S(1)} %mul.134.half_rows, bf16[512,1024]{1,0:T(8,128)(2,1)S(1)} %dynamic-slice_bitcast_fusion.1.refs_0_, ...), custom_call_target="tpu_custom_call" | custom-call | flops 1610612736 | bytes 7864320 | tf_op jit(solution)/shard_map/build_tiles/pallas_call | solution.py:106
  25.3 9.7 %collective-permute-done.1.refs_0_ = bf16[512,1024]{1,0:T(8,128)(2,1)} collective-permute-done((bf16[512,1024]{1,0:T(8,128)(2,1)}, bf16[512,1024]{1,0:T(8,128)(2,1)}, u32[]{:S(2)}, u32[]{:S(2)}) %collective-permute-start.1) | collective-permute-done | bytes 1048608 | tf_op jit(solution)/shard_map/ppermute | solution.py:421
  36.8 2.7 %collective-permute-start.8 = (bf16[512,1024]{1,0:T(8,128)(2,1)S(1)}, bf16[512,1024]{1,0:T(8,128)(2,1)S(1)}, u32[]{:S(2)}, u32[]{:S(2)}) collective-permute-start(bf16[512,1024]{1,0:T(8,128)(2,1)S(1)} %get-tuple-element.62), channel_id=1, source_target_pairs={{0,1},{8,25},{1,16},{9,8},{16,17},{24,9},{17,0},{25,24},{2,3},{10,... | collective-permute-start | bytes 3145736 | tf_op jit(solution)/shard_map/ppermute | solution.py:417
  41.0 4.8 %build_tiles.7 = (bf16[24,512,512]{2,1,0:T(8,128)(2,1)}, f32[8,512]{1,0:T(8,128)S(1)}) custom-call(s32[121]{0:T(128)S(1)} %concatenate.13.info, bf16[8,512,1024]{2,1,0:T(8,128)(2,1)S(1)} %bitcast.39, f32[8,512]{1,0:T(8,128)S(1)} %mul.134.half_rows, bf16[512,1024]{1,0:T(8,128)(2,1)} %collective-permute-done.1.refs_0_, ...), custom_call_target="tpu_custom_call", output_to_operand_aliasing={{0}: (6, {})} | custom-call | flops 2147483648 | bytes 10485760 | tf_op jit(solution)/shard_map/build_tiles/pallas_call | solution.py:106
  45.8 2.4 %collective-permute-start.10 = (bf16[512,1024]{1,0:T(8,128)(2,1)S(1)}, bf16[512,1024]{1,0:T(8,128)(2,1)S(1)}, u32[]{:S(2)}, u32[]{:S(2)}) collective-permute-start(bf16[512,1024]{1,0:T(8,128)(2,1)S(1)} %get-tuple-element.45), channel_id=1, source_target_pairs={{0,32},{8,104},{32,64},{40,8},{64,96},{72,40},{96,0},{104,72},{1,3... | collective-permute-start | bytes 3145736 | tf_op jit(solution)/shard_map/ppermute | solution.py:404
  49.0 2.2 %collective-permute-done.8 = bf16[512,1024]{1,0:T(8,128)(2,1)S(1)} collective-permute-done((bf16[512,1024]{1,0:T(8,128)(2,1)S(1)}, bf16[512,1024]{1,0:T(8,128)(2,1)S(1)}, u32[]{:S(2)}, u32[]{:S(2)}) %collective-permute-start.8) | collective-permute-done | bytes 1048608 | tf_op jit(solution)/shard_map/ppermute | solution.py:417
  51.3 2.4 %collective-permute-done.7.refs_0_ = bf16[512,1024]{1,0:T(8,128)(2,1)S(1)} collective-permute-done((bf16[512,1024]{1,0:T(8,128)(2,1)}, bf16[512,1024]{1,0:T(8,128)(2,1)S(1)}, u32[]{:S(2)}, u32[]{:S(2)}) %collective-permute-start.7) | collective-permute-done | bytes 1048608 | tf_op jit(solution)/shard_map/ppermute | solution.py:404
  54.7 1.7 collective-permute-start.9
  56.4 8.5 %collective-permute-done.10.refs_2_ = bf16[512,1024]{1,0:T(8,128)(2,1)S(1)} collective-permute-done((bf16[512,1024]{1,0:T(8,128)(2,1)S(1)}, bf16[512,1024]{1,0:T(8,128)(2,1)S(1)}, u32[]{:S(2)}, u32[]{:S(2)}) %collective-permute-start.10) | collective-permute-done | bytes 1048608 | tf_op jit(solution)/shard_map/ppermute | solution.py:404
  64.9 2.7 %collective-permute-done.11.refs_3_ = bf16[512,1024]{1,0:T(8,128)(2,1)S(1)} collective-permute-done((bf16[512,1024]{1,0:T(8,128)(2,1)S(1)}, bf16[512,1024]{1,0:T(8,128)(2,1)S(1)}, u32[]{:S(2)}, u32[]{:S(2)}) %collective-permute-start.11) | collective-permute-done | bytes 1048608 | tf_op jit(solution)/shard_map/ppermute | solution.py:417
  67.6 1.6 collective-permute-start.15
  69.9 6.0 %collective-permute-done.12.refs_2_ = bf16[512,1024]{1,0:T(8,128)(2,1)S(1)} collective-permute-done((bf16[512,1024]{1,0:T(8,128)(2,1)S(1)}, bf16[512,1024]{1,0:T(8,128)(2,1)S(1)}, u32[]{:S(2)}, u32[]{:S(2)}) %collective-permute-start.12) | collective-permute-done | bytes 1048608 | tf_op jit(solution)/shard_map/ppermute | solution.py:404
  76.0 2.3 %build_tiles.10 = (bf16[24,512,512]{2,1,0:T(8,128)(2,1)}, f32[8,512]{1,0:T(8,128)S(1)}) custom-call(s32[121]{0:T(128)S(1)} %concatenate.13.info, bf16[8,512,1024]{2,1,0:T(8,128)(2,1)S(1)} %bitcast.42, f32[8,512]{1,0:T(8,128)S(1)} %mul.134.half_rows, bf16[512,1024]{1,0:T(8,128)(2,1)S(1)} %collective-permute-done.14.refs_0_, ...), custom_call_target="tpu_custom_call", output_to_operand_aliasing={{0}: (6, {})} | custom-call | flops 2147483648 | bytes 10485760 | tf_op jit(solution)/shard_map/build_tiles/pallas_call | solution.py:106
  79.2 26.4 %all_to_all.25 = f32[64,8,128]{2,1,0:T(8,128)S(1)} all-to-all(f32[64,8,128]{2,1,0:T(8,128)S(1)} %bitcast.46), channel_id=1, replica_groups=mesh['y'=4,'zh'=2,'core'=2,'x'=4,'zl'=2] {'y','zh','x','zl'}, dimensions={0} | all-to-all | bytes 524288 | tf_op jit(solution)/shard_map/all_to_all | solution.py:508
  105.6 1.7 collective-permute-start.16
  108.2 3.3 %product.2 = bf16[8,64,512]{2,1,0:T(8,128)(2,1)S(1)} custom-call(s32[121]{0:T(128)S(1)} %concatenate.13.info, bf16[24,512,512]{2,1,0:T(8,128)(2,1)} %get-tuple-element.55.tiles, f32[8,8,128]{2,1,0:T(8,128)S(1)} %bitcast_reduce_fusion.refs_0_.known, f32[8,8,128]{2,1,0:T(8,128)S(1)} %collective-permute-done.16.refs_1_), custom_call_target="tpu_custom_call" | custom-call | tf_op jit(solution)/shard_map/product/pallas_call | solution.py:232
  111.5 9.8 %all_to_all.26.parts = bf16[8,64,512]{2,1,0:T(8,128)(2,1)S(1)} all-to-all(bf16[8,64,512]{2,1,0:T(8,128)(2,1)S(1)} %product.2), channel_id=1, replica_groups=mesh['y'=4,'zh'=2,'core'=2,'x'=4,'zl'=2] {'x','zl'}, dimensions={0} | all-to-all | bytes 1048576 | tf_op jit(solution)/shard_map/all_to_all | solution.py:516
  122.5 18.6 %all_to_all.27.refs_0_ = bf16[8,80,512]{2,1,0:T(8,128)(2,1)S(1)} all-to-all(bf16[8,80,512]{2,1,0:T(8,128)(2,1)S(1)} %broadcast_in_dim.112), channel_id=1, replica_groups=mesh['y'=4,'zh'=2,'core'=2,'x'=4,'zl'=2] {'y','zh'}, dimensions={0} | all-to-all | bytes 1310720 | tf_op jit(solution)/shard_map/all_to_all | solution.py:374
  141.1 2.9 %collective-permute-start.17 = (bf16[8,80,512]{2,1,0:T(8,128)(2,1)S(1)}, bf16[8,80,512]{2,1,0:T(8,128)(2,1)S(1)}, u32[]{:S(2)}, u32[]{:S(2)}) collective-permute-start(bf16[8,80,512]{2,1,0:T(8,128)(2,1)S(1)} %all_to_all.27.refs_0_), channel_id=1, source_target_pairs={{0,8},{8,0},{1,9},{9,1},{2,10},{10,2},{3,11},{11,3},{4,12},{12,4},... | collective-permute-start | bytes 1966088 | tf_op jit(solution)/shard_map/ppermute | solution.py:369
  144.1 1.7 collective-permute-done.17.refs_1_
  145.8 4.4 %product.3 = bf16[8,80,512]{2,1,0:T(8,128)(2,1)} custom-call(s32[121]{0:T(128)S(1)} %concatenate.13.info, bf16[24,512,512]{2,1,0:T(8,128)(2,1)} %get-tuple-element.55.tiles, bf16[8,80,512]{2,1,0:T(8,128)(2,1)S(1)} %all_to_all.27.refs_0_, bf16[8,80,512]{2,1,0:T(8,128)(2,1)S(1)} %collective-permute-done.17.refs_1_, f32[8,512]{1,0:T(8,128)S(1)} %get-tuple-element.56.refs_2_), custom_call_target="tpu_custom_call" | custom-call | tf_op jit(solution)/shard_map/product/pallas_call | solution.py:232
  150.2 3.6 %all-to-all-start.3 = ((bf16[8,80,512]{2,1,0:T(8,128)(2,1)}), bf16[8,80,512]{2,1,0:T(8,128)(2,1)S(1)}, u32[]{:S(2)}, u32[]{:S(2)}) async-start(bf16[8,80,512]{2,1,0:T(8,128)(2,1)} %product.3), calls=%async_computation.3 | async-start | bytes 1310720 | tf_op jit(solution)/shard_map/all_to_all | solution.py:521
  153.8 9.6 %all-to-all-done.3.parts = bf16[8,80,512]{2,1,0:T(8,128)(2,1)S(1)} async-done(((bf16[8,80,512]{2,1,0:T(8,128)(2,1)}), bf16[8,80,512]{2,1,0:T(8,128)(2,1)S(1)}, u32[]{:S(2)}, u32[]{:S(2)}) %all-to-all-start.3) | async-done | bytes 655392 | tf_op jit(solution)/shard_map/all_to_all | solution.py:521
  163.3 3.5 %middle.1 = (f32[64,512]{1,0:T(8,128)S(1)}, f32[32,128]{1,0:T(8,128)S(1)}) custom-call(s32[121]{0:T(128)S(1)} %concatenate.13.info, bf16[8,80,512]{2,1,0:T(8,128)(2,1)S(1)} %all-to-all-done.3.parts, f32[8,8,128]{2,1,0:T(8,128)S(1)} %bitcast_reduce_fusion.refs_0_.known, f32[8,8,8,128]{3,2,1,0:T(8,128)S(1)} %bitcast.44), custom_call_target="tpu_custom_call" | custom-call | tf_op jit(solution)/shard_map/middle/pallas_call | solution.py:358
  166.9 2.3 %collective-permute-start.18 = (f32[16,128]{1,0:T(8,128)S(1)}, f32[16,128]{1,0:T(8,128)S(1)}, u32[]{:S(2)}, u32[]{:S(2)}) collective-permute-start(f32[16,128]{1,0:T(8,128)S(1)} %constant_dynamic-slice_fusion), channel_id=1, source_target_pairs={{0,8},{8,0},{1,9},{9,1},{2,10},{10,2},{3,11},{11,3},{4,12},{12,4},... | collective-permute-start | bytes 24584 | tf_op jit(solution)/shard_map/ppermute | solution.py:369
  170.0 19.3 %all_to_all.28 = f32[64,16,128]{2,1,0:T(8,128)S(1)} all-to-all(f32[64,16,128]{2,1,0:T(8,128)S(1)} %broadcast_in_dim.113), channel_id=1, replica_groups=mesh['y'=4,'zh'=2,'core'=2,'x'=4,'zl'=2] {'y','zh','x','zl'}, dimensions={0} | all-to-all | bytes 1048576 | tf_op jit(solution)/shard_map/all_to_all | solution.py:374
  189.4 2.0 collective-permute-start.19
  192.1 3.5 %last.1 = f32[64,512]{1,0:T(8,128)} custom-call(s32[121]{0:T(128)S(1)} %concatenate.13.info, f32[32,128]{1,0:T(8,128)S(1)} %pad_maximum_fusion.1.message, f32[64,512]{1,0:T(8,128)S(1)} %get-tuple-element.58.image, f32[8,8,128]{2,1,0:T(8,128)S(1)} %bitcast_reduce_fusion.refs_0_.known), custom_call_target="tpu_custom_call" | custom-call | tf_op jit(solution)/shard_map/last/pallas_call | solution.py:358
  (67 shorter events, 17.3 us)
Async XLA Ops:
  0.0 17.6 %copy-start.3 = (s32[1,1,24]{2,1,0:T(1,128)S(1)}, s32[1,1,24]{2,1,0:T(1,128)}, u32[]{:S(2)}) copy-start(s32[1,1,24]{2,1,0:T(1,128)} %param.8) | copy-start | bytes 292
  0.0 17.9 %copy-start.4 = (s32[1,1,24]{2,1,0:T(1,128)S(1)}, s32[1,1,24]{2,1,0:T(1,128)}, u32[]{:S(2)}) copy-start(s32[1,1,24]{2,1,0:T(1,128)} %param.7) | copy-start | bytes 292
  1.3 17.3 %collective-permute-start = (bf16[512,1024]{1,0:T(8,128)(2,1)S(1)}, bf16[512,1024]{1,0:T(8,128)(2,1)}, u32[]{:S(2)}, u32[]{:S(2)}) collective-permute-start(bf16[512,1024]{1,0:T(8,128)(2,1)S(1)} %dynamic-slice_bitcast_fusion.1.refs_0_), channel_id=1, source_target_pairs={{0,8},{8,0},{1,9},{9,1},{2,10},{10,2},{3,11},{11,3},{4,12},{12,4},... | collective-permute-start | bytes 3145736 | tf_op jit(solution)/shard_map/ppermute | solution.py:369
  2.8 32.2 %collective-permute-start.2 = (bf16[512,1024]{1,0:T(8,128)(2,1)S(1)}, bf16[512,1024]{1,0:T(8,128)(2,1)S(1)}, u32[]{:S(2)}, u32[]{:S(2)}) collective-permute-start(bf16[512,1024]{1,0:T(8,128)(2,1)S(1)} %dynamic-slice_bitcast_fusion.1.refs_0_), channel_id=1, source_target_pairs={{0,32},{32,64},{64,96},{96,0},{1,33},{33,65},{65,97},{97,1},{2,34}... | collective-permute-start | bytes 3145736 | tf_op jit(solution)/shard_map/ppermute | solution.py:396
  4.2 30.8 %collective-permute-start.3 = (bf16[512,1024]{1,0:T(8,128)(2,1)S(1)}, bf16[512,1024]{1,0:T(8,128)(2,1)S(1)}, u32[]{:S(2)}, u32[]{:S(2)}) collective-permute-start(bf16[512,1024]{1,0:T(8,128)(2,1)S(1)} %dynamic-slice_bitcast_fusion.1.refs_0_), channel_id=1, source_target_pairs={{0,96},{32,0},{64,32},{96,64},{1,97},{33,1},{65,33},{97,65},{2,98}... | collective-permute-start | bytes 3145736 | tf_op jit(solution)/shard_map/ppermute | solution.py:400
  7.9 27.1 %collective-permute-start.1 = (bf16[512,1024]{1,0:T(8,128)(2,1)}, bf16[512,1024]{1,0:T(8,128)(2,1)}, u32[]{:S(2)}, u32[]{:S(2)}) collective-permute-start(bf16[512,1024]{1,0:T(8,128)(2,1)} %dynamic-slice_bitcast_fusion), channel_id=1, source_target_pairs={{0,17},{17,0},{1,16},{16,1},{2,19},{19,2},{3,18},{18,3},{4,21},{21... | collective-permute-start | bytes 3145736 | tf_op jit(solution)/shard_map/ppermute | solution.py:421
  18.6 3.4 %copy-start = (bf16[4096,1024]{1,0:T(8,128)(2,1)S(1)}, bf16[4096,1024]{1,0:T(8,128)(2,1)}, u32[]{:S(2)}) copy-start(bf16[4096,1024]{1,0:T(8,128)(2,1)} %param.5) | copy-start | bytes 25165828
  22.0 19.0 %copy-start.1 = (bf16[4096,1024]{1,0:T(8,128)(2,1)S(1)}, bf16[4096,1024]{1,0:T(8,128)(2,1)}, u32[]{:S(2)}) copy-start(bf16[4096,1024]{1,0:T(8,128)(2,1)} %param.5) | copy-start | bytes 25165828
  35.0 10.8 %collective-permute-start.4 = (bf16[512,1024]{1,0:T(8,128)(2,1)}, bf16[512,1024]{1,0:T(8,128)(2,1)S(1)}, u32[]{:S(2)}, u32[]{:S(2)}) collective-permute-start(bf16[512,1024]{1,0:T(8,128)(2,1)} %collective-permute-done.1.refs_0_), channel_id=1, source_target_pairs={{0,8},{8,0},{1,9},{9,1},{2,10},{10,2},{3,11},{11,3},{4,12},{12,4},... | collective-permute-start | bytes 3145736 | tf_op jit(solution)/shard_map/ppermute | solution.py:369
  36.1 12.1 %collective-permute-start.5 = (bf16[512,1024]{1,0:T(8,128)(2,1)S(1)}, bf16[512,1024]{1,0:T(8,128)(2,1)S(1)}, u32[]{:S(2)}, u32[]{:S(2)}) collective-permute-start(bf16[512,1024]{1,0:T(8,128)(2,1)S(1)} %collective-permute-done.2.refs_1_), channel_id=1, source_target_pairs={{0,8},{8,0},{1,9},{9,1},{2,10},{10,2},{3,11},{11,3},{4,12},{12,4},... | collective-permute-start | bytes 3145736 | tf_op jit(solution)/shard_map/ppermute | solution.py:369
  36.2 12.0 %collective-permute-start.6 = (bf16[512,1024]{1,0:T(8,128)(2,1)S(1)}, bf16[512,1024]{1,0:T(8,128)(2,1)S(1)}, u32[]{:S(2)}, u32[]{:S(2)}) collective-permute-start(bf16[512,1024]{1,0:T(8,128)(2,1)S(1)} %collective-permute-done.3.refs_2_), channel_id=1, source_target_pairs={{0,8},{8,0},{1,9},{9,1},{2,10},{10,2},{3,11},{11,3},{4,12},{12,4},... | collective-permute-start | bytes 3145736 | tf_op jit(solution)/shard_map/ppermute | solution.py:369
  36.8 14.5 %collective-permute-start.8 = (bf16[512,1024]{1,0:T(8,128)(2,1)S(1)}, bf16[512,1024]{1,0:T(8,128)(2,1)S(1)}, u32[]{:S(2)}, u32[]{:S(2)}) collective-permute-start(bf16[512,1024]{1,0:T(8,128)(2,1)S(1)} %get-tuple-element.62), channel_id=1, source_target_pairs={{0,1},{8,25},{1,16},{9,8},{16,17},{24,9},{17,0},{25,24},{2,3},{10,... | collective-permute-start | bytes 3145736 | tf_op jit(solution)/shard_map/ppermute | solution.py:417
  39.5 14.2 %collective-permute-start.7 = (bf16[512,1024]{1,0:T(8,128)(2,1)}, bf16[512,1024]{1,0:T(8,128)(2,1)S(1)}, u32[]{:S(2)}, u32[]{:S(2)}) collective-permute-start(bf16[512,1024]{1,0:T(8,128)(2,1)} %collective-permute-done.1.refs_0_), channel_id=1, source_target_pairs={{0,32},{8,104},{32,64},{40,8},{64,96},{72,40},{96,0},{104,72},{1,3... | collective-permute-start | bytes 3145736 | tf_op jit(solution)/shard_map/ppermute | solution.py:404
  45.8 19.1 %collective-permute-start.10 = (bf16[512,1024]{1,0:T(8,128)(2,1)S(1)}, bf16[512,1024]{1,0:T(8,128)(2,1)S(1)}, u32[]{:S(2)}, u32[]{:S(2)}) collective-permute-start(bf16[512,1024]{1,0:T(8,128)(2,1)S(1)} %get-tuple-element.45), channel_id=1, source_target_pairs={{0,32},{8,104},{32,64},{40,8},{64,96},{72,40},{96,0},{104,72},{1,3... | collective-permute-start | bytes 3145736 | tf_op jit(solution)/shard_map/ppermute | solution.py:404
  53.7 13.9 %collective-permute-start.11 = (bf16[512,1024]{1,0:T(8,128)(2,1)S(1)}, bf16[512,1024]{1,0:T(8,128)(2,1)S(1)}, u32[]{:S(2)}, u32[]{:S(2)}) collective-permute-start(bf16[512,1024]{1,0:T(8,128)(2,1)S(1)} %collective-permute-done.8), channel_id=1, source_target_pairs={{0,1},{8,25},{1,16},{9,8},{16,17},{24,9},{17,0},{25,24},{2,3},{10,... | collective-permute-start | bytes 3145736 | tf_op jit(solution)/shard_map/ppermute | solution.py:417
  54.7 14.6 %collective-permute-start.9 = (bf16[512,1024]{1,0:T(8,128)(2,1)S(1)}, bf16[512,1024]{1,0:T(8,128)(2,1)S(1)}, u32[]{:S(2)}, u32[]{:S(2)}) collective-permute-start(bf16[512,1024]{1,0:T(8,128)(2,1)S(1)} %collective-permute-done.7.refs_0_), channel_id=1, source_target_pairs={{0,8},{8,0},{1,9},{9,1},{2,10},{10,2},{3,11},{11,3},{4,12},{12,4},... | collective-permute-start | bytes 3145736 | tf_op jit(solution)/shard_map/ppermute | solution.py:369
  56.4 19.4 %collective-permute-start.12 = (bf16[512,1024]{1,0:T(8,128)(2,1)S(1)}, bf16[512,1024]{1,0:T(8,128)(2,1)S(1)}, u32[]{:S(2)}, u32[]{:S(2)}) collective-permute-start(bf16[512,1024]{1,0:T(8,128)(2,1)S(1)} %collective-permute-done.7.refs_0_), channel_id=1, source_target_pairs={{0,32},{8,104},{32,64},{40,8},{64,96},{72,40},{96,0},{104,72},{1,3... | collective-permute-start | bytes 3145736 | tf_op jit(solution)/shard_map/ppermute | solution.py:404
  64.9 11.0 %collective-permute-start.14 = (bf16[512,1024]{1,0:T(8,128)(2,1)S(1)}, bf16[512,1024]{1,0:T(8,128)(2,1)S(1)}, u32[]{:S(2)}, u32[]{:S(2)}) collective-permute-start(bf16[512,1024]{1,0:T(8,128)(2,1)S(1)} %collective-permute-done.10.refs_2_), channel_id=1, source_target_pairs={{0,8},{8,0},{1,9},{9,1},{2,10},{10,2},{3,11},{11,3},{4,12},{12,4},... | collective-permute-start | bytes 3145736 | tf_op jit(solution)/shard_map/ppermute | solution.py:369
  67.6 8.3 %collective-permute-start.15 = (bf16[512,1024]{1,0:T(8,128)(2,1)S(1)}, bf16[512,1024]{1,0:T(8,128)(2,1)S(1)}, u32[]{:S(2)}, u32[]{:S(2)}) collective-permute-start(bf16[512,1024]{1,0:T(8,128)(2,1)S(1)} %collective-permute-done.11.refs_3_), channel_id=1, source_target_pairs={{0,8},{8,0},{1,9},{9,1},{2,10},{10,2},{3,11},{11,3},{4,12},{12,4},... | collective-permute-start | bytes 3145736 | tf_op jit(solution)/shard_map/ppermute | solution.py:369
  69.3 6.6 %copy-start.2 = (s32[512]{0:T(512)S(1)}, s32[512]{0:T(512)}, u32[]{:S(2)}) copy-start(s32[512]{0:T(512)} %param.6) | copy-start | bytes 6148
  75.9 2.7 %collective-permute-start.13 = (bf16[512,1024]{1,0:T(8,128)(2,1)S(1)}, bf16[512,1024]{1,0:T(8,128)(2,1)S(1)}, u32[]{:S(2)}, u32[]{:S(2)}) collective-permute-start(bf16[512,1024]{1,0:T(8,128)(2,1)S(1)} %collective-permute-done.12.refs_2_), channel_id=1, source_target_pairs={{0,8},{8,0},{1,9},{9,1},{2,10},{10,2},{3,11},{11,3},{4,12},{12,4},... | collective-permute-start | bytes 3145736 | tf_op jit(solution)/shard_map/ppermute | solution.py:369
  105.6 2.6 %collective-permute-start.16 = (f32[8,8,128]{2,1,0:T(8,128)S(1)}, f32[8,8,128]{2,1,0:T(8,128)S(1)}, u32[]{:S(2)}, u32[]{:S(2)}) collective-permute-start(f32[8,8,128]{2,1,0:T(8,128)S(1)} %bitcast_reduce_fusion.refs_0_.known), channel_id=1, source_target_pairs={{0,8},{8,0},{1,9},{9,1},{2,10},{10,2},{3,11},{11,3},{4,12},{12,4},... | collective-permute-start | bytes 98312 | tf_op jit(solution)/shard_map/ppermute | solution.py:369
  141.1 4.6 %collective-permute-start.17 = (bf16[8,80,512]{2,1,0:T(8,128)(2,1)S(1)}, bf16[8,80,512]{2,1,0:T(8,128)(2,1)S(1)}, u32[]{:S(2)}, u32[]{:S(2)}) collective-permute-start(bf16[8,80,512]{2,1,0:T(8,128)(2,1)S(1)} %all_to_all.27.refs_0_), channel_id=1, source_target_pairs={{0,8},{8,0},{1,9},{9,1},{2,10},{10,2},{3,11},{11,3},{4,12},{12,4},... | collective-permute-start | bytes 1966088 | tf_op jit(solution)/shard_map/ppermute | solution.py:369
  150.2 13.1 %all-to-all-start.3 = ((bf16[8,80,512]{2,1,0:T(8,128)(2,1)}), bf16[8,80,512]{2,1,0:T(8,128)(2,1)S(1)}, u32[]{:S(2)}, u32[]{:S(2)}) async-start(bf16[8,80,512]{2,1,0:T(8,128)(2,1)} %product.3), calls=%async_computation.3 | async-start | bytes 1310720 | tf_op jit(solution)/shard_map/all_to_all | solution.py:521
  166.9 3.1 %collective-permute-start.18 = (f32[16,128]{1,0:T(8,128)S(1)}, f32[16,128]{1,0:T(8,128)S(1)}, u32[]{:S(2)}, u32[]{:S(2)}) collective-permute-start(f32[16,128]{1,0:T(8,128)S(1)} %constant_dynamic-slice_fusion), channel_id=1, source_target_pairs={{0,8},{8,0},{1,9},{9,1},{2,10},{10,2},{3,11},{11,3},{4,12},{12,4},... | collective-permute-start | bytes 24584 | tf_op jit(solution)/shard_map/ppermute | solution.py:369
  189.4 2.8 %collective-permute-start.19 = (f32[16,128]{1,0:T(8,128)S(1)}, f32[16,128]{1,0:T(8,128)S(1)}, u32[]{:S(2)}, u32[]{:S(2)}) collective-permute-start(f32[16,128]{1,0:T(8,128)S(1)} %reduce_sum.99), channel_id=1, source_target_pairs={{0,8},{8,0},{1,9},{9,1},{2,10},{10,2},{3,11},{11,3},{4,12},{12,4},... | collective-permute-start | bytes 24584 | tf_op jit(solution)/shard_map/ppermute | solution.py:369

commit v13 on v12

--- a/solution.py
+++ b/solution.py
@@ -298,19 +298,19 @@
     work = jnp.concatenate([gram, (rows == columns).astype(F32)], axis=1)
     index = lax.broadcasted_iota(jnp.int32, (K, 2 * K), 0)
     pivots = jnp.ones((K, 2 * K), F32)
-    for start in range(0, K, 8):
+    for start in range(0, K, 16):
         index = index[-(K - start) :]
         spread = [
-            jnp.broadcast_to(work[start:, j : j + 1], (K - start, 2 * K)) for j in range(start, start + 8)
+            jnp.broadcast_to(work[start:, j : j + 1], (K - start, 2 * K)) for j in range(start, start + 16)
         ]
         rest = work[start:]
         below = pivots[start:]
-        for a in range(8):
+        for a in range(16):
             pivot = spread[a][a : a + 1, :]
             below = jnp.where(index == start + a, pivot, below)
             ratio = jnp.where(index > start + a, spread[a] * (1.0 / pivot), 0.0)
             rest = rest - ratio * rest[a : a + 1, :]
-            for b in range(a + 1, 8):
+            for b in range(a + 1, 16):
                 spread[b] = spread[b] - ratio * spread[b][a : a + 1, :]
         work = jnp.concatenate([work[:start], rest], axis=0) if start else rest
         pivots = jnp.concatenate([pivots[:start], below], axis=0) if start else below
@@ -496,9 +496,9 @@
     made, (near, other) = after(made, near, other)
     far = apart(near)
     other = apart_z(other)
-    made = build(8, info, slab, half_rows, [near, swap_cores(near), beyond, other], made)
+    made = build(8, info, slab, half_rows, [near, swap_cores(near), beyond, other, swap_cores(beyond)], made)
     made, (far,) = after(made, far)
-    made = build(12, info, slab, half_rows, [swap_cores(beyond), swap_cores(other), far], made)
+    made = build(13, info, slab, half_rows, [swap_cores(other), far], made)
     made = build(15, info, slab, half_rows, [swap_cores(far)], made)
     tiles, partial_degree = made
 

time: 196 us -> 196 us (level)
  blocking collectives: 74.1 us -> 64.8 us
  Pallas kernels: 28.2 us -> 33.7 us
  starting transfers between devices: 33.1 us -> 35.2 us
    all_to_all x1, blocking collectives: 26.4 us -> 18.4 us  [shards(): lax.all_to_all(jnp.broadcast_to(sent[None], (8,) + sent.shape).reshape(8...]
    ppermute x3, waiting for transfers between devices: 16.9 us -> 11 us  [apart(): lax.ppermute(value, ('y', 'core'), [(2 * i + k, 2 * ((i + 1 + 2 * k) % 4)...]
    pallas_call x6, Pallas kernels: 12.4 us -> 16.7 us  [build(): pl.pallas_call(functools.partial(build_kernel, first, arrived), out_shape...]
    ppermute x2, waiting for transfers between devices: 4.95 us -> 8.99 us  [apart_z(): return lax.ppermute(value, ('zh', 'core', 'zl'), moves)]
    all_to_all x2, blocking collectives: 37.9 us -> 34.5 us  [share(): lax.all_to_all(jnp.broadcast_to(value[None], (size,) + value.shape), axes...]
    ppermute x2, starting transfers between devices: 3.75 us -> 6.09 us  [apart_z(): return lax.ppermute(value, ('zh', 'core', 'zl'), moves)]
    all_to_all x1, waiting for transfers between devices: 9.57 us -> 11.8 us  [shards(): parts = lax.all_to_all(running, COL, 0, 0, tiled=True)]
    all_to_all x1, blocking collectives: 9.81 us -> 11.9 us  [shards(): parts = lax.all_to_all(running, COL, 0, 0, tiled=True)]
  transfers between devices with their start and end apart: 21 -> 21, of which waited for: 12 -> 11; matrix products, arithmetic and copies ran while one was open for 4% -> 4% of each run, Pallas kernels for 6% -> 7%
where the time goes in v13:
time: 196 us; the launch traced here: 195 us
  blocking collectives  64.8 us (33%)
  waiting for transfers between devices  46.4 us (24%)
  starting transfers between devices  35.2 us (18%)
  Pallas kernels  33.7 us (17%)
  local copies, waits for them, and re-layouts  7.31 us (4%)
  other arithmetic  6.29 us (3%)
    all_to_all x2, blocking collectives, share(): lax.all_to_all(jnp.broadcast_to(value[None], (size,) + value.shape), axes...  34.5 us
    all_to_all x1, blocking collectives, shards(): lax.all_to_all(jnp.broadcast_to(sent[None], (8,) + sent.shape).reshape(8...  18.4 us
    ppermute x12, starting transfers between devices, swap_cores(): return lax.ppermute(value, 'core', [(0, 1), (1, 0)])  16.9 us
    pallas_call x6, Pallas kernels, build(): pl.pallas_call(functools.partial(build_kernel, first, arrived), out_shape...  16.7 us
    all_to_all x1, blocking collectives, shards(): parts = lax.all_to_all(running, COL, 0, 0, tiled=True)  11.9 us
    all_to_all x1, waiting for transfers between devices, shards(): parts = lax.all_to_all(running, COL, 0, 0, tiled=True)  11.8 us
    ppermute x3, waiting for transfers between devices, apart(): lax.ppermute(value, ('y', 'core'), [(2 * i + k, 2 * ((i + 1 + 2 * k) % 4)...  11 us
    pallas_call x2, Pallas kernels, product(): pl.pallas_call(functools.partial(product_kernel, first), out_shape=jax.Sh...  9.02 us
  transfers between devices with their start and end apart: 21, of which 11 were waited for; matrix products, arithmetic and copies ran while one was open for 4% of the time, Pallas kernels for 7%

profile of v13, /device:TPU:1, one launch (start us, length us, event | category | flops | bytes accessed | tf_op | source)
XLA Modules:
  0.0 194.8 jit_solution(3163336943572842306)
XLA Ops:
  5.7 2.3 %dynamic-slice_bitcast_fusion = bf16[512,1024]{1,0:T(8,128)(2,1)} fusion(bf16[8,512,1024]{2,1,0:T(8,128)(2,1)} %bitcast.37, s32[]{:T(128)S(6)} %select_n.198), kind=kLoop, calls=%fused_computation.1 | loop fusion | bytes 2097156 | tf_op jit(solution)/shard_map/jit(dynamic_index_in_dim)/squeeze | solution.py:478
  7.9 3.8 %collective-permute-start.1 = (bf16[512,1024]{1,0:T(8,128)(2,1)}, bf16[512,1024]{1,0:T(8,128)(2,1)}, u32[]{:S(2)}, u32[]{:S(2)}) collective-permute-start(bf16[512,1024]{1,0:T(8,128)(2,1)} %dynamic-slice_bitcast_fusion), channel_id=1, source_target_pairs={{0,17},{17,0},{1,16},{16,1},{2,19},{19,2},{3,18},{18,3},{4,21},{21... | collective-permute-start | bytes 3145736 | tf_op jit(solution)/shard_map/ppermute | solution.py:421
  11.7 5.1 %multiply_reduce_fusion = f32[4096]{0:T(1024)S(1)} fusion(bf16[4096,1024]{1,0:T(8,128)(2,1)} %param.5), kind=kLoop, calls=%fused_computation | loop fusion | flops 12578816 | bytes 8404992 | tf_op jit(solution)/shard_map/reduce_sum | solution.py:480
  18.6 3.4 %copy-done = bf16[4096,1024]{1,0:T(8,128)(2,1)S(1)} copy-done((bf16[4096,1024]{1,0:T(8,128)(2,1)S(1)}, bf16[4096,1024]{1,0:T(8,128)(2,1)}, u32[]{:S(2)}) %copy-start) | copy-done | bytes 8388632
  22.0 4.2 %build_tiles.6 = (bf16[24,512,512]{2,1,0:T(8,128)(2,1)}, f32[8,512]{1,0:T(8,128)S(1)}) custom-call(s32[121]{0:T(128)S(1)} %concatenate.13.info, bf16[8,512,1024]{2,1,0:T(8,128)(2,1)S(1)} %bitcast.38, f32[8,512]{1,0:T(8,128)S(1)} %mul.134.half_rows, bf16[512,1024]{1,0:T(8,128)(2,1)S(1)} %dynamic-slice_bitcast_fusion.1.refs_0_, ...), custom_call_target="tpu_custom_call" | custom-call | flops 1610612736 | bytes 7864320 | tf_op jit(solution)/shard_map/build_tiles/pallas_call | solution.py:106
  26.2 8.8 %collective-permute-done.1.refs_0_ = bf16[512,1024]{1,0:T(8,128)(2,1)} collective-permute-done((bf16[512,1024]{1,0:T(8,128)(2,1)}, bf16[512,1024]{1,0:T(8,128)(2,1)}, u32[]{:S(2)}, u32[]{:S(2)}) %collective-permute-start.1) | collective-permute-done | bytes 1048608 | tf_op jit(solution)/shard_map/ppermute | solution.py:421
  38.3 2.7 %collective-permute-start.8 = (bf16[512,1024]{1,0:T(8,128)(2,1)S(1)}, bf16[512,1024]{1,0:T(8,128)(2,1)S(1)}, u32[]{:S(2)}, u32[]{:S(2)}) collective-permute-start(bf16[512,1024]{1,0:T(8,128)(2,1)S(1)} %get-tuple-element.62), channel_id=1, source_target_pairs={{0,1},{8,25},{1,16},{9,8},{16,17},{24,9},{17,0},{25,24},{2,3},{10,... | collective-permute-start | bytes 3145736 | tf_op jit(solution)/shard_map/ppermute | solution.py:417
  41.0 4.8 %build_tiles.7 = (bf16[24,512,512]{2,1,0:T(8,128)(2,1)}, f32[8,512]{1,0:T(8,128)S(1)}) custom-call(s32[121]{0:T(128)S(1)} %concatenate.13.info, bf16[8,512,1024]{2,1,0:T(8,128)(2,1)S(1)} %bitcast.39, f32[8,512]{1,0:T(8,128)S(1)} %mul.134.half_rows, bf16[512,1024]{1,0:T(8,128)(2,1)} %collective-permute-done.1.refs_0_, ...), custom_call_target="tpu_custom_call", output_to_operand_aliasing={{0}: (6, {})} | custom-call | flops 2147483648 | bytes 10485760 | tf_op jit(solution)/shard_map/build_tiles/pallas_call | solution.py:106
  46.7 6.0 %collective-permute-done.8 = bf16[512,1024]{1,0:T(8,128)(2,1)S(1)} collective-permute-done((bf16[512,1024]{1,0:T(8,128)(2,1)S(1)}, bf16[512,1024]{1,0:T(8,128)(2,1)S(1)}, u32[]{:S(2)}, u32[]{:S(2)}) %collective-permute-start.8) | collective-permute-done | bytes 1048608 | tf_op jit(solution)/shard_map/ppermute | solution.py:417
  52.8 3.4 %collective-permute-start.11 = (bf16[512,1024]{1,0:T(8,128)(2,1)S(1)}, bf16[512,1024]{1,0:T(8,128)(2,1)S(1)}, u32[]{:S(2)}, u32[]{:S(2)}) collective-permute-start(bf16[512,1024]{1,0:T(8,128)(2,1)S(1)} %collective-permute-done.8), channel_id=1, source_target_pairs={{0,1},{8,25},{1,16},{9,8},{16,17},{24,9},{17,0},{25,24},{2,3},{10,... | collective-permute-start | bytes 3145736 | tf_op jit(solution)/shard_map/ppermute | solution.py:417
  56.2 6.1 %collective-permute-done.10.refs_2_ = bf16[512,1024]{1,0:T(8,128)(2,1)S(1)} collective-permute-done((bf16[512,1024]{1,0:T(8,128)(2,1)S(1)}, bf16[512,1024]{1,0:T(8,128)(2,1)S(1)}, u32[]{:S(2)}, u32[]{:S(2)}) %collective-permute-start.10) | collective-permute-done | bytes 1048608 | tf_op jit(solution)/shard_map/ppermute | solution.py:404
  62.3 2.2 %collective-permute-start.12 = (bf16[512,1024]{1,0:T(8,128)(2,1)S(1)}, bf16[512,1024]{1,0:T(8,128)(2,1)S(1)}, u32[]{:S(2)}, u32[]{:S(2)}) collective-permute-start(bf16[512,1024]{1,0:T(8,128)(2,1)S(1)} %collective-permute-done.10.refs_2_), channel_id=1, source_target_pairs={{0,8},{8,0},{1,9},{9,1},{2,10},{10,2},{3,11},{11,3},{4,12},{12,4},... | collective-permute-start | bytes 3145736 | tf_op jit(solution)/shard_map/ppermute | solution.py:369
  64.9 3.0 %collective-permute-done.11.refs_3_ = bf16[512,1024]{1,0:T(8,128)(2,1)S(1)} collective-permute-done((bf16[512,1024]{1,0:T(8,128)(2,1)S(1)}, bf16[512,1024]{1,0:T(8,128)(2,1)S(1)}, u32[]{:S(2)}, u32[]{:S(2)}) %collective-permute-start.11) | collective-permute-done | bytes 1048608 | tf_op jit(solution)/shard_map/ppermute | solution.py:417
  69.3 4.1 %build_tiles.9 = (bf16[24,512,512]{2,1,0:T(8,128)(2,1)}, f32[8,512]{1,0:T(8,128)S(1)}) custom-call(s32[121]{0:T(128)S(1)} %concatenate.13.info, bf16[8,512,1024]{2,1,0:T(8,128)(2,1)S(1)} %bitcast.41, f32[8,512]{1,0:T(8,128)S(1)} %mul.134.half_rows, bf16[512,1024]{1,0:T(8,128)(2,1)S(1)} %collective-permute-done.7.refs_0_, ...), custom_call_target="tpu_custom_call", output_to_operand_aliasing={{0}: (8, {})} | custom-call | flops 3758096384 | bytes 18350080 | tf_op jit(solution)/shard_map/build_tiles/pallas_call | solution.py:106
  73.4 4.9 %collective-permute-done.13.refs_1_ = bf16[512,1024]{1,0:T(8,128)(2,1)S(1)} collective-permute-done((bf16[512,1024]{1,0:T(8,128)(2,1)S(1)}, bf16[512,1024]{1,0:T(8,128)(2,1)S(1)}, u32[]{:S(2)}, u32[]{:S(2)}) %collective-permute-start.13) | collective-permute-done | bytes 1048608 | tf_op jit(solution)/shard_map/ppermute | solution.py:404
  78.3 2.1 %collective-permute-start.14 = (bf16[512,1024]{1,0:T(8,128)(2,1)S(1)}, bf16[512,1024]{1,0:T(8,128)(2,1)S(1)}, u32[]{:S(2)}, u32[]{:S(2)}) collective-permute-start(bf16[512,1024]{1,0:T(8,128)(2,1)S(1)} %collective-permute-done.13.refs_1_), channel_id=1, source_target_pairs={{0,8},{8,0},{1,9},{9,1},{2,10},{10,2},{3,11},{11,3},{4,12},{12,4},... | collective-permute-start | bytes 3145736 | tf_op jit(solution)/shard_map/ppermute | solution.py:369
  81.1 1.6 collective-permute-done.14.refs_0_
  82.7 2.3 %build_tiles.11 = (bf16[24,512,512]{2,1,0:T(8,128)(2,1)}, f32[8,512]{1,0:T(8,128)S(1)}) custom-call(s32[121]{0:T(128)S(1)} %concatenate.13.info, bf16[8,512,1024]{2,1,0:T(8,128)(2,1)S(1)} %bitcast.43, f32[8,512]{1,0:T(8,128)S(1)} %mul.134.half_rows, bf16[512,1024]{1,0:T(8,128)(2,1)S(1)} %collective-permute-done.14.refs_0_, ...), custom_call_target="tpu_custom_call", output_to_operand_aliasing={{0}: (4, {})} | custom-call | flops 536870912 | bytes 2621440 | tf_op jit(solution)/shard_map/build_tiles/pallas_call | solution.py:106
  85.0 18.4 %all_to_all.25 = f32[64,8,128]{2,1,0:T(8,128)S(1)} all-to-all(f32[64,8,128]{2,1,0:T(8,128)S(1)} %bitcast.46), channel_id=1, replica_groups=mesh['y'=4,'zh'=2,'core'=2,'x'=4,'zl'=2] {'y','zh','x','zl'}, dimensions={0} | all-to-all | bytes 524288 | tf_op jit(solution)/shard_map/all_to_all | solution.py:508
  103.5 2.9 %collective-permute-start.16 = (f32[8,8,128]{2,1,0:T(8,128)S(1)}, f32[8,8,128]{2,1,0:T(8,128)S(1)}, u32[]{:S(2)}, u32[]{:S(2)}) collective-permute-start(f32[8,8,128]{2,1,0:T(8,128)S(1)} %bitcast_reduce_fusion.refs_0_.known), channel_id=1, source_target_pairs={{0,8},{8,0},{1,9},{9,1},{2,10},{10,2},{3,11},{11,3},{4,12},{12,4},... | collective-permute-start | bytes 98312 | tf_op jit(solution)/shard_map/ppermute | solution.py:369
  107.3 4.0 %product.2 = bf16[8,64,512]{2,1,0:T(8,128)(2,1)S(1)} custom-call(s32[121]{0:T(128)S(1)} %concatenate.13.info, bf16[24,512,512]{2,1,0:T(8,128)(2,1)} %get-tuple-element.55.tiles, f32[8,8,128]{2,1,0:T(8,128)S(1)} %bitcast_reduce_fusion.refs_0_.known, f32[8,8,128]{2,1,0:T(8,128)S(1)} %collective-permute-done.16.refs_1_), custom_call_target="tpu_custom_call" | custom-call | tf_op jit(solution)/shard_map/product/pallas_call | solution.py:232
  111.2 11.9 %all_to_all.26.parts = bf16[8,64,512]{2,1,0:T(8,128)(2,1)S(1)} all-to-all(bf16[8,64,512]{2,1,0:T(8,128)(2,1)S(1)} %product.2), channel_id=1, replica_groups=mesh['y'=4,'zh'=2,'core'=2,'x'=4,'zl'=2] {'x','zl'}, dimensions={0} | all-to-all | bytes 1048576 | tf_op jit(solution)/shard_map/all_to_all | solution.py:516
  124.3 16.5 %all_to_all.27.refs_0_ = bf16[8,80,512]{2,1,0:T(8,128)(2,1)S(1)} all-to-all(bf16[8,80,512]{2,1,0:T(8,128)(2,1)S(1)} %broadcast_in_dim.112), channel_id=1, replica_groups=mesh['y'=4,'zh'=2,'core'=2,'x'=4,'zl'=2] {'y','zh'}, dimensions={0} | all-to-all | bytes 1310720 | tf_op jit(solution)/shard_map/all_to_all | solution.py:374
  140.8 2.5 %collective-permute-start.17 = (bf16[8,80,512]{2,1,0:T(8,128)(2,1)S(1)}, bf16[8,80,512]{2,1,0:T(8,128)(2,1)S(1)}, u32[]{:S(2)}, u32[]{:S(2)}) collective-permute-start(bf16[8,80,512]{2,1,0:T(8,128)(2,1)S(1)} %all_to_all.27.refs_0_), channel_id=1, source_target_pairs={{0,8},{8,0},{1,9},{9,1},{2,10},{10,2},{3,11},{11,3},{4,12},{12,4},... | collective-permute-start | bytes 1966088 | tf_op jit(solution)/shard_map/ppermute | solution.py:369
  143.4 1.7 collective-permute-done.17.refs_1_
  145.1 5.1 %product.3 = bf16[8,80,512]{2,1,0:T(8,128)(2,1)} custom-call(s32[121]{0:T(128)S(1)} %concatenate.13.info, bf16[24,512,512]{2,1,0:T(8,128)(2,1)} %get-tuple-element.55.tiles, bf16[8,80,512]{2,1,0:T(8,128)(2,1)S(1)} %all_to_all.27.refs_0_, bf16[8,80,512]{2,1,0:T(8,128)(2,1)S(1)} %collective-permute-done.17.refs_1_, f32[8,512]{1,0:T(8,128)S(1)} %get-tuple-element.56.refs_2_), custom_call_target="tpu_custom_call" | custom-call | tf_op jit(solution)/shard_map/product/pallas_call | solution.py:232
  150.2 3.6 %all-to-all-start.3 = ((bf16[8,80,512]{2,1,0:T(8,128)(2,1)}), bf16[8,80,512]{2,1,0:T(8,128)(2,1)S(1)}, u32[]{:S(2)}, u32[]{:S(2)}) async-start(bf16[8,80,512]{2,1,0:T(8,128)(2,1)} %product.3), calls=%async_computation.3 | async-start | bytes 1310720 | tf_op jit(solution)/shard_map/all_to_all | solution.py:521
  153.7 11.8 %all-to-all-done.3.parts = bf16[8,80,512]{2,1,0:T(8,128)(2,1)S(1)} async-done(((bf16[8,80,512]{2,1,0:T(8,128)(2,1)}), bf16[8,80,512]{2,1,0:T(8,128)(2,1)S(1)}, u32[]{:S(2)}, u32[]{:S(2)}) %all-to-all-start.3) | async-done | bytes 655392 | tf_op jit(solution)/shard_map/all_to_all | solution.py:521
  165.5 3.5 %middle.1 = (f32[64,512]{1,0:T(8,128)S(1)}, f32[32,128]{1,0:T(8,128)S(1)}) custom-call(s32[121]{0:T(128)S(1)} %concatenate.13.info, bf16[8,80,512]{2,1,0:T(8,128)(2,1)S(1)} %all-to-all-done.3.parts, f32[8,8,128]{2,1,0:T(8,128)S(1)} %bitcast_reduce_fusion.refs_0_.known, f32[8,8,8,128]{3,2,1,0:T(8,128)S(1)} %bitcast.44), custom_call_target="tpu_custom_call" | custom-call | tf_op jit(solution)/shard_map/middle/pallas_call | solution.py:358
  170.6 18.0 %all_to_all.28 = f32[64,16,128]{2,1,0:T(8,128)S(1)} all-to-all(f32[64,16,128]{2,1,0:T(8,128)S(1)} %broadcast_in_dim.113), channel_id=1, replica_groups=mesh['y'=4,'zh'=2,'core'=2,'x'=4,'zl'=2] {'y','zh','x','zl'}, dimensions={0} | all-to-all | bytes 1048576 | tf_op jit(solution)/shard_map/all_to_all | solution.py:374
  188.6 2.0 %collective-permute-start.19 = (f32[16,128]{1,0:T(8,128)S(1)}, f32[16,128]{1,0:T(8,128)S(1)}, u32[]{:S(2)}, u32[]{:S(2)}) collective-permute-start(f32[16,128]{1,0:T(8,128)S(1)} %reduce_sum.99), channel_id=1, source_target_pairs={{0,8},{8,0},{1,9},{9,1},{2,10},{10,2},{3,11},{11,3},{4,12},{12,4},... | collective-permute-start | bytes 24584 | tf_op jit(solution)/shard_map/ppermute | solution.py:369
  191.4 3.4 %last.1 = f32[64,512]{1,0:T(8,128)} custom-call(s32[121]{0:T(128)S(1)} %concatenate.13.info, f32[32,128]{1,0:T(8,128)S(1)} %pad_maximum_fusion.1.message, f32[64,512]{1,0:T(8,128)S(1)} %get-tuple-element.58.image, f32[8,8,128]{2,1,0:T(8,128)S(1)} %bitcast_reduce_fusion.refs_0_.known), custom_call_target="tpu_custom_call" | custom-call | tf_op jit(solution)/shard_map/last/pallas_call | solution.py:358
  (67 shorter events, 18.1 us)
Async XLA Ops:
  0.0 17.6 %copy-start.3 = (s32[1,1,24]{2,1,0:T(1,128)S(1)}, s32[1,1,24]{2,1,0:T(1,128)}, u32[]{:S(2)}) copy-start(s32[1,1,24]{2,1,0:T(1,128)} %param.8) | copy-start | bytes 292
  0.0 17.9 %copy-start.4 = (s32[1,1,24]{2,1,0:T(1,128)S(1)}, s32[1,1,24]{2,1,0:T(1,128)}, u32[]{:S(2)}) copy-start(s32[1,1,24]{2,1,0:T(1,128)} %param.7) | copy-start | bytes 292
  1.3 17.3 %collective-permute-start = (bf16[512,1024]{1,0:T(8,128)(2,1)S(1)}, bf16[512,1024]{1,0:T(8,128)(2,1)}, u32[]{:S(2)}, u32[]{:S(2)}) collective-permute-start(bf16[512,1024]{1,0:T(8,128)(2,1)S(1)} %dynamic-slice_bitcast_fusion.1.refs_0_), channel_id=1, source_target_pairs={{0,8},{8,0},{1,9},{9,1},{2,10},{10,2},{3,11},{11,3},{4,12},{12,4},... | collective-permute-start | bytes 3145736 | tf_op jit(solution)/shard_map/ppermute | solution.py:369
  2.8 32.2 %collective-permute-start.2 = (bf16[512,1024]{1,0:T(8,128)(2,1)S(1)}, bf16[512,1024]{1,0:T(8,128)(2,1)S(1)}, u32[]{:S(2)}, u32[]{:S(2)}) collective-permute-start(bf16[512,1024]{1,0:T(8,128)(2,1)S(1)} %dynamic-slice_bitcast_fusion.1.refs_0_), channel_id=1, source_target_pairs={{0,32},{32,64},{64,96},{96,0},{1,33},{33,65},{65,97},{97,1},{2,34}... | collective-permute-start | bytes 3145736 | tf_op jit(solution)/shard_map/ppermute | solution.py:396
  4.2 30.8 %collective-permute-start.3 = (bf16[512,1024]{1,0:T(8,128)(2,1)S(1)}, bf16[512,1024]{1,0:T(8,128)(2,1)S(1)}, u32[]{:S(2)}, u32[]{:S(2)}) collective-permute-start(bf16[512,1024]{1,0:T(8,128)(2,1)S(1)} %dynamic-slice_bitcast_fusion.1.refs_0_), channel_id=1, source_target_pairs={{0,96},{32,0},{64,32},{96,64},{1,97},{33,1},{65,33},{97,65},{2,98}... | collective-permute-start | bytes 3145736 | tf_op jit(solution)/shard_map/ppermute | solution.py:400
  7.9 27.1 %collective-permute-start.1 = (bf16[512,1024]{1,0:T(8,128)(2,1)}, bf16[512,1024]{1,0:T(8,128)(2,1)}, u32[]{:S(2)}, u32[]{:S(2)}) collective-permute-start(bf16[512,1024]{1,0:T(8,128)(2,1)} %dynamic-slice_bitcast_fusion), channel_id=1, source_target_pairs={{0,17},{17,0},{1,16},{16,1},{2,19},{19,2},{3,18},{18,3},{4,21},{21... | collective-permute-start | bytes 3145736 | tf_op jit(solution)/shard_map/ppermute | solution.py:421
  18.6 3.4 %copy-start = (bf16[4096,1024]{1,0:T(8,128)(2,1)S(1)}, bf16[4096,1024]{1,0:T(8,128)(2,1)}, u32[]{:S(2)}) copy-start(bf16[4096,1024]{1,0:T(8,128)(2,1)} %param.5) | copy-start | bytes 25165828
  22.0 19.0 %copy-start.1 = (bf16[4096,1024]{1,0:T(8,128)(2,1)S(1)}, bf16[4096,1024]{1,0:T(8,128)(2,1)}, u32[]{:S(2)}) copy-start(bf16[4096,1024]{1,0:T(8,128)(2,1)} %param.5) | copy-start | bytes 25165828
  35.0 10.8 %collective-permute-start.4 = (bf16[512,1024]{1,0:T(8,128)(2,1)}, bf16[512,1024]{1,0:T(8,128)(2,1)S(1)}, u32[]{:S(2)}, u32[]{:S(2)}) collective-permute-start(bf16[512,1024]{1,0:T(8,128)(2,1)} %collective-permute-done.1.refs_0_), channel_id=1, source_target_pairs={{0,8},{8,0},{1,9},{9,1},{2,10},{10,2},{3,11},{11,3},{4,12},{12,4},... | collective-permute-start | bytes 3145736 | tf_op jit(solution)/shard_map/ppermute | solution.py:369
  36.1 9.8 %collective-permute-start.5 = (bf16[512,1024]{1,0:T(8,128)(2,1)S(1)}, bf16[512,1024]{1,0:T(8,128)(2,1)S(1)}, u32[]{:S(2)}, u32[]{:S(2)}) collective-permute-start(bf16[512,1024]{1,0:T(8,128)(2,1)S(1)} %collective-permute-done.2.refs_1_), channel_id=1, source_target_pairs={{0,8},{8,0},{1,9},{9,1},{2,10},{10,2},{3,11},{11,3},{4,12},{12,4},... | collective-permute-start | bytes 3145736 | tf_op jit(solution)/shard_map/ppermute | solution.py:369
  36.4 9.6 %collective-permute-start.6 = (bf16[512,1024]{1,0:T(8,128)(2,1)S(1)}, bf16[512,1024]{1,0:T(8,128)(2,1)S(1)}, u32[]{:S(2)}, u32[]{:S(2)}) collective-permute-start(bf16[512,1024]{1,0:T(8,128)(2,1)S(1)} %collective-permute-done.3.refs_2_), channel_id=1, source_target_pairs={{0,8},{8,0},{1,9},{9,1},{2,10},{10,2},{3,11},{11,3},{4,12},{12,4},... | collective-permute-start | bytes 3145736 | tf_op jit(solution)/shard_map/ppermute | solution.py:369
  36.9 15.9 %collective-permute-start.7 = (bf16[512,1024]{1,0:T(8,128)(2,1)}, bf16[512,1024]{1,0:T(8,128)(2,1)S(1)}, u32[]{:S(2)}, u32[]{:S(2)}) collective-permute-start(bf16[512,1024]{1,0:T(8,128)(2,1)} %collective-permute-done.1.refs_0_), channel_id=1, source_target_pairs={{0,32},{8,104},{32,64},{40,8},{64,96},{72,40},{96,0},{104,72},{1,3... | collective-permute-start | bytes 3145736 | tf_op jit(solution)/shard_map/ppermute | solution.py:404
  38.3 14.4 %collective-permute-start.8 = (bf16[512,1024]{1,0:T(8,128)(2,1)S(1)}, bf16[512,1024]{1,0:T(8,128)(2,1)S(1)}, u32[]{:S(2)}, u32[]{:S(2)}) collective-permute-start(bf16[512,1024]{1,0:T(8,128)(2,1)S(1)} %get-tuple-element.62), channel_id=1, source_target_pairs={{0,1},{8,25},{1,16},{9,8},{16,17},{24,9},{17,0},{25,24},{2,3},{10,... | collective-permute-start | bytes 3145736 | tf_op jit(solution)/shard_map/ppermute | solution.py:417
  45.8 16.4 %collective-permute-start.10 = (bf16[512,1024]{1,0:T(8,128)(2,1)S(1)}, bf16[512,1024]{1,0:T(8,128)(2,1)S(1)}, u32[]{:S(2)}, u32[]{:S(2)}) collective-permute-start(bf16[512,1024]{1,0:T(8,128)(2,1)S(1)} %get-tuple-element.45), channel_id=1, source_target_pairs={{0,32},{8,104},{32,64},{40,8},{64,96},{72,40},{96,0},{104,72},{1,3... | collective-permute-start | bytes 3145736 | tf_op jit(solution)/shard_map/ppermute | solution.py:404
  52.8 15.2 %collective-permute-start.11 = (bf16[512,1024]{1,0:T(8,128)(2,1)S(1)}, bf16[512,1024]{1,0:T(8,128)(2,1)S(1)}, u32[]{:S(2)}, u32[]{:S(2)}) collective-permute-start(bf16[512,1024]{1,0:T(8,128)(2,1)S(1)} %collective-permute-done.8), channel_id=1, source_target_pairs={{0,1},{8,25},{1,16},{9,8},{16,17},{24,9},{17,0},{25,24},{2,3},{10,... | collective-permute-start | bytes 3145736 | tf_op jit(solution)/shard_map/ppermute | solution.py:417
  56.2 13.1 %collective-permute-start.9 = (bf16[512,1024]{1,0:T(8,128)(2,1)S(1)}, bf16[512,1024]{1,0:T(8,128)(2,1)S(1)}, u32[]{:S(2)}, u32[]{:S(2)}) collective-permute-start(bf16[512,1024]{1,0:T(8,128)(2,1)S(1)} %collective-permute-done.7.refs_0_), channel_id=1, source_target_pairs={{0,8},{8,0},{1,9},{9,1},{2,10},{10,2},{3,11},{11,3},{4,12},{12,4},... | collective-permute-start | bytes 3145736 | tf_op jit(solution)/shard_map/ppermute | solution.py:369
  62.3 7.0 %collective-permute-start.12 = (bf16[512,1024]{1,0:T(8,128)(2,1)S(1)}, bf16[512,1024]{1,0:T(8,128)(2,1)S(1)}, u32[]{:S(2)}, u32[]{:S(2)}) collective-permute-start(bf16[512,1024]{1,0:T(8,128)(2,1)S(1)} %collective-permute-done.10.refs_2_), channel_id=1, source_target_pairs={{0,8},{8,0},{1,9},{9,1},{2,10},{10,2},{3,11},{11,3},{4,12},{12,4},... | collective-permute-start | bytes 3145736 | tf_op jit(solution)/shard_map/ppermute | solution.py:369
  64.4 13.9 %collective-permute-start.13 = (bf16[512,1024]{1,0:T(8,128)(2,1)S(1)}, bf16[512,1024]{1,0:T(8,128)(2,1)S(1)}, u32[]{:S(2)}, u32[]{:S(2)}) collective-permute-start(bf16[512,1024]{1,0:T(8,128)(2,1)S(1)} %collective-permute-done.7.refs_0_), channel_id=1, source_target_pairs={{0,32},{8,104},{32,64},{40,8},{64,96},{72,40},{96,0},{104,72},{1,3... | collective-permute-start | bytes 3145736 | tf_op jit(solution)/shard_map/ppermute | solution.py:404
  67.9 12.6 %collective-permute-start.15 = (bf16[512,1024]{1,0:T(8,128)(2,1)S(1)}, bf16[512,1024]{1,0:T(8,128)(2,1)S(1)}, u32[]{:S(2)}, u32[]{:S(2)}) collective-permute-start(bf16[512,1024]{1,0:T(8,128)(2,1)S(1)} %collective-permute-done.11.refs_3_), channel_id=1, source_target_pairs={{0,8},{8,0},{1,9},{9,1},{2,10},{10,2},{3,11},{11,3},{4,12},{12,4},... | collective-permute-start | bytes 3145736 | tf_op jit(solution)/shard_map/ppermute | solution.py:369
  69.3 11.1 %copy-start.2 = (s32[512]{0:T(512)S(1)}, s32[512]{0:T(512)}, u32[]{:S(2)}) copy-start(s32[512]{0:T(512)} %param.6) | copy-start | bytes 6148
  78.3 4.4 %collective-permute-start.14 = (bf16[512,1024]{1,0:T(8,128)(2,1)S(1)}, bf16[512,1024]{1,0:T(8,128)(2,1)S(1)}, u32[]{:S(2)}, u32[]{:S(2)}) collective-permute-start(bf16[512,1024]{1,0:T(8,128)(2,1)S(1)} %collective-permute-done.13.refs_1_), channel_id=1, source_target_pairs={{0,8},{8,0},{1,9},{9,1},{2,10},{10,2},{3,11},{11,3},{4,12},{12,4},... | collective-permute-start | bytes 3145736 | tf_op jit(solution)/shard_map/ppermute | solution.py:369
  103.5 3.8 %collective-permute-start.16 = (f32[8,8,128]{2,1,0:T(8,128)S(1)}, f32[8,8,128]{2,1,0:T(8,128)S(1)}, u32[]{:S(2)}, u32[]{:S(2)}) collective-permute-start(f32[8,8,128]{2,1,0:T(8,128)S(1)} %bitcast_reduce_fusion.refs_0_.known), channel_id=1, source_target_pairs={{0,8},{8,0},{1,9},{9,1},{2,10},{10,2},{3,11},{11,3},{4,12},{12,4},... | collective-permute-start | bytes 98312 | tf_op jit(solution)/shard_map/ppermute | solution.py:369
  140.8 4.2 %collective-permute-start.17 = (bf16[8,80,512]{2,1,0:T(8,128)(2,1)S(1)}, bf16[8,80,512]{2,1,0:T(8,128)(2,1)S(1)}, u32[]{:S(2)}, u32[]{:S(2)}) collective-permute-start(bf16[8,80,512]{2,1,0:T(8,128)(2,1)S(1)} %all_to_all.27.refs_0_), channel_id=1, source_target_pairs={{0,8},{8,0},{1,9},{9,1},{2,10},{10,2},{3,11},{11,3},{4,12},{12,4},... | collective-permute-start | bytes 1966088 | tf_op jit(solution)/shard_map/ppermute | solution.py:369
  150.2 15.3 %all-to-all-start.3 = ((bf16[8,80,512]{2,1,0:T(8,128)(2,1)}), bf16[8,80,512]{2,1,0:T(8,128)(2,1)S(1)}, u32[]{:S(2)}, u32[]{:S(2)}) async-start(bf16[8,80,512]{2,1,0:T(8,128)(2,1)} %product.3), calls=%async_computation.3 | async-start | bytes 1310720 | tf_op jit(solution)/shard_map/all_to_all | solution.py:521
  169.0 1.5 collective-permute-start.18
  188.6 2.8 %collective-permute-start.19 = (f32[16,128]{1,0:T(8,128)S(1)}, f32[16,128]{1,0:T(8,128)S(1)}, u32[]{:S(2)}, u32[]{:S(2)}) collective-permute-start(f32[16,128]{1,0:T(8,128)S(1)} %reduce_sum.99), channel_id=1, source_target_pairs={{0,8},{8,0},{1,9},{9,1},{2,10},{10,2},{3,11},{11,3},{4,12},{12,4},... | collective-permute-start | bytes 24584 | tf_op jit(solution)/shard_map/ppermute | solution.py:369

commit v14 on v13

--- a/solution.py
+++ b/solution.py
@@ -156,11 +156,15 @@
     return jnp.concatenate([rows[start + i : start + i + 1] for i in range(4)], axis=1)
 
 
+def seeds_of(label, value):
+    value = jnp.where(label < K, value, -value)
+    label = jnp.where(label < K, label, label - K)
+    same = label == lax.broadcasted_iota(jnp.int32, (K, TILE), 0).astype(F32)
+    return jnp.where(same, jnp.broadcast_to(value, (K, TILE)), 0.0)
+
+
 def product_kernel(first, info, tiles, *refs):
-    if first:
-        mine, others, out, running, held, sem = refs
-    else:
-        mine, others, degree, out, running, held, sem = refs
+    mine, others, degree, out, running, held, sem = refs
     count = info[0]
     core = info[2]
     depth = held.shape[0]
@@ -174,11 +178,7 @@
         own = q % 2 == core
         if first:
             known = jnp.where(own, mine[q // 2], others[q // 2])
-            value, label = lax.rsqrt(row_of(known, 0)), row_of(known, 4)
-            value = jnp.where(label < K, value, -value)
-            label = jnp.where(label < K, label, label - K)
-            same = label == lax.broadcasted_iota(jnp.int32, (K, TILE), 0).astype(F32)
-            return jnp.where(same, jnp.broadcast_to(value, (K, TILE)), 0.0).astype(BF16)
+            return seeds_of(row_of(known, 4), lax.rsqrt(row_of(known, 0))).astype(BF16)
         return jnp.where(own, mine[q // 2, :K, :], others[q // 2, :K, :])
 
     def term(entry):
@@ -191,12 +191,33 @@
             fetch(jnp.int32(entry)).start()
 
     running[...] = jnp.zeros_like(running)
-    if not first:
+    if first:
+        weights = jnp.zeros((K, TILE), F32)
+        degrees = jnp.zeros((1, TILE), F32)
+        for known in (mine, others):
+            for chip in range(8):
+                value, label = row_of(known[chip], 0), row_of(known[chip], 4)
+                degrees = degrees + value
+                weights = weights + seeds_of(label, jnp.sqrt(value))
+        weights = jnp.sum(weights, axis=1, keepdims=True)
+        total = jnp.sum(degrees, axis=1, keepdims=True)
+        half = K // 2
+        sums = jnp.concatenate(
+            [
+                jnp.zeros((half, K + 1), F32),
+                weights[:half],
+                weights[half:],
+                jnp.broadcast_to(total, (half, 1)),
+                jnp.zeros((half, 12), F32),
+            ],
+            axis=1,
+        )
+    else:
         sums = jnp.sum(mine[:, K:, :].astype(F32), axis=0) + jnp.sum(others[:, K:, :].astype(F32), axis=0)
         sums = value_of(sums)
-        terms = terms_of(sums)
-        for t in range(SLAB_TILES):
-            out[t, K:, :] = terms
+    terms = terms_of(sums)
+    for t in range(SLAB_TILES):
+        out[t, K:, :] = terms
 
     def step(turn, carry):
         entries = [4 * turn + i for i in range(4)]
@@ -218,21 +239,17 @@
         return carry
 
     lax.fori_loop(0, (count + 3) // 4, step, 0)
-    if first:
-        out[...] = running[...].astype(BF16)
-    else:
-        lead, _ = lead_of(sums)
-        for t in range(SLAB_TILES):
-            out[t, :K, :] = (running[t] - lead * degree[t : t + 1, :]).astype(BF16)
-
-
-def product(info, tiles, *operands):
+    lead, _ = lead_of(sums)
+    for t in range(SLAB_TILES):
+        out[t, :K, :] = (running[t] - lead * degree[t : t + 1, :]).astype(BF16)
+
+
+def product(first, info, tiles, *operands):
     vmem = pl.BlockSpec(memory_space=pltpu.VMEM)
-    first = len(operands) == 2
     return pl.pallas_call(
         functools.partial(product_kernel, first),
         out_shape=jax.ShapeDtypeStruct(
-            (SLAB_TILES, K if first else K + 16, TILE), BF16
+            (SLAB_TILES, K + 16, TILE), BF16
         ),
         in_specs=[
             pl.BlockSpec(memory_space=pltpu.SMEM),
@@ -326,22 +343,27 @@
     return lax.rsqrt(degree), jnp.sqrt(degree)
 
 
-def weigh_kernel(info, parts, known, out):
+def whole_of(parts, columns, lead, by_column):
+    whole = jnp.sum(parts[:, :K, :].astype(F32), axis=0)
+    for c in range(SLAB_TILES):
+        whole = whole + (lead_of(columns[c])[0] - lead) * row_of(by_column[c], 0)
+    return whole
+
+
+def weigh_kernel(info, parts, known, by_column, out):
     inv_root, root = roots_of(info, known)
-    image = jnp.sum(parts[...].astype(F32), axis=0) * inv_root
+    columns = [value_of(parts[c, K:, :].astype(F32)) for c in range(SLAB_TILES)]
+    shift, _ = lead_of(sum(columns))
+    image = whole_of(parts, columns, shift, by_column[info[3]]) * inv_root
     out[:K, :] = (image * inv_root).astype(BF16)
     out[K:, :] = terms_of(weights_of(image, root))
 
 
 def middle_kernel(scale, info, parts, known, by_column, image, message):
     inv_root, root = roots_of(info, known)
-    own = by_column[info[3]]
     columns = [value_of(parts[c, K:, :].astype(F32)) for c in range(SLAB_TILES)]
     factor, lead = factor_of(sum(columns), scale)
-    whole = jnp.sum(parts[:, :K, :].astype(F32), axis=0)
-    for c in range(SLAB_TILES):
-        whole = whole + (lead_of(columns[c])[0] - lead) * row_of(own[c], 0)
-    block = times(factor, whole * inv_root)
+    block = times(factor, whole_of(parts, columns, lead, by_column[info[3]]) * inv_root)
     image[...] = block
     message[:, :80] = weights_of(block, root)
     message[:, 80:] = jnp.zeros((K // 2, 48), F32)
@@ -512,12 +534,12 @@
 
     scale = 1.0 / (BLOCK_TILES * SLAB_TILES * TILE)
     block = jax.ShapeDtypeStruct((K, TILE), F32)
-    running = product(info, tiles, known, swap_cores(known))
+    running = product(True, info, tiles, known, swap_cores(known), partial_degree)
     parts = lax.all_to_all(running, COL, 0, 0, tiled=True)
     weighed = local(
-        weigh_kernel, "weigh", jax.ShapeDtypeStruct((K + 16, TILE), BF16), info, parts, known
-    )
-    running = product(info, tiles, *share_row(weighed), partial_degree)
+        weigh_kernel, "weigh", jax.ShapeDtypeStruct((K + 16, TILE), BF16), info, parts, known, by_column
+    )
+    running = product(False, info, tiles, *share_row(weighed), partial_degree)
     parts = lax.all_to_all(running, COL, 0, 0, tiled=True)
     image, message = local(
         functools.partial(middle_kernel, scale),

time: 196 us -> 196 us (level)
  blocking collectives: 64.8 us -> 71.1 us
  waiting for transfers between devices: 46.4 us -> 40.1 us
  starting transfers between devices: 35.2 us -> 37.7 us
    ppermute x3, starting transfers between devices: 2.09 us -> 6.18 us  [apart(): lax.ppermute(value, ('y', 'core'), [(2 * i + k, 2 * ((i + 1 + 2 * k) % 4)...]
    ppermute x2, waiting for transfers between devices: 8.99 us -> 5.22 us  [apart_z(): return lax.ppermute(value, ('zh', 'core', 'zl'), moves)]
    all_to_all x1, blocking collectives: 18.4 us -> 22.2 us  [shards(): lax.all_to_all(jnp.broadcast_to(sent[None], (8,) + sent.shape).reshape(8...]
  transfers between devices with their start and end apart: 21 -> 21, of which waited for: 11 -> 10; matrix products, arithmetic and copies ran while one was open for 4% -> 4% of each run, Pallas kernels for 7% -> 8%
where the time goes in v14:
time: 196 us
  blocking collectives  71.1 us (36%)
  waiting for transfers between devices  40.1 us (20%)
  starting transfers between devices  37.7 us (19%)
  Pallas kernels  32.9 us (17%)
  local copies, waits for them, and re-layouts  7.31 us (4%)
  other arithmetic  6.29 us (3%)
    all_to_all x2, blocking collectives, share(): lax.all_to_all(jnp.broadcast_to(value[None], (size,) + value.shape), axes...  35.4 us
    all_to_all x1, blocking collectives, shards(): lax.all_to_all(jnp.broadcast_to(sent[None], (8,) + sent.shape).reshape(8...  22.2 us
    pallas_call x6, Pallas kernels, build(): pl.pallas_call(functools.partial(build_kernel, first, arrived), out_shape...  16.4 us
    ppermute x12, starting transfers between devices, swap_cores(): return lax.ppermute(value, 'core', [(0, 1), (1, 0)])  15.3 us
    all_to_all x1, blocking collectives, shards(): parts = lax.all_to_all(running, COL, 0, 0, tiled=True)  13.5 us
    ppermute x3, waiting for transfers between devices, apart(): lax.ppermute(value, ('y', 'core'), [(2 * i + k, 2 * ((i + 1 + 2 * k) % 4)...  11 us
    all_to_all x1, waiting for transfers between devices, shards(): parts = lax.all_to_all(running, COL, 0, 0, tiled=True)  10.8 us
    ppermute x1, waiting for transfers between devices, cross(): return lax.ppermute(value, ('zh', 'zl'), [(0, 3), (3, 0), (1, 2), (2, 1)])  8.8 us
  transfers between devices with their start and end apart: 21, of which 10 were waited for; matrix products, arithmetic and copies ran while one was open for 4% of the time, Pallas kernels for 8%

profile of v14, /device:TPU:1, one launch (start us, length us, event | category | flops | bytes accessed | tf_op | source)
XLA Modules:
  0.0 196.4 jit_solution(2490670974965630913)
XLA Ops:
  5.7 2.3 %dynamic-slice_bitcast_fusion = bf16[512,1024]{1,0:T(8,128)(2,1)} fusion(bf16[8,512,1024]{2,1,0:T(8,128)(2,1)} %bitcast.37, s32[]{:T(128)S(6)} %select_n.198), kind=kLoop, calls=%fused_computation.1 | loop fusion | bytes 2097156 | tf_op jit(solution)/shard_map/jit(dynamic_index_in_dim)/squeeze | solution.py:500
  7.9 3.8 %collective-permute-start.1 = (bf16[512,1024]{1,0:T(8,128)(2,1)}, bf16[512,1024]{1,0:T(8,128)(2,1)}, u32[]{:S(2)}, u32[]{:S(2)}) collective-permute-start(bf16[512,1024]{1,0:T(8,128)(2,1)} %dynamic-slice_bitcast_fusion), channel_id=1, source_target_pairs={{0,17},{17,0},{1,16},{16,1},{2,19},{19,2},{3,18},{18,3},{4,21},{21... | collective-permute-start | bytes 3145736 | tf_op jit(solution)/shard_map/ppermute | solution.py:443
  11.7 5.1 %multiply_reduce_fusion = f32[4096]{0:T(1024)S(1)} fusion(bf16[4096,1024]{1,0:T(8,128)(2,1)} %param.5), kind=kLoop, calls=%fused_computation | loop fusion | flops 12578816 | bytes 8404992 | tf_op jit(solution)/shard_map/reduce_sum | solution.py:502
  18.6 3.4 %copy-done = bf16[4096,1024]{1,0:T(8,128)(2,1)S(1)} copy-done((bf16[4096,1024]{1,0:T(8,128)(2,1)S(1)}, bf16[4096,1024]{1,0:T(8,128)(2,1)}, u32[]{:S(2)}) %copy-start) | copy-done | bytes 8388632
  22.0 4.2 %build_tiles.6 = (bf16[24,512,512]{2,1,0:T(8,128)(2,1)}, f32[8,512]{1,0:T(8,128)S(1)}) custom-call(s32[121]{0:T(128)S(1)} %concatenate.13.info, bf16[8,512,1024]{2,1,0:T(8,128)(2,1)S(1)} %bitcast.38, f32[8,512]{1,0:T(8,128)S(1)} %mul.134.half_rows, bf16[512,1024]{1,0:T(8,128)(2,1)S(1)} %dynamic-slice_bitcast_fusion.1.refs_0_, ...), custom_call_target="tpu_custom_call" | custom-call | flops 1610612736 | bytes 7864320 | tf_op jit(solution)/shard_map/build_tiles/pallas_call | solution.py:106
  26.2 8.8 %collective-permute-done.1.refs_0_ = bf16[512,1024]{1,0:T(8,128)(2,1)} collective-permute-done((bf16[512,1024]{1,0:T(8,128)(2,1)}, bf16[512,1024]{1,0:T(8,128)(2,1)}, u32[]{:S(2)}, u32[]{:S(2)}) %collective-permute-start.1) | collective-permute-done | bytes 1048608 | tf_op jit(solution)/shard_map/ppermute | solution.py:443
  38.3 2.7 %collective-permute-start.8 = (bf16[512,1024]{1,0:T(8,128)(2,1)S(1)}, bf16[512,1024]{1,0:T(8,128)(2,1)S(1)}, u32[]{:S(2)}, u32[]{:S(2)}) collective-permute-start(bf16[512,1024]{1,0:T(8,128)(2,1)S(1)} %get-tuple-element.62), channel_id=1, source_target_pairs={{0,1},{8,25},{1,16},{9,8},{16,17},{24,9},{17,0},{25,24},{2,3},{10,... | collective-permute-start | bytes 3145736 | tf_op jit(solution)/shard_map/ppermute | solution.py:439
  41.0 3.0 %build_tiles.7 = (bf16[24,512,512]{2,1,0:T(8,128)(2,1)}, f32[8,512]{1,0:T(8,128)S(1)}) custom-call(s32[121]{0:T(128)S(1)} %concatenate.13.info, bf16[8,512,1024]{2,1,0:T(8,128)(2,1)S(1)} %bitcast.39, f32[8,512]{1,0:T(8,128)S(1)} %mul.134.half_rows, bf16[512,1024]{1,0:T(8,128)(2,1)} %collective-permute-done.1.refs_0_, ...), custom_call_target="tpu_custom_call", output_to_operand_aliasing={{0}: (6, {})} | custom-call | flops 2147483648 | bytes 10485760 | tf_op jit(solution)/shard_map/build_tiles/pallas_call | solution.py:106
  44.0 4.2 %collective-permute-start.10 = (bf16[512,1024]{1,0:T(8,128)(2,1)S(1)}, bf16[512,1024]{1,0:T(8,128)(2,1)S(1)}, u32[]{:S(2)}, u32[]{:S(2)}) collective-permute-start(bf16[512,1024]{1,0:T(8,128)(2,1)S(1)} %get-tuple-element.45), channel_id=1, source_target_pairs={{0,32},{8,104},{32,64},{40,8},{64,96},{72,40},{96,0},{104,72},{1,3... | collective-permute-start | bytes 3145736 | tf_op jit(solution)/shard_map/ppermute | solution.py:426
  48.2 2.3 %build_tiles.8 = (bf16[24,512,512]{2,1,0:T(8,128)(2,1)}, f32[8,512]{1,0:T(8,128)S(1)}) custom-call(s32[121]{0:T(128)S(1)} %concatenate.13.info, bf16[8,512,1024]{2,1,0:T(8,128)(2,1)S(1)} %bitcast.40, f32[8,512]{1,0:T(8,128)S(1)} %mul.134.half_rows, bf16[512,1024]{1,0:T(8,128)(2,1)S(1)} %collective-permute-done.4.refs_0_, ...), custom_call_target="tpu_custom_call", output_to_operand_aliasing={{0}: (6, {})} | custom-call | flops 2147483648 | bytes 10485760 | tf_op jit(solution)/shard_map/build_tiles/pallas_call | solution.py:106
  50.5 2.2 %collective-permute-done.8 = bf16[512,1024]{1,0:T(8,128)(2,1)S(1)} collective-permute-done((bf16[512,1024]{1,0:T(8,128)(2,1)S(1)}, bf16[512,1024]{1,0:T(8,128)(2,1)S(1)}, u32[]{:S(2)}, u32[]{:S(2)}) %collective-permute-start.8) | collective-permute-done | bytes 1048608 | tf_op jit(solution)/shard_map/ppermute | solution.py:439
  52.8 3.4 %collective-permute-start.11 = (bf16[512,1024]{1,0:T(8,128)(2,1)S(1)}, bf16[512,1024]{1,0:T(8,128)(2,1)S(1)}, u32[]{:S(2)}, u32[]{:S(2)}) collective-permute-start(bf16[512,1024]{1,0:T(8,128)(2,1)S(1)} %collective-permute-done.8), channel_id=1, source_target_pairs={{0,1},{8,25},{1,16},{9,8},{16,17},{24,9},{17,0},{25,24},{2,3},{10,... | collective-permute-start | bytes 3145736 | tf_op jit(solution)/shard_map/ppermute | solution.py:439
  56.2 6.1 %collective-permute-done.10.refs_2_ = bf16[512,1024]{1,0:T(8,128)(2,1)S(1)} collective-permute-done((bf16[512,1024]{1,0:T(8,128)(2,1)S(1)}, bf16[512,1024]{1,0:T(8,128)(2,1)S(1)}, u32[]{:S(2)}, u32[]{:S(2)}) %collective-permute-start.10) | collective-permute-done | bytes 1048608 | tf_op jit(solution)/shard_map/ppermute | solution.py:426
  62.3 2.2 %collective-permute-start.12 = (bf16[512,1024]{1,0:T(8,128)(2,1)S(1)}, bf16[512,1024]{1,0:T(8,128)(2,1)S(1)}, u32[]{:S(2)}, u32[]{:S(2)}) collective-permute-start(bf16[512,1024]{1,0:T(8,128)(2,1)S(1)} %collective-permute-done.10.refs_2_), channel_id=1, source_target_pairs={{0,8},{8,0},{1,9},{9,1},{2,10},{10,2},{3,11},{11,3},{4,12},{12,4},... | collective-permute-start | bytes 3145736 | tf_op jit(solution)/shard_map/ppermute | solution.py:391
  64.9 3.0 %collective-permute-done.11.refs_3_ = bf16[512,1024]{1,0:T(8,128)(2,1)S(1)} collective-permute-done((bf16[512,1024]{1,0:T(8,128)(2,1)S(1)}, bf16[512,1024]{1,0:T(8,128)(2,1)S(1)}, u32[]{:S(2)}, u32[]{:S(2)}) %collective-permute-start.11) | collective-permute-done | bytes 1048608 | tf_op jit(solution)/shard_map/ppermute | solution.py:439
  69.3 4.1 %build_tiles.9 = (bf16[24,512,512]{2,1,0:T(8,128)(2,1)}, f32[8,512]{1,0:T(8,128)S(1)}) custom-call(s32[121]{0:T(128)S(1)} %concatenate.13.info, bf16[8,512,1024]{2,1,0:T(8,128)(2,1)S(1)} %bitcast.41, f32[8,512]{1,0:T(8,128)S(1)} %mul.134.half_rows, bf16[512,1024]{1,0:T(8,128)(2,1)S(1)} %collective-permute-done.7.refs_0_, ...), custom_call_target="tpu_custom_call", output_to_operand_aliasing={{0}: (8, {})} | custom-call | flops 3758096384 | bytes 18350080 | tf_op jit(solution)/shard_map/build_tiles/pallas_call | solution.py:106
  73.4 4.9 %collective-permute-done.13.refs_1_ = bf16[512,1024]{1,0:T(8,128)(2,1)S(1)} collective-permute-done((bf16[512,1024]{1,0:T(8,128)(2,1)S(1)}, bf16[512,1024]{1,0:T(8,128)(2,1)S(1)}, u32[]{:S(2)}, u32[]{:S(2)}) %collective-permute-start.13) | collective-permute-done | bytes 1048608 | tf_op jit(solution)/shard_map/ppermute | solution.py:426
  78.3 2.1 %collective-permute-start.14 = (bf16[512,1024]{1,0:T(8,128)(2,1)S(1)}, bf16[512,1024]{1,0:T(8,128)(2,1)S(1)}, u32[]{:S(2)}, u32[]{:S(2)}) collective-permute-start(bf16[512,1024]{1,0:T(8,128)(2,1)S(1)} %collective-permute-done.13.refs_1_), channel_id=1, source_target_pairs={{0,8},{8,0},{1,9},{9,1},{2,10},{10,2},{3,11},{11,3},{4,12},{12,4},... | collective-permute-start | bytes 3145736 | tf_op jit(solution)/shard_map/ppermute | solution.py:391
  80.5 2.3 %build_tiles.10 = (bf16[24,512,512]{2,1,0:T(8,128)(2,1)}, f32[8,512]{1,0:T(8,128)S(1)}) custom-call(s32[121]{0:T(128)S(1)} %concatenate.13.info, bf16[8,512,1024]{2,1,0:T(8,128)(2,1)S(1)} %bitcast.42, f32[8,512]{1,0:T(8,128)S(1)} %mul.134.half_rows, bf16[512,1024]{1,0:T(8,128)(2,1)S(1)} %collective-permute-done.15.refs_0_, ...), custom_call_target="tpu_custom_call", output_to_operand_aliasing={{0}: (5, {})} | custom-call | flops 1610612736 | bytes 7864320 | tf_op jit(solution)/shard_map/build_tiles/pallas_call | solution.py:106
  83.5 22.2 %all_to_all.25 = f32[64,8,128]{2,1,0:T(8,128)S(1)} all-to-all(f32[64,8,128]{2,1,0:T(8,128)S(1)} %bitcast.47), channel_id=1, replica_groups=mesh['y'=4,'zh'=2,'core'=2,'x'=4,'zl'=2] {'y','zh','x','zl'}, dimensions={0} | all-to-all | bytes 524288 | tf_op jit(solution)/shard_map/all_to_all | solution.py:530
  106.9 3.6 %product.2 = bf16[8,80,512]{2,1,0:T(8,128)(2,1)S(1)} custom-call(s32[121]{0:T(128)S(1)} %concatenate.13.info, bf16[24,512,512]{2,1,0:T(8,128)(2,1)} %get-tuple-element.55.tiles, f32[8,8,128]{2,1,0:T(8,128)S(1)} %bitcast_reduce_fusion.refs_0_.known, f32[8,8,128]{2,1,0:T(8,128)S(1)} %collective-permute-done.16.refs_1_, f32[8,512]{1,0:T(8,128)S(1)} %get-tuple-element.56.refs_2_), custom_call_target="tpu_custom_call" | custom-call | tf_op jit(solution)/shard_map/product/pallas_call | solution.py:249
  110.6 13.5 %all_to_all.26.parts = bf16[8,80,512]{2,1,0:T(8,128)(2,1)S(1)} all-to-all(bf16[8,80,512]{2,1,0:T(8,128)(2,1)S(1)} %product.2), channel_id=1, replica_groups=mesh['y'=4,'zh'=2,'core'=2,'x'=4,'zl'=2] {'x','zl'}, dimensions={0} | all-to-all | bytes 1310720 | tf_op jit(solution)/shard_map/all_to_all | solution.py:538
  125.7 16.4 %all_to_all.27.refs_0_ = bf16[8,80,512]{2,1,0:T(8,128)(2,1)S(1)} all-to-all(bf16[8,80,512]{2,1,0:T(8,128)(2,1)S(1)} %broadcast_in_dim.112), channel_id=1, replica_groups=mesh['y'=4,'zh'=2,'core'=2,'x'=4,'zl'=2] {'y','zh'}, dimensions={0} | all-to-all | bytes 1310720 | tf_op jit(solution)/shard_map/all_to_all | solution.py:396
  142.1 2.9 %collective-permute-start.17 = (bf16[8,80,512]{2,1,0:T(8,128)(2,1)S(1)}, bf16[8,80,512]{2,1,0:T(8,128)(2,1)S(1)}, u32[]{:S(2)}, u32[]{:S(2)}) collective-permute-start(bf16[8,80,512]{2,1,0:T(8,128)(2,1)S(1)} %all_to_all.27.refs_0_), channel_id=1, source_target_pairs={{0,8},{8,0},{1,9},{9,1},{2,10},{10,2},{3,11},{11,3},{4,12},{12,4},... | collective-permute-start | bytes 1966088 | tf_op jit(solution)/shard_map/ppermute | solution.py:391
  145.0 1.7 collective-permute-done.17.refs_1_
  146.7 4.5 %product.3 = bf16[8,80,512]{2,1,0:T(8,128)(2,1)} custom-call(s32[121]{0:T(128)S(1)} %concatenate.13.info, bf16[24,512,512]{2,1,0:T(8,128)(2,1)} %get-tuple-element.55.tiles, bf16[8,80,512]{2,1,0:T(8,128)(2,1)S(1)} %all_to_all.27.refs_0_, bf16[8,80,512]{2,1,0:T(8,128)(2,1)S(1)} %collective-permute-done.17.refs_1_, f32[8,512]{1,0:T(8,128)S(1)} %get-tuple-element.56.refs_2_), custom_call_target="tpu_custom_call" | custom-call | tf_op jit(solution)/shard_map/product/pallas_call | solution.py:249
  151.3 3.6 %all-to-all-start.3 = ((bf16[8,80,512]{2,1,0:T(8,128)(2,1)}), bf16[8,80,512]{2,1,0:T(8,128)(2,1)S(1)}, u32[]{:S(2)}, u32[]{:S(2)}) async-start(bf16[8,80,512]{2,1,0:T(8,128)(2,1)} %product.3), calls=%async_computation.3 | async-start | bytes 1310720 | tf_op jit(solution)/shard_map/all_to_all | solution.py:543
  154.8 10.8 %all-to-all-done.3.parts = bf16[8,80,512]{2,1,0:T(8,128)(2,1)S(1)} async-done(((bf16[8,80,512]{2,1,0:T(8,128)(2,1)}), bf16[8,80,512]{2,1,0:T(8,128)(2,1)S(1)}, u32[]{:S(2)}, u32[]{:S(2)}) %all-to-all-start.3) | async-done | bytes 655392 | tf_op jit(solution)/shard_map/all_to_all | solution.py:543
  165.6 3.5 %middle.1 = (f32[64,512]{1,0:T(8,128)S(1)}, f32[32,128]{1,0:T(8,128)S(1)}) custom-call(s32[121]{0:T(128)S(1)} %concatenate.13.info, bf16[8,80,512]{2,1,0:T(8,128)(2,1)S(1)} %all-to-all-done.3.parts, f32[8,8,128]{2,1,0:T(8,128)S(1)} %bitcast_reduce_fusion.refs_0_.known, f32[8,8,8,128]{3,2,1,0:T(8,128)S(1)} %bitcast.45), custom_call_target="tpu_custom_call" | custom-call | tf_op jit(solution)/shard_map/middle/pallas_call | solution.py:380
  171.2 19.0 %all_to_all.28 = f32[64,16,128]{2,1,0:T(8,128)S(1)} all-to-all(f32[64,16,128]{2,1,0:T(8,128)S(1)} %broadcast_in_dim.113), channel_id=1, replica_groups=mesh['y'=4,'zh'=2,'core'=2,'x'=4,'zl'=2] {'y','zh','x','zl'}, dimensions={0} | all-to-all | bytes 1048576 | tf_op jit(solution)/shard_map/all_to_all | solution.py:396
  190.2 2.0 collective-permute-start.19
  193.0 3.4 %last.1 = f32[64,512]{1,0:T(8,128)} custom-call(s32[121]{0:T(128)S(1)} %concatenate.13.info, f32[32,128]{1,0:T(8,128)S(1)} %pad_maximum_fusion.1.message, f32[64,512]{1,0:T(8,128)S(1)} %get-tuple-element.58.image, f32[8,8,128]{2,1,0:T(8,128)S(1)} %bitcast_reduce_fusion.refs_0_.known), custom_call_target="tpu_custom_call" | custom-call | tf_op jit(solution)/shard_map/last/pallas_call | solution.py:380
  (67 shorter events, 18.6 us)
Async XLA Ops:
  0.0 17.6 %copy-start.3 = (s32[1,1,24]{2,1,0:T(1,128)S(1)}, s32[1,1,24]{2,1,0:T(1,128)}, u32[]{:S(2)}) copy-start(s32[1,1,24]{2,1,0:T(1,128)} %param.8) | copy-start | bytes 292
  0.0 17.9 %copy-start.4 = (s32[1,1,24]{2,1,0:T(1,128)S(1)}, s32[1,1,24]{2,1,0:T(1,128)}, u32[]{:S(2)}) copy-start(s32[1,1,24]{2,1,0:T(1,128)} %param.7) | copy-start | bytes 292
  1.3 17.3 %collective-permute-start = (bf16[512,1024]{1,0:T(8,128)(2,1)S(1)}, bf16[512,1024]{1,0:T(8,128)(2,1)}, u32[]{:S(2)}, u32[]{:S(2)}) collective-permute-start(bf16[512,1024]{1,0:T(8,128)(2,1)S(1)} %dynamic-slice_bitcast_fusion.1.refs_0_), channel_id=1, source_target_pairs={{0,8},{8,0},{1,9},{9,1},{2,10},{10,2},{3,11},{11,3},{4,12},{12,4},... | collective-permute-start | bytes 3145736 | tf_op jit(solution)/shard_map/ppermute | solution.py:391
  2.8 32.2 %collective-permute-start.2 = (bf16[512,1024]{1,0:T(8,128)(2,1)S(1)}, bf16[512,1024]{1,0:T(8,128)(2,1)S(1)}, u32[]{:S(2)}, u32[]{:S(2)}) collective-permute-start(bf16[512,1024]{1,0:T(8,128)(2,1)S(1)} %dynamic-slice_bitcast_fusion.1.refs_0_), channel_id=1, source_target_pairs={{0,32},{32,64},{64,96},{96,0},{1,33},{33,65},{65,97},{97,1},{2,34}... | collective-permute-start | bytes 3145736 | tf_op jit(solution)/shard_map/ppermute | solution.py:418
  4.2 30.8 %collective-permute-start.3 = (bf16[512,1024]{1,0:T(8,128)(2,1)S(1)}, bf16[512,1024]{1,0:T(8,128)(2,1)S(1)}, u32[]{:S(2)}, u32[]{:S(2)}) collective-permute-start(bf16[512,1024]{1,0:T(8,128)(2,1)S(1)} %dynamic-slice_bitcast_fusion.1.refs_0_), channel_id=1, source_target_pairs={{0,96},{32,0},{64,32},{96,64},{1,97},{33,1},{65,33},{97,65},{2,98}... | collective-permute-start | bytes 3145736 | tf_op jit(solution)/shard_map/ppermute | solution.py:422
  7.9 27.1 %collective-permute-start.1 = (bf16[512,1024]{1,0:T(8,128)(2,1)}, bf16[512,1024]{1,0:T(8,128)(2,1)}, u32[]{:S(2)}, u32[]{:S(2)}) collective-permute-start(bf16[512,1024]{1,0:T(8,128)(2,1)} %dynamic-slice_bitcast_fusion), channel_id=1, source_target_pairs={{0,17},{17,0},{1,16},{16,1},{2,19},{19,2},{3,18},{18,3},{4,21},{21... | collective-permute-start | bytes 3145736 | tf_op jit(solution)/shard_map/ppermute | solution.py:443
  18.6 3.4 %copy-start = (bf16[4096,1024]{1,0:T(8,128)(2,1)S(1)}, bf16[4096,1024]{1,0:T(8,128)(2,1)}, u32[]{:S(2)}) copy-start(bf16[4096,1024]{1,0:T(8,128)(2,1)} %param.5) | copy-start | bytes 25165828
  22.0 19.0 %copy-start.1 = (bf16[4096,1024]{1,0:T(8,128)(2,1)S(1)}, bf16[4096,1024]{1,0:T(8,128)(2,1)}, u32[]{:S(2)}) copy-start(bf16[4096,1024]{1,0:T(8,128)(2,1)} %param.5) | copy-start | bytes 25165828
  35.0 9.0 %collective-permute-start.4 = (bf16[512,1024]{1,0:T(8,128)(2,1)}, bf16[512,1024]{1,0:T(8,128)(2,1)S(1)}, u32[]{:S(2)}, u32[]{:S(2)}) collective-permute-start(bf16[512,1024]{1,0:T(8,128)(2,1)} %collective-permute-done.1.refs_0_), channel_id=1, source_target_pairs={{0,8},{8,0},{1,9},{9,1},{2,10},{10,2},{3,11},{11,3},{4,12},{12,4},... | collective-permute-start | bytes 3145736 | tf_op jit(solution)/shard_map/ppermute | solution.py:391
  36.1 12.1 %collective-permute-start.5 = (bf16[512,1024]{1,0:T(8,128)(2,1)S(1)}, bf16[512,1024]{1,0:T(8,128)(2,1)S(1)}, u32[]{:S(2)}, u32[]{:S(2)}) collective-permute-start(bf16[512,1024]{1,0:T(8,128)(2,1)S(1)} %collective-permute-done.2.refs_1_), channel_id=1, source_target_pairs={{0,8},{8,0},{1,9},{9,1},{2,10},{10,2},{3,11},{11,3},{4,12},{12,4},... | collective-permute-start | bytes 3145736 | tf_op jit(solution)/shard_map/ppermute | solution.py:391
  36.4 11.8 %collective-permute-start.6 = (bf16[512,1024]{1,0:T(8,128)(2,1)S(1)}, bf16[512,1024]{1,0:T(8,128)(2,1)S(1)}, u32[]{:S(2)}, u32[]{:S(2)}) collective-permute-start(bf16[512,1024]{1,0:T(8,128)(2,1)S(1)} %collective-permute-done.3.refs_2_), channel_id=1, source_target_pairs={{0,8},{8,0},{1,9},{9,1},{2,10},{10,2},{3,11},{11,3},{4,12},{12,4},... | collective-permute-start | bytes 3145736 | tf_op jit(solution)/shard_map/ppermute | solution.py:391
  36.9 15.9 %collective-permute-start.7 = (bf16[512,1024]{1,0:T(8,128)(2,1)}, bf16[512,1024]{1,0:T(8,128)(2,1)S(1)}, u32[]{:S(2)}, u32[]{:S(2)}) collective-permute-start(bf16[512,1024]{1,0:T(8,128)(2,1)} %collective-permute-done.1.refs_0_), channel_id=1, source_target_pairs={{0,32},{8,104},{32,64},{40,8},{64,96},{72,40},{96,0},{104,72},{1,3... | collective-permute-start | bytes 3145736 | tf_op jit(solution)/shard_map/ppermute | solution.py:426
  38.3 14.4 %collective-permute-start.8 = (bf16[512,1024]{1,0:T(8,128)(2,1)S(1)}, bf16[512,1024]{1,0:T(8,128)(2,1)S(1)}, u32[]{:S(2)}, u32[]{:S(2)}) collective-permute-start(bf16[512,1024]{1,0:T(8,128)(2,1)S(1)} %get-tuple-element.62), channel_id=1, source_target_pairs={{0,1},{8,25},{1,16},{9,8},{16,17},{24,9},{17,0},{25,24},{2,3},{10,... | collective-permute-start | bytes 3145736 | tf_op jit(solution)/shard_map/ppermute | solution.py:439
  44.0 18.2 %collective-permute-start.10 = (bf16[512,1024]{1,0:T(8,128)(2,1)S(1)}, bf16[512,1024]{1,0:T(8,128)(2,1)S(1)}, u32[]{:S(2)}, u32[]{:S(2)}) collective-permute-start(bf16[512,1024]{1,0:T(8,128)(2,1)S(1)} %get-tuple-element.45), channel_id=1, source_target_pairs={{0,32},{8,104},{32,64},{40,8},{64,96},{72,40},{96,0},{104,72},{1,3... | collective-permute-start | bytes 3145736 | tf_op jit(solution)/shard_map/ppermute | solution.py:426
  52.8 15.2 %collective-permute-start.11 = (bf16[512,1024]{1,0:T(8,128)(2,1)S(1)}, bf16[512,1024]{1,0:T(8,128)(2,1)S(1)}, u32[]{:S(2)}, u32[]{:S(2)}) collective-permute-start(bf16[512,1024]{1,0:T(8,128)(2,1)S(1)} %collective-permute-done.8), channel_id=1, source_target_pairs={{0,1},{8,25},{1,16},{9,8},{16,17},{24,9},{17,0},{25,24},{2,3},{10,... | collective-permute-start | bytes 3145736 | tf_op jit(solution)/shard_map/ppermute | solution.py:439
  56.2 13.1 %collective-permute-start.9 = (bf16[512,1024]{1,0:T(8,128)(2,1)S(1)}, bf16[512,1024]{1,0:T(8,128)(2,1)S(1)}, u32[]{:S(2)}, u32[]{:S(2)}) collective-permute-start(bf16[512,1024]{1,0:T(8,128)(2,1)S(1)} %collective-permute-done.7.refs_0_), channel_id=1, source_target_pairs={{0,8},{8,0},{1,9},{9,1},{2,10},{10,2},{3,11},{11,3},{4,12},{12,4},... | collective-permute-start | bytes 3145736 | tf_op jit(solution)/shard_map/ppermute | solution.py:391
  62.3 7.0 %collective-permute-start.12 = (bf16[512,1024]{1,0:T(8,128)(2,1)S(1)}, bf16[512,1024]{1,0:T(8,128)(2,1)S(1)}, u32[]{:S(2)}, u32[]{:S(2)}) collective-permute-start(bf16[512,1024]{1,0:T(8,128)(2,1)S(1)} %collective-permute-done.10.refs_2_), channel_id=1, source_target_pairs={{0,8},{8,0},{1,9},{9,1},{2,10},{10,2},{3,11},{11,3},{4,12},{12,4},... | collective-permute-start | bytes 3145736 | tf_op jit(solution)/shard_map/ppermute | solution.py:391
  64.4 13.9 %collective-permute-start.13 = (bf16[512,1024]{1,0:T(8,128)(2,1)S(1)}, bf16[512,1024]{1,0:T(8,128)(2,1)S(1)}, u32[]{:S(2)}, u32[]{:S(2)}) collective-permute-start(bf16[512,1024]{1,0:T(8,128)(2,1)S(1)} %collective-permute-done.7.refs_0_), channel_id=1, source_target_pairs={{0,32},{8,104},{32,64},{40,8},{64,96},{72,40},{96,0},{104,72},{1,3... | collective-permute-start | bytes 3145736 | tf_op jit(solution)/shard_map/ppermute | solution.py:426
  67.9 12.6 %collective-permute-start.15 = (bf16[512,1024]{1,0:T(8,128)(2,1)S(1)}, bf16[512,1024]{1,0:T(8,128)(2,1)S(1)}, u32[]{:S(2)}, u32[]{:S(2)}) collective-permute-start(bf16[512,1024]{1,0:T(8,128)(2,1)S(1)} %collective-permute-done.11.refs_3_), channel_id=1, source_target_pairs={{0,8},{8,0},{1,9},{9,1},{2,10},{10,2},{3,11},{11,3},{4,12},{12,4},... | collective-permute-start | bytes 3145736 | tf_op jit(solution)/shard_map/ppermute | solution.py:391
  69.3 11.1 %copy-start.2 = (s32[512]{0:T(512)S(1)}, s32[512]{0:T(512)}, u32[]{:S(2)}) copy-start(s32[512]{0:T(512)} %param.6) | copy-start | bytes 6148
  78.3 4.4 %collective-permute-start.14 = (bf16[512,1024]{1,0:T(8,128)(2,1)S(1)}, bf16[512,1024]{1,0:T(8,128)(2,1)S(1)}, u32[]{:S(2)}, u32[]{:S(2)}) collective-permute-start(bf16[512,1024]{1,0:T(8,128)(2,1)S(1)} %collective-permute-done.13.refs_1_), channel_id=1, source_target_pairs={{0,8},{8,0},{1,9},{9,1},{2,10},{10,2},{3,11},{11,3},{4,12},{12,4},... | collective-permute-start | bytes 3145736 | tf_op jit(solution)/shard_map/ppermute | solution.py:391
  105.6 1.3 collective-permute-start.16
  142.1 4.6 %collective-permute-start.17 = (bf16[8,80,512]{2,1,0:T(8,128)(2,1)S(1)}, bf16[8,80,512]{2,1,0:T(8,128)(2,1)S(1)}, u32[]{:S(2)}, u32[]{:S(2)}) collective-permute-start(bf16[8,80,512]{2,1,0:T(8,128)(2,1)S(1)} %all_to_all.27.refs_0_), channel_id=1, source_target_pairs={{0,8},{8,0},{1,9},{9,1},{2,10},{10,2},{3,11},{11,3},{4,12},{12,4},... | collective-permute-start | bytes 1966088 | tf_op jit(solution)/shard_map/ppermute | solution.py:391
  151.3 14.4 %all-to-all-start.3 = ((bf16[8,80,512]{2,1,0:T(8,128)(2,1)}), bf16[8,80,512]{2,1,0:T(8,128)(2,1)S(1)}, u32[]{:S(2)}, u32[]{:S(2)}) async-start(bf16[8,80,512]{2,1,0:T(8,128)(2,1)} %product.3), calls=%async_computation.3 | async-start | bytes 1310720 | tf_op jit(solution)/shard_map/all_to_all | solution.py:543
  169.1 2.0 %collective-permute-start.18 = (f32[16,128]{1,0:T(8,128)S(1)}, f32[16,128]{1,0:T(8,128)S(1)}, u32[]{:S(2)}, u32[]{:S(2)}) collective-permute-start(f32[16,128]{1,0:T(8,128)S(1)} %constant_dynamic-slice_fusion), channel_id=1, source_target_pairs={{0,8},{8,0},{1,9},{9,1},{2,10},{10,2},{3,11},{11,3},{4,12},{12,4},... | collective-permute-start | bytes 24584 | tf_op jit(solution)/shard_map/ppermute | solution.py:391
  190.2 2.8 %collective-permute-start.19 = (f32[16,128]{1,0:T(8,128)S(1)}, f32[16,128]{1,0:T(8,128)S(1)}, u32[]{:S(2)}, u32[]{:S(2)}) collective-permute-start(f32[16,128]{1,0:T(8,128)S(1)} %reduce_sum.99), channel_id=1, source_target_pairs={{0,8},{8,0},{1,9},{9,1},{2,10},{10,2},{3,11},{11,3},{4,12},{12,4},... | collective-permute-start | bytes 24584 | tf_op jit(solution)/shard_map/ppermute | solution.py:391

commit v15 on v13

--- a/solution.py
+++ b/solution.py
@@ -41,14 +41,18 @@
 
     begin, end = info[STARTS + first], info[STARTS + first + arrived]
 
-    def store(entry):
+    def store(entry, n):
         slot = lax.rem(entry, stores)
-        return pltpu.make_async_copy(made.at[slot], tiles.at[entry], sem_out.at[slot])
+        lanes = pl.ds(n * 256, 256)
+        return pltpu.make_async_copy(
+            made.at[slot, :, lanes], tiles.at[entry, :, lanes], sem_out.at[slot, n]
+        )
 
     def step(column, own, entry, carry):
         @pl.when(entry - begin >= stores)
         def _():
-            store(entry - stores).wait()
+            for n in range(2):
+                store(entry - stores, n).wait()
 
         slot = lax.rem(entry, stores)
         t = info[ROWS + entry]
@@ -63,6 +67,8 @@
             half_row = half_rows[pl.ds(t, 1), lanes]
             w = jnp.exp2(RATE * ((inner - half_row) - half_column)).astype(BF16)
             made[slot, :, lanes] = w
+            if not own:
+                store(entry, n).start()
             sums.append(jnp.sum(w.astype(F32), axis=0, keepdims=True))
         old = degree[pl.ds(t, 1), :]
         degree[pl.ds(t, 1), :] = old + jnp.concatenate(sums, axis=1)
@@ -77,7 +83,8 @@
                 made[slot] = w
                 degree[pl.ds(t, 1), :] = old + jnp.sum(w.astype(F32), axis=0, keepdims=True)
 
-        store(entry).start()
+            for n in range(2):
+                store(entry, n).start()
         return carry
 
     for s, column in enumerate(columns):
@@ -87,7 +94,8 @@
 
         @pl.when(end - begin > back)
         def _():
-            store(end - 1 - back).wait()
+            for n in range(2):
+                store(end - 1 - back, n).wait()
 
 
 def in_hbm(value):
@@ -115,7 +123,7 @@
         out_specs=(hbm, vmem),
         scratch_shapes=[
             pltpu.VMEM((4, TILE, TILE), BF16),
-            pltpu.SemaphoreType.DMA((4,)),
+            pltpu.SemaphoreType.DMA((4, 2)),
         ],
         input_output_aliases={3 + arrived: 0} if made else {},
         compiler_params=pltpu.CompilerParams(vmem_limit_bytes=16 * 1024 * 1024),

time: 196 us -> 195 us (level)
  waiting for transfers between devices: 46.4 us -> 42.1 us
    ppermute x3, starting transfers between devices: 2.09 us -> 5.31 us  [apart(): lax.ppermute(value, ('y', 'core'), [(2 * i + k, 2 * ((i + 1 + 2 * k) % 4)...]
    ppermute x2, waiting for transfers between devices: 8.99 us -> 6.03 us  [apart_z(): return lax.ppermute(value, ('zh', 'core', 'zl'), moves)]
    ppermute x12, starting transfers between devices: 16.9 us -> 14.4 us  [swap_cores(): return lax.ppermute(value, 'core', [(0, 1), (1, 0)])]
  transfers between devices with their start and end apart: 21 -> 21, of which waited for: 11 -> 10; matrix products, arithmetic and copies ran while one was open for 4% -> 4% of each run, Pallas kernels for 7% -> 8%
where the time goes in v15:
time: 195 us; the launch traced here: 194 us
  blocking collectives  66.1 us (34%)
  waiting for transfers between devices  42.1 us (22%)
  starting transfers between devices  36 us (18%)
  Pallas kernels  35.4 us (18%)
  local copies, waits for them, and re-layouts  7.31 us (4%)
  other arithmetic  6.29 us (3%)
    all_to_all x2, blocking collectives, share(): lax.all_to_all(jnp.broadcast_to(value[None], (size,) + value.shape), axes...  33.8 us
    all_to_all x1, blocking collectives, shards(): lax.all_to_all(jnp.broadcast_to(sent[None], (8,) + sent.shape).reshape(8...  20.3 us
    pallas_call x6, Pallas kernels, build(): pl.pallas_call(functools.partial(build_kernel, first, arrived), out_shape...  18.4 us
    ppermute x12, starting transfers between devices, swap_cores(): return lax.ppermute(value, 'core', [(0, 1), (1, 0)])  14.4 us
    all_to_all x1, blocking collectives, shards(): parts = lax.all_to_all(running, COL, 0, 0, tiled=True)  12 us
    all_to_all x1, waiting for transfers between devices, shards(): parts = lax.all_to_all(running, COL, 0, 0, tiled=True)  11.8 us
    ppermute x3, waiting for transfers between devices, apart(): lax.ppermute(value, ('y', 'core'), [(2 * i + k, 2 * ((i + 1 + 2 * k) % 4)...  10 us
    ppermute x1, waiting for transfers between devices, cross(): return lax.ppermute(value, ('zh', 'zl'), [(0, 3), (3, 0), (1, 2), (2, 1)])  9.66 us
  transfers between devices with their start and end apart: 21, of which 10 were waited for; matrix products, arithmetic and copies ran while one was open for 4% of the time, Pallas kernels for 8%

profile of v15, /device:TPU:1, one launch (start us, length us, event | category | flops | bytes accessed | tf_op | source)
XLA Modules:
  0.0 194.2 jit_solution(3565671398745875667)
XLA Ops:
  5.7 2.3 %dynamic-slice_bitcast_fusion = bf16[512,1024]{1,0:T(8,128)(2,1)} fusion(bf16[8,512,1024]{2,1,0:T(8,128)(2,1)} %bitcast.37, s32[]{:T(128)S(6)} %select_n.198), kind=kLoop, calls=%fused_computation.1 | loop fusion | bytes 2097156 | tf_op jit(solution)/shard_map/jit(dynamic_index_in_dim)/squeeze | solution.py:486
  7.9 3.8 %collective-permute-start.1 = (bf16[512,1024]{1,0:T(8,128)(2,1)}, bf16[512,1024]{1,0:T(8,128)(2,1)}, u32[]{:S(2)}, u32[]{:S(2)}) collective-permute-start(bf16[512,1024]{1,0:T(8,128)(2,1)} %dynamic-slice_bitcast_fusion), channel_id=1, source_target_pairs={{0,17},{17,0},{1,16},{16,1},{2,19},{19,2},{3,18},{18,3},{4,21},{21... | collective-permute-start | bytes 3145736 | tf_op jit(solution)/shard_map/ppermute | solution.py:429
  11.7 5.1 %multiply_reduce_fusion = f32[4096]{0:T(1024)S(1)} fusion(bf16[4096,1024]{1,0:T(8,128)(2,1)} %param.5), kind=kLoop, calls=%fused_computation | loop fusion | flops 12578816 | bytes 8404992 | tf_op jit(solution)/shard_map/reduce_sum | solution.py:488
  18.6 3.4 %copy-done = bf16[4096,1024]{1,0:T(8,128)(2,1)S(1)} copy-done((bf16[4096,1024]{1,0:T(8,128)(2,1)S(1)}, bf16[4096,1024]{1,0:T(8,128)(2,1)}, u32[]{:S(2)}) %copy-start) | copy-done | bytes 8388632
  22.0 3.3 %build_tiles.6 = (bf16[24,512,512]{2,1,0:T(8,128)(2,1)}, f32[8,512]{1,0:T(8,128)S(1)}) custom-call(s32[121]{0:T(128)S(1)} %concatenate.13.info, bf16[8,512,1024]{2,1,0:T(8,128)(2,1)S(1)} %bitcast.38, f32[8,512]{1,0:T(8,128)S(1)} %mul.134.half_rows, bf16[512,1024]{1,0:T(8,128)(2,1)S(1)} %dynamic-slice_bitcast_fusion.1.refs_0_, ...), custom_call_target="tpu_custom_call" | custom-call | flops 1610612736 | bytes 7864320 | tf_op jit(solution)/shard_map/build_tiles/pallas_call | solution.py:114
  25.3 9.7 %collective-permute-done.1.refs_0_ = bf16[512,1024]{1,0:T(8,128)(2,1)} collective-permute-done((bf16[512,1024]{1,0:T(8,128)(2,1)}, bf16[512,1024]{1,0:T(8,128)(2,1)}, u32[]{:S(2)}, u32[]{:S(2)}) %collective-permute-start.1) | collective-permute-done | bytes 1048608 | tf_op jit(solution)/shard_map/ppermute | solution.py:429
  38.3 2.7 %collective-permute-start.8 = (bf16[512,1024]{1,0:T(8,128)(2,1)S(1)}, bf16[512,1024]{1,0:T(8,128)(2,1)S(1)}, u32[]{:S(2)}, u32[]{:S(2)}) collective-permute-start(bf16[512,1024]{1,0:T(8,128)(2,1)S(1)} %get-tuple-element.62), channel_id=1, source_target_pairs={{0,1},{8,25},{1,16},{9,8},{16,17},{24,9},{17,0},{25,24},{2,3},{10,... | collective-permute-start | bytes 3145736 | tf_op jit(solution)/shard_map/ppermute | solution.py:425
  41.0 3.0 %build_tiles.7 = (bf16[24,512,512]{2,1,0:T(8,128)(2,1)}, f32[8,512]{1,0:T(8,128)S(1)}) custom-call(s32[121]{0:T(128)S(1)} %concatenate.13.info, bf16[8,512,1024]{2,1,0:T(8,128)(2,1)S(1)} %bitcast.39, f32[8,512]{1,0:T(8,128)S(1)} %mul.134.half_rows, bf16[512,1024]{1,0:T(8,128)(2,1)} %collective-permute-done.1.refs_0_, ...), custom_call_target="tpu_custom_call", output_to_operand_aliasing={{0}: (6, {})} | custom-call | flops 2147483648 | bytes 10485760 | tf_op jit(solution)/shard_map/build_tiles/pallas_call | solution.py:114
  44.1 3.3 %collective-permute-start.10 = (bf16[512,1024]{1,0:T(8,128)(2,1)S(1)}, bf16[512,1024]{1,0:T(8,128)(2,1)S(1)}, u32[]{:S(2)}, u32[]{:S(2)}) collective-permute-start(bf16[512,1024]{1,0:T(8,128)(2,1)S(1)} %get-tuple-element.45), channel_id=1, source_target_pairs={{0,32},{8,104},{32,64},{40,8},{64,96},{72,40},{96,0},{104,72},{1,3... | collective-permute-start | bytes 3145736 | tf_op jit(solution)/shard_map/ppermute | solution.py:412
  47.4 2.3 %build_tiles.8 = (bf16[24,512,512]{2,1,0:T(8,128)(2,1)}, f32[8,512]{1,0:T(8,128)S(1)}) custom-call(s32[121]{0:T(128)S(1)} %concatenate.13.info, bf16[8,512,1024]{2,1,0:T(8,128)(2,1)S(1)} %bitcast.40, f32[8,512]{1,0:T(8,128)S(1)} %mul.134.half_rows, bf16[512,1024]{1,0:T(8,128)(2,1)S(1)} %collective-permute-done.4.refs_0_, ...), custom_call_target="tpu_custom_call", output_to_operand_aliasing={{0}: (6, {})} | custom-call | flops 2147483648 | bytes 10485760 | tf_op jit(solution)/shard_map/build_tiles/pallas_call | solution.py:114
  49.7 3.1 %collective-permute-done.8 = bf16[512,1024]{1,0:T(8,128)(2,1)S(1)} collective-permute-done((bf16[512,1024]{1,0:T(8,128)(2,1)S(1)}, bf16[512,1024]{1,0:T(8,128)(2,1)S(1)}, u32[]{:S(2)}, u32[]{:S(2)}) %collective-permute-start.8) | collective-permute-done | bytes 1048608 | tf_op jit(solution)/shard_map/ppermute | solution.py:425
  52.8 3.4 %collective-permute-start.11 = (bf16[512,1024]{1,0:T(8,128)(2,1)S(1)}, bf16[512,1024]{1,0:T(8,128)(2,1)S(1)}, u32[]{:S(2)}, u32[]{:S(2)}) collective-permute-start(bf16[512,1024]{1,0:T(8,128)(2,1)S(1)} %collective-permute-done.8), channel_id=1, source_target_pairs={{0,1},{8,25},{1,16},{9,8},{16,17},{24,9},{17,0},{25,24},{2,3},{10,... | collective-permute-start | bytes 3145736 | tf_op jit(solution)/shard_map/ppermute | solution.py:425
  56.2 6.1 %collective-permute-done.10.refs_2_ = bf16[512,1024]{1,0:T(8,128)(2,1)S(1)} collective-permute-done((bf16[512,1024]{1,0:T(8,128)(2,1)S(1)}, bf16[512,1024]{1,0:T(8,128)(2,1)S(1)}, u32[]{:S(2)}, u32[]{:S(2)}) %collective-permute-start.10) | collective-permute-done | bytes 1048608 | tf_op jit(solution)/shard_map/ppermute | solution.py:412
  62.3 2.2 %collective-permute-start.12 = (bf16[512,1024]{1,0:T(8,128)(2,1)S(1)}, bf16[512,1024]{1,0:T(8,128)(2,1)S(1)}, u32[]{:S(2)}, u32[]{:S(2)}) collective-permute-start(bf16[512,1024]{1,0:T(8,128)(2,1)S(1)} %collective-permute-done.10.refs_2_), channel_id=1, source_target_pairs={{0,8},{8,0},{1,9},{9,1},{2,10},{10,2},{3,11},{11,3},{4,12},{12,4},... | collective-permute-start | bytes 3145736 | tf_op jit(solution)/shard_map/ppermute | solution.py:377
  64.9 3.0 %collective-permute-done.11.refs_3_ = bf16[512,1024]{1,0:T(8,128)(2,1)S(1)} collective-permute-done((bf16[512,1024]{1,0:T(8,128)(2,1)S(1)}, bf16[512,1024]{1,0:T(8,128)(2,1)S(1)}, u32[]{:S(2)}, u32[]{:S(2)}) %collective-permute-start.11) | collective-permute-done | bytes 1048608 | tf_op jit(solution)/shard_map/ppermute | solution.py:425
  69.3 5.1 %build_tiles.9 = (bf16[24,512,512]{2,1,0:T(8,128)(2,1)}, f32[8,512]{1,0:T(8,128)S(1)}) custom-call(s32[121]{0:T(128)S(1)} %concatenate.13.info, bf16[8,512,1024]{2,1,0:T(8,128)(2,1)S(1)} %bitcast.41, f32[8,512]{1,0:T(8,128)S(1)} %mul.134.half_rows, bf16[512,1024]{1,0:T(8,128)(2,1)S(1)} %collective-permute-done.7.refs_0_, ...), custom_call_target="tpu_custom_call", output_to_operand_aliasing={{0}: (8, {})} | custom-call | flops 3758096384 | bytes 18350080 | tf_op jit(solution)/shard_map/build_tiles/pallas_call | solution.py:114
  74.4 3.9 %collective-permute-done.13.refs_1_ = bf16[512,1024]{1,0:T(8,128)(2,1)S(1)} collective-permute-done((bf16[512,1024]{1,0:T(8,128)(2,1)S(1)}, bf16[512,1024]{1,0:T(8,128)(2,1)S(1)}, u32[]{:S(2)}, u32[]{:S(2)}) %collective-permute-start.13) | collective-permute-done | bytes 1048608 | tf_op jit(solution)/shard_map/ppermute | solution.py:412
  78.3 2.1 %collective-permute-start.14 = (bf16[512,1024]{1,0:T(8,128)(2,1)S(1)}, bf16[512,1024]{1,0:T(8,128)(2,1)S(1)}, u32[]{:S(2)}, u32[]{:S(2)}) collective-permute-start(bf16[512,1024]{1,0:T(8,128)(2,1)S(1)} %collective-permute-done.13.refs_1_), channel_id=1, source_target_pairs={{0,8},{8,0},{1,9},{9,1},{2,10},{10,2},{3,11},{11,3},{4,12},{12,4},... | collective-permute-start | bytes 3145736 | tf_op jit(solution)/shard_map/ppermute | solution.py:377
  80.5 2.3 %build_tiles.10 = (bf16[24,512,512]{2,1,0:T(8,128)(2,1)}, f32[8,512]{1,0:T(8,128)S(1)}) custom-call(s32[121]{0:T(128)S(1)} %concatenate.13.info, bf16[8,512,1024]{2,1,0:T(8,128)(2,1)S(1)} %bitcast.42, f32[8,512]{1,0:T(8,128)S(1)} %mul.134.half_rows, bf16[512,1024]{1,0:T(8,128)(2,1)S(1)} %collective-permute-done.15.refs_0_, ...), custom_call_target="tpu_custom_call", output_to_operand_aliasing={{0}: (5, {})} | custom-call | flops 1610612736 | bytes 7864320 | tf_op jit(solution)/shard_map/build_tiles/pallas_call | solution.py:114
  82.9 2.3 %build_tiles.11 = (bf16[24,512,512]{2,1,0:T(8,128)(2,1)}, f32[8,512]{1,0:T(8,128)S(1)}) custom-call(s32[121]{0:T(128)S(1)} %concatenate.13.info, bf16[8,512,1024]{2,1,0:T(8,128)(2,1)S(1)} %bitcast.43, f32[8,512]{1,0:T(8,128)S(1)} %mul.134.half_rows, bf16[512,1024]{1,0:T(8,128)(2,1)S(1)} %collective-permute-done.14.refs_0_, ...), custom_call_target="tpu_custom_call", output_to_operand_aliasing={{0}: (4, {})} | custom-call | flops 536870912 | bytes 2621440 | tf_op jit(solution)/shard_map/build_tiles/pallas_call | solution.py:114
  85.2 20.3 %all_to_all.25 = f32[64,8,128]{2,1,0:T(8,128)S(1)} all-to-all(f32[64,8,128]{2,1,0:T(8,128)S(1)} %bitcast.46), channel_id=1, replica_groups=mesh['y'=4,'zh'=2,'core'=2,'x'=4,'zl'=2] {'y','zh','x','zl'}, dimensions={0} | all-to-all | bytes 524288 | tf_op jit(solution)/shard_map/all_to_all | solution.py:516
  106.8 4.0 %product.2 = bf16[8,64,512]{2,1,0:T(8,128)(2,1)S(1)} custom-call(s32[121]{0:T(128)S(1)} %concatenate.13.info, bf16[24,512,512]{2,1,0:T(8,128)(2,1)} %get-tuple-element.55.tiles, f32[8,8,128]{2,1,0:T(8,128)S(1)} %bitcast_reduce_fusion.refs_0_.known, f32[8,8,128]{2,1,0:T(8,128)S(1)} %collective-permute-done.16.refs_1_), custom_call_target="tpu_custom_call" | custom-call | tf_op jit(solution)/shard_map/product/pallas_call | solution.py:240
  110.8 12.0 %all_to_all.26.parts = bf16[8,64,512]{2,1,0:T(8,128)(2,1)S(1)} all-to-all(bf16[8,64,512]{2,1,0:T(8,128)(2,1)S(1)} %product.2), channel_id=1, replica_groups=mesh['y'=4,'zh'=2,'core'=2,'x'=4,'zl'=2] {'x','zl'}, dimensions={0} | all-to-all | bytes 1048576 | tf_op jit(solution)/shard_map/all_to_all | solution.py:524
  124.0 15.8 %all_to_all.27.refs_0_ = bf16[8,80,512]{2,1,0:T(8,128)(2,1)S(1)} all-to-all(bf16[8,80,512]{2,1,0:T(8,128)(2,1)S(1)} %broadcast_in_dim.112), channel_id=1, replica_groups=mesh['y'=4,'zh'=2,'core'=2,'x'=4,'zl'=2] {'y','zh'}, dimensions={0} | all-to-all | bytes 1310720 | tf_op jit(solution)/shard_map/all_to_all | solution.py:382
  139.8 2.9 %collective-permute-start.17 = (bf16[8,80,512]{2,1,0:T(8,128)(2,1)S(1)}, bf16[8,80,512]{2,1,0:T(8,128)(2,1)S(1)}, u32[]{:S(2)}, u32[]{:S(2)}) collective-permute-start(bf16[8,80,512]{2,1,0:T(8,128)(2,1)S(1)} %all_to_all.27.refs_0_), channel_id=1, source_target_pairs={{0,8},{8,0},{1,9},{9,1},{2,10},{10,2},{3,11},{11,3},{4,12},{12,4},... | collective-permute-start | bytes 1966088 | tf_op jit(solution)/shard_map/ppermute | solution.py:377
  144.4 5.1 %product.3 = bf16[8,80,512]{2,1,0:T(8,128)(2,1)} custom-call(s32[121]{0:T(128)S(1)} %concatenate.13.info, bf16[24,512,512]{2,1,0:T(8,128)(2,1)} %get-tuple-element.55.tiles, bf16[8,80,512]{2,1,0:T(8,128)(2,1)S(1)} %all_to_all.27.refs_0_, bf16[8,80,512]{2,1,0:T(8,128)(2,1)S(1)} %collective-permute-done.17.refs_1_, f32[8,512]{1,0:T(8,128)S(1)} %get-tuple-element.56.refs_2_), custom_call_target="tpu_custom_call" | custom-call | tf_op jit(solution)/shard_map/product/pallas_call | solution.py:240
  149.5 3.6 %all-to-all-start.3 = ((bf16[8,80,512]{2,1,0:T(8,128)(2,1)}), bf16[8,80,512]{2,1,0:T(8,128)(2,1)S(1)}, u32[]{:S(2)}, u32[]{:S(2)}) async-start(bf16[8,80,512]{2,1,0:T(8,128)(2,1)} %product.3), calls=%async_computation.3 | async-start | bytes 1310720 | tf_op jit(solution)/shard_map/all_to_all | solution.py:529
  153.0 11.8 %all-to-all-done.3.parts = bf16[8,80,512]{2,1,0:T(8,128)(2,1)S(1)} async-done(((bf16[8,80,512]{2,1,0:T(8,128)(2,1)}), bf16[8,80,512]{2,1,0:T(8,128)(2,1)S(1)}, u32[]{:S(2)}, u32[]{:S(2)}) %all-to-all-start.3) | async-done | bytes 655392 | tf_op jit(solution)/shard_map/all_to_all | solution.py:529
  164.8 3.5 %middle.1 = (f32[64,512]{1,0:T(8,128)S(1)}, f32[32,128]{1,0:T(8,128)S(1)}) custom-call(s32[121]{0:T(128)S(1)} %concatenate.13.info, bf16[8,80,512]{2,1,0:T(8,128)(2,1)S(1)} %all-to-all-done.3.parts, f32[8,8,128]{2,1,0:T(8,128)S(1)} %bitcast_reduce_fusion.refs_0_.known, f32[8,8,8,128]{3,2,1,0:T(8,128)S(1)} %bitcast.44), custom_call_target="tpu_custom_call" | custom-call | tf_op jit(solution)/shard_map/middle/pallas_call | solution.py:366
  169.9 18.1 %all_to_all.28 = f32[64,16,128]{2,1,0:T(8,128)S(1)} all-to-all(f32[64,16,128]{2,1,0:T(8,128)S(1)} %broadcast_in_dim.113), channel_id=1, replica_groups=mesh['y'=4,'zh'=2,'core'=2,'x'=4,'zl'=2] {'y','zh','x','zl'}, dimensions={0} | all-to-all | bytes 1048576 | tf_op jit(solution)/shard_map/all_to_all | solution.py:382
  188.0 2.0 %collective-permute-start.19 = (f32[16,128]{1,0:T(8,128)S(1)}, f32[16,128]{1,0:T(8,128)S(1)}, u32[]{:S(2)}, u32[]{:S(2)}) collective-permute-start(f32[16,128]{1,0:T(8,128)S(1)} %reduce_sum.99), channel_id=1, source_target_pairs={{0,8},{8,0},{1,9},{9,1},{2,10},{10,2},{3,11},{11,3},{4,12},{12,4},... | collective-permute-start | bytes 24584 | tf_op jit(solution)/shard_map/ppermute | solution.py:377
  190.8 3.4 %last.1 = f32[64,512]{1,0:T(8,128)} custom-call(s32[121]{0:T(128)S(1)} %concatenate.13.info, f32[32,128]{1,0:T(8,128)S(1)} %pad_maximum_fusion.1.message, f32[64,512]{1,0:T(8,128)S(1)} %get-tuple-element.58.image, f32[8,8,128]{2,1,0:T(8,128)S(1)} %bitcast_reduce_fusion.refs_0_.known), custom_call_target="tpu_custom_call" | custom-call | tf_op jit(solution)/shard_map/last/pallas_call | solution.py:366
  (67 shorter events, 18.8 us)
Async XLA Ops:
  0.0 17.6 %copy-start.3 = (s32[1,1,24]{2,1,0:T(1,128)S(1)}, s32[1,1,24]{2,1,0:T(1,128)}, u32[]{:S(2)}) copy-start(s32[1,1,24]{2,1,0:T(1,128)} %param.8) | copy-start | bytes 292
  0.0 17.9 %copy-start.4 = (s32[1,1,24]{2,1,0:T(1,128)S(1)}, s32[1,1,24]{2,1,0:T(1,128)}, u32[]{:S(2)}) copy-start(s32[1,1,24]{2,1,0:T(1,128)} %param.7) | copy-start | bytes 292
  1.3 17.3 %collective-permute-start = (bf16[512,1024]{1,0:T(8,128)(2,1)S(1)}, bf16[512,1024]{1,0:T(8,128)(2,1)}, u32[]{:S(2)}, u32[]{:S(2)}) collective-permute-start(bf16[512,1024]{1,0:T(8,128)(2,1)S(1)} %dynamic-slice_bitcast_fusion.1.refs_0_), channel_id=1, source_target_pairs={{0,8},{8,0},{1,9},{9,1},{2,10},{10,2},{3,11},{11,3},{4,12},{12,4},... | collective-permute-start | bytes 3145736 | tf_op jit(solution)/shard_map/ppermute | solution.py:377
  2.8 32.2 %collective-permute-start.2 = (bf16[512,1024]{1,0:T(8,128)(2,1)S(1)}, bf16[512,1024]{1,0:T(8,128)(2,1)S(1)}, u32[]{:S(2)}, u32[]{:S(2)}) collective-permute-start(bf16[512,1024]{1,0:T(8,128)(2,1)S(1)} %dynamic-slice_bitcast_fusion.1.refs_0_), channel_id=1, source_target_pairs={{0,32},{32,64},{64,96},{96,0},{1,33},{33,65},{65,97},{97,1},{2,34}... | collective-permute-start | bytes 3145736 | tf_op jit(solution)/shard_map/ppermute | solution.py:404
  4.2 30.8 %collective-permute-start.3 = (bf16[512,1024]{1,0:T(8,128)(2,1)S(1)}, bf16[512,1024]{1,0:T(8,128)(2,1)S(1)}, u32[]{:S(2)}, u32[]{:S(2)}) collective-permute-start(bf16[512,1024]{1,0:T(8,128)(2,1)S(1)} %dynamic-slice_bitcast_fusion.1.refs_0_), channel_id=1, source_target_pairs={{0,96},{32,0},{64,32},{96,64},{1,97},{33,1},{65,33},{97,65},{2,98}... | collective-permute-start | bytes 3145736 | tf_op jit(solution)/shard_map/ppermute | solution.py:408
  7.9 27.1 %collective-permute-start.1 = (bf16[512,1024]{1,0:T(8,128)(2,1)}, bf16[512,1024]{1,0:T(8,128)(2,1)}, u32[]{:S(2)}, u32[]{:S(2)}) collective-permute-start(bf16[512,1024]{1,0:T(8,128)(2,1)} %dynamic-slice_bitcast_fusion), channel_id=1, source_target_pairs={{0,17},{17,0},{1,16},{16,1},{2,19},{19,2},{3,18},{18,3},{4,21},{21... | collective-permute-start | bytes 3145736 | tf_op jit(solution)/shard_map/ppermute | solution.py:429
  18.6 3.4 %copy-start = (bf16[4096,1024]{1,0:T(8,128)(2,1)S(1)}, bf16[4096,1024]{1,0:T(8,128)(2,1)}, u32[]{:S(2)}) copy-start(bf16[4096,1024]{1,0:T(8,128)(2,1)} %param.5) | copy-start | bytes 25165828
  22.0 19.0 %copy-start.1 = (bf16[4096,1024]{1,0:T(8,128)(2,1)S(1)}, bf16[4096,1024]{1,0:T(8,128)(2,1)}, u32[]{:S(2)}) copy-start(bf16[4096,1024]{1,0:T(8,128)(2,1)} %param.5) | copy-start | bytes 25165828
  35.0 9.1 %collective-permute-start.4 = (bf16[512,1024]{1,0:T(8,128)(2,1)}, bf16[512,1024]{1,0:T(8,128)(2,1)S(1)}, u32[]{:S(2)}, u32[]{:S(2)}) collective-permute-start(bf16[512,1024]{1,0:T(8,128)(2,1)} %collective-permute-done.1.refs_0_), channel_id=1, source_target_pairs={{0,8},{8,0},{1,9},{9,1},{2,10},{10,2},{3,11},{11,3},{4,12},{12,4},... | collective-permute-start | bytes 3145736 | tf_op jit(solution)/shard_map/ppermute | solution.py:377
  36.1 11.2 %collective-permute-start.5 = (bf16[512,1024]{1,0:T(8,128)(2,1)S(1)}, bf16[512,1024]{1,0:T(8,128)(2,1)S(1)}, u32[]{:S(2)}, u32[]{:S(2)}) collective-permute-start(bf16[512,1024]{1,0:T(8,128)(2,1)S(1)} %collective-permute-done.2.refs_1_), channel_id=1, source_target_pairs={{0,8},{8,0},{1,9},{9,1},{2,10},{10,2},{3,11},{11,3},{4,12},{12,4},... | collective-permute-start | bytes 3145736 | tf_op jit(solution)/shard_map/ppermute | solution.py:377
  36.4 11.0 %collective-permute-start.6 = (bf16[512,1024]{1,0:T(8,128)(2,1)S(1)}, bf16[512,1024]{1,0:T(8,128)(2,1)S(1)}, u32[]{:S(2)}, u32[]{:S(2)}) collective-permute-start(bf16[512,1024]{1,0:T(8,128)(2,1)S(1)} %collective-permute-done.3.refs_2_), channel_id=1, source_target_pairs={{0,8},{8,0},{1,9},{9,1},{2,10},{10,2},{3,11},{11,3},{4,12},{12,4},... | collective-permute-start | bytes 3145736 | tf_op jit(solution)/shard_map/ppermute | solution.py:377
  36.9 15.9 %collective-permute-start.7 = (bf16[512,1024]{1,0:T(8,128)(2,1)}, bf16[512,1024]{1,0:T(8,128)(2,1)S(1)}, u32[]{:S(2)}, u32[]{:S(2)}) collective-permute-start(bf16[512,1024]{1,0:T(8,128)(2,1)} %collective-permute-done.1.refs_0_), channel_id=1, source_target_pairs={{0,32},{8,104},{32,64},{40,8},{64,96},{72,40},{96,0},{104,72},{1,3... | collective-permute-start | bytes 3145736 | tf_op jit(solution)/shard_map/ppermute | solution.py:412
  38.3 14.4 %collective-permute-start.8 = (bf16[512,1024]{1,0:T(8,128)(2,1)S(1)}, bf16[512,1024]{1,0:T(8,128)(2,1)S(1)}, u32[]{:S(2)}, u32[]{:S(2)}) collective-permute-start(bf16[512,1024]{1,0:T(8,128)(2,1)S(1)} %get-tuple-element.62), channel_id=1, source_target_pairs={{0,1},{8,25},{1,16},{9,8},{16,17},{24,9},{17,0},{25,24},{2,3},{10,... | collective-permute-start | bytes 3145736 | tf_op jit(solution)/shard_map/ppermute | solution.py:425
  44.1 18.2 %collective-permute-start.10 = (bf16[512,1024]{1,0:T(8,128)(2,1)S(1)}, bf16[512,1024]{1,0:T(8,128)(2,1)S(1)}, u32[]{:S(2)}, u32[]{:S(2)}) collective-permute-start(bf16[512,1024]{1,0:T(8,128)(2,1)S(1)} %get-tuple-element.45), channel_id=1, source_target_pairs={{0,32},{8,104},{32,64},{40,8},{64,96},{72,40},{96,0},{104,72},{1,3... | collective-permute-start | bytes 3145736 | tf_op jit(solution)/shard_map/ppermute | solution.py:412
  52.8 15.2 %collective-permute-start.11 = (bf16[512,1024]{1,0:T(8,128)(2,1)S(1)}, bf16[512,1024]{1,0:T(8,128)(2,1)S(1)}, u32[]{:S(2)}, u32[]{:S(2)}) collective-permute-start(bf16[512,1024]{1,0:T(8,128)(2,1)S(1)} %collective-permute-done.8), channel_id=1, source_target_pairs={{0,1},{8,25},{1,16},{9,8},{16,17},{24,9},{17,0},{25,24},{2,3},{10,... | collective-permute-start | bytes 3145736 | tf_op jit(solution)/shard_map/ppermute | solution.py:425
  56.2 13.1 %collective-permute-start.9 = (bf16[512,1024]{1,0:T(8,128)(2,1)S(1)}, bf16[512,1024]{1,0:T(8,128)(2,1)S(1)}, u32[]{:S(2)}, u32[]{:S(2)}) collective-permute-start(bf16[512,1024]{1,0:T(8,128)(2,1)S(1)} %collective-permute-done.7.refs_0_), channel_id=1, source_target_pairs={{0,8},{8,0},{1,9},{9,1},{2,10},{10,2},{3,11},{11,3},{4,12},{12,4},... | collective-permute-start | bytes 3145736 | tf_op jit(solution)/shard_map/ppermute | solution.py:377
  62.3 7.0 %collective-permute-start.12 = (bf16[512,1024]{1,0:T(8,128)(2,1)S(1)}, bf16[512,1024]{1,0:T(8,128)(2,1)S(1)}, u32[]{:S(2)}, u32[]{:S(2)}) collective-permute-start(bf16[512,1024]{1,0:T(8,128)(2,1)S(1)} %collective-permute-done.10.refs_2_), channel_id=1, source_target_pairs={{0,8},{8,0},{1,9},{9,1},{2,10},{10,2},{3,11},{11,3},{4,12},{12,4},... | collective-permute-start | bytes 3145736 | tf_op jit(solution)/shard_map/ppermute | solution.py:377
  64.4 13.9 %collective-permute-start.13 = (bf16[512,1024]{1,0:T(8,128)(2,1)S(1)}, bf16[512,1024]{1,0:T(8,128)(2,1)S(1)}, u32[]{:S(2)}, u32[]{:S(2)}) collective-permute-start(bf16[512,1024]{1,0:T(8,128)(2,1)S(1)} %collective-permute-done.7.refs_0_), channel_id=1, source_target_pairs={{0,32},{8,104},{32,64},{40,8},{64,96},{72,40},{96,0},{104,72},{1,3... | collective-permute-start | bytes 3145736 | tf_op jit(solution)/shard_map/ppermute | solution.py:412
  67.9 12.6 %collective-permute-start.15 = (bf16[512,1024]{1,0:T(8,128)(2,1)S(1)}, bf16[512,1024]{1,0:T(8,128)(2,1)S(1)}, u32[]{:S(2)}, u32[]{:S(2)}) collective-permute-start(bf16[512,1024]{1,0:T(8,128)(2,1)S(1)} %collective-permute-done.11.refs_3_), channel_id=1, source_target_pairs={{0,8},{8,0},{1,9},{9,1},{2,10},{10,2},{3,11},{11,3},{4,12},{12,4},... | collective-permute-start | bytes 3145736 | tf_op jit(solution)/shard_map/ppermute | solution.py:377
  69.3 11.1 %copy-start.2 = (s32[512]{0:T(512)S(1)}, s32[512]{0:T(512)}, u32[]{:S(2)}) copy-start(s32[512]{0:T(512)} %param.6) | copy-start | bytes 6148
  78.3 4.5 %collective-permute-start.14 = (bf16[512,1024]{1,0:T(8,128)(2,1)S(1)}, bf16[512,1024]{1,0:T(8,128)(2,1)S(1)}, u32[]{:S(2)}, u32[]{:S(2)}) collective-permute-start(bf16[512,1024]{1,0:T(8,128)(2,1)S(1)} %collective-permute-done.13.refs_1_), channel_id=1, source_target_pairs={{0,8},{8,0},{1,9},{9,1},{2,10},{10,2},{3,11},{11,3},{4,12},{12,4},... | collective-permute-start | bytes 3145736 | tf_op jit(solution)/shard_map/ppermute | solution.py:377
  105.5 1.3 collective-permute-start.16
  139.8 4.6 %collective-permute-start.17 = (bf16[8,80,512]{2,1,0:T(8,128)(2,1)S(1)}, bf16[8,80,512]{2,1,0:T(8,128)(2,1)S(1)}, u32[]{:S(2)}, u32[]{:S(2)}) collective-permute-start(bf16[8,80,512]{2,1,0:T(8,128)(2,1)S(1)} %all_to_all.27.refs_0_), channel_id=1, source_target_pairs={{0,8},{8,0},{1,9},{9,1},{2,10},{10,2},{3,11},{11,3},{4,12},{12,4},... | collective-permute-start | bytes 1966088 | tf_op jit(solution)/shard_map/ppermute | solution.py:377
  149.5 15.3 %all-to-all-start.3 = ((bf16[8,80,512]{2,1,0:T(8,128)(2,1)}), bf16[8,80,512]{2,1,0:T(8,128)(2,1)S(1)}, u32[]{:S(2)}, u32[]{:S(2)}) async-start(bf16[8,80,512]{2,1,0:T(8,128)(2,1)} %product.3), calls=%async_computation.3 | async-start | bytes 1310720 | tf_op jit(solution)/shard_map/all_to_all | solution.py:529
  168.3 1.5 collective-permute-start.18
  188.0 2.8 %collective-permute-start.19 = (f32[16,128]{1,0:T(8,128)S(1)}, f32[16,128]{1,0:T(8,128)S(1)}, u32[]{:S(2)}, u32[]{:S(2)}) collective-permute-start(f32[16,128]{1,0:T(8,128)S(1)} %reduce_sum.99), channel_id=1, source_target_pairs={{0,8},{8,0},{1,9},{9,1},{2,10},{10,2},{3,11},{11,3},{4,12},{12,4},... | collective-permute-start | bytes 24584 | tf_op jit(solution)/shard_map/ppermute | solution.py:377

commit v16 on v15

--- a/solution.py
+++ b/solution.py
@@ -306,19 +306,19 @@
     work = jnp.concatenate([gram, (rows == columns).astype(F32)], axis=1)
     index = lax.broadcasted_iota(jnp.int32, (K, 2 * K), 0)
     pivots = jnp.ones((K, 2 * K), F32)
-    for start in range(0, K, 16):
+    for start in range(0, K, 32):
         index = index[-(K - start) :]
         spread = [
-            jnp.broadcast_to(work[start:, j : j + 1], (K - start, 2 * K)) for j in range(start, start + 16)
+            jnp.broadcast_to(work[start:, j : j + 1], (K - start, 2 * K)) for j in range(start, start + 32)
         ]
         rest = work[start:]
         below = pivots[start:]
-        for a in range(16):
+        for a in range(32):
             pivot = spread[a][a : a + 1, :]
             below = jnp.where(index == start + a, pivot, below)
             ratio = jnp.where(index > start + a, spread[a] * (1.0 / pivot), 0.0)
             rest = rest - ratio * rest[a : a + 1, :]
-            for b in range(a + 1, 16):
+            for b in range(a + 1, 32):
                 spread[b] = spread[b] - ratio * spread[b][a : a + 1, :]
         work = jnp.concatenate([work[:start], rest], axis=0) if start else rest
         pivots = jnp.concatenate([pivots[:start], below], axis=0) if start else below

time: 195 us -> 196 us (level)
  Pallas kernels: 35.4 us -> 29.3 us
  starting transfers between devices: 36 us -> 39.2 us
  waiting for transfers between devices: 42.1 us -> 44.6 us
    pallas_call x6, Pallas kernels: 18.4 us -> 12.7 us  [build(): pl.pallas_call(functools.partial(build_kernel, first, arrived), out_shape...]
    ppermute x12, starting transfers between devices: 14.4 us -> 17.9 us  [swap_cores(): return lax.ppermute(value, 'core', [(0, 1), (1, 0)])]
  transfers between devices with their start and end apart: 21 -> 21, of which waited for: 10 -> 11; matrix products, arithmetic and copies ran while one was open for 4% -> 4% of each run, Pallas kernels for 8% -> 6%
where the time goes in v16:
time: 196 us; the launch traced here: 195 us
  blocking collectives  67.6 us (34%)
  waiting for transfers between devices  44.6 us (23%)
  starting transfers between devices  39.2 us (20%)
  Pallas kernels  29.3 us (15%)
  local copies, waits for them, and re-layouts  7.31 us (4%)
  other arithmetic  6.29 us (3%)
    all_to_all x2, blocking collectives, share(): lax.all_to_all(jnp.broadcast_to(value[None], (size,) + value.shape), axes...  35.6 us
    all_to_all x1, blocking collectives, shards(): lax.all_to_all(jnp.broadcast_to(sent[None], (8,) + sent.shape).reshape(8...  20 us
    ppermute x12, starting transfers between devices, swap_cores(): return lax.ppermute(value, 'core', [(0, 1), (1, 0)])  17.9 us
    pallas_call x6, Pallas kernels, build(): pl.pallas_call(functools.partial(build_kernel, first, arrived), out_shape...  12.7 us
    all_to_all x1, blocking collectives, shards(): parts = lax.all_to_all(running, COL, 0, 0, tiled=True)  12 us
    ppermute x3, waiting for transfers between devices, apart(): lax.ppermute(value, ('y', 'core'), [(2 * i + k, 2 * ((i + 1 + 2 * k) % 4)...  11.8 us
    all_to_all x1, waiting for transfers between devices, shards(): parts = lax.all_to_all(running, COL, 0, 0, tiled=True)  10.6 us
    pallas_call x3, Pallas kernels, local(): pl.pallas_call(kernel, out_shape=out_shape, in_specs=[pl.BlockSpec(memory...  8.88 us
  transfers between devices with their start and end apart: 21, of which 11 were waited for; matrix products, arithmetic and copies ran while one was open for 4% of the time, Pallas kernels for 6%

profile of v16, /device:TPU:1, one launch (start us, length us, event | category | flops | bytes accessed | tf_op | source)
XLA Modules:
  0.0 195.4 jit_solution(7534953925130859353)
XLA Ops:
  5.7 2.3 %dynamic-slice_bitcast_fusion = bf16[512,1024]{1,0:T(8,128)(2,1)} fusion(bf16[8,512,1024]{2,1,0:T(8,128)(2,1)} %bitcast.37, s32[]{:T(128)S(6)} %select_n.198), kind=kLoop, calls=%fused_computation.1 | loop fusion | bytes 2097156 | tf_op jit(solution)/shard_map/jit(dynamic_index_in_dim)/squeeze | solution.py:486
  7.9 3.8 %collective-permute-start.1 = (bf16[512,1024]{1,0:T(8,128)(2,1)}, bf16[512,1024]{1,0:T(8,128)(2,1)}, u32[]{:S(2)}, u32[]{:S(2)}) collective-permute-start(bf16[512,1024]{1,0:T(8,128)(2,1)} %dynamic-slice_bitcast_fusion), channel_id=1, source_target_pairs={{0,17},{17,0},{1,16},{16,1},{2,19},{19,2},{3,18},{18,3},{4,21},{21... | collective-permute-start | bytes 3145736 | tf_op jit(solution)/shard_map/ppermute | solution.py:429
  11.7 5.1 %multiply_reduce_fusion = f32[4096]{0:T(1024)S(1)} fusion(bf16[4096,1024]{1,0:T(8,128)(2,1)} %param.5), kind=kLoop, calls=%fused_computation | loop fusion | flops 12578816 | bytes 8404992 | tf_op jit(solution)/shard_map/reduce_sum | solution.py:488
  18.6 3.4 %copy-done = bf16[4096,1024]{1,0:T(8,128)(2,1)S(1)} copy-done((bf16[4096,1024]{1,0:T(8,128)(2,1)S(1)}, bf16[4096,1024]{1,0:T(8,128)(2,1)}, u32[]{:S(2)}) %copy-start) | copy-done | bytes 8388632
  22.0 4.2 %build_tiles.6 = (bf16[24,512,512]{2,1,0:T(8,128)(2,1)}, f32[8,512]{1,0:T(8,128)S(1)}) custom-call(s32[121]{0:T(128)S(1)} %concatenate.13.info, bf16[8,512,1024]{2,1,0:T(8,128)(2,1)S(1)} %bitcast.38, f32[8,512]{1,0:T(8,128)S(1)} %mul.134.half_rows, bf16[512,1024]{1,0:T(8,128)(2,1)S(1)} %dynamic-slice_bitcast_fusion.1.refs_0_, ...), custom_call_target="tpu_custom_call" | custom-call | flops 1610612736 | bytes 7864320 | tf_op jit(solution)/shard_map/build_tiles/pallas_call | solution.py:114
  26.2 8.7 %collective-permute-done.1.refs_0_ = bf16[512,1024]{1,0:T(8,128)(2,1)} collective-permute-done((bf16[512,1024]{1,0:T(8,128)(2,1)}, bf16[512,1024]{1,0:T(8,128)(2,1)}, u32[]{:S(2)}, u32[]{:S(2)}) %collective-permute-start.1) | collective-permute-done | bytes 1048608 | tf_op jit(solution)/shard_map/ppermute | solution.py:429
  38.3 2.7 %collective-permute-start.8 = (bf16[512,1024]{1,0:T(8,128)(2,1)S(1)}, bf16[512,1024]{1,0:T(8,128)(2,1)S(1)}, u32[]{:S(2)}, u32[]{:S(2)}) collective-permute-start(bf16[512,1024]{1,0:T(8,128)(2,1)S(1)} %get-tuple-element.62), channel_id=1, source_target_pairs={{0,1},{8,25},{1,16},{9,8},{16,17},{24,9},{17,0},{25,24},{2,3},{10,... | collective-permute-start | bytes 3145736 | tf_op jit(solution)/shard_map/ppermute | solution.py:425
  42.4 3.1 %collective-permute-start.10 = (bf16[512,1024]{1,0:T(8,128)(2,1)S(1)}, bf16[512,1024]{1,0:T(8,128)(2,1)S(1)}, u32[]{:S(2)}, u32[]{:S(2)}) collective-permute-start(bf16[512,1024]{1,0:T(8,128)(2,1)S(1)} %get-tuple-element.45), channel_id=1, source_target_pairs={{0,32},{8,104},{32,64},{40,8},{64,96},{72,40},{96,0},{104,72},{1,3... | collective-permute-start | bytes 3145736 | tf_op jit(solution)/shard_map/ppermute | solution.py:412
  45.5 2.5 %build_tiles.8 = (bf16[24,512,512]{2,1,0:T(8,128)(2,1)}, f32[8,512]{1,0:T(8,128)S(1)}) custom-call(s32[121]{0:T(128)S(1)} %concatenate.13.info, bf16[8,512,1024]{2,1,0:T(8,128)(2,1)S(1)} %bitcast.40, f32[8,512]{1,0:T(8,128)S(1)} %mul.134.half_rows, bf16[512,1024]{1,0:T(8,128)(2,1)S(1)} %collective-permute-done.4.refs_0_, ...), custom_call_target="tpu_custom_call", output_to_operand_aliasing={{0}: (6, {})} | custom-call | flops 2147483648 | bytes 10485760 | tf_op jit(solution)/shard_map/build_tiles/pallas_call | solution.py:114
  48.1 4.7 %collective-permute-done.8 = bf16[512,1024]{1,0:T(8,128)(2,1)S(1)} collective-permute-done((bf16[512,1024]{1,0:T(8,128)(2,1)S(1)}, bf16[512,1024]{1,0:T(8,128)(2,1)S(1)}, u32[]{:S(2)}, u32[]{:S(2)}) %collective-permute-start.8) | collective-permute-done | bytes 1048608 | tf_op jit(solution)/shard_map/ppermute | solution.py:425
  52.8 3.4 %collective-permute-start.11 = (bf16[512,1024]{1,0:T(8,128)(2,1)S(1)}, bf16[512,1024]{1,0:T(8,128)(2,1)S(1)}, u32[]{:S(2)}, u32[]{:S(2)}) collective-permute-start(bf16[512,1024]{1,0:T(8,128)(2,1)S(1)} %collective-permute-done.8), channel_id=1, source_target_pairs={{0,1},{8,25},{1,16},{9,8},{16,17},{24,9},{17,0},{25,24},{2,3},{10,... | collective-permute-start | bytes 3145736 | tf_op jit(solution)/shard_map/ppermute | solution.py:425
  56.2 6.1 %collective-permute-done.10.refs_2_ = bf16[512,1024]{1,0:T(8,128)(2,1)S(1)} collective-permute-done((bf16[512,1024]{1,0:T(8,128)(2,1)S(1)}, bf16[512,1024]{1,0:T(8,128)(2,1)S(1)}, u32[]{:S(2)}, u32[]{:S(2)}) %collective-permute-start.10) | collective-permute-done | bytes 1048608 | tf_op jit(solution)/shard_map/ppermute | solution.py:412
  62.3 2.2 %collective-permute-start.12 = (bf16[512,1024]{1,0:T(8,128)(2,1)S(1)}, bf16[512,1024]{1,0:T(8,128)(2,1)S(1)}, u32[]{:S(2)}, u32[]{:S(2)}) collective-permute-start(bf16[512,1024]{1,0:T(8,128)(2,1)S(1)} %collective-permute-done.10.refs_2_), channel_id=1, source_target_pairs={{0,8},{8,0},{1,9},{9,1},{2,10},{10,2},{3,11},{11,3},{4,12},{12,4},... | collective-permute-start | bytes 3145736 | tf_op jit(solution)/shard_map/ppermute | solution.py:377
  64.9 3.0 %collective-permute-done.11.refs_3_ = bf16[512,1024]{1,0:T(8,128)(2,1)S(1)} collective-permute-done((bf16[512,1024]{1,0:T(8,128)(2,1)S(1)}, bf16[512,1024]{1,0:T(8,128)(2,1)S(1)}, u32[]{:S(2)}, u32[]{:S(2)}) %collective-permute-start.11) | collective-permute-done | bytes 1048608 | tf_op jit(solution)/shard_map/ppermute | solution.py:425
  69.3 3.3 %build_tiles.9 = (bf16[24,512,512]{2,1,0:T(8,128)(2,1)}, f32[8,512]{1,0:T(8,128)S(1)}) custom-call(s32[121]{0:T(128)S(1)} %concatenate.13.info, bf16[8,512,1024]{2,1,0:T(8,128)(2,1)S(1)} %bitcast.41, f32[8,512]{1,0:T(8,128)S(1)} %mul.134.half_rows, bf16[512,1024]{1,0:T(8,128)(2,1)S(1)} %collective-permute-done.7.refs_0_, ...), custom_call_target="tpu_custom_call", output_to_operand_aliasing={{0}: (8, {})} | custom-call | flops 3758096384 | bytes 18350080 | tf_op jit(solution)/shard_map/build_tiles/pallas_call | solution.py:114
  72.6 5.8 %collective-permute-done.13.refs_1_ = bf16[512,1024]{1,0:T(8,128)(2,1)S(1)} collective-permute-done((bf16[512,1024]{1,0:T(8,128)(2,1)S(1)}, bf16[512,1024]{1,0:T(8,128)(2,1)S(1)}, u32[]{:S(2)}, u32[]{:S(2)}) %collective-permute-start.13) | collective-permute-done | bytes 1048608 | tf_op jit(solution)/shard_map/ppermute | solution.py:412
  78.3 2.1 %collective-permute-start.14 = (bf16[512,1024]{1,0:T(8,128)(2,1)S(1)}, bf16[512,1024]{1,0:T(8,128)(2,1)S(1)}, u32[]{:S(2)}, u32[]{:S(2)}) collective-permute-start(bf16[512,1024]{1,0:T(8,128)(2,1)S(1)} %collective-permute-done.13.refs_1_), channel_id=1, source_target_pairs={{0,8},{8,0},{1,9},{9,1},{2,10},{10,2},{3,11},{11,3},{4,12},{12,4},... | collective-permute-start | bytes 3145736 | tf_op jit(solution)/shard_map/ppermute | solution.py:377
  81.2 1.5 collective-permute-done.14.refs_0_
  83.4 20.0 %all_to_all.25 = f32[64,8,128]{2,1,0:T(8,128)S(1)} all-to-all(f32[64,8,128]{2,1,0:T(8,128)S(1)} %bitcast.46), channel_id=1, replica_groups=mesh['y'=4,'zh'=2,'core'=2,'x'=4,'zl'=2] {'y','zh','x','zl'}, dimensions={0} | all-to-all | bytes 524288 | tf_op jit(solution)/shard_map/all_to_all | solution.py:516
  103.4 3.0 %collective-permute-start.16 = (f32[8,8,128]{2,1,0:T(8,128)S(1)}, f32[8,8,128]{2,1,0:T(8,128)S(1)}, u32[]{:S(2)}, u32[]{:S(2)}) collective-permute-start(f32[8,8,128]{2,1,0:T(8,128)S(1)} %bitcast_reduce_fusion.refs_0_.known), channel_id=1, source_target_pairs={{0,8},{8,0},{1,9},{9,1},{2,10},{10,2},{3,11},{11,3},{4,12},{12,4},... | collective-permute-start | bytes 98312 | tf_op jit(solution)/shard_map/ppermute | solution.py:377
  107.3 3.3 %product.2 = bf16[8,64,512]{2,1,0:T(8,128)(2,1)S(1)} custom-call(s32[121]{0:T(128)S(1)} %concatenate.13.info, bf16[24,512,512]{2,1,0:T(8,128)(2,1)} %get-tuple-element.55.tiles, f32[8,8,128]{2,1,0:T(8,128)S(1)} %bitcast_reduce_fusion.refs_0_.known, f32[8,8,128]{2,1,0:T(8,128)S(1)} %collective-permute-done.16.refs_1_), custom_call_target="tpu_custom_call" | custom-call | tf_op jit(solution)/shard_map/product/pallas_call | solution.py:240
  110.6 12.0 %all_to_all.26.parts = bf16[8,64,512]{2,1,0:T(8,128)(2,1)S(1)} all-to-all(bf16[8,64,512]{2,1,0:T(8,128)(2,1)S(1)} %product.2), channel_id=1, replica_groups=mesh['y'=4,'zh'=2,'core'=2,'x'=4,'zl'=2] {'x','zl'}, dimensions={0} | all-to-all | bytes 1048576 | tf_op jit(solution)/shard_map/all_to_all | solution.py:524
  123.8 16.6 %all_to_all.27.refs_0_ = bf16[8,80,512]{2,1,0:T(8,128)(2,1)S(1)} all-to-all(bf16[8,80,512]{2,1,0:T(8,128)(2,1)S(1)} %broadcast_in_dim.112), channel_id=1, replica_groups=mesh['y'=4,'zh'=2,'core'=2,'x'=4,'zl'=2] {'y','zh'}, dimensions={0} | all-to-all | bytes 1310720 | tf_op jit(solution)/shard_map/all_to_all | solution.py:382
  140.4 2.8 %collective-permute-start.17 = (bf16[8,80,512]{2,1,0:T(8,128)(2,1)S(1)}, bf16[8,80,512]{2,1,0:T(8,128)(2,1)S(1)}, u32[]{:S(2)}, u32[]{:S(2)}) collective-permute-start(bf16[8,80,512]{2,1,0:T(8,128)(2,1)S(1)} %all_to_all.27.refs_0_), channel_id=1, source_target_pairs={{0,8},{8,0},{1,9},{9,1},{2,10},{10,2},{3,11},{11,3},{4,12},{12,4},... | collective-permute-start | bytes 1966088 | tf_op jit(solution)/shard_map/ppermute | solution.py:377
  143.2 1.7 collective-permute-done.17.refs_1_
  144.9 4.4 %product.3 = bf16[8,80,512]{2,1,0:T(8,128)(2,1)} custom-call(s32[121]{0:T(128)S(1)} %concatenate.13.info, bf16[24,512,512]{2,1,0:T(8,128)(2,1)} %get-tuple-element.55.tiles, bf16[8,80,512]{2,1,0:T(8,128)(2,1)S(1)} %all_to_all.27.refs_0_, bf16[8,80,512]{2,1,0:T(8,128)(2,1)S(1)} %collective-permute-done.17.refs_1_, f32[8,512]{1,0:T(8,128)S(1)} %get-tuple-element.56.refs_2_), custom_call_target="tpu_custom_call" | custom-call | tf_op jit(solution)/shard_map/product/pallas_call | solution.py:240
  149.3 3.6 %all-to-all-start.3 = ((bf16[8,80,512]{2,1,0:T(8,128)(2,1)}), bf16[8,80,512]{2,1,0:T(8,128)(2,1)S(1)}, u32[]{:S(2)}, u32[]{:S(2)}) async-start(bf16[8,80,512]{2,1,0:T(8,128)(2,1)} %product.3), calls=%async_computation.3 | async-start | bytes 1310720 | tf_op jit(solution)/shard_map/all_to_all | solution.py:529
  152.9 10.6 %all-to-all-done.3.parts = bf16[8,80,512]{2,1,0:T(8,128)(2,1)S(1)} async-done(((bf16[8,80,512]{2,1,0:T(8,128)(2,1)}), bf16[8,80,512]{2,1,0:T(8,128)(2,1)S(1)}, u32[]{:S(2)}, u32[]{:S(2)}) %all-to-all-start.3) | async-done | bytes 655392 | tf_op jit(solution)/shard_map/all_to_all | solution.py:529
  163.5 3.9 %middle.1 = (f32[64,512]{1,0:T(8,128)S(1)}, f32[32,128]{1,0:T(8,128)S(1)}) custom-call(s32[121]{0:T(128)S(1)} %concatenate.13.info, bf16[8,80,512]{2,1,0:T(8,128)(2,1)S(1)} %all-to-all-done.3.parts, f32[8,8,128]{2,1,0:T(8,128)S(1)} %bitcast_reduce_fusion.refs_0_.known, f32[8,8,8,128]{3,2,1,0:T(8,128)S(1)} %bitcast.44), custom_call_target="tpu_custom_call" | custom-call | tf_op jit(solution)/shard_map/middle/pallas_call | solution.py:366
  169.6 19.1 %all_to_all.28 = f32[64,16,128]{2,1,0:T(8,128)S(1)} all-to-all(f32[64,16,128]{2,1,0:T(8,128)S(1)} %broadcast_in_dim.113), channel_id=1, replica_groups=mesh['y'=4,'zh'=2,'core'=2,'x'=4,'zl'=2] {'y','zh','x','zl'}, dimensions={0} | all-to-all | bytes 1048576 | tf_op jit(solution)/shard_map/all_to_all | solution.py:382
  188.7 2.0 collective-permute-start.19
  191.5 3.9 %last.1 = f32[64,512]{1,0:T(8,128)} custom-call(s32[121]{0:T(128)S(1)} %concatenate.13.info, f32[32,128]{1,0:T(8,128)S(1)} %pad_maximum_fusion.1.message, f32[64,512]{1,0:T(8,128)S(1)} %get-tuple-element.58.image, f32[8,8,128]{2,1,0:T(8,128)S(1)} %bitcast_reduce_fusion.refs_0_.known), custom_call_target="tpu_custom_call" | custom-call | tf_op jit(solution)/shard_map/last/pallas_call | solution.py:366
  (67 shorter events, 19.9 us)
Async XLA Ops:
  0.0 17.6 %copy-start.3 = (s32[1,1,24]{2,1,0:T(1,128)S(1)}, s32[1,1,24]{2,1,0:T(1,128)}, u32[]{:S(2)}) copy-start(s32[1,1,24]{2,1,0:T(1,128)} %param.8) | copy-start | bytes 292
  0.0 17.9 %copy-start.4 = (s32[1,1,24]{2,1,0:T(1,128)S(1)}, s32[1,1,24]{2,1,0:T(1,128)}, u32[]{:S(2)}) copy-start(s32[1,1,24]{2,1,0:T(1,128)} %param.7) | copy-start | bytes 292
  1.3 17.3 %collective-permute-start = (bf16[512,1024]{1,0:T(8,128)(2,1)S(1)}, bf16[512,1024]{1,0:T(8,128)(2,1)}, u32[]{:S(2)}, u32[]{:S(2)}) collective-permute-start(bf16[512,1024]{1,0:T(8,128)(2,1)S(1)} %dynamic-slice_bitcast_fusion.1.refs_0_), channel_id=1, source_target_pairs={{0,8},{8,0},{1,9},{9,1},{2,10},{10,2},{3,11},{11,3},{4,12},{12,4},... | collective-permute-start | bytes 3145736 | tf_op jit(solution)/shard_map/ppermute | solution.py:377
  2.8 32.2 %collective-permute-start.2 = (bf16[512,1024]{1,0:T(8,128)(2,1)S(1)}, bf16[512,1024]{1,0:T(8,128)(2,1)S(1)}, u32[]{:S(2)}, u32[]{:S(2)}) collective-permute-start(bf16[512,1024]{1,0:T(8,128)(2,1)S(1)} %dynamic-slice_bitcast_fusion.1.refs_0_), channel_id=1, source_target_pairs={{0,32},{32,64},{64,96},{96,0},{1,33},{33,65},{65,97},{97,1},{2,34}... | collective-permute-start | bytes 3145736 | tf_op jit(solution)/shard_map/ppermute | solution.py:404
  4.2 30.8 %collective-permute-start.3 = (bf16[512,1024]{1,0:T(8,128)(2,1)S(1)}, bf16[512,1024]{1,0:T(8,128)(2,1)S(1)}, u32[]{:S(2)}, u32[]{:S(2)}) collective-permute-start(bf16[512,1024]{1,0:T(8,128)(2,1)S(1)} %dynamic-slice_bitcast_fusion.1.refs_0_), channel_id=1, source_target_pairs={{0,96},{32,0},{64,32},{96,64},{1,97},{33,1},{65,33},{97,65},{2,98}... | collective-permute-start | bytes 3145736 | tf_op jit(solution)/shard_map/ppermute | solution.py:408
  7.9 27.1 %collective-permute-start.1 = (bf16[512,1024]{1,0:T(8,128)(2,1)}, bf16[512,1024]{1,0:T(8,128)(2,1)}, u32[]{:S(2)}, u32[]{:S(2)}) collective-permute-start(bf16[512,1024]{1,0:T(8,128)(2,1)} %dynamic-slice_bitcast_fusion), channel_id=1, source_target_pairs={{0,17},{17,0},{1,16},{16,1},{2,19},{19,2},{3,18},{18,3},{4,21},{21... | collective-permute-start | bytes 3145736 | tf_op jit(solution)/shard_map/ppermute | solution.py:429
  18.6 3.4 %copy-start = (bf16[4096,1024]{1,0:T(8,128)(2,1)S(1)}, bf16[4096,1024]{1,0:T(8,128)(2,1)}, u32[]{:S(2)}) copy-start(bf16[4096,1024]{1,0:T(8,128)(2,1)} %param.5) | copy-start | bytes 25165828
  22.0 19.0 %copy-start.1 = (bf16[4096,1024]{1,0:T(8,128)(2,1)S(1)}, bf16[4096,1024]{1,0:T(8,128)(2,1)}, u32[]{:S(2)}) copy-start(bf16[4096,1024]{1,0:T(8,128)(2,1)} %param.5) | copy-start | bytes 25165828
  35.0 7.4 %collective-permute-start.4 = (bf16[512,1024]{1,0:T(8,128)(2,1)}, bf16[512,1024]{1,0:T(8,128)(2,1)S(1)}, u32[]{:S(2)}, u32[]{:S(2)}) collective-permute-start(bf16[512,1024]{1,0:T(8,128)(2,1)} %collective-permute-done.1.refs_0_), channel_id=1, source_target_pairs={{0,8},{8,0},{1,9},{9,1},{2,10},{10,2},{3,11},{11,3},{4,12},{12,4},... | collective-permute-start | bytes 3145736 | tf_op jit(solution)/shard_map/ppermute | solution.py:377
  36.1 9.4 %collective-permute-start.5 = (bf16[512,1024]{1,0:T(8,128)(2,1)S(1)}, bf16[512,1024]{1,0:T(8,128)(2,1)S(1)}, u32[]{:S(2)}, u32[]{:S(2)}) collective-permute-start(bf16[512,1024]{1,0:T(8,128)(2,1)S(1)} %collective-permute-done.2.refs_1_), channel_id=1, source_target_pairs={{0,8},{8,0},{1,9},{9,1},{2,10},{10,2},{3,11},{11,3},{4,12},{12,4},... | collective-permute-start | bytes 3145736 | tf_op jit(solution)/shard_map/ppermute | solution.py:377
  36.4 9.2 %collective-permute-start.6 = (bf16[512,1024]{1,0:T(8,128)(2,1)S(1)}, bf16[512,1024]{1,0:T(8,128)(2,1)S(1)}, u32[]{:S(2)}, u32[]{:S(2)}) collective-permute-start(bf16[512,1024]{1,0:T(8,128)(2,1)S(1)} %collective-permute-done.3.refs_2_), channel_id=1, source_target_pairs={{0,8},{8,0},{1,9},{9,1},{2,10},{10,2},{3,11},{11,3},{4,12},{12,4},... | collective-permute-start | bytes 3145736 | tf_op jit(solution)/shard_map/ppermute | solution.py:377
  36.9 15.9 %collective-permute-start.7 = (bf16[512,1024]{1,0:T(8,128)(2,1)}, bf16[512,1024]{1,0:T(8,128)(2,1)S(1)}, u32[]{:S(2)}, u32[]{:S(2)}) collective-permute-start(bf16[512,1024]{1,0:T(8,128)(2,1)} %collective-permute-done.1.refs_0_), channel_id=1, source_target_pairs={{0,32},{8,104},{32,64},{40,8},{64,96},{72,40},{96,0},{104,72},{1,3... | collective-permute-start | bytes 3145736 | tf_op jit(solution)/shard_map/ppermute | solution.py:412
  38.3 14.4 %collective-permute-start.8 = (bf16[512,1024]{1,0:T(8,128)(2,1)S(1)}, bf16[512,1024]{1,0:T(8,128)(2,1)S(1)}, u32[]{:S(2)}, u32[]{:S(2)}) collective-permute-start(bf16[512,1024]{1,0:T(8,128)(2,1)S(1)} %get-tuple-element.62), channel_id=1, source_target_pairs={{0,1},{8,25},{1,16},{9,8},{16,17},{24,9},{17,0},{25,24},{2,3},{10,... | collective-permute-start | bytes 3145736 | tf_op jit(solution)/shard_map/ppermute | solution.py:425
  42.4 19.9 %collective-permute-start.10 = (bf16[512,1024]{1,0:T(8,128)(2,1)S(1)}, bf16[512,1024]{1,0:T(8,128)(2,1)S(1)}, u32[]{:S(2)}, u32[]{:S(2)}) collective-permute-start(bf16[512,1024]{1,0:T(8,128)(2,1)S(1)} %get-tuple-element.45), channel_id=1, source_target_pairs={{0,32},{8,104},{32,64},{40,8},{64,96},{72,40},{96,0},{104,72},{1,3... | collective-permute-start | bytes 3145736 | tf_op jit(solution)/shard_map/ppermute | solution.py:412
  52.8 15.2 %collective-permute-start.11 = (bf16[512,1024]{1,0:T(8,128)(2,1)S(1)}, bf16[512,1024]{1,0:T(8,128)(2,1)S(1)}, u32[]{:S(2)}, u32[]{:S(2)}) collective-permute-start(bf16[512,1024]{1,0:T(8,128)(2,1)S(1)} %collective-permute-done.8), channel_id=1, source_target_pairs={{0,1},{8,25},{1,16},{9,8},{16,17},{24,9},{17,0},{25,24},{2,3},{10,... | collective-permute-start | bytes 3145736 | tf_op jit(solution)/shard_map/ppermute | solution.py:425
  56.2 13.1 %collective-permute-start.9 = (bf16[512,1024]{1,0:T(8,128)(2,1)S(1)}, bf16[512,1024]{1,0:T(8,128)(2,1)S(1)}, u32[]{:S(2)}, u32[]{:S(2)}) collective-permute-start(bf16[512,1024]{1,0:T(8,128)(2,1)S(1)} %collective-permute-done.7.refs_0_), channel_id=1, source_target_pairs={{0,8},{8,0},{1,9},{9,1},{2,10},{10,2},{3,11},{11,3},{4,12},{12,4},... | collective-permute-start | bytes 3145736 | tf_op jit(solution)/shard_map/ppermute | solution.py:377
  62.3 7.0 %collective-permute-start.12 = (bf16[512,1024]{1,0:T(8,128)(2,1)S(1)}, bf16[512,1024]{1,0:T(8,128)(2,1)S(1)}, u32[]{:S(2)}, u32[]{:S(2)}) collective-permute-start(bf16[512,1024]{1,0:T(8,128)(2,1)S(1)} %collective-permute-done.10.refs_2_), channel_id=1, source_target_pairs={{0,8},{8,0},{1,9},{9,1},{2,10},{10,2},{3,11},{11,3},{4,12},{12,4},... | collective-permute-start | bytes 3145736 | tf_op jit(solution)/shard_map/ppermute | solution.py:377
  64.4 13.9 %collective-permute-start.13 = (bf16[512,1024]{1,0:T(8,128)(2,1)S(1)}, bf16[512,1024]{1,0:T(8,128)(2,1)S(1)}, u32[]{:S(2)}, u32[]{:S(2)}) collective-permute-start(bf16[512,1024]{1,0:T(8,128)(2,1)S(1)} %collective-permute-done.7.refs_0_), channel_id=1, source_target_pairs={{0,32},{8,104},{32,64},{40,8},{64,96},{72,40},{96,0},{104,72},{1,3... | collective-permute-start | bytes 3145736 | tf_op jit(solution)/shard_map/ppermute | solution.py:412
  67.9 12.6 %collective-permute-start.15 = (bf16[512,1024]{1,0:T(8,128)(2,1)S(1)}, bf16[512,1024]{1,0:T(8,128)(2,1)S(1)}, u32[]{:S(2)}, u32[]{:S(2)}) collective-permute-start(bf16[512,1024]{1,0:T(8,128)(2,1)S(1)} %collective-permute-done.11.refs_3_), channel_id=1, source_target_pairs={{0,8},{8,0},{1,9},{9,1},{2,10},{10,2},{3,11},{11,3},{4,12},{12,4},... | collective-permute-start | bytes 3145736 | tf_op jit(solution)/shard_map/ppermute | solution.py:377
  69.3 11.1 %copy-start.2 = (s32[512]{0:T(512)S(1)}, s32[512]{0:T(512)}, u32[]{:S(2)}) copy-start(s32[512]{0:T(512)} %param.6) | copy-start | bytes 6148
  78.3 4.4 %collective-permute-start.14 = (bf16[512,1024]{1,0:T(8,128)(2,1)S(1)}, bf16[512,1024]{1,0:T(8,128)(2,1)S(1)}, u32[]{:S(2)}, u32[]{:S(2)}) collective-permute-start(bf16[512,1024]{1,0:T(8,128)(2,1)S(1)} %collective-permute-done.13.refs_1_), channel_id=1, source_target_pairs={{0,8},{8,0},{1,9},{9,1},{2,10},{10,2},{3,11},{11,3},{4,12},{12,4},... | collective-permute-start | bytes 3145736 | tf_op jit(solution)/shard_map/ppermute | solution.py:377
  103.4 3.9 %collective-permute-start.16 = (f32[8,8,128]{2,1,0:T(8,128)S(1)}, f32[8,8,128]{2,1,0:T(8,128)S(1)}, u32[]{:S(2)}, u32[]{:S(2)}) collective-permute-start(f32[8,8,128]{2,1,0:T(8,128)S(1)} %bitcast_reduce_fusion.refs_0_.known), channel_id=1, source_target_pairs={{0,8},{8,0},{1,9},{9,1},{2,10},{10,2},{3,11},{11,3},{4,12},{12,4},... | collective-permute-start | bytes 98312 | tf_op jit(solution)/shard_map/ppermute | solution.py:377
  140.4 4.5 %collective-permute-start.17 = (bf16[8,80,512]{2,1,0:T(8,128)(2,1)S(1)}, bf16[8,80,512]{2,1,0:T(8,128)(2,1)S(1)}, u32[]{:S(2)}, u32[]{:S(2)}) collective-permute-start(bf16[8,80,512]{2,1,0:T(8,128)(2,1)S(1)} %all_to_all.27.refs_0_), channel_id=1, source_target_pairs={{0,8},{8,0},{1,9},{9,1},{2,10},{10,2},{3,11},{11,3},{4,12},{12,4},... | collective-permute-start | bytes 1966088 | tf_op jit(solution)/shard_map/ppermute | solution.py:377
  149.3 14.2 %all-to-all-start.3 = ((bf16[8,80,512]{2,1,0:T(8,128)(2,1)}), bf16[8,80,512]{2,1,0:T(8,128)(2,1)S(1)}, u32[]{:S(2)}, u32[]{:S(2)}) async-start(bf16[8,80,512]{2,1,0:T(8,128)(2,1)} %product.3), calls=%async_computation.3 | async-start | bytes 1310720 | tf_op jit(solution)/shard_map/all_to_all | solution.py:529
  167.4 2.1 %collective-permute-start.18 = (f32[16,128]{1,0:T(8,128)S(1)}, f32[16,128]{1,0:T(8,128)S(1)}, u32[]{:S(2)}, u32[]{:S(2)}) collective-permute-start(f32[16,128]{1,0:T(8,128)S(1)} %constant_dynamic-slice_fusion), channel_id=1, source_target_pairs={{0,8},{8,0},{1,9},{9,1},{2,10},{10,2},{3,11},{11,3},{4,12},{12,4},... | collective-permute-start | bytes 24584 | tf_op jit(solution)/shard_map/ppermute | solution.py:377
  188.7 2.8 %collective-permute-start.19 = (f32[16,128]{1,0:T(8,128)S(1)}, f32[16,128]{1,0:T(8,128)S(1)}, u32[]{:S(2)}, u32[]{:S(2)}) collective-permute-start(f32[16,128]{1,0:T(8,128)S(1)} %reduce_sum.99), channel_id=1, source_target_pairs={{0,8},{8,0},{1,9},{9,1},{2,10},{10,2},{3,11},{11,3},{4,12},{12,4},... | collective-permute-start | bytes 24584 | tf_op jit(solution)/shard_map/ppermute | solution.py:377
